TPU v7x, 32 devices: a whole 2x2x4 slice. The times are simulated.
32 devices in a mesh: dp: 2 (over z_hi), head: 8 (over y, x, core), state: 2 (over z_lo).
Axes of the slice: x: 2, y: 2, z: 4 (z_hi: 2, z_lo: 2; z = z_hi * 2 + z_lo), core: 2. Of those that a mesh axis runs over, the one named last changes fastest.
Arguments:
- hidden: bfloat16 [4096, 2048], P(('dp', 'state')), may hold values from -6 to 6
- embedding: bfloat16 [4096, 2048], P(('dp', 'state')), may hold values from -6 to 6
- cotangent: bfloat16 [4096, 2048], P('dp'), may hold values from -6 to 6
- lengths: int32 [2, 4], P('dp'), may hold values from 1 to 1024, as said below
- gain_attn: bfloat16 [4096], P(('dp', 'state')), may hold values from 0.5 to 1.5
- w_query: bfloat16 [4096, 4096], P(('dp', 'state'), 'head'), may hold values from -0.09375 to 0.09375
- w_key: bfloat16 [4096, 4096], P(('dp', 'state'), 'head'), may hold values from -0.09375 to 0.09375
- w_value: bfloat16 [4096, 4096], P(('dp', 'state'), 'head'), may hold values from -0.09375 to 0.09375
- down_query: bfloat16 [4096, 128], P(('dp', 'state')), may hold values from -0.09375 to 0.09375
- down_key: bfloat16 [4096, 128], P(('dp', 'state')), may hold values from -0.09375 to 0.09375
- down_value: bfloat16 [4096, 128], P(('dp', 'state')), may hold values from -0.09375 to 0.09375
- up_query: bfloat16 [128, 4096], P(('dp', 'state'), 'head'), may hold values from -0.5 to 0.5
- up_key: bfloat16 [128, 4096], P(('dp', 'state'), 'head'), may hold values from -0.5 to 0.5
- up_value: bfloat16 [128, 4096], P(('dp', 'state'), 'head'), may hold values from -0.5 to 0.5
- attn_output: bfloat16 [4096, 2048], P('head', ('dp', 'state')), may hold values from -0.25 to 0.25
- gain_mlp: bfloat16 [2048], P(('dp', 'state')), may hold values from 0.5 to 1.5
- mlp_input: bfloat16 [2048, 8192], P(('dp', 'state'), 'head'), may hold values from -0.125 to 0.125
- down_mlp: bfloat16 [2048, 128], P(('dp', 'state')), may hold values from -0.125 to 0.125
- up_mlp: bfloat16 [128, 8192], P(('dp', 'state'), 'head'), may hold values from -0.5 to 0.5
- mlp_output: bfloat16 [8192, 2048], P('head', ('dp', 'state')), may hold values from -0.0625 to 0.0625
- gain_mixer: bfloat16 [2048], P(('dp', 'state')), may hold values from 0.5 to 1.5
- proj_inner: bfloat16 [2048, 4096], P(('dp', 'state'), 'head'), may hold values from -0.125 to 0.125
- proj_gate: bfloat16 [2048, 4096], P(('dp', 'state'), 'head'), may hold values from -0.125 to 0.125
- proj_step: bfloat16 [2048, 64], P(('dp', 'state'), 'head'), may hold values from -0.125 to 0.125
- proj_input: bfloat16 [2048, 64], replicated, may hold values from -0.125 to 0.125
- proj_read: bfloat16 [2048, 64], replicated, may hold values from -0.125 to 0.125
- taps_inner: bfloat16 [4, 4096], P(None, 'head'), may hold values from -3 to 3
- taps_input: bfloat16 [4, 64], replicated, may hold values from -3 to 3
- taps_read: bfloat16 [4, 64], replicated, may hold values from -3 to 3
- step_bias: bfloat16 [64], P('head'), may hold values from -4 to -1
- log_rate: bfloat16 [64], P('head'), may hold values from -2.5 to 1.5
- skip_gain: bfloat16 [64], P('head'), may hold values from 0.5 to 1.5
- gain_gated: bfloat16 [4096], P('head'), may hold values from 0.5 to 1.5
- proj_output: bfloat16 [4096, 2048], P('head', ('dp', 'state')), may hold values from -0.09375 to 0.09375
Outputs:
- layer_out: bfloat16 [4096, 2048], P('dp')
- grad_hidden: bfloat16 [4096, 2048], P(('dp', 'state'))
- grad_embedding: bfloat16 [4096, 2048], P(('dp', 'state'))
- grad_gain_attn: float32 [4096], P(('dp', 'state'))
- grad_w_query: float32 [4096, 4096], P(('dp', 'state'), 'head')
- grad_w_key: float32 [4096, 4096], P(('dp', 'state'), 'head')
- grad_w_value: float32 [4096, 4096], P(('dp', 'state'), 'head')
- grad_down_query: float32 [4096, 128], P(('dp', 'state'))
- grad_down_key: float32 [4096, 128], P(('dp', 'state'))
- grad_down_value: float32 [4096, 128], P(('dp', 'state'))
- grad_up_query: float32 [128, 4096], P(('dp', 'state'), 'head')
- grad_up_key: float32 [128, 4096], P(('dp', 'state'), 'head')
- grad_up_value: float32 [128, 4096], P(('dp', 'state'), 'head')
- grad_attn_output: float32 [4096, 2048], P('head', ('dp', 'state'))
- grad_gain_mlp: float32 [2048], P(('dp', 'state'))
- grad_mlp_input: float32 [2048, 8192], P(('dp', 'state'), 'head')
- grad_down_mlp: float32 [2048, 128], P(('dp', 'state'))
- grad_up_mlp: float32 [128, 8192], P(('dp', 'state'), 'head')
- grad_mlp_output: float32 [8192, 2048], P('head', ('dp', 'state'))
- grad_gain_mixer: float32 [2048], P(('dp', 'state'))
- grad_proj_inner: float32 [2048, 4096], P(('dp', 'state'), 'head')
- grad_proj_gate: float32 [2048, 4096], P(('dp', 'state'), 'head')
- grad_proj_step: float32 [2048, 64], P(('dp', 'state'), 'head')
- grad_proj_input: float32 [2048, 64], replicated
- grad_proj_read: float32 [2048, 64], replicated
- grad_taps_inner: float32 [4, 4096], P(None, 'head')
- grad_taps_input: float32 [4, 64], replicated
- grad_taps_read: float32 [4, 64], replicated
- grad_step_bias: float32 [64], P('head')
- grad_log_rate: float32 [64], P('head')
- grad_skip_gain: float32 [64], P('head')
- grad_gain_gated: float32 [4096], P('head')
- grad_proj_output: float32 [4096, 2048], P('head', ('dp', 'state'))
- grad_norm: float32 [], replicated
Inputs may be any that keep to these rules, and one draw needn't show every extreme that they name: `lengths`: each row has 4 documents and a padding tail of 1 to 256 positions; the second document starts before position 768 and ends at or after position 1280.
All inputs are finite; a program needn't handle non-finite values.
Results may differ from a plain program's by a relative error of at most 0.028.
The roundings to bfloat16 on the way count: a program that leaves them out, or rounds other values in their place, can miss the bound.
Values may be sent and summed in bfloat16 or wider, within the bound.
No kernel may reach another device: no remote copies, remote signals or barrier semaphores. Data moves between devices by JAX's collectives and lax.ppermute only.
A program may use at most 448 MiB of HBM per device.

v0:
```python
import jax
import jax.numpy as jnp
from jax import lax
from jax.sharding import PartitionSpec as P

HDIM = 128
MDIM = 64
DIN = 4096
GROUP = 256


highest = lax.Precision.HIGHEST
epsilon = 1e-05


def plain_dot(left, right):
    return jnp.dot(left, right, preferred_element_type=jnp.float32)


def left_dot(left, right):
    return lax.dot_general(
        left, right, (((0,), (0,)), ((), ())), preferred_element_type=jnp.float32
    )


def right_dot(left, right):
    return lax.dot_general(
        left, right, (((1,), (1,)), ((), ())), preferred_element_type=jnp.float32
    )


def exact_left(left, right):
    return lax.dot_general(
        left.astype(jnp.float32), right, (((0,), (0,)), ((), ())), precision=highest
    )


def exact_right(left, right):
    return lax.dot_general(
        left, right.astype(jnp.float32), (((1,), (1,)), ((), ())), precision=highest
    )


def rms_norm(values, gain):
    return values * lax.rsqrt(jnp.mean(values * values, -1, keepdims=True) + epsilon) * gain


def row_layout(doc_lengths, length):
    ends = jnp.cumsum(doc_lengths)
    places = jnp.arange(length, dtype=jnp.int32)
    segment = jnp.sum((places[:, None] >= ends[None, :]).astype(jnp.int32), axis=1)
    starts = jnp.concatenate([ends - doc_lengths, ends[-1:]])
    choose = segment[:, None] == jnp.arange(starts.shape[0], dtype=jnp.int32)[None, :]
    first_place = jnp.sum(jnp.where(choose, starts[None, :], 0), axis=1)
    position = (places - first_place).astype(jnp.float32)
    valid = (segment < doc_lengths.shape[0]).astype(jnp.float32)
    return (segment, position, valid)


def rotate(values, position):
    half = values.shape[-1] // 2
    freqs = 10000.0 ** (-jnp.arange(half, dtype=jnp.float32) / half)
    angle = position[:, None] * freqs[None, :]
    cosine = jnp.cos(angle)[:, None, :]
    sine = jnp.sin(angle)[:, None, :]
    former = values[..., :half]
    latter = values[..., half:]
    return jnp.concatenate([former * cosine - latter * sine, former * sine + latter * cosine], -1)


def head_probs(query_in, key_in, allowed):
    scale = query_in.shape[-1] ** (-0.5)
    scores = (
        jnp.einsum("thd,shd->hts", query_in, key_in, preferred_element_type=jnp.float32) * scale
    )
    scores = jnp.where(allowed[None, :, :], scores, -1e30)
    shifted = scores - jnp.max(scores, -1, keepdims=True)
    weights = jnp.exp(shifted)
    return weights / jnp.sum(weights, -1, keepdims=True)


def conv_mask(values, taps, segment):
    total = taps[0][None, :] * values
    for offset in range(1, taps.shape[0]):
        moved = jnp.concatenate(
            [jnp.zeros((offset, values.shape[1]), values.dtype), values[:-offset]], 0
        )
        moved_seg = jnp.concatenate([jnp.full((offset,), -1, jnp.int32), segment[:-offset]], 0)
        same = (moved_seg == segment).astype(values.dtype)[:, None]
        total = total + taps[offset][None, :] * moved * same
    return total


def state_scan(inputs, step_sizes, decay, input_vecs, read_vecs, segment, block):
    length, heads, width = inputs.shape
    count = length // block
    states = input_vecs.shape[1]

    def one_block(carry, pieces):
        state, before = carry
        group_in, group_dt, group_b, group_c, group_seg = pieces
        logs = group_dt * decay[None, :]
        cumul = jnp.cumsum(logs, 0)
        places = jnp.arange(block, dtype=jnp.int32)
        allowed = (group_seg[:, None] == group_seg[None, :]) & (places[None, :] <= places[:, None])
        gaps = cumul[:, None, :] - cumul[None, :, :]
        fading = jnp.where(
            allowed[:, :, None], jnp.exp(jnp.where(allowed[:, :, None], gaps, 0.0)), 0.0
        )
        inner = jnp.dot(group_c, group_b.T, precision=highest)
        scaled = group_in * group_dt[:, :, None]
        local_out = jnp.einsum(
            "tsh,shp->thp", inner[:, :, None] * fading, scaled, precision=highest
        )
        carried = (group_seg == before).astype(inputs.dtype)
        entry = jnp.exp(cumul) * carried[:, None]
        from_state = (
            jnp.einsum("tn,hnp->thp", group_c, state, precision=highest) * entry[:, :, None]
        )
        last_seg = group_seg[-1]
        reach = (group_seg == last_seg).astype(inputs.dtype)
        to_end = jnp.exp(cumul[-1][None, :] - cumul) * reach[:, None]
        retain = jnp.exp(cumul[-1]) * (last_seg == before).astype(inputs.dtype)
        fresh = jnp.einsum("sn,sh,shp->hnp", group_b, to_end, scaled, precision=highest)
        state = state * retain[:, None, None] + fresh
        return ((state, last_seg), local_out + from_state)

    pieces = (
        inputs.reshape(count, block, heads, width),
        step_sizes.reshape(count, block, heads),
        input_vecs.reshape(count, block, states),
        read_vecs.reshape(count, block, states),
        segment.reshape(count, block),
    )
    start = (jnp.zeros((heads, states, width), inputs.dtype), jnp.array(-1, jnp.int32))
    unused, outputs = lax.scan(jax.checkpoint(one_block), start, pieces)
    return outputs.reshape(length, heads, width)


def mixer_core(
    inner_pre,
    input_pre,
    read_pre,
    step_pre,
    taps_x,
    taps_b,
    taps_c,
    shift_in,
    rate_in,
    segment,
    width,
    block,
):
    inner_conv = jax.nn.silu(conv_mask(inner_pre, taps_x, segment))
    input_conv = jax.nn.silu(conv_mask(input_pre, taps_b, segment))
    read_conv = jax.nn.silu(conv_mask(read_pre, taps_c, segment))
    step_sizes = jax.nn.softplus(step_pre + shift_in[None, :])
    heads = step_sizes.shape[1]
    length = inner_conv.shape[0]
    outputs = state_scan(
        inner_conv.reshape(length, heads, width),
        step_sizes,
        -jnp.exp(rate_in),
        input_conv,
        read_conv,
        segment,
        block,
    )
    return (outputs.reshape(length, heads * width), inner_conv)


def place_slice(piece, index, parts, axis):
    shape = list(piece.shape)
    shape[axis] = shape[axis] * parts
    holder = jnp.zeros(tuple(shape), jnp.float32)
    return lax.dynamic_update_slice_in_dim(holder, piece, index * piece.shape[axis], axis)


def take_slice(whole, index, width, axis):
    return lax.dynamic_slice_in_dim(whole, index * width, width, axis)


def per_device(
    hidden,
    embedding,
    cotangent,
    lengths,
    gain_attn,
    w_query,
    w_key,
    w_value,
    down_query,
    down_key,
    down_value,
    up_query,
    up_key,
    up_value,
    attn_output,
    gain_mlp,
    mlp_input,
    down_mlp,
    up_mlp,
    mlp_output,
    gain_mixer,
    proj_inner,
    proj_gate,
    proj_step,
    proj_input,
    proj_read,
    taps_inner,
    taps_input,
    taps_read,
    step_bias,
    log_rate,
    skip_gain,
    gain_gated,
    proj_output,
):
    row_count = hidden.shape[0]
    length = cotangent.shape[0]
    model_width = hidden.shape[1]
    head_parts = lax.axis_size("head")
    state_parts = lax.axis_size("state")
    state_index = lax.axis_index("state")
    head_index = lax.axis_index("head")
    own_start = state_index * row_count
    segment, position, valid = row_layout(lengths[0], length)
    own_segment = lax.dynamic_slice_in_dim(segment, own_start, row_count)
    own_position = lax.dynamic_slice_in_dim(position, own_start, row_count)
    own_valid = lax.dynamic_slice_in_dim(valid, own_start, row_count)[:, None]
    full_valid = valid[:, None]
    places = jnp.arange(length, dtype=jnp.int32)
    own_places = own_start + jnp.arange(row_count, dtype=jnp.int32)
    own_mask = ((places >= own_start) & (places < own_start + row_count)).astype(jnp.float32)[
        :, None
    ]
    allowed = (own_segment[:, None] == segment[None, :]) & (places[None, :] <= own_places[:, None])
    gathered = (
        lax.all_gather(gain_attn, ("dp", "state"), axis=0, tiled=True),
        lax.all_gather(w_query, ("dp", "state"), axis=0, tiled=True),
        lax.all_gather(w_key, ("dp", "state"), axis=0, tiled=True),
        lax.all_gather(w_value, ("dp", "state"), axis=0, tiled=True),
        lax.all_gather(down_query, ("dp", "state"), axis=0, tiled=True),
        lax.all_gather(down_key, ("dp", "state"), axis=0, tiled=True),
        lax.all_gather(down_value, ("dp", "state"), axis=0, tiled=True),
        lax.all_gather(up_query, ("dp", "state"), axis=0, tiled=True),
        lax.all_gather(up_key, ("dp", "state"), axis=0, tiled=True),
        lax.all_gather(up_value, ("dp", "state"), axis=0, tiled=True),
        lax.all_gather(attn_output, ("dp", "state"), axis=1, tiled=True),
        lax.all_gather(gain_mlp, ("dp", "state"), axis=0, tiled=True),
        lax.all_gather(mlp_input, ("dp", "state"), axis=0, tiled=True),
        lax.all_gather(down_mlp, ("dp", "state"), axis=0, tiled=True),
        lax.all_gather(up_mlp, ("dp", "state"), axis=0, tiled=True),
        lax.all_gather(mlp_output, ("dp", "state"), axis=1, tiled=True),
        lax.all_gather(gain_mixer, ("dp", "state"), axis=0, tiled=True),
        lax.all_gather(proj_inner, ("dp", "state"), axis=0, tiled=True),
        lax.all_gather(proj_gate, ("dp", "state"), axis=0, tiled=True),
        lax.all_gather(proj_step, ("dp", "state"), axis=0, tiled=True),
        lax.all_gather(proj_output, ("dp", "state"), axis=1, tiled=True),
    )
    (
        attn_gain,
        query_main,
        key_main,
        value_main,
        query_down,
        key_down,
        value_down,
        query_upper,
        key_upper,
        value_upper,
        attn_proj,
        mlp_gain,
        mlp_main,
        mlp_down,
        mlp_upper,
        mlp_proj,
        mixer_gain,
        inner_main,
        gate_main,
        step_main,
        output_main,
    ) = gathered
    joined = jnp.concatenate([hidden, embedding], 1).astype(jnp.float32)
    attn_gain_f = attn_gain.astype(jnp.float32)
    normed = rms_norm(joined, attn_gain_f).astype(jnp.bfloat16)
    head_count = query_main.shape[1] // HDIM

    def project(main, down, upper):
        reduced = plain_dot(normed, down).astype(jnp.bfloat16)
        return (plain_dot(normed, main) + plain_dot(reduced, upper), reduced)

    query_pre, query_red = project(query_main, query_down, query_upper)
    key_pre, key_red = project(key_main, key_down, key_upper)
    value_pre, value_red = project(value_main, value_down, value_upper)
    queries = rotate(query_pre.reshape(row_count, head_count, HDIM), own_position).astype(
        jnp.bfloat16
    )
    keys_own = rotate(key_pre.reshape(row_count, head_count, HDIM), own_position).astype(
        jnp.bfloat16
    )
    values_own = value_pre.reshape(row_count, head_count, HDIM).astype(jnp.bfloat16)
    keys_all, values_all = (
        lax.all_gather(keys_own, "state", axis=0, tiled=True),
        lax.all_gather(values_own, "state", axis=0, tiled=True),
    )
    probs_full = head_probs(queries, keys_all, allowed)
    attended_f = jnp.einsum(
        "hts,shd->thd",
        probs_full.astype(jnp.bfloat16),
        values_all,
        preferred_element_type=jnp.float32,
    )
    attended = attended_f.reshape(row_count, head_count * HDIM).astype(jnp.bfloat16)
    branch = lax.psum(plain_dot(attended, attn_proj), "head")
    first = hidden.astype(jnp.float32) + own_valid * branch
    mlp_gain_f = mlp_gain.astype(jnp.float32)
    mlp_normed = rms_norm(first, mlp_gain_f).astype(jnp.bfloat16)
    mlp_red = plain_dot(mlp_normed, mlp_down).astype(jnp.bfloat16)
    hidden_pre = plain_dot(mlp_normed, mlp_main) + plain_dot(mlp_red, mlp_upper)
    activated = jax.nn.gelu(hidden_pre, approximate=False).astype(jnp.bfloat16)
    mlp_branch = lax.psum(plain_dot(activated, mlp_proj), "head")
    second = first + own_valid * mlp_branch
    second_all = lax.all_gather(second, "state", axis=0, tiled=True)
    mixer_gain_f = mixer_gain.astype(jnp.float32)
    mixer_normed = rms_norm(second_all, mixer_gain_f).astype(jnp.bfloat16)
    states_own = proj_input.shape[1] // state_parts
    input_half = take_slice(proj_input, state_index, states_own, 1)
    read_half = take_slice(proj_read, state_index, states_own, 1)
    taps_input_half = take_slice(taps_input, state_index, states_own, 1).astype(jnp.float32)
    taps_read_half = take_slice(taps_read, state_index, states_own, 1).astype(jnp.float32)
    inner_pre = plain_dot(mixer_normed, inner_main)
    gate_pre = plain_dot(mixer_normed, gate_main)
    step_pre = plain_dot(mixer_normed, step_main)
    input_pre = plain_dot(mixer_normed, input_half)
    read_pre = plain_dot(mixer_normed, read_half)

    def mixer_piece(
        inner_in, input_in, read_in, step_in, taps_x, taps_b, taps_c, shift_in, rate_in
    ):
        return mixer_core(
            inner_in,
            input_in,
            read_in,
            step_in,
            taps_x,
            taps_b,
            taps_c,
            shift_in,
            rate_in,
            segment,
            MDIM,
            GROUP,
        )

    (scanned_part, inner_conv), mixer_back = jax.vjp(
        mixer_piece,
        inner_pre,
        input_pre,
        read_pre,
        step_pre,
        taps_inner.astype(jnp.float32),
        taps_input_half,
        taps_read_half,
        step_bias.astype(jnp.float32),
        log_rate.astype(jnp.float32),
    )
    scanned = lax.psum(scanned_part, "state")
    skip_full = jnp.repeat(skip_gain.astype(jnp.float32), MDIM)[None, :]
    combined = scanned + skip_full * inner_conv
    gate_act = jax.nn.silu(gate_pre)
    united = combined * gate_act
    squares = lax.psum(jnp.sum(united * united, 1), "head")
    row_scale = lax.rsqrt(squares / DIN + epsilon)[:, None]
    gated_gain = gain_gated.astype(jnp.float32)[None, :]
    united_own = lax.dynamic_slice_in_dim(united, own_start, row_count, 0)
    scale_own = lax.dynamic_slice_in_dim(row_scale, own_start, row_count, 0)
    gated_own = (united_own * scale_own * gated_gain).astype(jnp.bfloat16)
    mixed_own = lax.psum(plain_dot(gated_own, output_main), "head")
    mixed = lax.all_gather(mixed_own, "state", axis=0, tiled=True)
    layer_out = (second_all + full_valid * mixed).astype(jnp.bfloat16)
    upstream = cotangent.astype(jnp.float32)
    mix_grad = (full_valid * upstream).astype(jnp.bfloat16)
    mix_grad_own = lax.dynamic_slice_in_dim(mix_grad, own_start, row_count, 0)
    grad_output_main = left_dot(gated_own, mix_grad_own)
    gated_grad = right_dot(mix_grad, output_main)
    row_total = jnp.sum(mix_grad.astype(jnp.float32) * mixed, 1)[:, None] / row_scale
    grad_gated_gain = jnp.sum(gated_grad * united * row_scale * own_mask, 0)
    united_grad = (
        row_scale * gated_gain * gated_grad
        - united * row_scale * row_scale * row_scale * row_total / DIN
    )
    combined_grad = united_grad * gate_act
    sigmoid_gate = jax.nn.sigmoid(gate_pre)
    gate_grad = (
        united_grad * combined * sigmoid_gate * (1.0 + gate_pre * (1.0 - sigmoid_gate)) * own_mask
    )
    mixer_heads = step_pre.shape[1]
    grad_skip = jnp.sum(
        (combined_grad * inner_conv * own_mask).reshape(length, mixer_heads, MDIM), (0, 2)
    )
    conv_extra = skip_full * combined_grad * own_mask
    (
        inner_grad,
        input_grad,
        read_grad,
        step_grad,
        grad_taps_x,
        grad_taps_b,
        grad_taps_c,
        grad_shift,
        grad_rate,
    ) = mixer_back((combined_grad, conv_extra))
    mixer_part = (
        exact_right(inner_grad, inner_main)
        + exact_right(gate_grad, gate_main)
        + exact_right(step_grad, step_main)
        + exact_right(input_grad, input_half)
        + exact_right(read_grad, read_half)
    )
    grad_inner_main = exact_left(mixer_normed, inner_grad)
    grad_gate_main = exact_left(mixer_normed, gate_grad)
    grad_step_main = exact_left(mixer_normed, step_grad)
    grad_input_half = exact_left(mixer_normed, input_grad)
    grad_read_half = exact_left(mixer_normed, read_grad)
    mixer_rows_own = lax.psum_scatter(mixer_part, "state", scatter_dimension=0, tiled=True)
    mixer_own = lax.psum(mixer_rows_own, "head")
    unused_norm, second_back = jax.vjp(rms_norm, second, mixer_gain_f)
    second_norm_grad, grad_mixer_gain = second_back(mixer_own)
    upstream_own = lax.dynamic_slice_in_dim(upstream, own_start, row_count, 0)
    second_grad = upstream_own + second_norm_grad
    mlp_grad = (own_valid * second_grad).astype(jnp.bfloat16)
    grad_mlp_proj = left_dot(activated, mlp_grad)
    activated_grad = right_dot(mlp_grad, mlp_proj)
    unused_gelu, gelu_back = jax.vjp(
        lambda preact: jax.nn.gelu(preact, approximate=False), hidden_pre
    )
    hidden_grad = gelu_back(activated_grad)[0].astype(jnp.bfloat16)
    grad_mlp_main = left_dot(mlp_normed, hidden_grad)
    grad_mlp_upper = left_dot(mlp_red, hidden_grad)
    mlp_middle = right_dot(hidden_grad, mlp_upper)
    mlp_part = right_dot(hidden_grad, mlp_main)
    mlp_sum, middle_sum = lax.psum((mlp_part, mlp_middle), "head")
    middle_low = middle_sum.astype(jnp.bfloat16)
    mlp_normed_grad = mlp_sum + right_dot(middle_low, mlp_down)
    grad_mlp_down = left_dot(mlp_normed, middle_low)
    unused_first, first_back = jax.vjp(rms_norm, first, mlp_gain_f)
    first_norm_grad, grad_mlp_gain = first_back(mlp_normed_grad)
    first_grad = second_grad + first_norm_grad
    branch_grad = (own_valid * first_grad).astype(jnp.bfloat16)
    grad_attn_proj = left_dot(attended, branch_grad)
    attended_grad = right_dot(branch_grad, attn_proj).reshape(row_count, head_count, HDIM)
    probs_back = head_probs(queries, keys_all, allowed)
    score_scale = HDIM ** (-0.5)
    out_low = attended_grad.astype(jnp.bfloat16)
    prob_grad = jnp.einsum("thd,shd->hts", out_low, values_all, preferred_element_type=jnp.float32)
    score_grad = probs_back * (prob_grad - jnp.sum(probs_back * prob_grad, -1, keepdims=True))
    score_low = score_grad.astype(jnp.bfloat16)
    query_back = (
        jnp.einsum("hts,shd->thd", score_low, keys_all, preferred_element_type=jnp.float32)
        * score_scale
    )
    keys_back = (
        jnp.einsum("hts,thd->shd", score_low, queries, preferred_element_type=jnp.float32)
        * score_scale
    )
    values_back = jnp.einsum(
        "hts,thd->shd", probs_back.astype(jnp.bfloat16), out_low, preferred_element_type=jnp.float32
    )
    keys_grad_own, values_grad_own = (
        lax.psum_scatter(keys_back, "state", scatter_dimension=0, tiled=True),
        lax.psum_scatter(values_back, "state", scatter_dimension=0, tiled=True),
    )
    query_grad = (
        rotate(query_back, -own_position).reshape(row_count, head_count * HDIM).astype(jnp.bfloat16)
    )
    key_grad = (
        rotate(keys_grad_own, -own_position)
        .reshape(row_count, head_count * HDIM)
        .astype(jnp.bfloat16)
    )
    value_grad = values_grad_own.reshape(row_count, head_count * HDIM).astype(jnp.bfloat16)
    grad_query_main = left_dot(normed, query_grad)
    grad_key_main = left_dot(normed, key_grad)
    grad_value_main = left_dot(normed, value_grad)
    grad_query_upper = left_dot(query_red, query_grad)
    grad_key_upper = left_dot(key_red, key_grad)
    grad_value_upper = left_dot(value_red, value_grad)
    query_middle = right_dot(query_grad, query_upper)
    key_middle = right_dot(key_grad, key_upper)
    value_middle = right_dot(value_grad, value_upper)
    normed_part = (
        right_dot(query_grad, query_main)
        + right_dot(key_grad, key_main)
        + right_dot(value_grad, value_main)
    )
    normed_sum, query_msum, key_msum, value_msum = lax.psum(
        (normed_part, query_middle, key_middle, value_middle), "head"
    )
    query_low = query_msum.astype(jnp.bfloat16)
    key_low = key_msum.astype(jnp.bfloat16)
    value_low = value_msum.astype(jnp.bfloat16)
    normed_grad = (
        normed_sum
        + right_dot(query_low, query_down)
        + right_dot(key_low, key_down)
        + right_dot(value_low, value_down)
    )
    grad_query_down = left_dot(normed, query_low)
    grad_key_down = left_dot(normed, key_low)
    grad_value_down = left_dot(normed, value_low)
    unused_joined, joined_back = jax.vjp(rms_norm, joined, attn_gain_f)
    joined_grad, grad_attn_gain = joined_back(normed_grad)
    grad_hidden = (first_grad + joined_grad[:, :model_width]).astype(jnp.bfloat16)
    grad_embedding = joined_grad[:, model_width:].astype(jnp.bfloat16)
    scattered = (
        lax.psum_scatter(grad_attn_gain, ("dp", "state"), scatter_dimension=0, tiled=True),
        lax.psum_scatter(grad_query_main, ("dp", "state"), scatter_dimension=0, tiled=True),
        lax.psum_scatter(grad_key_main, ("dp", "state"), scatter_dimension=0, tiled=True),
        lax.psum_scatter(grad_value_main, ("dp", "state"), scatter_dimension=0, tiled=True),
        lax.psum_scatter(grad_query_down, ("dp", "state"), scatter_dimension=0, tiled=True),
        lax.psum_scatter(grad_key_down, ("dp", "state"), scatter_dimension=0, tiled=True),
        lax.psum_scatter(grad_value_down, ("dp", "state"), scatter_dimension=0, tiled=True),
        lax.psum_scatter(grad_query_upper, ("dp", "state"), scatter_dimension=0, tiled=True),
        lax.psum_scatter(grad_key_upper, ("dp", "state"), scatter_dimension=0, tiled=True),
        lax.psum_scatter(grad_value_upper, ("dp", "state"), scatter_dimension=0, tiled=True),
        lax.psum_scatter(grad_attn_proj, ("dp", "state"), scatter_dimension=1, tiled=True),
        lax.psum_scatter(grad_mlp_gain, ("dp", "state"), scatter_dimension=0, tiled=True),
        lax.psum_scatter(grad_mlp_main, ("dp", "state"), scatter_dimension=0, tiled=True),
        lax.psum_scatter(grad_mlp_down, ("dp", "state"), scatter_dimension=0, tiled=True),
        lax.psum_scatter(grad_mlp_upper, ("dp", "state"), scatter_dimension=0, tiled=True),
        lax.psum_scatter(grad_mlp_proj, ("dp", "state"), scatter_dimension=1, tiled=True),
        lax.psum_scatter(grad_mixer_gain, ("dp", "state"), scatter_dimension=0, tiled=True),
        lax.psum_scatter(grad_inner_main, ("dp", "state"), scatter_dimension=0, tiled=True),
        lax.psum_scatter(grad_gate_main, ("dp", "state"), scatter_dimension=0, tiled=True),
        lax.psum_scatter(grad_step_main, ("dp", "state"), scatter_dimension=0, tiled=True),
        lax.psum_scatter(grad_output_main, ("dp", "state"), scatter_dimension=1, tiled=True),
    )
    first_head = (head_index == 0).astype(jnp.float32)
    square_sum = jnp.zeros((), jnp.float32)
    for index in [1, 2, 3, 7, 8, 9, 10, 12, 14, 15]:
        square_sum = square_sum + jnp.sum(scattered[index] * scattered[index])
    for index in [4, 5, 6, 13]:
        square_sum = square_sum + first_head * jnp.sum(scattered[index] * scattered[index])
    head_params = jnp.stack([grad_shift, grad_rate, grad_skip], 0)
    totals = lax.psum(
        (
            square_sum,
            place_slice(grad_gated_gain, head_index, head_parts, 0),
            place_slice(grad_taps_x, head_index, head_parts, 1),
            place_slice(head_params, head_index, head_parts, 1),
            place_slice(grad_input_half, state_index, state_parts, 1),
            place_slice(grad_read_half, state_index, state_parts, 1),
            place_slice(grad_taps_b, state_index, state_parts, 1),
            place_slice(grad_taps_c, state_index, state_parts, 1),
        ),
        ("dp", "head", "state"),
    )
    (
        square_total,
        gated_full,
        taps_full,
        heads_full,
        input_full,
        read_full,
        taps_input_full,
        taps_read_full,
    ) = totals
    head_width = gain_gated.shape[0]
    tap_width = taps_inner.shape[1]
    param_width = step_bias.shape[0]
    heads_own = take_slice(heads_full, head_index, param_width, 1)
    return (
        layer_out,
        grad_hidden,
        grad_embedding,
        scattered[0],
        scattered[1],
        scattered[2],
        scattered[3],
        scattered[4],
        scattered[5],
        scattered[6],
        scattered[7],
        scattered[8],
        scattered[9],
        scattered[10],
        scattered[11],
        scattered[12],
        scattered[13],
        scattered[14],
        scattered[15],
        scattered[16],
        scattered[17],
        scattered[18],
        scattered[19],
        input_full,
        read_full,
        take_slice(taps_full, head_index, tap_width, 1),
        taps_input_full,
        taps_read_full,
        heads_own[0],
        heads_own[1],
        heads_own[2],
        take_slice(gated_full, head_index, head_width, 0),
        scattered[20],
        jnp.sqrt(square_total),
    )


def solution(mesh):
    in_specs = (
        P(("dp", "state"), None),
        P(("dp", "state"), None),
        P("dp", None),
        P("dp", None),
        P(("dp", "state")),
        P(("dp", "state"), "head"),
        P(("dp", "state"), "head"),
        P(("dp", "state"), "head"),
        P(("dp", "state"), None),
        P(("dp", "state"), None),
        P(("dp", "state"), None),
        P(("dp", "state"), "head"),
        P(("dp", "state"), "head"),
        P(("dp", "state"), "head"),
        P("head", ("dp", "state")),
        P(("dp", "state")),
        P(("dp", "state"), "head"),
        P(("dp", "state"), None),
        P(("dp", "state"), "head"),
        P("head", ("dp", "state")),
        P(("dp", "state")),
        P(("dp", "state"), "head"),
        P(("dp", "state"), "head"),
        P(("dp", "state"), "head"),
        P(),
        P(),
        P(None, "head"),
        P(),
        P(),
        P("head"),
        P("head"),
        P("head"),
        P("head"),
        P("head", ("dp", "state")),
    )
    out_specs = (
        P("dp", None),
        P(("dp", "state"), None),
        P(("dp", "state"), None),
        P(("dp", "state")),
        P(("dp", "state"), "head"),
        P(("dp", "state"), "head"),
        P(("dp", "state"), "head"),
        P(("dp", "state"), None),
        P(("dp", "state"), None),
        P(("dp", "state"), None),
        P(("dp", "state"), "head"),
        P(("dp", "state"), "head"),
        P(("dp", "state"), "head"),
        P("head", ("dp", "state")),
        P(("dp", "state")),
        P(("dp", "state"), "head"),
        P(("dp", "state"), None),
        P(("dp", "state"), "head"),
        P("head", ("dp", "state")),
        P(("dp", "state")),
        P(("dp", "state"), "head"),
        P(("dp", "state"), "head"),
        P(("dp", "state"), "head"),
        P(),
        P(),
        P(None, "head"),
        P(),
        P(),
        P("head"),
        P("head"),
        P("head"),
        P("head"),
        P("head", ("dp", "state")),
        P(),
    )
    return jax.shard_map(
        per_device, mesh=mesh, in_specs=in_specs, out_specs=out_specs, check_vma=False
    )
```

profile of v0, /device:TPU:0, one launch (start us, length us, event | category | flops | bytes accessed | tf_op | source)
XLA Modules:
  0.0 4564.8 jit_solution(9885249469543148391)
XLA Ops:
  98.8 55.5 %all-gather.25.cloned.1.call-done = bf16[4096,512]{1,0:T(8,128)(2,1)} async-done(((bf16[1024,512]{1,0:T(8,128)(2,1)}), bf16[4096,512]{1,0:T(8,128)(2,1)}) %all-gather.25.cloned.1.call-update) | async-done | bytes 4194320 | tf_op jit(solution)/shard_map/all_gather | solution.py:240
  168.1 67.0 %all-gather.29.cloned.1.call-done = bf16[4096,512]{1,0:T(8,128)(2,1)} async-done(((bf16[1024,512]{1,0:T(8,128)(2,1)}), bf16[4096,512]{1,0:T(8,128)(2,1)}) %all-gather.29.cloned.1.call-update) | async-done | bytes 4194320 | tf_op jit(solution)/shard_map/all_gather | solution.py:241
  269.0 75.8 %all-gather.19.cloned.1.call-done = bf16[4096,512]{1,0:T(8,128)(2,1)} async-done(((bf16[1024,512]{1,0:T(8,128)(2,1)}), bf16[4096,512]{1,0:T(8,128)(2,1)}) %all-gather.19.cloned.1.call-update) | async-done | bytes 4194320 | tf_op jit(solution)/shard_map/all_gather | solution.py:242
  359.4 19.1 all-gather.33.cloned.1.call-done
  431.6 29.7 all-gather.35.cloned.1.call-done
  512.9 81.7 %all-reduce.52.cloned.1.call-done = f32[1024,2048]{1,0:T(8,128)} async-done(((f32[1024,2048]{1,0:T(8,128)}), f32[1024,2048]{1,0:T(8,128)}) %all-reduce.52.cloned.1.call-update) | async-done | bytes 8388624 | tf_op jit(solution)/shard_map/psum | solution.py:315
  606.8 70.4 %all-gather.37.cloned.1.call-done = bf16[2048,1024]{1,0:T(8,128)(2,1)} async-done(((bf16[512,1024]{1,0:T(8,128)(2,1)}), bf16[2048,1024]{1,0:T(8,128)(2,1)}) %all-gather.37.cloned.1.call-update) | async-done | bytes 4194320 | tf_op jit(solution)/shard_map/all_gather | solution.py:251
  695.9 62.2 %all-gather.39.cloned.1.call-done = bf16[1024,2048]{1,0:T(8,128)(2,1)} async-done(((bf16[1024,512]{1,0:T(8,128)(2,1)}), bf16[1024,2048]{1,0:T(8,128)(2,1)}) %all-gather.39.cloned.1.call-update) | async-done | bytes 4194320 | tf_op jit(solution)/shard_map/all_gather | solution.py:254
  767.0 125.2 %all-reduce.54.cloned.1.call-done = f32[1024,2048]{1,0:T(8,128)} async-done(((f32[1024,2048]{1,0:T(8,128)}), f32[1024,2048]{1,0:T(8,128)}) %all-reduce.54.cloned.1.call-update) | async-done | bytes 8388624 | tf_op jit(solution)/shard_map/psum | solution.py:322
  930.6 171.9 %all-gather.41.cloned.1.call-done = f32[2048,2048]{1,0:T(8,128)} async-done(((f32[1024,2048]{1,0:T(8,128)}), f32[2048,2048]{1,0:T(8,128)}) %all-gather.41.cloned.1.call-update) | async-done | bytes 16777232 | tf_op jit(solution)/shard_map/all_gather | solution.py:324
  1125.6 24.2 all-gather.43.cloned.1.call-done
  1185.8 108.1 %while.46 = (s32[]{:T(128)}, f32[8,32,64]{2,1,0:T(8,128)S(1)}, s32[]{:T(128)}, f32[8,256,8,64]{1,3,2,0:T(8,128)}, f32[8,8,32,64]{3,2,1,0:T(8,128)}, /*index=5*/s...) while((s32[]{:T(128)}, f32[8,32,64]{2,1,0:T(8,128)S(1)}, ...), condition=%wide.region_13.14_spmd.clone, body=%wide.region_10.13_spmd.clone.sunk | while | flops 531784736 | bytes 3945399 | solution.py:136
  1309.1 106.5 %all-reduce.56.cloned.1.call-done = f32[2048,512]{1,0:T(8,128)} async-done(((f32[2048,512]{1,0:T(8,128)}), f32[2048,512]{1,0:T(8,128)}) %all-reduce.56.cloned.1.call-update) | async-done | bytes 4194320 | tf_op jit(solution)/shard_map/psum | solution.py:368
  1471.2 125.4 %all-reduce.58.cloned.1.call-done = f32[1024,2048]{1,0:T(8,128)} async-done(((f32[1024,2048]{1,0:T(8,128)}), f32[1024,2048]{1,0:T(8,128)}) %all-reduce.58.cloned.1.call-update) | async-done | bytes 8388624 | tf_op jit(solution)/shard_map/psum | solution.py:379
  1596.7 200.4 %all-gather.49.cloned.1.call-done = f32[2048,2048]{1,0:T(8,128)} async-done(((f32[1024,2048]{1,0:T(8,128)}), f32[2048,2048]{1,0:T(8,128)}) %all-gather.49.cloned.1.call-update) | async-done | bytes 16777232 | tf_op jit(solution)/shard_map/all_gather | solution.py:380
  1797.1 18.0 multiply_reduce_fusion.4
  1850.9 201.4 %while.47 = (s32[]{:T(128)}, f32[8]{0:T(128)S(1)}, f32[8,32,64]{2,1,0:T(8,128)S(1)}, f32[8,256,8,64]{1,3,2,0:T(8,128)}, f32[8,256,8]{1,2,0:T(8,128)S(1)}, /*inde...) while((s32[]{:T(128)}, f32[8]{0:T(128)S(1)}, ...), condition=%wide.region_32.33_spmd.clone, body=%wide.region_19.32_spmd.clone.sunk | while | flops 1143088128 | bytes 12638738 | solution.py:136
  2145.3 29.8 add_add_fusion.3
  2175.2 189.2 %reduce-scatter.22.cloned.1.call-done = f32[1024,2048]{1,0:T(8,128)} async-done(((f32[2048,2048]{1,0:T(8,128)}), f32[1024,2048]{1,0:T(8,128)}) %reduce-scatter.22.cloned.1.call-update) | async-done | bytes 8388624 | tf_op jit(solution)/shard_map/reduce_scatter | solution.py:426
  2376.3 118.6 %all-reduce.60.cloned.1.call-done = f32[1024,2048]{1,0:T(8,128)} async-done(((f32[1024,2048]{1,0:T(8,128)}), f32[1024,2048]{1,0:T(8,128)}) %all-reduce.60.cloned.1.call-update) | async-done | bytes 8388624 | tf_op jit(solution)/shard_map/psum | solution.py:427
  2536.5 40.8 all-reduce.67
  2577.4 93.1 %all-reduce.62.cloned.1.call-done = f32[1024,2048]{1,0:T(8,128)} async-done(((f32[1024,2048]{1,0:T(8,128)}), f32[1024,2048]{1,0:T(8,128)}) %all-reduce.62.cloned.1.call-update) | async-done | bytes 8388624 | tf_op jit(solution)/shard_map/psum | solution.py:443
  2689.0 21.7 multiply_reduce_fusion.3
  2710.8 27.7 multiply_convert_fusion
  2749.4 19.4 fusion.127
  2817.9 42.7 reduce-scatter.26.cloned.1.call-done
  2892.2 54.6 %all-reduce.68 = (bf16[1024,128]{1,0:T(8,128)(2,1)}, bf16[1024,128]{1,0:T(8,128)(2,1)}, bf16[1024,128]{1,0:T(8,128)(2,1)S(1)}) all-reduce(f32[1024,128]{1,0:T(8,128)} %fusion.228, f32[1024,128]{1,0:T(8,128)} %fusion.227, f32[1024,128]{1,0:T(8,128)} %fusion.229), channel_id=1, replica_groups=mesh['dp'=2,'head'=8,'state'=2] {'head'}, use_global_device_ids=true, to_apply=%region_45.46 | all-reduce | flops 393216 | bytes 2359296 | tf_op jit(solution)/shard_map/psum | solution.py:497
  2987.7 20.5 add_add_fusion.2
  3055.0 18.5 fusion.238
  3077.0 18.4 fusion.239
  3109.9 20.6 reduce-scatter.46.cloned.1.call-done
  3154.8 19.5 reduce-scatter.42.cloned.1.call-done
  3175.7 19.2 reduce-scatter.44.cloned.1.call-done
  3196.4 144.3 %reduce-scatter.48.cloned.1.call-done = f32[512,1024]{1,0:T(8,128)} async-done(((f32[2048,1024]{1,0:T(8,128)}), f32[512,1024]{1,0:T(8,128)}) %reduce-scatter.48.cloned.1.call-update) | async-done | bytes 2097168 | tf_op jit(solution)/shard_map/reduce_scatter | solution.py:529
  3343.4 145.6 %reduce-scatter.54.cloned.1.call-done = f32[1024,512]{1,0:T(8,128)} async-done(((f32[1024,2048]{1,0:T(8,128)}), f32[1024,512]{1,0:T(8,128)}) %reduce-scatter.54.cloned.1.call-update) | async-done | bytes 2097168 | tf_op jit(solution)/shard_map/reduce_scatter | solution.py:532
  3491.7 44.8 reduce-scatter.34.cloned.1.call-done
  3538.9 43.5 reduce-scatter.36.cloned.1.call-done
  3584.9 43.6 reduce-scatter.38.cloned.1.call-done
  3631.0 218.5 %all-reduce.64.cloned.1.call-done = f32[1024,4096]{1,0:T(8,128)} async-done(((f32[1024,4096]{1,0:T(8,128)}), f32[1024,4096]{1,0:T(8,128)}) %all-reduce.64.cloned.1.call-update) | async-done | bytes 16777232 | tf_op jit(solution)/shard_map/psum | solution.py:497
  3849.4 26.4 fusion.99
  3875.9 21.8 all-reduce.40
  3927.4 70.4 %reduce-scatter.28.cloned.1.call-done = f32[1024,512]{1,0:T(8,128)} async-done(((f32[4096,512]{1,0:T(8,128)}), f32[1024,512]{1,0:T(8,128)}) %reduce-scatter.28.cloned.1.call-update) | async-done | bytes 2097168 | tf_op jit(solution)/shard_map/reduce_scatter | solution.py:518
  4000.6 145.6 %reduce-scatter.30.cloned.1.call-done = f32[1024,512]{1,0:T(8,128)} async-done(((f32[4096,512]{1,0:T(8,128)}), f32[1024,512]{1,0:T(8,128)}) %reduce-scatter.30.cloned.1.call-update) | async-done | bytes 2097168 | tf_op jit(solution)/shard_map/reduce_scatter | solution.py:519
  4150.2 144.2 %reduce-scatter.32.cloned.1.call-done = f32[1024,512]{1,0:T(8,128)} async-done(((f32[4096,512]{1,0:T(8,128)}), f32[1024,512]{1,0:T(8,128)}) %reduce-scatter.32.cloned.1.call-update) | async-done | bytes 2097168 | tf_op jit(solution)/shard_map/reduce_scatter | solution.py:520
  4302.4 44.6 all-reduce.37
  4348.9 46.3 %reduce-scatter.62.cloned.1.call-done = f32[512,512]{1,0:T(8,128)} async-done(((f32[512,2048]{1,0:T(8,128)}), f32[512,512]{1,0:T(8,128)}) %reduce-scatter.62.cloned.1.call-update) | async-done | bytes 1048592 | tf_op jit(solution)/shard_map/reduce_scatter | solution.py:537
  4395.3 80.1 %reduce-scatter.56.cloned.1.call-done = f32[512,512]{1,0:T(8,128)} async-done(((f32[2048,512]{1,0:T(8,128)}), f32[512,512]{1,0:T(8,128)}) %reduce-scatter.56.cloned.1.call-update) | async-done | bytes 1048592 | tf_op jit(solution)/shard_map/reduce_scatter | solution.py:534
  4475.4 80.0 %reduce-scatter.58.cloned.1.call-done = f32[512,512]{1,0:T(8,128)} async-done(((f32[2048,512]{1,0:T(8,128)}), f32[512,512]{1,0:T(8,128)}) %reduce-scatter.58.cloned.1.call-update) | async-done | bytes 1048592 | tf_op jit(solution)/shard_map/reduce_scatter | solution.py:535
  (1176 shorter events, 1225.7 us)
Async XLA Ops:
  7.2 1112.9 %copy-start = (bf16[2048,64]{0,1:T(8,128)(2,1)S(1)}, bf16[2048,64]{0,1:T(8,128)(2,1)}, u32[]{:S(2)}) copy-start(bf16[2048,64]{0,1:T(8,128)(2,1)} %param.62) | copy-start | bytes 786436
  7.2 78.8 %all-gather.27.cloned.1.call-start = ((), (), s32[]{:S(2)}) async-start(), calls=%async_computation.25 | async-start | bytes 1310720 | tf_op jit(solution)/shard_map/all_gather | solution.py:243
  8.0 84.1 %all-gather.31.cloned.1.call-start = ((), (), s32[]{:S(2)}) async-start(), calls=%async_computation.27 | async-start | bytes 1310720 | tf_op jit(solution)/shard_map/all_gather | solution.py:244
  8.7 145.6 %all-gather.25.cloned.1.call-start = ((), (), s32[]{:S(2)}) async-start(), calls=%async_computation.24 | async-start | bytes 5242880 | tf_op jit(solution)/shard_map/all_gather | solution.py:240
  9.4 225.6 %all-gather.29.cloned.1.call-start = ((), (), s32[]{:S(2)}) async-start(), calls=%async_computation.26 | async-start | bytes 5242880 | tf_op jit(solution)/shard_map/all_gather | solution.py:241
  10.0 253.0 %all-gather.21.cloned.1.call-start = ((), (), s32[]{:S(2)}) async-start(), calls=%async_computation.22 | async-start | bytes 1310720 | tf_op jit(solution)/shard_map/all_gather | solution.py:245
  10.6 334.1 %all-gather.19.cloned.1.call-start = ((), (), s32[]{:S(2)}) async-start(), calls=%async_computation.21 | async-start | bytes 5242880 | tf_op jit(solution)/shard_map/all_gather | solution.py:242
  11.2 367.4 %all-gather.33.cloned.1.call-start = ((), (), s32[]{:S(2)}) async-start(), calls=%async_computation.28 | async-start | bytes 3145728 | tf_op jit(solution)/shard_map/all_gather | solution.py:304
  257.5 156.3 %all-gather.23.cloned.1.call-start = ((), (), s32[]{:S(2)}) async-start(), calls=%async_computation.23 | async-start | bytes 3145728 | tf_op jit(solution)/shard_map/all_gather | solution.py:305
  354.5 106.9 %all-gather.35.cloned.1.call-start = ((), (), s32[]{:S(2)}) async-start(), calls=%async_computation.29 | async-start | bytes 2621440 | tf_op jit(solution)/shard_map/all_gather | solution.py:249
  355.2 239.3 %all-reduce.52.cloned.1.call-start = ((), (), s32[]{:S(2)}) async-start(), calls=%async_computation.30 | async-start | bytes 16777216 | tf_op jit(solution)/shard_map/psum | solution.py:315
  469.1 208.1 %all-gather.37.cloned.1.call-start = ((), (), s32[]{:S(2)}) async-start(), calls=%async_computation.31 | async-start | bytes 5242880 | tf_op jit(solution)/shard_map/all_gather | solution.py:251
  469.8 288.3 %all-gather.39.cloned.1.call-start = ((), (), s32[]{:S(2)}) async-start(), calls=%async_computation.32 | async-start | bytes 5242880 | tf_op jit(solution)/shard_map/all_gather | solution.py:254
  470.4 421.8 %all-reduce.54.cloned.1.call-start = ((), (), s32[]{:S(2)}) async-start(), calls=%async_computation.33 | async-start | bytes 16777216 | tf_op jit(solution)/shard_map/psum | solution.py:322
  767.0 335.5 %all-gather.41.cloned.1.call-start = ((), (), s32[]{:S(2)}) async-start(), calls=%async_computation.34 | async-start | bytes 25165824 | tf_op jit(solution)/shard_map/all_gather | solution.py:324
  903.0 246.8 %all-gather.43.cloned.1.call-start = ((), (), s32[]{:S(2)}) async-start(), calls=%async_computation.35 | async-start | bytes 2621440 | tf_op jit(solution)/shard_map/all_gather | solution.py:256
  903.6 405.5 %all-gather.45.cloned.1.call-start = ((), (), s32[]{:S(2)}) async-start(), calls=%async_computation.37 | async-start | bytes 2621440 | tf_op jit(solution)/shard_map/all_gather | solution.py:257
  904.2 511.4 %all-reduce.56.cloned.1.call-start = ((), (), s32[]{:S(2)}) async-start(), calls=%async_computation.36 | async-start | bytes 8388608 | tf_op jit(solution)/shard_map/psum | solution.py:368
  1308.3 154.8 %all-gather.47.cloned.1.call-start = ((), (), s32[]{:S(2)}) async-start(), calls=%async_computation.38 | async-start | bytes 2621440 | tf_op jit(solution)/shard_map/all_gather | solution.py:259
  1308.9 287.7 %all-reduce.58.cloned.1.call-start = ((), (), s32[]{:S(2)}) async-start(), calls=%async_computation.39 | async-start | bytes 16777216 | tf_op jit(solution)/shard_map/psum | solution.py:379
  1471.1 326.0 %all-gather.49.cloned.1.call-start = ((), (), s32[]{:S(2)}) async-start(), calls=%async_computation.40 | async-start | bytes 25165824 | tf_op jit(solution)/shard_map/all_gather | solution.py:380
  1596.6 767.8 %reduce-scatter.22.cloned.1.call-start = ((), (), s32[]{:S(2)}) async-start(), calls=%async_computation.41 | async-start | bytes 25165824 | tf_op jit(solution)/shard_map/reduce_scatter | solution.py:426
  2175.1 319.8 %all-reduce.60.cloned.1.call-start = ((), (), s32[]{:S(2)}) async-start(), calls=%async_computation.42 | async-start | bytes 16777216 | tf_op jit(solution)/shard_map/psum | solution.py:427
  2364.4 306.0 %all-reduce.62.cloned.1.call-start = ((), (), s32[]{:S(2)}) async-start(), calls=%async_computation.43 | async-start | bytes 16777216 | tf_op jit(solution)/shard_map/psum | solution.py:443
  2534.9 276.5 %reduce-scatter.24.cloned.1.call-start = ((), (), s32[]{:S(2)}) async-start(), calls=%async_computation.44 | async-start | bytes 6291456 | tf_op jit(solution)/shard_map/reduce_scatter | solution.py:471
  2749.3 111.3 %reduce-scatter.26.cloned.1.call-start = ((), (), s32[]{:S(2)}) async-start(), calls=%async_computation.45 | async-start | bytes 6291456 | tf_op jit(solution)/shard_map/reduce_scatter | solution.py:472
  2768.9 327.8 %all-reduce.66.cloned.1.call-start = ((), (), s32[]{:S(2)}) async-start(), calls=%async_computation.65 | async-start | bytes 2228224 | tf_op jit(solution)/shard_map/psum | solution.py:546
  2784.7 313.3 %reduce-scatter.52.cloned.1.call-start = ((), (), s32[]{:S(2)}) async-start(), calls=%async_computation.59 | async-start | bytes 655360 | tf_op jit(solution)/shard_map/reduce_scatter | solution.py:531
  2786.1 313.5 %reduce-scatter.50.cloned.1.call-start = ((), (), s32[]{:S(2)}) async-start(), calls=%async_computation.58 | async-start | bytes 1310720 | tf_op jit(solution)/shard_map/reduce_scatter | solution.py:530
  2791.1 339.5 %reduce-scatter.46.cloned.1.call-start = ((), (), s32[]{:S(2)}) async-start(), calls=%async_computation.56 | async-start | bytes 5242880 | tf_op jit(solution)/shard_map/reduce_scatter | solution.py:527
  2799.1 354.2 %reduce-scatter.40.cloned.1.call-start = ((), (), s32[]{:S(2)}) async-start(), calls=%async_computation.53 | async-start | bytes 327680 | tf_op jit(solution)/shard_map/reduce_scatter | solution.py:524
  2816.5 357.7 %reduce-scatter.42.cloned.1.call-start = ((), (), s32[]{:S(2)}) async-start(), calls=%async_computation.54 | async-start | bytes 327680 | tf_op jit(solution)/shard_map/reduce_scatter | solution.py:525
  2817.9 377.1 %reduce-scatter.44.cloned.1.call-start = ((), (), s32[]{:S(2)}) async-start(), calls=%async_computation.55 | async-start | bytes 327680 | tf_op jit(solution)/shard_map/reduce_scatter | solution.py:526
  2864.5 476.1 %reduce-scatter.48.cloned.1.call-start = ((), (), s32[]{:S(2)}) async-start(), calls=%async_computation.57 | async-start | bytes 10485760 | tf_op jit(solution)/shard_map/reduce_scatter | solution.py:529
  2875.4 613.5 %reduce-scatter.54.cloned.1.call-start = ((), (), s32[]{:S(2)}) async-start(), calls=%async_computation.60 | async-start | bytes 10485760 | tf_op jit(solution)/shard_map/reduce_scatter | solution.py:532
  2887.5 649.0 %reduce-scatter.34.cloned.1.call-start = ((), (), s32[]{:S(2)}) async-start(), calls=%async_computation.50 | async-start | bytes 2621440 | tf_op jit(solution)/shard_map/reduce_scatter | solution.py:521
  2953.9 628.6 %reduce-scatter.36.cloned.1.call-start = ((), (), s32[]{:S(2)}) async-start(), calls=%async_computation.51 | async-start | bytes 2621440 | tf_op jit(solution)/shard_map/reduce_scatter | solution.py:522
  2961.2 667.3 %reduce-scatter.38.cloned.1.call-start = ((), (), s32[]{:S(2)}) async-start(), calls=%async_computation.52 | async-start | bytes 2621440 | tf_op jit(solution)/shard_map/reduce_scatter | solution.py:523
  2968.4 881.0 %all-reduce.64.cloned.1.call-start = ((), (), s32[]{:S(2)}) async-start(), calls=%async_computation.46 | async-start | bytes 33554432 | tf_op jit(solution)/shard_map/psum | solution.py:497
  3008.3 989.6 %reduce-scatter.28.cloned.1.call-start = ((), (), s32[]{:S(2)}) async-start(), calls=%async_computation.47 | async-start | bytes 10485760 | tf_op jit(solution)/shard_map/reduce_scatter | solution.py:518
  3018.8 1127.4 %reduce-scatter.30.cloned.1.call-start = ((), (), s32[]{:S(2)}) async-start(), calls=%async_computation.48 | async-start | bytes 10485760 | tf_op jit(solution)/shard_map/reduce_scatter | solution.py:519
  3029.5 1264.9 %reduce-scatter.32.cloned.1.call-start = ((), (), s32[]{:S(2)}) async-start(), calls=%async_computation.49 | async-start | bytes 10485760 | tf_op jit(solution)/shard_map/reduce_scatter | solution.py:520
  3040.2 1308.7 %reduce-scatter.60.cloned.1.call-start = ((), (), s32[]{:S(2)}) async-start(), calls=%async_computation.63 | async-start | bytes 81920 | tf_op jit(solution)/shard_map/reduce_scatter | solution.py:536
  3047.3 1347.9 %reduce-scatter.62.cloned.1.call-start = ((), (), s32[]{:S(2)}) async-start(), calls=%async_computation.64 | async-start | bytes 5242880 | tf_op jit(solution)/shard_map/reduce_scatter | solution.py:537
  3054.7 1420.7 %reduce-scatter.56.cloned.1.call-start = ((), (), s32[]{:S(2)}) async-start(), calls=%async_computation.61 | async-start | bytes 5242880 | tf_op jit(solution)/shard_map/reduce_scatter | solution.py:534
  3073.6 1481.8 %reduce-scatter.58.cloned.1.call-start = ((), (), s32[]{:S(2)}) async-start(), calls=%async_computation.62 | async-start | bytes 5242880 | tf_op jit(solution)/shard_map/reduce_scatter | solution.py:535
  3140.7 708.7 %copy-start.67 = (f32[4096]{0:T(1024)S(1)}, f32[4096]{0:T(1024)}, u32[]{:S(2)}) copy-start(f32[4096]{0:T(1024)} %copy-done.66) | copy-start | bytes 49156
  3140.7 708.7 %copy-start.79 = (f32[1024]{0:T(1024)S(1)}, f32[1024]{0:T(1024)}, u32[]{:S(2)}) copy-start(f32[1024]{0:T(1024)} %copy-done.78) | copy-start | bytes 12292
  (160 other events, 11630.4 us)
Sparse Core Ops, SparseCore 0:
  9.6 30.7 all-gather.26
  42.0 30.2 all-gather.30
  73.9 80.3 all-gather.24
  155.7 79.2 all-gather.28
  236.5 26.4 all-gather.20
  264.4 80.2 all-gather.18
  346.8 31.6 all-gather.32
  380.7 33.1 all-gather.22
  415.4 45.9 all-gather.34
  469.2 125.2 all-reduce.51
  596.2 80.9 all-gather.36
  678.7 79.3 all-gather.38
  767.1 125.0 all-reduce.53
  903.1 199.3 all-gather.40
  1103.9 45.8 all-gather.42
  1151.2 44.6 all-gather.44
  1308.4 107.1 all-reduce.55
  1417.1 45.9 all-gather.46
  1471.2 125.2 all-reduce.57
  1598.0 199.0 all-gather.48
  2175.2 189.0 reduce-scatter.21
  2368.3 126.5 all-reduce.59
  2535.0 135.3 all-reduce.61
  2749.4 54.4 reduce-scatter.23
  2806.3 54.2 reduce-scatter.25
  2867.8 130.9 all-reduce.65
  3002.1 21.6 reduce-scatter.51
  3026.7 25.3 reduce-scatter.49
  3055.1 75.4 reduce-scatter.45
  3133.2 20.0 reduce-scatter.39
  3156.2 17.9 reduce-scatter.41
  3177.1 17.8 reduce-scatter.43
  3197.8 142.7 reduce-scatter.47
  3343.7 145.1 reduce-scatter.53
  3491.9 44.5 reduce-scatter.33
  3539.2 43.1 reduce-scatter.35
  3585.3 43.1 reduce-scatter.37
  3632.3 217.1 all-reduce.63
  3852.3 145.4 reduce-scatter.27
  4000.9 145.2 reduce-scatter.29
  4149.2 145.1 reduce-scatter.31
  4297.4 19.7 reduce-scatter.59
  4319.9 75.3 reduce-scatter.61
  4398.2 77.1 reduce-scatter.55
  4478.1 77.2 reduce-scatter.57
where the time goes:
time: 4570 us; the launch traced here: 4560 us
  waiting for transfers between devices  2980 us (65%)
  matrix products  744 us (16%)
  blocking collectives  300 us (7%)
  other arithmetic  295 us (6%)
  local copies, waits for them, and re-layouts  187 us (4%)
    psum x1, waiting for transfers between devices, per_device(): lax.psum((normed_part, query_middle, key_middle, value_middle), 'head')  218 us
    all_gather x1, waiting for transfers between devices, per_device(): mixed = lax.all_gather(mixed_own, 'state', axis=0, tiled=True)  200 us
    reduce_scatter x1, waiting for transfers between devices, per_device(): lax.psum_scatter(mixer_part, 'state', scatter_dimension=0, tiled=True)  189 us
    all_gather x1, waiting for transfers between devices, per_device(): second_all = lax.all_gather(second, 'state', axis=0, tiled=True)  172 us
    reduce_scatter x1, waiting for transfers between devices, per_device(): lax.psum_scatter(grad_key_main, ('dp', 'state'), scatter_dimension=0, til...  146 us
    reduce_scatter x1, waiting for transfers between devices, per_device(): lax.psum_scatter(grad_mlp_proj, ('dp', 'state'), scatter_dimension=1, til...  146 us
    reduce_scatter x1, waiting for transfers between devices, per_device(): lax.psum_scatter(grad_mlp_main, ('dp', 'state'), scatter_dimension=0, til...  144 us
    reduce_scatter x1, waiting for transfers between devices, per_device(): lax.psum_scatter(grad_value_main, ('dp', 'state'), scatter_dimension=0, t...  144 us
  transfers between devices with their start and end apart: 45, of which 37 were waited for; matrix products, arithmetic and copies ran while one was open for 15% of the time, Pallas kernels for 0%

commit v1 on v0

--- a/solution.py
+++ b/solution.py
@@ -7,6 +7,9 @@
 MDIM = 64
 DIN = 4096
 GROUP = 256
+DP, HEAD, STATE = "dp", "head", "state"
+ZED = (DP, STATE)
+EVERY = (DP, HEAD, STATE)
 
 
 highest = lax.Precision.HIGHEST
@@ -180,7 +183,7 @@
     return lax.dynamic_slice_in_dim(whole, index * width, width, axis)
 
 
-def per_device(
+def general_device(
     hidden,
     embedding,
     cotangent,
@@ -219,10 +222,10 @@
     row_count = hidden.shape[0]
     length = cotangent.shape[0]
     model_width = hidden.shape[1]
-    head_parts = lax.axis_size("head")
-    state_parts = lax.axis_size("state")
-    state_index = lax.axis_index("state")
-    head_index = lax.axis_index("head")
+    head_parts = lax.axis_size(HEAD)
+    state_parts = lax.axis_size(STATE)
+    state_index = lax.axis_index(STATE)
+    head_index = lax.axis_index(HEAD)
     own_start = state_index * row_count
     segment, position, valid = row_layout(lengths[0], length)
     own_segment = lax.dynamic_slice_in_dim(segment, own_start, row_count)
@@ -236,27 +239,27 @@
     ]
     allowed = (own_segment[:, None] == segment[None, :]) & (places[None, :] <= own_places[:, None])
     gathered = (
-        lax.all_gather(gain_attn, ("dp", "state"), axis=0, tiled=True),
-        lax.all_gather(w_query, ("dp", "state"), axis=0, tiled=True),
-        lax.all_gather(w_key, ("dp", "state"), axis=0, tiled=True),
-        lax.all_gather(w_value, ("dp", "state"), axis=0, tiled=True),
-        lax.all_gather(down_query, ("dp", "state"), axis=0, tiled=True),
-        lax.all_gather(down_key, ("dp", "state"), axis=0, tiled=True),
-        lax.all_gather(down_value, ("dp", "state"), axis=0, tiled=True),
-        lax.all_gather(up_query, ("dp", "state"), axis=0, tiled=True),
-        lax.all_gather(up_key, ("dp", "state"), axis=0, tiled=True),
-        lax.all_gather(up_value, ("dp", "state"), axis=0, tiled=True),
-        lax.all_gather(attn_output, ("dp", "state"), axis=1, tiled=True),
-        lax.all_gather(gain_mlp, ("dp", "state"), axis=0, tiled=True),
-        lax.all_gather(mlp_input, ("dp", "state"), axis=0, tiled=True),
-        lax.all_gather(down_mlp, ("dp", "state"), axis=0, tiled=True),
-        lax.all_gather(up_mlp, ("dp", "state"), axis=0, tiled=True),
-        lax.all_gather(mlp_output, ("dp", "state"), axis=1, tiled=True),
-        lax.all_gather(gain_mixer, ("dp", "state"), axis=0, tiled=True),
-        lax.all_gather(proj_inner, ("dp", "state"), axis=0, tiled=True),
-        lax.all_gather(proj_gate, ("dp", "state"), axis=0, tiled=True),
-        lax.all_gather(proj_step, ("dp", "state"), axis=0, tiled=True),
-        lax.all_gather(proj_output, ("dp", "state"), axis=1, tiled=True),
+        lax.all_gather(gain_attn, ZED, axis=0, tiled=True),
+        lax.all_gather(w_query, ZED, axis=0, tiled=True),
+        lax.all_gather(w_key, ZED, axis=0, tiled=True),
+        lax.all_gather(w_value, ZED, axis=0, tiled=True),
+        lax.all_gather(down_query, ZED, axis=0, tiled=True),
+        lax.all_gather(down_key, ZED, axis=0, tiled=True),
+        lax.all_gather(down_value, ZED, axis=0, tiled=True),
+        lax.all_gather(up_query, ZED, axis=0, tiled=True),
+        lax.all_gather(up_key, ZED, axis=0, tiled=True),
+        lax.all_gather(up_value, ZED, axis=0, tiled=True),
+        lax.all_gather(attn_output, ZED, axis=1, tiled=True),
+        lax.all_gather(gain_mlp, ZED, axis=0, tiled=True),
+        lax.all_gather(mlp_input, ZED, axis=0, tiled=True),
+        lax.all_gather(down_mlp, ZED, axis=0, tiled=True),
+        lax.all_gather(up_mlp, ZED, axis=0, tiled=True),
+        lax.all_gather(mlp_output, ZED, axis=1, tiled=True),
+        lax.all_gather(gain_mixer, ZED, axis=0, tiled=True),
+        lax.all_gather(proj_inner, ZED, axis=0, tiled=True),
+        lax.all_gather(proj_gate, ZED, axis=0, tiled=True),
+        lax.all_gather(proj_step, ZED, axis=0, tiled=True),
+        lax.all_gather(proj_output, ZED, axis=1, tiled=True),
     )
     (
         attn_gain,
@@ -301,8 +304,8 @@
     )
     values_own = value_pre.reshape(row_count, head_count, HDIM).astype(jnp.bfloat16)
     keys_all, values_all = (
-        lax.all_gather(keys_own, "state", axis=0, tiled=True),
-        lax.all_gather(values_own, "state", axis=0, tiled=True),
+        lax.all_gather(keys_own, STATE, axis=0, tiled=True),
+        lax.all_gather(values_own, STATE, axis=0, tiled=True),
     )
     probs_full = head_probs(queries, keys_all, allowed)
     attended_f = jnp.einsum(
@@ -312,16 +315,16 @@
         preferred_element_type=jnp.float32,
     )
     attended = attended_f.reshape(row_count, head_count * HDIM).astype(jnp.bfloat16)
-    branch = lax.psum(plain_dot(attended, attn_proj), "head")
+    branch = lax.psum(plain_dot(attended, attn_proj), HEAD)
     first = hidden.astype(jnp.float32) + own_valid * branch
     mlp_gain_f = mlp_gain.astype(jnp.float32)
     mlp_normed = rms_norm(first, mlp_gain_f).astype(jnp.bfloat16)
     mlp_red = plain_dot(mlp_normed, mlp_down).astype(jnp.bfloat16)
     hidden_pre = plain_dot(mlp_normed, mlp_main) + plain_dot(mlp_red, mlp_upper)
     activated = jax.nn.gelu(hidden_pre, approximate=False).astype(jnp.bfloat16)
-    mlp_branch = lax.psum(plain_dot(activated, mlp_proj), "head")
+    mlp_branch = lax.psum(plain_dot(activated, mlp_proj), HEAD)
     second = first + own_valid * mlp_branch
-    second_all = lax.all_gather(second, "state", axis=0, tiled=True)
+    second_all = lax.all_gather(second, STATE, axis=0, tiled=True)
     mixer_gain_f = mixer_gain.astype(jnp.float32)
     mixer_normed = rms_norm(second_all, mixer_gain_f).astype(jnp.bfloat16)
     states_own = proj_input.shape[1] // state_parts
@@ -365,19 +368,19 @@
         step_bias.astype(jnp.float32),
         log_rate.astype(jnp.float32),
     )
-    scanned = lax.psum(scanned_part, "state")
+    scanned = lax.psum(scanned_part, STATE)
     skip_full = jnp.repeat(skip_gain.astype(jnp.float32), MDIM)[None, :]
     combined = scanned + skip_full * inner_conv
     gate_act = jax.nn.silu(gate_pre)
     united = combined * gate_act
-    squares = lax.psum(jnp.sum(united * united, 1), "head")
+    squares = lax.psum(jnp.sum(united * united, 1), HEAD)
     row_scale = lax.rsqrt(squares / DIN + epsilon)[:, None]
     gated_gain = gain_gated.astype(jnp.float32)[None, :]
     united_own = lax.dynamic_slice_in_dim(united, own_start, row_count, 0)
     scale_own = lax.dynamic_slice_in_dim(row_scale, own_start, row_count, 0)
     gated_own = (united_own * scale_own * gated_gain).astype(jnp.bfloat16)
-    mixed_own = lax.psum(plain_dot(gated_own, output_main), "head")
-    mixed = lax.all_gather(mixed_own, "state", axis=0, tiled=True)
+    mixed_own = lax.psum(plain_dot(gated_own, output_main), HEAD)
+    mixed = lax.all_gather(mixed_own, STATE, axis=0, tiled=True)
     layer_out = (second_all + full_valid * mixed).astype(jnp.bfloat16)
     upstream = cotangent.astype(jnp.float32)
     mix_grad = (full_valid * upstream).astype(jnp.bfloat16)
@@ -423,8 +426,8 @@
     grad_step_main = exact_left(mixer_normed, step_grad)
     grad_input_half = exact_left(mixer_normed, input_grad)
     grad_read_half = exact_left(mixer_normed, read_grad)
-    mixer_rows_own = lax.psum_scatter(mixer_part, "state", scatter_dimension=0, tiled=True)
-    mixer_own = lax.psum(mixer_rows_own, "head")
+    mixer_rows_own = lax.psum_scatter(mixer_part, STATE, scatter_dimension=0, tiled=True)
+    mixer_own = lax.psum(mixer_rows_own, HEAD)
     unused_norm, second_back = jax.vjp(rms_norm, second, mixer_gain_f)
     second_norm_grad, grad_mixer_gain = second_back(mixer_own)
     upstream_own = lax.dynamic_slice_in_dim(upstream, own_start, row_count, 0)
@@ -440,7 +443,7 @@
     grad_mlp_upper = left_dot(mlp_red, hidden_grad)
     mlp_middle = right_dot(hidden_grad, mlp_upper)
     mlp_part = right_dot(hidden_grad, mlp_main)
-    mlp_sum, middle_sum = lax.psum((mlp_part, mlp_middle), "head")
+    mlp_sum, middle_sum = lax.psum((mlp_part, mlp_middle), HEAD)
     middle_low = middle_sum.astype(jnp.bfloat16)
     mlp_normed_grad = mlp_sum + right_dot(middle_low, mlp_down)
     grad_mlp_down = left_dot(mlp_normed, middle_low)
@@ -468,8 +471,8 @@
         "hts,thd->shd", probs_back.astype(jnp.bfloat16), out_low, preferred_element_type=jnp.float32
     )
     keys_grad_own, values_grad_own = (
-        lax.psum_scatter(keys_back, "state", scatter_dimension=0, tiled=True),
-        lax.psum_scatter(values_back, "state", scatter_dimension=0, tiled=True),
+        lax.psum_scatter(keys_back, STATE, scatter_dimension=0, tiled=True),
+        lax.psum_scatter(values_back, STATE, scatter_dimension=0, tiled=True),
     )
     query_grad = (
         rotate(query_back, -own_position).reshape(row_count, head_count * HDIM).astype(jnp.bfloat16)
@@ -495,7 +498,7 @@
         + right_dot(value_grad, value_main)
     )
     normed_sum, query_msum, key_msum, value_msum = lax.psum(
-        (normed_part, query_middle, key_middle, value_middle), "head"
+        (normed_part, query_middle, key_middle, value_middle), HEAD
     )
     query_low = query_msum.astype(jnp.bfloat16)
     key_low = key_msum.astype(jnp.bfloat16)
@@ -514,27 +517,27 @@
     grad_hidden = (first_grad + joined_grad[:, :model_width]).astype(jnp.bfloat16)
     grad_embedding = joined_grad[:, model_width:].astype(jnp.bfloat16)
     scattered = (
-        lax.psum_scatter(grad_attn_gain, ("dp", "state"), scatter_dimension=0, tiled=True),
-        lax.psum_scatter(grad_query_main, ("dp", "state"), scatter_dimension=0, tiled=True),
-        lax.psum_scatter(grad_key_main, ("dp", "state"), scatter_dimension=0, tiled=True),
-        lax.psum_scatter(grad_value_main, ("dp", "state"), scatter_dimension=0, tiled=True),
-        lax.psum_scatter(grad_query_down, ("dp", "state"), scatter_dimension=0, tiled=True),
-        lax.psum_scatter(grad_key_down, ("dp", "state"), scatter_dimension=0, tiled=True),
-        lax.psum_scatter(grad_value_down, ("dp", "state"), scatter_dimension=0, tiled=True),
-        lax.psum_scatter(grad_query_upper, ("dp", "state"), scatter_dimension=0, tiled=True),
-        lax.psum_scatter(grad_key_upper, ("dp", "state"), scatter_dimension=0, tiled=True),
-        lax.psum_scatter(grad_value_upper, ("dp", "state"), scatter_dimension=0, tiled=True),
-        lax.psum_scatter(grad_attn_proj, ("dp", "state"), scatter_dimension=1, tiled=True),
-        lax.psum_scatter(grad_mlp_gain, ("dp", "state"), scatter_dimension=0, tiled=True),
-        lax.psum_scatter(grad_mlp_main, ("dp", "state"), scatter_dimension=0, tiled=True),
-        lax.psum_scatter(grad_mlp_down, ("dp", "state"), scatter_dimension=0, tiled=True),
-        lax.psum_scatter(grad_mlp_upper, ("dp", "state"), scatter_dimension=0, tiled=True),
-        lax.psum_scatter(grad_mlp_proj, ("dp", "state"), scatter_dimension=1, tiled=True),
-        lax.psum_scatter(grad_mixer_gain, ("dp", "state"), scatter_dimension=0, tiled=True),
-        lax.psum_scatter(grad_inner_main, ("dp", "state"), scatter_dimension=0, tiled=True),
-        lax.psum_scatter(grad_gate_main, ("dp", "state"), scatter_dimension=0, tiled=True),
-        lax.psum_scatter(grad_step_main, ("dp", "state"), scatter_dimension=0, tiled=True),
-        lax.psum_scatter(grad_output_main, ("dp", "state"), scatter_dimension=1, tiled=True),
+        lax.psum_scatter(grad_attn_gain, ZED, scatter_dimension=0, tiled=True),
+        lax.psum_scatter(grad_query_main, ZED, scatter_dimension=0, tiled=True),
+        lax.psum_scatter(grad_key_main, ZED, scatter_dimension=0, tiled=True),
+        lax.psum_scatter(grad_value_main, ZED, scatter_dimension=0, tiled=True),
+        lax.psum_scatter(grad_query_down, ZED, scatter_dimension=0, tiled=True),
+        lax.psum_scatter(grad_key_down, ZED, scatter_dimension=0, tiled=True),
+        lax.psum_scatter(grad_value_down, ZED, scatter_dimension=0, tiled=True),
+        lax.psum_scatter(grad_query_upper, ZED, scatter_dimension=0, tiled=True),
+        lax.psum_scatter(grad_key_upper, ZED, scatter_dimension=0, tiled=True),
+        lax.psum_scatter(grad_value_upper, ZED, scatter_dimension=0, tiled=True),
+        lax.psum_scatter(grad_attn_proj, ZED, scatter_dimension=1, tiled=True),
+        lax.psum_scatter(grad_mlp_gain, ZED, scatter_dimension=0, tiled=True),
+        lax.psum_scatter(grad_mlp_main, ZED, scatter_dimension=0, tiled=True),
+        lax.psum_scatter(grad_mlp_down, ZED, scatter_dimension=0, tiled=True),
+        lax.psum_scatter(grad_mlp_upper, ZED, scatter_dimension=0, tiled=True),
+        lax.psum_scatter(grad_mlp_proj, ZED, scatter_dimension=1, tiled=True),
+        lax.psum_scatter(grad_mixer_gain, ZED, scatter_dimension=0, tiled=True),
+        lax.psum_scatter(grad_inner_main, ZED, scatter_dimension=0, tiled=True),
+        lax.psum_scatter(grad_gate_main, ZED, scatter_dimension=0, tiled=True),
+        lax.psum_scatter(grad_step_main, ZED, scatter_dimension=0, tiled=True),
+        lax.psum_scatter(grad_output_main, ZED, scatter_dimension=1, tiled=True),
     )
     first_head = (head_index == 0).astype(jnp.float32)
     square_sum = jnp.zeros((), jnp.float32)
@@ -554,7 +557,7 @@
             place_slice(grad_taps_b, state_index, state_parts, 1),
             place_slice(grad_taps_c, state_index, state_parts, 1),
         ),
-        ("dp", "head", "state"),
+        EVERY,
     )
     (
         square_total,
@@ -608,79 +611,869 @@
     )
 
 
+low = jnp.bfloat16
+full = jnp.float32
+
+
+def head_masks():
+    count = lax.axis_size(HEAD)
+    masks = [1 << bit for bit in range(count.bit_length() - 1)]
+    return masks[:1] + masks[1:], masks[:1] + masks[1:][::-1]
+
+
+def head_swap(value, mask):
+    count = lax.axis_size(HEAD)
+    return lax.ppermute(value, HEAD, [(i, i ^ mask) for i in range(count)])
+
+
+def state_swap(value):
+    return lax.ppermute(value, STATE, [(0, 1), (1, 0)])
+
+
+def dp_swap(value):
+    return lax.ppermute(value, DP, [(0, 1), (1, 0)])
+
+
+def state_forward(value):
+    return lax.ppermute(value, STATE, [(0, 1)])
+
+
+def state_backward(value):
+    return lax.ppermute(value, STATE, [(1, 0)])
+
+
+def bit_of(mask):
+    return (lax.axis_index(HEAD) // mask) % 2
+
+
+def chunk_of(masks):
+    chunk = 0
+    for mask in masks:
+        chunk = chunk * 2 + bit_of(mask)
+    return chunk
+
+
+def sum_rows(value, masks, axis):
+    for mask in masks:
+        bit = bit_of(mask)
+        half = value.shape[axis] // 2
+        away = lax.dynamic_slice_in_dim(value, (1 - bit) * half, half, axis).astype(low)
+        kept = lax.dynamic_slice_in_dim(value, bit * half, half, axis)
+        value = kept.astype(full) + head_swap(away, mask).astype(full)
+    return value
+
+
+def gather_rows(value, masks, axis):
+    for mask in masks[::-1]:
+        bit = bit_of(mask)
+        got = head_swap(value, mask)
+        value = jnp.concatenate(
+            [jnp.where(bit == 1, got, value), jnp.where(bit == 1, value, got)], axis
+        )
+    return value
+
+
+def sum_row16(value, masks):
+    state = lax.axis_index(STATE)
+    value = sum_rows(value, masks, 1)
+    away = lax.dynamic_index_in_dim(value, 1 - state, 0, False).astype(low)
+    kept = lax.dynamic_index_in_dim(value, state, 0, False)
+    return kept + state_swap(away).astype(full)
+
+
+def gather_row16(value, masks):
+    state = lax.axis_index(STATE)
+    got = state_swap(value)
+    both = jnp.stack([jnp.where(state == 0, value, got), jnp.where(state == 0, got, value)], 0)
+    return gather_rows(both, masks, 1)
+
+
+def pick_state(pair, index):
+    return jnp.where(index == 0, pair[0], pair[1])
+
+
+def weight_pieces(shard, axis):
+    state = lax.axis_index(STATE)
+    dp = lax.axis_index(DP)
+    half = shard.shape[axis] // 2
+    mine = lax.dynamic_slice_in_dim(shard, state * half, half, axis)
+    got = state_swap(lax.dynamic_slice_in_dim(shard, (1 - state) * half, half, axis))
+    far_mine = dp_swap(mine)
+    far_got = dp_swap(got)
+    near = [jnp.where(state == 0, mine, got), jnp.where(state == 0, got, mine)]
+    far = [jnp.where(state == 0, far_mine, far_got), jnp.where(state == 0, far_got, far_mine)]
+    lower = [jnp.where(dp == 0, a, b) for a, b in zip(near, far)]
+    upper = [jnp.where(dp == 0, b, a) for a, b in zip(near, far)]
+    return jnp.concatenate(lower + upper, 1 - axis)
+
+
+def grad_pieces(grad, axis):
+    state = lax.axis_index(STATE)
+    dp = lax.axis_index(DP)
+    half = grad.shape[1 - axis] // 2
+    away = lax.dynamic_slice_in_dim(grad, (1 - dp) * half, half, 1 - axis).astype(low)
+    kept = lax.dynamic_slice_in_dim(grad, dp * half, half, 1 - axis)
+    total = kept + dp_swap(away).astype(full)
+    quarter = half // 2
+    away = lax.dynamic_slice_in_dim(total, (1 - state) * quarter, quarter, 1 - axis).astype(low)
+    kept = lax.dynamic_slice_in_dim(total, state * quarter, quarter, 1 - axis)
+    got = state_swap(away).astype(full)
+    return jnp.concatenate(
+        [jnp.where(state == 0, kept, got), jnp.where(state == 0, got, kept)], axis
+    )
+
+
+def norm_scale(values):
+    return lax.rsqrt(jnp.mean(values * values, -1, keepdims=True) + epsilon)
+
+
+def norm_back(values, gain, grad):
+    scale = norm_scale(values)
+    scaled = grad * gain
+    inner = jnp.mean(scaled * values, -1, keepdims=True)
+    return (
+        scale * scaled - values * (scale * scale * scale * inner),
+        jnp.sum(grad * values * scale, 0),
+    )
+
+
+def conv_edge(values, edge, taps, segment, edge_segment):
+    reach = taps.shape[0] - 1
+    rows = values.shape[0]
+    joined = jnp.concatenate([edge, values], 0)
+    segs = jnp.concatenate([edge_segment, segment], 0)
+    total = taps[0][None, :] * values
+    for offset in range(1, taps.shape[0]):
+        lower = reach - offset
+        same = (segs[lower : lower + rows] == segment).astype(values.dtype)[:, None]
+        total = total + taps[offset][None, :] * joined[lower : lower + rows] * same
+    return total
+
+
+def scan_blocks(inputs, step_sizes, decay, input_vecs, read_vecs, segment, before, block):
+    length, heads = step_sizes.shape
+    width = inputs.shape[1] // heads
+    count = length // block
+    states = input_vecs.shape[1]
+    state = jnp.zeros((heads, states, width), full)
+    last = before
+    outputs, entries = [], []
+    since = jnp.zeros((heads,), full)
+    for index in range(count):
+        part = slice(index * block, (index + 1) * block)
+        group_in = inputs[part].reshape(block, heads, width).transpose(1, 0, 2)
+        group_dt = step_sizes[part].T
+        group_b, group_c, group_seg = input_vecs[part], read_vecs[part], segment[part]
+        cumul = jnp.cumsum(group_dt * decay[:, None], 1)
+        places = jnp.arange(block, dtype=jnp.int32)
+        allowed = (group_seg[:, None] == group_seg[None, :]) & (places[None, :] <= places[:, None])
+        gaps = cumul[:, :, None] - cumul[:, None, :]
+        fading = jnp.where(allowed, jnp.exp(jnp.where(allowed, gaps, 0.0)), 0.0)
+        inner = right_dot(group_c, group_b)
+        scaled = group_in * group_dt[:, :, None]
+        local_out = jnp.einsum(
+            "hts,hsp->htp", inner[None] * fading, scaled, preferred_element_type=full
+        )
+        carried = (group_seg == last).astype(full)
+        entry = jnp.exp(cumul) * carried[None, :]
+        from_state = jnp.einsum("tn,hnp->htp", group_c, state) * entry[:, :, None]
+        first_seg = (group_seg == before).astype(full)
+        entries.append((jnp.exp(cumul + since[:, None]) * first_seg[None, :]).T)
+        since = since + cumul[:, -1]
+        last_seg = group_seg[-1]
+        reach = (group_seg == last_seg).astype(full)
+        to_end = jnp.exp(cumul[:, -1:] - cumul) * reach[None, :]
+        retain = jnp.exp(cumul[:, -1]) * (last_seg == last).astype(full)
+        fresh = jnp.einsum("sn,hsp->hnp", group_b, to_end[:, :, None] * scaled)
+        state = state * retain[:, None, None] + fresh
+        last = last_seg
+        outputs.append(
+            (local_out + from_state).transpose(1, 0, 2).reshape(block, heads * width)
+        )
+    carry = jnp.exp(since) * (last == before).astype(full)
+    return jnp.concatenate(outputs, 0), state, jnp.concatenate(entries, 0), carry
+
+
+def fast_device(
+    hidden,
+    embedding,
+    cotangent,
+    lengths,
+    gain_attn,
+    w_query,
+    w_key,
+    w_value,
+    down_query,
+    down_key,
+    down_value,
+    up_query,
+    up_key,
+    up_value,
+    attn_output,
+    gain_mlp,
+    mlp_input,
+    down_mlp,
+    up_mlp,
+    mlp_output,
+    gain_mixer,
+    proj_inner,
+    proj_gate,
+    proj_step,
+    proj_input,
+    proj_read,
+    taps_inner,
+    taps_input,
+    taps_read,
+    step_bias,
+    log_rate,
+    skip_gain,
+    gain_gated,
+    proj_output,
+):
+    zed = ZED
+    everywhere = EVERY
+    rows = hidden.shape[0]
+    length = cotangent.shape[0]
+    width = hidden.shape[1]
+    middle = rows // 2
+    head_parts = lax.axis_size(HEAD)
+    piece = middle // head_parts
+    state = lax.axis_index(STATE)
+    dp = lax.axis_index(DP)
+    head = lax.axis_index(HEAD)
+    own_start = state * rows
+    orders = head_masks()
+    offsets = [chunk_of(orders[0]) * piece, middle + chunk_of(orders[1]) * piece]
+    halves = [(offset, order) for offset, order in zip(offsets, orders)]
+    segment, position, valid = row_layout(lengths[0], length)
+    own_segment = lax.dynamic_slice_in_dim(segment, own_start, rows)
+    own_valid = lax.dynamic_slice_in_dim(valid, own_start, rows)[:, None]
+
+    def cut(value):
+        return [lax.dynamic_slice_in_dim(value, offset, piece, 0) for offset in offsets]
+
+    valid_cut = cut(own_valid)
+
+    gains = lax.all_gather(
+        jnp.concatenate([gain_attn, gain_mlp, gain_mixer]), zed, axis=0, tiled=False
+    ).astype(full)
+    split_a, split_m = gain_attn.shape[0], gain_mlp.shape[0]
+    attn_gain = gains[:, :split_a].reshape(-1)
+    mlp_gain = gains[:, split_a : split_a + split_m].reshape(-1)
+    mixer_gain = gains[:, split_a + split_m :].reshape(-1)
+
+    query_main = weight_pieces(w_query, 1)
+    key_main = weight_pieces(w_key, 1)
+    value_main = weight_pieces(w_value, 1)
+    ups = jnp.stack([up_query, up_key, up_value], 0)
+    half_cols = up_query.shape[1] // 2
+    ups_mine = lax.dynamic_slice_in_dim(ups, state * half_cols, half_cols, 2)
+    ups_got = state_swap(lax.dynamic_slice_in_dim(ups, (1 - state) * half_cols, half_cols, 2))
+    ups_near = jnp.concatenate(
+        [jnp.where(state == 0, ups_mine, ups_got), jnp.where(state == 0, ups_got, ups_mine)], 1
+    )
+    ups_far = dp_swap(ups_near)
+    ups_all = jnp.concatenate(
+        [jnp.where(dp == 0, ups_near, ups_far), jnp.where(dp == 0, ups_far, ups_near)], 1
+    )
+    query_upper, key_upper, value_upper = ups_all[0], ups_all[1], ups_all[2]
+
+    rank = down_query.shape[1]
+    part_a = down_query.shape[0] // head_parts
+    part_m = down_mlp.shape[0] // head_parts
+    downs = jnp.concatenate(
+        [
+            lax.dynamic_slice_in_dim(down_query, head * part_a, part_a, 0),
+            lax.dynamic_slice_in_dim(down_key, head * part_a, part_a, 0),
+            lax.dynamic_slice_in_dim(down_value, head * part_a, part_a, 0),
+            lax.dynamic_slice_in_dim(down_mlp, head * part_m, part_m, 0),
+        ],
+        0,
+    )
+    downs_got = state_swap(downs)
+    downs_near = jnp.stack(
+        [jnp.where(state == 0, downs, downs_got), jnp.where(state == 0, downs_got, downs)], 0
+    )
+    downs_far = dp_swap(downs_near)
+    downs_all = jnp.concatenate(
+        [jnp.where(dp == 0, downs_near, downs_far), jnp.where(dp == 0, downs_far, downs_near)], 0
+    )
+    masks = orders[0][::-1]
+    downs_all = gather_rows(downs_all[None], masks, 0)
+
+    def down_of(lower, part):
+        return downs_all[:, :, lower : lower + part].transpose(1, 0, 2, 3).reshape(-1, rank)
+
+    query_down = down_of(0, part_a)
+    key_down = down_of(part_a, part_a)
+    value_down = down_of(2 * part_a, part_a)
+    mlp_down = down_of(3 * part_a, part_m)
+
+    joined = jnp.concatenate([hidden, embedding], 1).astype(full)
+    normed_own = rms_norm(joined, attn_gain).astype(low)
+    joined_cut = [
+        jnp.concatenate([a, b], 1).astype(full) for a, b in zip(cut(hidden), cut(embedding))
+    ]
+    normed_far = jnp.concatenate(
+        [
+            gather_rows(state_swap(rms_norm(value, attn_gain).astype(low)), order, 0)
+            for value, (offset, order) in zip(joined_cut, halves)
+        ],
+        0,
+    )
+    normed = jnp.concatenate(
+        [
+            jnp.where(state == 0, normed_own, normed_far),
+            jnp.where(state == 0, normed_far, normed_own),
+        ],
+        0,
+    )
+    head_count = query_main.shape[1] // HDIM
+
+    def project(main, down, upper):
+        reduced = plain_dot(normed, down).astype(low)
+        return (plain_dot(normed, main) + plain_dot(reduced, upper), reduced)
+
+    def as_heads(value):
+        return value.reshape(length, head_count, HDIM)
+
+    query_pre, query_red = project(query_main, query_down, query_upper)
+    key_pre, key_red = project(key_main, key_down, key_upper)
+    value_pre, value_red = project(value_main, value_down, value_upper)
+    queries = rotate(as_heads(query_pre), position).astype(low)
+    keys = rotate(as_heads(key_pre), position).astype(low)
+    values = as_heads(value_pre).astype(low)
+
+    (
+        mlp_input,
+        up_mlp,
+        mlp_output,
+        proj_inner,
+        proj_gate,
+        proj_step,
+        proj_output,
+        value_main,
+    ) = lax.optimization_barrier(
+        (
+            mlp_input,
+            up_mlp,
+            mlp_output,
+            proj_inner,
+            proj_gate,
+            proj_step,
+            proj_output,
+            value_main,
+        )
+    )
+    attn_proj = weight_pieces(attn_output, 0)
+    mlp_main = lax.all_gather(mlp_input, zed, axis=0, tiled=True)
+    mlp_upper = lax.all_gather(up_mlp, zed, axis=0, tiled=True)
+    mlp_proj = lax.all_gather(mlp_output, zed, axis=1, tiled=True)
+    inner_main = lax.all_gather(proj_inner, zed, axis=0, tiled=True)
+    gate_main = lax.all_gather(proj_gate, zed, axis=0, tiled=True)
+    step_main = lax.all_gather(proj_step, zed, axis=0, tiled=True)
+    output_main = lax.all_gather(proj_output, zed, axis=1, tiled=True)
+
+    places = jnp.arange(length, dtype=jnp.int32)
+    allowed = (segment[:, None] == segment[None, :]) & (places[None, :] <= places[:, None])
+    probs = head_probs(queries, keys, allowed)
+    attended = (
+        jnp.einsum("hts,shd->thd", probs.astype(low), values, preferred_element_type=full)
+        .reshape(length, head_count * HDIM)
+        .astype(low)
+    )
+
+    def state_halves(value):
+        cubes = value.reshape(2, 2, middle, value.shape[1])
+        return [cubes[:, 0], cubes[:, 1]]
+
+    def from_halves(pair):
+        return jnp.stack(pair, 1).reshape(length, pair[0].shape[-1])
+
+    branch_cut = [
+        sum_row16(plain_dot(part.reshape(rows, -1), attn_proj).reshape(2, middle, width), order)
+        for part, (offset, order) in zip(state_halves(attended), halves)
+    ]
+    first_cut = [
+        value.astype(full) + good * branch
+        for value, good, branch in zip(cut(hidden), valid_cut, branch_cut)
+    ]
+    mlp_normed = [
+        gather_rows(rms_norm(value, mlp_gain).astype(low), order, 0)
+        for value, (offset, order) in zip(first_cut, halves)
+    ]
+    mlp_red = [plain_dot(value, mlp_down).astype(low) for value in mlp_normed]
+    hidden_pre = [
+        plain_dot(value, mlp_main) + plain_dot(red, mlp_upper)
+        for value, red in zip(mlp_normed, mlp_red)
+    ]
+    activated = [jax.nn.gelu(value, approximate=False).astype(low) for value in hidden_pre]
+    second_cut = [
+        value + good * sum_rows(plain_dot(part, mlp_proj), order, 0)
+        for value, good, part, (offset, order) in zip(first_cut, valid_cut, activated, halves)
+    ]
+    mixer_halves = [
+        gather_rows(rms_norm(value, mixer_gain).astype(low), order, 0)
+        for value, (offset, order) in zip(second_cut, halves)
+    ]
+    mixer_normed = jnp.concatenate(mixer_halves, 0)
+
+    inner_pre = plain_dot(mixer_normed, inner_main)
+    gate_pre = plain_dot(mixer_normed, gate_main)
+    small_main = jnp.concatenate([step_main, proj_input, proj_read], 1)
+    small_pre = plain_dot(mixer_normed, small_main)
+    mixer_heads = step_main.shape[1]
+    states = proj_input.shape[1]
+    reach = taps_inner.shape[0] - 1
+    edge = state_forward(
+        jnp.concatenate([inner_pre[rows - reach :], small_pre[rows - reach :, mixer_heads:]], 1)
+    )
+    inner_width = inner_pre.shape[1]
+    edge_start = jnp.maximum(own_start - reach, 0)
+    edge_segment = jnp.where(
+        state == 0, -1, lax.dynamic_slice_in_dim(segment, edge_start, reach)
+    )
+    before = edge_segment[-1]
+
+    def mixer_piece(inner_in, small_in, edge_in, taps_x, taps_b, taps_c, shift_in, rate_in):
+        step_in = small_in[:, :mixer_heads]
+        input_in = small_in[:, mixer_heads : mixer_heads + states]
+        read_in = small_in[:, mixer_heads + states :]
+        edge_b = edge_in[:, inner_width : inner_width + states]
+        edge_c = edge_in[:, inner_width + states :]
+        inner_conv = jax.nn.silu(
+            conv_edge(inner_in, edge_in[:, :inner_width], taps_x, own_segment, edge_segment)
+        )
+        input_conv = jax.nn.silu(conv_edge(input_in, edge_b, taps_b, own_segment, edge_segment))
+        read_conv = jax.nn.silu(conv_edge(read_in, edge_c, taps_c, own_segment, edge_segment))
+        step_sizes = jax.nn.softplus(step_in + shift_in[None, :])
+        outputs, last_state, entry, carry = scan_blocks(
+            inner_conv,
+            step_sizes,
+            -jnp.exp(rate_in),
+            input_conv,
+            read_conv,
+            own_segment,
+            before,
+            GROUP,
+        )
+        return outputs, inner_conv, last_state, read_conv, entry
+
+    (scanned_own, inner_conv, last_state, read_conv, entry), mixer_back = jax.vjp(
+        mixer_piece,
+        inner_pre,
+        small_pre,
+        edge,
+        taps_inner.astype(full),
+        taps_input.astype(full),
+        taps_read.astype(full),
+        step_bias.astype(full),
+        log_rate.astype(full),
+    )
+    first_state = state_forward(last_state)
+
+    def by_head(value):
+        return value.reshape(rows, mixer_heads, MDIM)
+
+    def flat(value):
+        return value.reshape(rows, mixer_heads * MDIM)
+
+    from_first = jnp.einsum("tn,hnp->thp", read_conv, first_state)
+    scanned = scanned_own + flat(from_first * entry[:, :, None])
+    skip_full = jnp.repeat(skip_gain.astype(full), MDIM)[None, :]
+    combined = scanned + skip_full * inner_conv
+    gate_act = jax.nn.silu(gate_pre)
+    united = combined * gate_act
+    gated_gain = gain_gated.astype(full)[None, :]
+    cot_own = lax.dynamic_slice_in_dim(cotangent, own_start, rows, 0)
+    mix_grad = cot_own * own_valid.astype(low)
+    gated_grad = right_dot(mix_grad, output_main)
+    pair = jnp.stack(
+        [jnp.sum(united * united, 1), jnp.sum(united * gated_gain * gated_grad, 1)], 0
+    )
+    for mask in orders[0]:
+        pair = pair + head_swap(pair, mask)
+    channels = inner_width * head_parts
+    row_scale = lax.rsqrt(pair[0] / channels + epsilon)[:, None]
+    row_total = pair[1][:, None]
+    gated = (united * row_scale * gated_gain).astype(low)
+    out_cut = [
+        (
+            value
+            + good
+            * sum_rows(
+                plain_dot(gated[index * middle : (index + 1) * middle], output_main), order, 0
+            )
+        ).astype(low)
+        for index, (value, good, (offset, order)) in enumerate(
+            zip(second_cut, valid_cut, halves)
+        )
+    ]
+    layer_out = from_halves(
+        [gather_row16(value, order) for value, (offset, order) in zip(out_cut, halves)]
+    )
+
+    grad_output_main = left_dot(gated, mix_grad).astype(low)
+    grad_gated_gain = jnp.sum(gated_grad * united * row_scale, 0)
+    united_grad = (
+        row_scale * gated_gain * gated_grad
+        - united * row_scale * row_scale * row_scale * row_total / channels
+    )
+    combined_grad = united_grad * gate_act
+    sigmoid_gate = jax.nn.sigmoid(gate_pre)
+    gate_grad = united_grad * combined * sigmoid_gate * (1.0 + gate_pre * (1.0 - sigmoid_gate))
+    grad_skip = jnp.sum(by_head(combined_grad * inner_conv), (0, 2))
+    conv_extra = skip_full * combined_grad
+    entry_grad = by_head(combined_grad) * entry[:, :, None]
+    first_state_grad = jnp.einsum("tn,thp->hnp", read_conv, entry_grad)
+    last_state_grad = state_backward(first_state_grad)
+    read_extra = jnp.einsum("thp,hnp->tn", entry_grad, first_state)
+    entry_extra = jnp.sum(by_head(combined_grad) * from_first, 2)
+    (
+        inner_grad,
+        small_grad,
+        edge_grad,
+        grad_taps_x,
+        grad_taps_b,
+        grad_taps_c,
+        grad_shift,
+        grad_rate,
+    ) = mixer_back((combined_grad, conv_extra, last_state_grad, read_extra, entry_extra))
+    edge_back = state_backward(edge_grad)
+    inner_grad = inner_grad.at[rows - reach :].add(edge_back[:, :inner_width])
+    small_grad = small_grad.at[rows - reach :, mixer_heads:].add(edge_back[:, inner_width:])
+    inner_low = inner_grad.astype(low)
+    gate_low = gate_grad.astype(low)
+    small_low = small_grad.astype(low)
+    mixer_sum = [
+        sum_rows(
+            right_dot(inner_low[part], inner_main)
+            + right_dot(gate_low[part], gate_main)
+            + right_dot(small_low[part], small_main),
+            order,
+            0,
+        )
+        for part, (offset, order) in zip((slice(0, middle), slice(middle, rows)), halves)
+    ]
+    grad_inner_main = left_dot(mixer_normed, inner_low).astype(low)
+    grad_gate_main = left_dot(mixer_normed, gate_low).astype(low)
+    grad_small_main = left_dot(mixer_normed, small_low)
+    upstream_cut = [value.astype(full) for value in cut(cot_own)]
+    mixer_backs = [
+        norm_back(value, mixer_gain, grad) for value, grad in zip(second_cut, mixer_sum)
+    ]
+    second_grad = [up + back[0] for up, back in zip(upstream_cut, mixer_backs)]
+    grad_mixer_gain = mixer_backs[0][1] + mixer_backs[1][1]
+    mlp_grad = [
+        gather_rows((good * grad).astype(low), order, 0)
+        for good, grad, (offset, order) in zip(valid_cut, second_grad, halves)
+    ]
+
+    def gelu_part(value):
+        return jax.nn.gelu(value, approximate=False)
+
+    hidden_grad = [
+        jax.vjp(gelu_part, pre)[1](right_dot(grad, mlp_proj))[0].astype(low)
+        for pre, grad in zip(hidden_pre, mlp_grad)
+    ]
+    mlp_sums = [
+        sum_rows(
+            jnp.concatenate([right_dot(grad, mlp_main), right_dot(grad, mlp_upper)], 1), order, 0
+        )
+        for grad, (offset, order) in zip(hidden_grad, halves)
+    ]
+    middle_low = [value[:, width:].astype(low) for value in mlp_sums]
+    mlp_backs = [
+        norm_back(value, mlp_gain, total[:, :width] + right_dot(mid, mlp_down))
+        for value, total, mid in zip(first_cut, mlp_sums, middle_low)
+    ]
+    first_grad = [grad + back[0] for grad, back in zip(second_grad, mlp_backs)]
+    grad_mlp_gain = mlp_backs[0][1] + mlp_backs[1][1]
+    branch_wide = [
+        gather_row16(jnp.concatenate([(good * grad).astype(low), mid], 1), order)
+        for good, grad, mid, (offset, order) in zip(valid_cut, first_grad, middle_low, halves)
+    ]
+    branch_all = from_halves(branch_wide)
+    branch_grad = branch_all[:, :width]
+    middle_own = lax.dynamic_slice(branch_all, (own_start, width), (rows, rank))
+    activated_own = jnp.concatenate(activated, 0)
+    mlp_normed_own = jnp.concatenate(mlp_normed, 0)
+    hidden_grad_own = jnp.concatenate(hidden_grad, 0)
+    grad_mlp_proj = left_dot(activated_own, jnp.concatenate(mlp_grad, 0)).astype(low)
+    grad_mlp_main = left_dot(mlp_normed_own, hidden_grad_own).astype(low)
+    grad_mlp_upper = left_dot(jnp.concatenate(mlp_red, 0), hidden_grad_own).astype(low)
+    grad_mlp_down = left_dot(mlp_normed_own, middle_own).astype(low)
+
+    def scatter(value, axis):
+        return lax.psum_scatter(value, zed, scatter_dimension=axis, tiled=True).astype(full)
+
+    out_output = scatter(grad_output_main, 1)
+    out_inner = scatter(grad_inner_main, 0)
+    out_gate = scatter(grad_gate_main, 0)
+    out_mlp_output = scatter(grad_mlp_proj, 1)
+    out_mlp_input = scatter(grad_mlp_main, 0)
+    out_up_mlp = scatter(grad_mlp_upper, 0)
+    out_down_mlp = scatter(grad_mlp_down, 0)
+
+    out_attn = grad_pieces(left_dot(attended, branch_grad), 0)
+    attended_grad = as_heads(right_dot(branch_grad, attn_proj))
+    probs_back = head_probs(queries, keys, allowed)
+    score_scale = HDIM ** (-0.5)
+    out_low = attended_grad.astype(low)
+    prob_grad = jnp.einsum("thd,shd->hts", out_low, values, preferred_element_type=full)
+    score_grad = probs_back * (prob_grad - jnp.sum(probs_back * prob_grad, -1, keepdims=True))
+    score_low = score_grad.astype(low)
+    query_back = (
+        jnp.einsum("hts,shd->thd", score_low, keys, preferred_element_type=full) * score_scale
+    )
+    keys_back = (
+        jnp.einsum("hts,thd->shd", score_low, queries, preferred_element_type=full) * score_scale
+    )
+    values_back = jnp.einsum(
+        "hts,thd->shd", probs_back.astype(low), out_low, preferred_element_type=full
+    )
+
+    def as_flat(value):
+        return value.reshape(length, head_count * HDIM).astype(low)
+
+    query_grad = as_flat(rotate(query_back, -position))
+    key_grad = as_flat(rotate(keys_back, -position))
+    value_grad = as_flat(values_back)
+    out_query = grad_pieces(left_dot(normed, query_grad), 1)
+    out_key = grad_pieces(left_dot(normed, key_grad), 1)
+    out_value = grad_pieces(left_dot(normed, value_grad), 1)
+    out_ups = jnp.concatenate(
+        [
+            left_dot(query_red, query_grad),
+            left_dot(key_red, key_grad),
+            left_dot(value_red, value_grad),
+        ],
+        1,
+    )
+    rank_half = rank // 2
+    ups_away = lax.dynamic_slice_in_dim(out_ups, (1 - dp) * rank_half, rank_half, 0)
+    ups_sum = lax.dynamic_slice_in_dim(out_ups, dp * rank_half, rank_half, 0) + dp_swap(ups_away)
+    rank_quarter = rank_half // 2
+    ups_kept = lax.dynamic_slice_in_dim(ups_sum, state * rank_quarter, rank_quarter, 0)
+    ups_back = state_swap(
+        lax.dynamic_slice_in_dim(ups_sum, (1 - state) * rank_quarter, rank_quarter, 0)
+    )
+
+    def up_of(index):
+        part = slice(index * half_cols, (index + 1) * half_cols)
+        return jnp.concatenate(
+            [
+                jnp.where(state == 0, ups_kept[:, part], ups_back[:, part]),
+                jnp.where(state == 0, ups_back[:, part], ups_kept[:, part]),
+            ],
+            1,
+        )
+
+    normed_parts = state_halves(
+        jnp.concatenate(
+            [
+                right_dot(query_grad, query_main)
+                + right_dot(key_grad, key_main)
+                + right_dot(value_grad, value_main),
+                right_dot(query_grad, query_upper),
+                right_dot(key_grad, key_upper),
+                right_dot(value_grad, value_upper),
+            ],
+            1,
+        )
+    )
+    normed_sums = [sum_row16(part, order) for part, (offset, order) in zip(normed_parts, halves)]
+    joint = 2 * width
+    lows = [value[:, joint:].astype(low) for value in normed_sums]
+    joined_backs = [
+        norm_back(
+            value,
+            attn_gain,
+            total[:, :joint]
+            + right_dot(mid[:, :rank], query_down)
+            + right_dot(mid[:, rank : 2 * rank], key_down)
+            + right_dot(mid[:, 2 * rank :], value_down),
+        )
+        for value, total, mid in zip(joined_cut, normed_sums, lows)
+    ]
+    grad_attn_gain = joined_backs[0][1] + joined_backs[1][1]
+    input_grads = jnp.concatenate(
+        [
+            gather_rows(
+                jnp.concatenate(
+                    [(grad + back[0][:, :width]).astype(low), back[0][:, width:].astype(low)], 1
+                ),
+                order,
+                0,
+            )
+            for grad, back, (offset, order) in zip(first_grad, joined_backs, halves)
+        ],
+        0,
+    )
+    grad_hidden = input_grads[:, :width]
+    grad_embedding = input_grads[:, width:]
+
+    lows_all = from_halves(
+        [gather_row16(value, order) for value, (offset, order) in zip(lows, halves)]
+    )
+    quarter = gain_attn.shape[0]
+
+    def down_rows(index):
+        start = (index * 2 + state) * quarter + head * part_a
+        columns = lax.dynamic_slice_in_dim(normed, start, part_a, 1)
+        return left_dot(columns, lows_all)
+
+    down_sum = down_rows(dp) + dp_swap(down_rows(1 - dp).astype(low)).astype(full)
+    down_all = gather_rows(down_sum.astype(low)[None], masks, 0)
+    down_all = down_all.reshape(quarter, 3 * rank).astype(full)
+    out_downs = [down_all[:, index * rank : (index + 1) * rank] for index in range(3)]
+
+    small_total, taps_b_total, taps_c_total = lax.psum(
+        (grad_small_main[:, mixer_heads:], grad_taps_b, grad_taps_c), everywhere
+    )
+    out_step = lax.psum_scatter(
+        grad_small_main[:, :mixer_heads], zed, scatter_dimension=0, tiled=True
+    )
+    gated_total, taps_x_total, head_total = lax.psum(
+        (grad_gated_gain, grad_taps_x, jnp.stack([grad_shift, grad_rate, grad_skip], 0)), zed
+    )
+    once = (head == 0).astype(full)
+    square_sum = jnp.zeros((), full)
+    out_up = [up_of(index) for index in range(3)]
+    for value in [out_query, out_key, out_value, out_attn, out_mlp_input, out_up_mlp]:
+        square_sum = square_sum + jnp.sum(value * value)
+    for value in [out_mlp_output] + out_up:
+        square_sum = square_sum + jnp.sum(value * value)
+    for value in out_downs + [out_down_mlp]:
+        square_sum = square_sum + once * jnp.sum(value * value)
+    square_total, gain_total = lax.psum(
+        (square_sum, jnp.concatenate([grad_attn_gain, grad_mlp_gain, grad_mixer_gain])),
+        everywhere,
+    )
+    place = dp * 2 + state
+    wide = 2 * width
+
+    def gain_of(start, size, total):
+        return lax.dynamic_slice_in_dim(gain_total[start : start + total], place * size, size)
+
+    return (
+        layer_out,
+        grad_hidden,
+        grad_embedding,
+        gain_of(0, split_a, wide),
+        out_query,
+        out_key,
+        out_value,
+        out_downs[0],
+        out_downs[1],
+        out_downs[2],
+        out_up[0],
+        out_up[1],
+        out_up[2],
+        out_attn,
+        gain_of(wide, split_m, width),
+        out_mlp_input,
+        out_down_mlp,
+        out_up_mlp,
+        out_mlp_output,
+        gain_of(wide + width, split_m, width),
+        out_inner,
+        out_gate,
+        out_step,
+        small_total[:, :states],
+        small_total[:, states:],
+        taps_x_total,
+        taps_b_total,
+        taps_c_total,
+        head_total[0],
+        head_total[1],
+        head_total[2],
+        gated_total,
+        out_output,
+        jnp.sqrt(square_total),
+    )
+
+
+def pick_device(mesh):
+    heads = mesh.shape[HEAD]
+    per_head = DIN // HDIM // heads
+    halves = mesh.shape[DP] == 2 and mesh.shape[STATE] == 2
+    return fast_device if halves and heads & (heads - 1) == 0 and per_head % 2 == 0 else general_device
+
+
 def solution(mesh):
     in_specs = (
-        P(("dp", "state"), None),
-        P(("dp", "state"), None),
-        P("dp", None),
-        P("dp", None),
-        P(("dp", "state")),
-        P(("dp", "state"), "head"),
-        P(("dp", "state"), "head"),
-        P(("dp", "state"), "head"),
-        P(("dp", "state"), None),
-        P(("dp", "state"), None),
-        P(("dp", "state"), None),
-        P(("dp", "state"), "head"),
-        P(("dp", "state"), "head"),
-        P(("dp", "state"), "head"),
-        P("head", ("dp", "state")),
-        P(("dp", "state")),
-        P(("dp", "state"), "head"),
-        P(("dp", "state"), None),
-        P(("dp", "state"), "head"),
-        P("head", ("dp", "state")),
-        P(("dp", "state")),
-        P(("dp", "state"), "head"),
-        P(("dp", "state"), "head"),
-        P(("dp", "state"), "head"),
+        P(ZED, None),
+        P(ZED, None),
+        P(DP, None),
+        P(DP, None),
+        P(ZED),
+        P(ZED, HEAD),
+        P(ZED, HEAD),
+        P(ZED, HEAD),
+        P(ZED, None),
+        P(ZED, None),
+        P(ZED, None),
+        P(ZED, HEAD),
+        P(ZED, HEAD),
+        P(ZED, HEAD),
+        P(HEAD, ZED),
+        P(ZED),
+        P(ZED, HEAD),
+        P(ZED, None),
+        P(ZED, HEAD),
+        P(HEAD, ZED),
+        P(ZED),
+        P(ZED, HEAD),
+        P(ZED, HEAD),
+        P(ZED, HEAD),
         P(),
         P(),
-        P(None, "head"),
+        P(None, HEAD),
         P(),
         P(),
-        P("head"),
-        P("head"),
-        P("head"),
-        P("head"),
-        P("head", ("dp", "state")),
+        P(HEAD),
+        P(HEAD),
+        P(HEAD),
+        P(HEAD),
+        P(HEAD, ZED),
     )
     out_specs = (
-        P("dp", None),
-        P(("dp", "state"), None),
-        P(("dp", "state"), None),
-        P(("dp", "state")),
-        P(("dp", "state"), "head"),
-        P(("dp", "state"), "head"),
-        P(("dp", "state"), "head"),
-        P(("dp", "state"), None),
-        P(("dp", "state"), None),
-        P(("dp", "state"), None),
-        P(("dp", "state"), "head"),
-        P(("dp", "state"), "head"),
-        P(("dp", "state"), "head"),
-        P("head", ("dp", "state")),
-        P(("dp", "state")),
-        P(("dp", "state"), "head"),
-        P(("dp", "state"), None),
-        P(("dp", "state"), "head"),
-        P("head", ("dp", "state")),
-        P(("dp", "state")),
-        P(("dp", "state"), "head"),
-        P(("dp", "state"), "head"),
-        P(("dp", "state"), "head"),
+        P(DP, None),
+        P(ZED, None),
+        P(ZED, None),
+        P(ZED),
+        P(ZED, HEAD),
+        P(ZED, HEAD),
+        P(ZED, HEAD),
+        P(ZED, None),
+        P(ZED, None),
+        P(ZED, None),
+        P(ZED, HEAD),
+        P(ZED, HEAD),
+        P(ZED, HEAD),
+        P(HEAD, ZED),
+        P(ZED),
+        P(ZED, HEAD),
+        P(ZED, None),
+        P(ZED, HEAD),
+        P(HEAD, ZED),
+        P(ZED),
+        P(ZED, HEAD),
+        P(ZED, HEAD),
+        P(ZED, HEAD),
         P(),
         P(),
-        P(None, "head"),
+        P(None, HEAD),
         P(),
         P(),
-        P("head"),
-        P("head"),
-        P("head"),
-        P("head"),
-        P("head", ("dp", "state")),
+        P(HEAD),
+        P(HEAD),
+        P(HEAD),
+        P(HEAD),
+        P(HEAD, ZED),
         P(),
     )
     return jax.shard_map(
-        per_device, mesh=mesh, in_specs=in_specs, out_specs=out_specs, check_vma=False
-    )
+        pick_device(mesh), mesh=mesh, in_specs=in_specs, out_specs=out_specs, check_vma=False
+    )

time: 4570 us -> 2060 us (0.45)
  waiting for transfers between devices: 2980 us -> 771 us
  matrix products: 744 us -> 425 us
  blocking collectives: 300 us -> 101 us
  starting transfers between devices: 3.44 us -> 133 us
  other arithmetic: 295 us -> 373 us
    reduce_scatter x21 -> x8, waiting for transfers between devices: 1290 us -> 0.05 us  [the longest x7 0.05 us: scatter(): lax.psum_scatter(value, zed, scatter_dimension=axis, tiled=True)]
    psum x8 -> x1, waiting for transfers between devices: 869 us -> 0.02 us  [fast_device(): lax.psum((grad_small_main[:, mixer_heads:], grad_taps_b, grad_taps_c), ev...]
    all_gather x16 -> x5, waiting for transfers between devices: 815 us -> 37.9 us  [the longest x1 26.7 us: fast_device(): mlp_proj = lax.all_gather(mlp_output, zed, axis=1, tiled=True)]
    ppermute x0 -> x136, waiting for transfers between devices: none -> 733 us  [the longest x93 331 us: head_swap(): return lax.ppermute(value, HEAD, [(i, i ^ mask) for i in range(count)])]
    dot_general x127 -> x42, matrix products: 364 us -> 103 us  [the longest x1 22.1 us: fast_device(): jnp.einsum('thd,shd->hts', out_low, values, preferred_element_type=full)]
    ppermute x0 -> x136, starting transfers between devices: none -> 132 us  [the longest x93 90.1 us: head_swap(): return lax.ppermute(value, HEAD, [(i, i ^ mask) for i in range(count)])]
    psum x4 -> x2, blocking collectives: 155 us -> 56 us  [the longest x1 37.4 us: fast_device(): lax.psum((square_sum, jnp.concatenate([grad_attn_gain, grad_mlp_gain, gra...]
    all_gather x9 -> x3, blocking collectives: 123 us -> 45.5 us  [the longest x1 17.6 us: fast_device(): mlp_upper = lax.all_gather(up_mlp, zed, axis=0, tiled=True)]
  transfers between devices with their start and end apart: 45 -> 150, of which waited for: 37 -> 78; matrix products, arithmetic and copies ran while one was open for 15% -> 37% of each run, Pallas kernels for 0% -> 0%
where the time goes in v1:
time: 2060 us; the launch traced here: 2050 us
  waiting for transfers between devices  771 us (37%)
  matrix products  425 us (21%)
  other arithmetic  373 us (18%)
  local copies, waits for them, and re-layouts  207 us (10%)
  starting transfers between devices  133 us (6%)
  blocking collectives  101 us (5%)
  between operations  38 us (2%)
    ppermute x93, waiting for transfers between devices, head_swap(): return lax.ppermute(value, HEAD, [(i, i ^ mask) for i in range(count)])  331 us
    ppermute x23, waiting for transfers between devices, state_swap(): return lax.ppermute(value, STATE, [(0, 1), (1, 0)])  206 us
    ppermute x16, waiting for transfers between devices, dp_swap(): return lax.ppermute(value, DP, [(0, 1), (1, 0)])  190 us
    dot_general x24, matrix products, plain_dot(): return jnp.dot(left, right, preferred_element_type=jnp.float32)  116 us
    dot_general x40, matrix products, right_dot(): lax.dot_general(left, right, (((1,), (1,)), ((), ())), preferred_element_...  115 us
    ppermute x93, starting transfers between devices, head_swap(): return lax.ppermute(value, HEAD, [(i, i ^ mask) for i in range(count)])  90.1 us
    unnamed x1016, local copies, waits for them, and re-layouts  89.6 us
    dot_general x17, matrix products, left_dot(): lax.dot_general(left, right, (((0,), (0,)), ((), ())), preferred_element_...  69.9 us
  transfers between devices with their start and end apart: 150, of which 78 were waited for; matrix products, arithmetic and copies ran while one was open for 37% of the time, Pallas kernels for 0%

profile of v1, /device:TPU:0, one launch (start us, length us, event | category | flops | bytes accessed | tf_op | source)
XLA Modules:
  0.0 2048.0 jit_solution(17178017041944661167)
XLA Ops:
  10.0 14.8 all-gather
  66.3 16.1 collective-permute-done.12
  102.0 27.3 %collective-permute-done.18 = bf16[1024,256]{0,1:T(8,128)(2,1)S(1)} collective-permute-done((bf16[1024,256]{0,1:T(8,128)(2,1)}, bf16[1024,256]{0,1:T(8,128)(2,1)S(1)}, u32[]{:S(2)}, u32[]{:S(2)}) %collective-permute-start.18) | collective-permute-done | bytes 524320 | tf_op jit(solution)/shard_map/ppermute | solution.py:630
  132.0 11.4 collective-permute-done.5
  146.2 26.3 %collective-permute-done.20 = bf16[1024,256]{0,1:T(8,128)(2,1)S(1)} collective-permute-done((bf16[1024,256]{0,1:T(8,128)(2,1)S(1)}, bf16[1024,256]{0,1:T(8,128)(2,1)S(1)}, u32[]{:S(2)}, u32[]{:S(2)}) %collective-permute-start.20) | collective-permute-done | bytes 524320 | tf_op jit(solution)/shard_map/ppermute | solution.py:634
  179.1 18.4 collective-permute-done.2
  199.7 17.7 collective-permute-done.22
  228.7 11.2 collective-permute-done.10
  239.9 11.1 collective-permute-done.23
  269.2 19.1 broadcast_select_fusion.1
  288.3 10.6 convolution_convert_fusion.4
  361.8 21.4 %fusion.672 = (f32[2,2048]{1,0:T(2,128)S(1)}, f32[2,2048,2048]{1,2,0:T(8,128)}) fusion(pred[2048,2048]{0,1:T(8,128)(4,1)} %fusion.7, bf16[2048,2,64]{2,0,1:T(8,128)(2,1)S(1)} %get-tuple-element.518, bf16[2048,2,64]{2,0,1:T(8,128)(2,1)S(1)} %get-tuple-element.519, bf16[2048,2,64]{2,0,1:T(8,128)(2,1)} %get-tuple-element.437, ...), kind=kOutput, calls=%fused_computation.1362 | convolution fusion | flops 2185234432 | bytes 39862272 | tf_op jit(solution)/shard_map/sub | solution.py:80
  393.0 12.4 fusion.40
  440.0 15.6 collective-permute-done.41
  477.5 24.7 %collective-permute-done.43 = bf16[64,2048]{1,0:T(8,128)(2,1)S(1)} collective-permute-done((bf16[64,2048]{1,0:T(8,128)(2,1)S(1)}, bf16[64,2048]{1,0:T(8,128)(2,1)S(1)}, u32[]{:S(2)}, u32[]{:S(2)}) %collective-permute-start.43) | collective-permute-done | bytes 262176 | tf_op jit(solution)/shard_map/ppermute | solution.py:630
  502.5 10.9 collective-permute-done.30
  541.0 17.6 all_gather.30
  563.6 11.2 multiply_convert_fusion.3
  574.8 26.7 %all-gather.9.cloned.1.call-done = bf16[1024,2048]{1,0:T(8,128)(2,1)} async-done(((bf16[1024,512]{1,0:T(8,128)(2,1)}), bf16[1024,2048]{1,0:T(8,128)(2,1)}) %all-gather.9.cloned.1.call-update) | async-done | bytes 4194320 | tf_op jit(solution)/shard_map/all_gather | solution.py:971
  665.4 13.1 all_gather.32
  757.8 11.2 all-gather.15.cloned.1.call-done
  1056.2 12.0 collective-permute-done.94
  1094.2 10.8 collective-permute-done.96
  1192.1 16.9 collective-permute-done.61
  1210.6 16.5 collective-permute-done.68
  1230.6 12.5 collective-permute-done.69
  1245.9 17.3 collective-permute-done.63
  1266.6 18.5 all-reduce.55
  1334.3 22.1 %multiply_reduce_fusion = (f32[2,2048]{1,0:T(2,128)S(1)}, f32[2,2048,2048]{1,2,0:T(8,128)}) fusion(f32[2,2048,2048]{1,2,0:T(8,128)} %get-tuple-element.759, f32[2,2048]{1,0:T(2,128)S(1)} %copy-done.377, bf16[2048,2,128]{0,2,1:T(8,128)(2,1)S(1)} %bitcast.1050, bf16[2048,2,128]{0,2,1:T(8,128)(2,1)S(1)} %bitcast.1049), kind=kOutput, calls=%fused_computation.4 | convolution fusion | flops 2172645376 | bytes 69238784 | tf_op jit(solution)/shard_map/thd,shd->hts/dot_general | solution.py:1223
  1356.4 29.5 %multiply_convert_fusion = bf16[2,2048,2048]{1,2,0:T(8,128)(2,1)} fusion(f32[2,2048,2048]{1,2,0:T(8,128)} %get-tuple-element.779, f32[2,2048]{1,0:T(2,128)S(1)} %get-tuple-element.778, f32[2,2048,2048]{1,2,0:T(8,128)} %get-tuple-element.759, f32[2,2048]{1,0:T(2,128)S(1)} %copy-done.377), kind=kLoop, calls=%fused_computation.3 | loop fusion | flops 33554432 | bytes 83918848 | tf_op jit(solution)/shard_map/convert_element_type | solution.py:1225
  1385.9 13.1 fusion.35
  1407.8 14.0 fusion.43
  1427.1 13.8 fusion.351
  1472.1 13.7 fusion.701
  1485.8 34.7 %add_add_fusion = f32[2048,4096]{1,0:T(8,128)} fusion(f32[2048,4096]{1,0:T(8,128)} %fusion.701, f32[2048,4096]{1,0:T(8,128)} %fusion.351, bf16[2048,256]{0,1:T(8,128)(2,1)S(1)} %bitcast.923, bf16[1024,256]{0,1:T(8,128)(2,1)} %get-tuple-element.525, bf16[1024,256]{0,1:T(8,128)(2,1)} %get-tuple-element.524, bf16[1024,256]{0,1:T(8,128)(2,1)} %get-tuple-element.523, ...), kind=kOutput, calls=%fused_computation.2 | convolution fusion | flops 4320133120 | bytes 103809024 | tf_op jit(solution)/shard_map/dot_general | solution.py:30
  1520.6 25.6 %pad_maximum_fusion = f32[2048,4480]{1,0:T(8,128)} fusion(f32[2048,128]{1,0:T(8,128)} %fusion.619, f32[2048,128]{1,0:T(8,128)S(1)} %fusion.615, f32[2048,128]{1,0:T(8,128)S(1)} %copy-done.129, f32[2048,4096]{1,0:T(8,128)} %add_add_fusion), kind=kLoop, calls=%fused_computation.1 | loop fusion | flops 27525120 | bytes 73400320 | tf_op jit(solution)/shard_map/concatenate | solution.py:1273
  1546.2 19.5 fusion.655
  1565.7 12.6 fusion.17
  1591.2 33.9 %collective-permute-done.132 = f32[64,768]{1,0:T(8,128)S(1)} collective-permute-done((f32[64,768]{1,0:T(8,128)S(1)}, f32[64,768]{1,0:T(8,128)S(1)}, u32[]{:S(2)}, u32[]{:S(2)}) %collective-permute-start.132) | collective-permute-done | bytes 196640 | tf_op jit(solution)/shard_map/ppermute | solution.py:634
  1625.4 35.5 %collective-permute-done.133 = f32[32,768]{1,0:T(8,128)S(1)} collective-permute-done((f32[32,768]{1,0:T(8,128)S(1)}, f32[32,768]{1,0:T(8,128)S(1)}, u32[]{:S(2)}, u32[]{:S(2)}) %collective-permute-start.133) | collective-permute-done | bytes 98336 | tf_op jit(solution)/shard_map/ppermute | solution.py:630
  1665.0 24.4 %collective-permute-done.135 = bf16[256,512]{1,0:T(8,128)(2,1)S(1)} collective-permute-done((bf16[256,512]{1,0:T(8,128)(2,1)S(1)}, bf16[256,512]{1,0:T(8,128)(2,1)S(1)}, u32[]{:S(2)}, u32[]{:S(2)}) %collective-permute-start.135) | collective-permute-done | bytes 262176 | tf_op jit(solution)/shard_map/ppermute | solution.py:630
  1695.2 35.7 %collective-permute-done.116 = bf16[2048,256]{0,1:T(8,128)(2,1)S(1)} collective-permute-done((bf16[2048,256]{0,1:T(8,128)(2,1)S(1)}, bf16[2048,256]{0,1:T(8,128)(2,1)S(1)}, u32[]{:S(2)}, u32[]{:S(2)}) %collective-permute-start.116) | collective-permute-done | bytes 1048608 | tf_op jit(solution)/shard_map/ppermute | solution.py:634
  1732.5 20.9 %collective-permute-done.114 = bf16[2048,256]{0,1:T(8,128)(2,1)S(1)} collective-permute-done((bf16[2048,256]{0,1:T(8,128)(2,1)S(1)}, bf16[2048,256]{0,1:T(8,128)(2,1)S(1)}, u32[]{:S(2)}, u32[]{:S(2)}) %collective-permute-start.114) | collective-permute-done | bytes 1048608 | tf_op jit(solution)/shard_map/ppermute | solution.py:634
  1816.8 26.2 %collective-permute-done.101 = bf16[2,128,4480]{2,1,0:T(8,128)(2,1)} collective-permute-done((bf16[2,128,4480]{2,1,0:T(8,128)(2,1)}, bf16[2,128,4480]{2,1,0:T(8,128)(2,1)}, u32[]{:S(2)}, u32[]{:S(2)}) %collective-permute-start.101) | collective-permute-done | bytes 2293792 | tf_op jit(solution)/shard_map/ppermute | solution.py:626
  1859.0 21.6 %collective-permute-done.102 = bf16[2,64,4480]{2,1,0:T(8,128)(2,1)S(1)} collective-permute-done((bf16[2,64,4480]{2,1,0:T(8,128)(2,1)S(1)}, bf16[2,64,4480]{2,1,0:T(8,128)(2,1)S(1)}, u32[]{:S(2)}, u32[]{:S(2)}) %collective-permute-start.102) | collective-permute-done | bytes 1146912 | tf_op jit(solution)/shard_map/ppermute | solution.py:626
  1883.5 13.4 collective-permute-done.103
  1952.1 17.8 collective-permute-done.130
  1989.6 37.4 %all-reduce.54 = (f32[8192]{0:T(1024)S(1)}, f32[4,64]{1,0:T(4,128)}, f32[4,64]{1,0:T(4,128)}, f32[]{:T(128)}) all-reduce(f32[8192]{0:T(1024)S(1)} %pad_maximum_fusion.105, f32[4,64]{1,0:T(4,128)S(1)} %copy-done.408, f32[4,64]{1,0:T(4,128)S(1)} %copy-done.407, ...), channel_id=1, replica_groups=mesh['dp'=2,'head'=8,'state'=2] {'dp','head','state'}, use_global_device_ids=true, to_apply=%region_79.80 | all-reduce | flops 8705 | bytes 69640 | tf_op jit(solution)/shard_map/psum | solution.py:1349
  (1897 shorter events, 1090.9 us)
Async XLA Ops:
  7.3 556.3 %all-gather.7.cloned.1.call-start = ((), (), s32[]{:S(2)}) async-start(), calls=%async_computation.8 | async-start | bytes 5242880 | tf_op jit(solution)/shard_map/all_gather | solution.py:969
  26.1 63.5 %collective-permute-start = (bf16[64,4096]{1,0:T(8,128)(2,1)}, bf16[64,4096]{1,0:T(8,128)(2,1)}, u32[]{:S(2)}, u32[]{:S(2)}) collective-permute-start(bf16[64,4096]{1,0:T(8,128)(2,1)} %get-tuple-element.684), channel_id=1, source_target_pairs={{0,1},{1,0},{2,3},{3,2},{4,5},{5,4},{6,7},{7,6},{8,9},{9,8},{10,11... | collective-permute-start | bytes 1572872 | tf_op jit(solution)/shard_map/ppermute | solution.py:630
  27.7 71.8 %collective-permute-start.4 = (bf16[64,4096]{1,0:T(8,128)(2,1)}, bf16[64,4096]{1,0:T(8,128)(2,1)}, u32[]{:S(2)}, u32[]{:S(2)}) collective-permute-start(bf16[64,4096]{1,0:T(8,128)(2,1)} %get-tuple-element.685), channel_id=1, source_target_pairs={{0,1},{1,0},{2,3},{3,2},{4,5},{5,4},{6,7},{7,6},{8,9},{9,8},{10,11... | collective-permute-start | bytes 1572872 | tf_op jit(solution)/shard_map/ppermute | solution.py:630
  83.7 92.1 %collective-permute-start.8 = (bf16[1024,256]{0,1:T(8,128)(2,1)S(1)}, bf16[1024,256]{0,1:T(8,128)(2,1)S(1)}, u32[]{:S(2)}, u32[]{:S(2)}) collective-permute-start(bf16[1024,256]{0,1:T(8,128)(2,1)S(1)} %copy-done.242), channel_id=1, source_target_pairs={{0,1},{1,0},{2,3},{3,2},{4,5},{5,4},{6,7},{7,6},{8,9},{9,8},{10,11... | collective-permute-start | bytes 1572872 | tf_op jit(solution)/shard_map/ppermute | solution.py:630
  89.6 39.7 %collective-permute-start.18 = (bf16[1024,256]{0,1:T(8,128)(2,1)}, bf16[1024,256]{0,1:T(8,128)(2,1)S(1)}, u32[]{:S(2)}, u32[]{:S(2)}) collective-permute-start(bf16[1024,256]{0,1:T(8,128)(2,1)} %copy.444), channel_id=1, source_target_pairs={{0,1},{1,0},{2,3},{3,2},{4,5},{5,4},{6,7},{7,6},{8,9},{9,8},{10,11... | collective-permute-start | bytes 1572872 | tf_op jit(solution)/shard_map/ppermute | solution.py:630
  99.3 76.5 %collective-permute-start.21 = (bf16[1024,256]{0,1:T(8,128)(2,1)S(1)}, bf16[1024,256]{0,1:T(8,128)(2,1)S(1)}, u32[]{:S(2)}, u32[]{:S(2)}) collective-permute-start(bf16[1024,256]{0,1:T(8,128)(2,1)S(1)} %copy-done.241), channel_id=1, source_target_pairs={{0,1},{1,0},{2,3},{3,2},{4,5},{5,4},{6,7},{7,6},{8,9},{9,8},{10,11... | collective-permute-start | bytes 1572872 | tf_op jit(solution)/shard_map/ppermute | solution.py:630
  99.5 46.6 %collective-permute-start.19 = (bf16[1024,256]{0,1:T(8,128)(2,1)S(1)}, bf16[1024,256]{0,1:T(8,128)(2,1)S(1)}, u32[]{:S(2)}, u32[]{:S(2)}) collective-permute-start(bf16[1024,256]{0,1:T(8,128)(2,1)S(1)} %copy.443), channel_id=1, source_target_pairs={{0,16},{16,0},{1,17},{17,1},{2,18},{18,2},{3,19},{19,3},{4,20},{20... | collective-permute-start | bytes 1572872 | tf_op jit(solution)/shard_map/ppermute | solution.py:634
  130.7 41.8 %collective-permute-start.20 = (bf16[1024,256]{0,1:T(8,128)(2,1)S(1)}, bf16[1024,256]{0,1:T(8,128)(2,1)S(1)}, u32[]{:S(2)}, u32[]{:S(2)}) collective-permute-start(bf16[1024,256]{0,1:T(8,128)(2,1)S(1)} %collective-permute-done.18), channel_id=1, source_target_pairs={{0,16},{16,0},{1,17},{17,1},{2,18},{18,2},{3,19},{19,3},{4,20},{20... | collective-permute-start | bytes 1572872 | tf_op jit(solution)/shard_map/ppermute | solution.py:634
  146.1 71.3 %collective-permute-start.22 = (bf16[1024,256]{0,1:T(8,128)(2,1)S(1)}, bf16[1024,256]{0,1:T(8,128)(2,1)S(1)}, u32[]{:S(2)}, u32[]{:S(2)}) collective-permute-start(bf16[1024,256]{0,1:T(8,128)(2,1)S(1)} %copy.447), channel_id=1, source_target_pairs={{0,16},{16,0},{1,17},{17,1},{2,18},{18,2},{3,19},{19,3},{4,20},{20... | collective-permute-start | bytes 1572872 | tf_op jit(solution)/shard_map/ppermute | solution.py:634
  175.7 53.0 %collective-permute-start.9 = (bf16[1024,256]{0,1:T(8,128)(2,1)S(1)}, bf16[1024,256]{0,1:T(8,128)(2,1)S(1)}, u32[]{:S(2)}, u32[]{:S(2)}) collective-permute-start(bf16[1024,256]{0,1:T(8,128)(2,1)S(1)} %copy.441), channel_id=1, source_target_pairs={{0,16},{16,0},{1,17},{17,1},{2,18},{18,2},{3,19},{19,3},{4,20},{20... | collective-permute-start | bytes 1572872 | tf_op jit(solution)/shard_map/ppermute | solution.py:634
  175.8 64.1 %collective-permute-start.10 = (bf16[1024,256]{0,1:T(8,128)(2,1)S(1)}, bf16[1024,256]{0,1:T(8,128)(2,1)S(1)}, u32[]{:S(2)}, u32[]{:S(2)}) collective-permute-start(bf16[1024,256]{0,1:T(8,128)(2,1)S(1)} %collective-permute-done.8), channel_id=1, source_target_pairs={{0,16},{16,0},{1,17},{17,1},{2,18},{18,2},{3,19},{19,3},{4,20},{20... | collective-permute-start | bytes 1572872 | tf_op jit(solution)/shard_map/ppermute | solution.py:634
  178.7 72.3 %collective-permute-start.23 = (bf16[1024,256]{0,1:T(8,128)(2,1)S(1)}, bf16[1024,256]{0,1:T(8,128)(2,1)S(1)}, u32[]{:S(2)}, u32[]{:S(2)}) collective-permute-start(bf16[1024,256]{0,1:T(8,128)(2,1)S(1)} %collective-permute-done.21), channel_id=1, source_target_pairs={{0,16},{16,0},{1,17},{17,1},{2,18},{18,2},{3,19},{19,3},{4,20},{20... | collective-permute-start | bytes 1572872 | tf_op jit(solution)/shard_map/ppermute | solution.py:634
  217.4 43.5 %collective-permute-start.15 = (bf16[4,4,448,128]{3,2,0,1:T(8,128)(2,1)S(1)}, bf16[4,4,448,128]{3,2,0,1:T(8,128)(2,1)S(1)}, u32[]{:S(2)}, u32[]{:S(2)}) collective-permute-start(bf16[4,4,448,128]{3,2,0,1:T(8,128)(2,1)S(1)} %pad_maximum_fusion.27), channel_id=1, source_target_pairs={{0,8},{2,10},{4,12},{6,14},{8,0},{10,2},{12,4},{14,6},{1,9},{3,11}... | collective-permute-start | bytes 5505032 | tf_op jit(solution)/shard_map/ppermute | solution.py:626
  223.2 40.1 %collective-permute-start.3 = (bf16[256,4096]{1,0:T(8,128)(2,1)S(1)}, bf16[256,4096]{1,0:T(8,128)(2,1)S(1)}, u32[]{:S(2)}, u32[]{:S(2)}) collective-permute-start(bf16[256,4096]{1,0:T(8,128)(2,1)S(1)} %pad_maximum_fusion.12), channel_id=1, source_target_pairs={{0,2},{2,0},{4,6},{6,4},{8,10},{10,8},{12,14},{14,12},{1,3},{3,1},... | collective-permute-start | bytes 6291464 | tf_op jit(solution)/shard_map/ppermute | solution.py:626
  228.7 35.6 %collective-permute-start.7 = (bf16[256,4096]{1,0:T(8,128)(2,1)S(1)}, bf16[256,4096]{1,0:T(8,128)(2,1)S(1)}, u32[]{:S(2)}, u32[]{:S(2)}) collective-permute-start(bf16[256,4096]{1,0:T(8,128)(2,1)S(1)} %pad_maximum_fusion.13), channel_id=1, source_target_pairs={{0,2},{2,0},{4,6},{6,4},{8,10},{10,8},{12,14},{14,12},{1,3},{3,1},... | collective-permute-start | bytes 6291464 | tf_op jit(solution)/shard_map/ppermute | solution.py:626
  426.0 175.4 %all-gather.9.cloned.1.call-start = ((), (), s32[]{:S(2)}) async-start(), calls=%async_computation.9 | async-start | bytes 5242880 | tf_op jit(solution)/shard_map/all_gather | solution.py:971
  477.4 36.0 %collective-permute-start.30 = (bf16[64,2048]{1,0:T(8,128)(2,1)S(1)}, bf16[64,2048]{1,0:T(8,128)(2,1)S(1)}, u32[]{:S(2)}, u32[]{:S(2)}) collective-permute-start(bf16[64,2048]{1,0:T(8,128)(2,1)S(1)} %fusion.360), channel_id=1, source_target_pairs={{0,1},{1,0},{2,3},{3,2},{4,5},{5,4},{6,7},{7,6},{8,9},{9,8},{10,11... | collective-permute-start | bytes 786440 | tf_op jit(solution)/shard_map/ppermute | solution.py:630
  516.7 189.6 %all-gather.11.cloned.1.call-start = ((), (), s32[]{:S(2)}) async-start(), calls=%async_computation.10 | async-start | bytes 2621440 | tf_op jit(solution)/shard_map/all_gather | solution.py:972
  560.0 49.5 %collective-permute-start.33 = (bf16[256,2048]{1,0:T(8,128)(2,1)}, bf16[256,2048]{1,0:T(8,128)(2,1)}, u32[]{:S(2)}, u32[]{:S(2)}) collective-permute-start(bf16[256,2048]{1,0:T(8,128)(2,1)} %pad_maximum_fusion.48), channel_id=1, source_target_pairs={{0,2},{2,0},{4,6},{6,4},{8,10},{10,8},{12,14},{14,12},{1,3},{3,1},... | collective-permute-start | bytes 3145736 | tf_op jit(solution)/shard_map/ppermute | solution.py:626
  630.5 97.9 %all-gather.13.cloned.1.call-start = ((), (), s32[]{:S(2)}) async-start(), calls=%async_computation.11 | async-start | bytes 2621440 | tf_op jit(solution)/shard_map/all_gather | solution.py:973
  658.8 110.1 %all-gather.15.cloned.1.call-start = ((), (), s32[]{:S(2)}) async-start(), calls=%async_computation.12 | async-start | bytes 2621440 | tf_op jit(solution)/shard_map/all_gather | solution.py:975
  698.5 593.6 %all-reduce.58.cloned.1.call-start = ((), (), s32[]{:S(2)}) async-start(), calls=%async_computation.20 | async-start | bytes 2097152 | tf_op jit(solution)/shard_map/psum | solution.py:1331
  823.2 129.2 %collective-permute-start.65 = (bf16[256,2048]{1,0:T(8,128)(2,1)}, bf16[256,2048]{1,0:T(8,128)(2,1)}, u32[]{:S(2)}, u32[]{:S(2)}) collective-permute-start(bf16[256,2048]{1,0:T(8,128)(2,1)} %dynamic-slice_convert_fusion.11), channel_id=1, source_target_pairs={{0,2},{2,0},{4,6},{6,4},{8,10},{10,8},{12,14},{14,12},{1,3},{3,1},... | collective-permute-start | bytes 3145736 | tf_op jit(solution)/shard_map/ppermute | solution.py:626
  826.5 130.5 %collective-permute-start.58 = (bf16[256,2048]{1,0:T(8,128)(2,1)}, bf16[256,2048]{1,0:T(8,128)(2,1)}, u32[]{:S(2)}, u32[]{:S(2)}) collective-permute-start(bf16[256,2048]{1,0:T(8,128)(2,1)} %dynamic-slice_convert_fusion.12), channel_id=1, source_target_pairs={{0,2},{2,0},{4,6},{6,4},{8,10},{10,8},{12,14},{14,12},{1,3},{3,1},... | collective-permute-start | bytes 3145736 | tf_op jit(solution)/shard_map/ppermute | solution.py:626
  952.2 342.8 %reduce-scatter.19.cloned.1.call-start = ((), (), s32[]{:S(2)}) async-start(), calls=%async_computation.18 | async-start | bytes 2621440 | tf_op jit(solution)/shard_map/reduce_scatter | solution.py:1208
  992.0 305.1 %reduce-scatter.23.cloned.1.call-start = ((), (), s32[]{:S(2)}) async-start(), calls=%async_computation.21 | async-start | bytes 2621440 | tf_op jit(solution)/shard_map/reduce_scatter | solution.py:1208
  1031.1 268.2 %reduce-scatter.17.cloned.1.call-start = ((), (), s32[]{:S(2)}) async-start(), calls=%async_computation.17 | async-start | bytes 2621440 | tf_op jit(solution)/shard_map/reduce_scatter | solution.py:1208
  1113.0 188.5 %reduce-scatter.13.cloned.1.call-start = ((), (), s32[]{:S(2)}) async-start(), calls=%async_computation.15 | async-start | bytes 327680 | tf_op jit(solution)/shard_map/reduce_scatter | solution.py:1208
  1141.1 614.1 %reduce-scatter.11.cloned.1.call-start = ((), (), s32[]{:S(2)}) async-start(), calls=%async_computation.14 | async-start | bytes 655360 | tf_op jit(solution)/shard_map/reduce_scatter | solution.py:1208
  1170.4 635.1 %reduce-scatter.9.cloned.1.call-start = ((), (), s32[]{:S(2)}) async-start(), calls=%async_computation.13 | async-start | bytes 5242880 | tf_op jit(solution)/shard_map/reduce_scatter | solution.py:1208
  1178.9 631.6 %reduce-scatter.15.cloned.1.call-start = ((), (), s32[]{:S(2)}) async-start(), calls=%async_computation.16 | async-start | bytes 5242880 | tf_op jit(solution)/shard_map/reduce_scatter | solution.py:1208
  1189.1 851.0 %reduce-scatter.21.cloned.1.call-start = ((), (), s32[]{:S(2)}) async-start(), calls=%async_computation.19 | async-start | bytes 81920 | tf_op jit(solution)/shard_map/reduce_scatter | solution.py:1334
  1191.0 36.1 %collective-permute-start.68 = (bf16[64,2048]{1,0:T(8,128)(2,1)S(1)}, bf16[64,2048]{1,0:T(8,128)(2,1)S(1)}, u32[]{:S(2)}, u32[]{:S(2)}) collective-permute-start(bf16[64,2048]{1,0:T(8,128)(2,1)S(1)} %copy-done.233), channel_id=1, source_target_pairs={{0,1},{1,0},{2,3},{3,2},{4,5},{5,4},{6,7},{7,6},{8,9},{9,8},{10,11... | collective-permute-start | bytes 786440 | tf_op jit(solution)/shard_map/ppermute | solution.py:630
  1244.4 40.7 %collective-permute-start.70 = (bf16[2,128,2048]{2,1,0:T(8,128)(2,1)}, bf16[2,128,2048]{2,1,0:T(8,128)(2,1)}, u32[]{:S(2)}, u32[]{:S(2)}) collective-permute-start(bf16[2,128,2048]{2,1,0:T(8,128)(2,1)} %pad_maximum_fusion.53), channel_id=1, source_target_pairs={{0,8},{2,10},{4,12},{6,14},{8,0},{10,2},{12,4},{14,6},{1,9},{3,11}... | collective-permute-start | bytes 3145736 | tf_op jit(solution)/shard_map/ppermute | solution.py:626
  1266.5 37.7 %collective-permute-start.64 = (bf16[2,256,2048]{2,1,0:T(8,128)(2,1)}, bf16[2,256,2048]{2,1,0:T(8,128)(2,1)}, u32[]{:S(2)}, u32[]{:S(2)}) collective-permute-start(bf16[2,256,2048]{2,1,0:T(8,128)(2,1)} %pad_maximum_fusion.19), channel_id=1, source_target_pairs={{0,2},{2,0},{4,6},{6,4},{8,10},{10,8},{12,14},{14,12},{1,3},{3,1},... | collective-permute-start | bytes 6291464 | tf_op jit(solution)/shard_map/ppermute | solution.py:626
  1578.3 204.9 %collective-permute-start.100 = (bf16[2,256,4480]{2,1,0:T(8,128)(2,1)}, bf16[2,256,4480]{2,1,0:T(8,128)(2,1)}, u32[]{:S(2)}, u32[]{:S(2)}) collective-permute-start(bf16[2,256,4480]{2,1,0:T(8,128)(2,1)} %fusion.17), channel_id=1, source_target_pairs={{0,2},{2,0},{4,6},{6,4},{8,10},{10,8},{12,14},{14,12},{1,3},{3,1},... | collective-permute-start | bytes 13762568 | tf_op jit(solution)/shard_map/ppermute | solution.py:626
  1581.4 211.8 %collective-permute-start.107 = (bf16[2,256,4480]{2,1,0:T(8,128)(2,1)}, bf16[2,256,4480]{2,1,0:T(8,128)(2,1)}, u32[]{:S(2)}, u32[]{:S(2)}) collective-permute-start(bf16[2,256,4480]{2,1,0:T(8,128)(2,1)} %fusion.18), channel_id=1, source_target_pairs={{0,2},{2,0},{4,6},{6,4},{8,10},{10,8},{12,14},{14,12},{1,3},{3,1},... | collective-permute-start | bytes 13762568 | tf_op jit(solution)/shard_map/ppermute | solution.py:626
  1581.5 43.7 %collective-permute-start.132 = (f32[64,768]{1,0:T(8,128)S(1)}, f32[64,768]{1,0:T(8,128)S(1)}, u32[]{:S(2)}, u32[]{:S(2)}) collective-permute-start(f32[64,768]{1,0:T(8,128)S(1)} %constant_dynamic-slice_fusion.1), channel_id=1, source_target_pairs={{0,16},{16,0},{1,17},{17,1},{2,18},{18,2},{3,19},{19,3},{4,20},{20... | collective-permute-start | bytes 589832 | tf_op jit(solution)/shard_map/ppermute | solution.py:634
  1587.8 73.1 %collective-permute-start.134 = (bf16[256,1024]{1,0:T(8,128)(2,1)S(1)}, bf16[256,1024]{1,0:T(8,128)(2,1)S(1)}, u32[]{:S(2)}, u32[]{:S(2)}) collective-permute-start(bf16[256,1024]{1,0:T(8,128)(2,1)S(1)} %dynamic-slice_convert_fusion.21), channel_id=1, source_target_pairs={{0,16},{16,0},{1,17},{17,1},{2,18},{18,2},{3,19},{19,3},{4,20},{20... | collective-permute-start | bytes 1572872 | tf_op jit(solution)/shard_map/ppermute | solution.py:634
  1590.9 103.1 %collective-permute-start.118 = (bf16[2048,256]{0,1:T(8,128)(2,1)S(1)}, bf16[2048,256]{0,1:T(8,128)(2,1)S(1)}, u32[]{:S(2)}, u32[]{:S(2)}) collective-permute-start(bf16[2048,256]{0,1:T(8,128)(2,1)S(1)} %dynamic-slice_convert_fusion.6), channel_id=1, source_target_pairs={{0,16},{16,0},{1,17},{17,1},{2,18},{18,2},{3,19},{19,3},{4,20},{20... | collective-permute-start | bytes 3145736 | tf_op jit(solution)/shard_map/ppermute | solution.py:634
  1625.2 35.7 %collective-permute-start.133 = (f32[32,768]{1,0:T(8,128)S(1)}, f32[32,768]{1,0:T(8,128)S(1)}, u32[]{:S(2)}, u32[]{:S(2)}) collective-permute-start(f32[32,768]{1,0:T(8,128)S(1)} %constant_dynamic-slice_fusion), channel_id=1, source_target_pairs={{0,1},{1,0},{2,3},{3,2},{4,5},{5,4},{6,7},{7,6},{8,9},{9,8},{10,11... | collective-permute-start | bytes 294920 | tf_op jit(solution)/shard_map/ppermute | solution.py:630
  1660.9 70.0 %collective-permute-start.116 = (bf16[2048,256]{0,1:T(8,128)(2,1)S(1)}, bf16[2048,256]{0,1:T(8,128)(2,1)S(1)}, u32[]{:S(2)}, u32[]{:S(2)}) collective-permute-start(bf16[2048,256]{0,1:T(8,128)(2,1)S(1)} %dynamic-slice_convert_fusion.7), channel_id=1, source_target_pairs={{0,16},{16,0},{1,17},{17,1},{2,18},{18,2},{3,19},{19,3},{4,20},{20... | collective-permute-start | bytes 3145736 | tf_op jit(solution)/shard_map/ppermute | solution.py:634
  1689.5 63.9 %collective-permute-start.114 = (bf16[2048,256]{0,1:T(8,128)(2,1)S(1)}, bf16[2048,256]{0,1:T(8,128)(2,1)S(1)}, u32[]{:S(2)}, u32[]{:S(2)}) collective-permute-start(bf16[2048,256]{0,1:T(8,128)(2,1)S(1)} %dynamic-slice_convert_fusion.8), channel_id=1, source_target_pairs={{0,16},{16,0},{1,17},{17,1},{2,18},{18,2},{3,19},{19,3},{4,20},{20... | collective-permute-start | bytes 3145736 | tf_op jit(solution)/shard_map/ppermute | solution.py:634
  1695.2 62.9 %collective-permute-start.119 = (bf16[1024,256]{0,1:T(8,128)(2,1)}, bf16[1024,256]{0,1:T(8,128)(2,1)}, u32[]{:S(2)}, u32[]{:S(2)}) collective-permute-start(bf16[1024,256]{0,1:T(8,128)(2,1)} %dynamic-slice_convert_fusion.22), channel_id=1, source_target_pairs={{0,1},{1,0},{2,3},{3,2},{4,5},{5,4},{6,7},{7,6},{8,9},{9,8},{10,11... | collective-permute-start | bytes 1572872 | tf_op jit(solution)/shard_map/ppermute | solution.py:630
  1790.9 52.1 %collective-permute-start.101 = (bf16[2,128,4480]{2,1,0:T(8,128)(2,1)}, bf16[2,128,4480]{2,1,0:T(8,128)(2,1)}, u32[]{:S(2)}, u32[]{:S(2)}) collective-permute-start(bf16[2,128,4480]{2,1,0:T(8,128)(2,1)} %dynamic-slice_convert_fusion.1), channel_id=1, source_target_pairs={{0,4},{2,6},{4,0},{6,2},{8,12},{10,14},{12,8},{14,10},{1,5},{3,7},... | collective-permute-start | bytes 6881288 | tf_op jit(solution)/shard_map/ppermute | solution.py:626
  1804.1 52.9 %collective-permute-start.108 = (bf16[2,128,4480]{2,1,0:T(8,128)(2,1)}, bf16[2,128,4480]{2,1,0:T(8,128)(2,1)S(1)}, u32[]{:S(2)}, u32[]{:S(2)}) collective-permute-start(bf16[2,128,4480]{2,1,0:T(8,128)(2,1)} %dynamic-slice_convert_fusion), channel_id=1, source_target_pairs={{0,8},{2,10},{4,12},{6,14},{8,0},{10,2},{12,4},{14,6},{1,9},{3,11}... | collective-permute-start | bytes 6881288 | tf_op jit(solution)/shard_map/ppermute | solution.py:626
  1972.1 57.5 %collective-permute-start.106 = (bf16[256,4096]{1,0:T(8,128)(2,1)}, bf16[256,4096]{1,0:T(8,128)(2,1)}, u32[]{:S(2)}, u32[]{:S(2)}) collective-permute-start(bf16[256,4096]{1,0:T(8,128)(2,1)} %pad_maximum_fusion.21), channel_id=1, source_target_pairs={{0,2},{2,0},{4,6},{6,4},{8,10},{10,8},{12,14},{14,12},{1,3},{3,1},... | collective-permute-start | bytes 6291464 | tf_op jit(solution)/shard_map/ppermute | solution.py:626
  1980.1 52.2 %collective-permute-start.113 = (bf16[256,4096]{1,0:T(8,128)(2,1)}, bf16[256,4096]{1,0:T(8,128)(2,1)}, u32[]{:S(2)}, u32[]{:S(2)}) collective-permute-start(bf16[256,4096]{1,0:T(8,128)(2,1)} %pad_maximum_fusion.22), channel_id=1, source_target_pairs={{0,2},{2,0},{4,6},{6,4},{8,10},{10,8},{12,14},{14,12},{1,3},{3,1},... | collective-permute-start | bytes 6291464 | tf_op jit(solution)/shard_map/ppermute | solution.py:626
  (599 other events, 8220.0 us)
Sparse Core Ops, SparseCore 0:
  426.2 88.4 all-gather.6
  516.8 84.6 all-gather.8
  630.7 44.8 all-gather.10
  677.0 44.6 all-gather.12
  723.1 45.8 all-gather.14
  952.3 130.3 all-reduce.57
  1085.7 45.0 reduce-scatter.18
  1133.1 43.5 reduce-scatter.22
  1179.6 54.1 reduce-scatter.16
  1235.9 19.0 reduce-scatter.12
  1257.4 19.9 reduce-scatter.10
  1279.6 74.9 reduce-scatter.8
  1356.9 77.2 reduce-scatter.14
  1437.0 19.4 reduce-scatter.20

commit v2 on v1

--- a/solution.py
+++ b/solution.py
@@ -1,6 +1,8 @@
 import jax
 import jax.numpy as jnp
 from jax import lax
+from jax.experimental import pallas as pl
+from jax.experimental.pallas import tpu as pltpu
 from jax.sharding import PartitionSpec as P
 
 HDIM = 128
@@ -750,48 +752,563 @@
     return total
 
 
-def scan_blocks(inputs, step_sizes, decay, input_vecs, read_vecs, segment, before, block):
-    length, heads = step_sizes.shape
-    width = inputs.shape[1] // heads
-    count = length // block
-    states = input_vecs.shape[1]
-    state = jnp.zeros((heads, states, width), full)
-    last = before
-    outputs, entries = [], []
-    since = jnp.zeros((heads,), full)
-    for index in range(count):
-        part = slice(index * block, (index + 1) * block)
-        group_in = inputs[part].reshape(block, heads, width).transpose(1, 0, 2)
-        group_dt = step_sizes[part].T
-        group_b, group_c, group_seg = input_vecs[part], read_vecs[part], segment[part]
-        cumul = jnp.cumsum(group_dt * decay[:, None], 1)
-        places = jnp.arange(block, dtype=jnp.int32)
-        allowed = (group_seg[:, None] == group_seg[None, :]) & (places[None, :] <= places[:, None])
-        gaps = cumul[:, :, None] - cumul[:, None, :]
-        fading = jnp.where(allowed, jnp.exp(jnp.where(allowed, gaps, 0.0)), 0.0)
-        inner = right_dot(group_c, group_b)
-        scaled = group_in * group_dt[:, :, None]
-        local_out = jnp.einsum(
-            "hts,hsp->htp", inner[None] * fading, scaled, preferred_element_type=full
+def vmem_limit(mebibytes):
+    return pltpu.CompilerParams(vmem_limit_bytes=mebibytes * 1024 * 1024)
+
+
+def dot_nt(left, right):
+    return lax.dot_general(left, right, (((1,), (1,)), ((), ())), preferred_element_type=full)
+
+
+def dot_tn(left, right):
+    return lax.dot_general(left, right, (((0,), (0,)), ((), ())), preferred_element_type=full)
+
+
+def dot_nn(left, right):
+    return lax.dot_general(left, right, (((1,), (0,)), ((), ())), preferred_element_type=full)
+
+
+def dot_exact(left, right):
+    return jnp.dot(left, right, preferred_element_type=full, precision=highest)
+
+
+ROWS_Q = 256
+ROWS_K = 512
+
+
+def attend_kernel(low_ref, q_ref, k_ref, v_ref, seg_col, seg_row, out_ref, lse_ref):
+    index = pl.program_id(1)
+    scale = q_ref.shape[1] ** (-0.5)
+    query = q_ref[...]
+    own = seg_col[...]
+    place = index * ROWS_Q + lax.broadcasted_iota(jnp.int32, (ROWS_Q, ROWS_K), 0)
+
+    def step(block, carry):
+        top, total, acc = carry
+        span = pl.ds(pl.multiple_of(block * ROWS_K, ROWS_K), ROWS_K)
+        scores = dot_nt(query, k_ref[span, :]) * scale
+        other = block * ROWS_K + lax.broadcasted_iota(jnp.int32, (ROWS_Q, ROWS_K), 1)
+        scores = jnp.where((own == seg_row[:, span]) & (other <= place), scores, -1e30)
+        higher = jnp.maximum(top, jnp.max(scores, -1, keepdims=True))
+        weights = jnp.exp(scores - higher)
+        fade = jnp.exp(top - higher)
+        total = total * fade + jnp.sum(weights, -1, keepdims=True)
+        acc = acc * fade + dot_nn(weights.astype(low), v_ref[span, :])
+        return higher, total, acc
+
+    start = (
+        jnp.full((ROWS_Q, 1), -1e30, full),
+        jnp.zeros((ROWS_Q, 1), full),
+        jnp.zeros((ROWS_Q, v_ref.shape[1]), full),
+    )
+    stop = (index * ROWS_Q + ROWS_Q + ROWS_K - 1) // ROWS_K
+    top, total, acc = lax.fori_loop(low_ref[index], stop, step, start)
+    out_ref[...] = (acc / total).astype(low)
+    lse = jnp.broadcast_to(top + jnp.log(total), (ROWS_Q, 128))
+    lse_ref[...] = lse.T[0:1, :][None]
+
+
+def attend(queries, keys, values, segment, lows):
+    length, columns = queries.shape
+    heads = columns // HDIM
+    whole = pl.BlockSpec((length, HDIM), lambda h, i, *_: (0, h))
+    block = pl.BlockSpec((ROWS_Q, HDIM), lambda h, i, *_: (i, h))
+    return pl.pallas_call(
+        attend_kernel,
+        grid_spec=pltpu.PrefetchScalarGridSpec(
+            num_scalar_prefetch=1,
+            grid=(heads, length // ROWS_Q),
+            in_specs=[
+                block,
+                whole,
+                whole,
+                pl.BlockSpec((ROWS_Q, 1), lambda h, i, *_: (i, 0)),
+                pl.BlockSpec((1, length), lambda h, i, *_: (0, 0)),
+            ],
+            out_specs=[block, pl.BlockSpec((1, 1, ROWS_Q), lambda h, i, *_: (h, 0, i))],
+        ),
+        out_shape=[
+            jax.ShapeDtypeStruct((length, columns), low),
+            jax.ShapeDtypeStruct((heads, 1, length), full),
+        ],
+        compiler_params=vmem_limit(40),
+        cost_estimate=pl.CostEstimate(
+            flops=2 * length * length * columns, bytes_accessed=8 * length * columns,
+            transcendentals=length * length * heads // 2,
+        ),
+    )(lows, queries, keys, values, segment[:, None], segment[None, :])
+
+
+def attend_back_kernel(
+    low_ref, q_ref, k_ref, v_ref, do_ref, lse_ref, delta_ref, seg_col, seg_row, dq_ref, dk_ref, dv_ref
+):
+    index = pl.program_id(1)
+    scale = q_ref.shape[1] ** (-0.5)
+    query = q_ref[...]
+    grad = do_ref[...]
+    own = seg_row[...]
+    lse = lse_ref[0]
+    delta = delta_ref[0]
+    place = index * ROWS_Q + lax.broadcasted_iota(jnp.int32, (ROWS_K, ROWS_Q), 1)
+
+    @pl.when(index == 0)
+    def clear():
+        dk_ref[...] = jnp.zeros_like(dk_ref)
+        dv_ref[...] = jnp.zeros_like(dv_ref)
+
+    def step(block, total):
+        span = pl.ds(pl.multiple_of(block * ROWS_K, ROWS_K), ROWS_K)
+        key = k_ref[span, :]
+        scores = dot_nt(key, query) * scale
+        other = block * ROWS_K + lax.broadcasted_iota(jnp.int32, (ROWS_K, ROWS_Q), 0)
+        counted = (seg_col[span, :] == own) & (other <= place)
+        probs = jnp.exp(jnp.where(counted, scores - lse, -1e30))
+        dv_ref[span, :] += dot_nn(probs.astype(low), grad)
+        slope = probs * (dot_nt(v_ref[span, :], grad) - delta)
+        slope = slope.astype(low)
+        dk_ref[span, :] += dot_nn(slope, query) * scale
+        return total + dot_tn(slope, key)
+
+    stop = (index * ROWS_Q + ROWS_Q + ROWS_K - 1) // ROWS_K
+    total = lax.fori_loop(low_ref[index], stop, step, jnp.zeros((ROWS_Q, HDIM), full))
+    dq_ref[...] = total * scale
+
+
+def attend_back(queries, keys, values, grads, lse, delta, segment, lows):
+    length, columns = queries.shape
+    heads = columns // HDIM
+    whole = pl.BlockSpec((length, HDIM), lambda h, i, *_: (0, h))
+    block = pl.BlockSpec((ROWS_Q, HDIM), lambda h, i, *_: (i, h))
+    line = pl.BlockSpec((1, 1, ROWS_Q), lambda h, i, *_: (h, 0, i))
+    shape = jax.ShapeDtypeStruct((length, columns), full)
+    return pl.pallas_call(
+        attend_back_kernel,
+        grid_spec=pltpu.PrefetchScalarGridSpec(
+            num_scalar_prefetch=1,
+            grid=(heads, length // ROWS_Q),
+            in_specs=[
+                block,
+                whole,
+                whole,
+                block,
+                line,
+                line,
+                pl.BlockSpec((length, 1), lambda h, i, *_: (0, 0)),
+                pl.BlockSpec((1, ROWS_Q), lambda h, i, *_: (0, i)),
+            ],
+            out_specs=[block, whole, whole],
+        ),
+        out_shape=[shape, shape, shape],
+        compiler_params=vmem_limit(40),
+        cost_estimate=pl.CostEstimate(
+            flops=5 * length * length * columns, bytes_accessed=20 * length * columns,
+            transcendentals=length * length * heads // 2,
+        ),
+    )(lows, queries, keys, values, grads, lse, delta, segment[:, None], segment[None, :])
+
+
+def first_blocks(segment):
+    length = segment.shape[0]
+    heads = segment[::ROWS_Q]
+    starts = jnp.sum((segment[None, :] < heads[:, None]).astype(jnp.int32), 1)
+    return starts // ROWS_K
+
+
+def pair_lanes(left, right):
+    lane = lax.broadcasted_iota(jnp.int32, (1, 2 * MDIM), 1)
+    return jnp.where(lane < MDIM, left, right)
+
+
+def block_decay(dt_ref, dt_row_ref, rate_ref, rate_col_ref):
+    rows = lax.broadcasted_iota(jnp.int32, (GROUP, GROUP), 0)
+    cols = lax.broadcasted_iota(jnp.int32, (GROUP, GROUP), 1)
+    cumul = dot_exact((cols <= rows).astype(full), dt_ref[...] * rate_ref[...])
+    cumul_row = dot_exact(dt_row_ref[...] * rate_col_ref[...], (rows <= cols).astype(full))
+    return cumul, cumul_row, rows, cols
+
+
+def edge_flags(ends_ref, index, seg_col):
+    before = ends_ref[index]
+    last = ends_ref[index + 1]
+    carried = (seg_col[...] == before).astype(full)
+    reach = (seg_col[...] == last).astype(full)
+    keep = (before == last).astype(full)
+    return carried, reach, keep
+
+
+def pair_columns(values, pair):
+    return pair_lanes(values[:, 2 * pair : 2 * pair + 1], values[:, 2 * pair + 1 : 2 * pair + 2])
+
+
+def step_state(state, pair, scaled, cumul, reach, keep, vec_low):
+    column = pair_columns(cumul, pair)
+    end = column[GROUP - 1 : GROUP, :]
+    weight = jnp.exp(end - column) * reach
+    return state * (jnp.exp(end) * keep) + dot_tn(vec_low, (scaled * weight).astype(low)), weight
+
+
+def scan_end_kernel(
+    ends_ref, x_ref, dt_ref, dt_row_ref, rate_ref, rate_col_ref, b_ref, seg_col, out_ref
+):
+    index = pl.program_id(0)
+    cumul, unused_row, unused_a, unused_b = block_decay(dt_ref, dt_row_ref, rate_ref, rate_col_ref)
+    unused_c, reach, keep = edge_flags(ends_ref, index, seg_col)
+    vec_low = b_ref[...].astype(low)
+
+    @pl.when(index == 0)
+    def clear():
+        out_ref[...] = jnp.zeros_like(out_ref)
+
+    for pair in range(dt_ref.shape[1] // 2):
+        lanes = slice(pair * 2 * MDIM, (pair + 1) * 2 * MDIM)
+        scaled = x_ref[:, lanes] * pair_columns(dt_ref[...], pair)
+        out_ref[:, lanes], unused_d = step_state(
+            out_ref[:, lanes], pair, scaled, cumul, reach, keep, vec_low
         )
-        carried = (group_seg == last).astype(full)
-        entry = jnp.exp(cumul) * carried[None, :]
-        from_state = jnp.einsum("tn,hnp->htp", group_c, state) * entry[:, :, None]
-        first_seg = (group_seg == before).astype(full)
-        entries.append((jnp.exp(cumul + since[:, None]) * first_seg[None, :]).T)
-        since = since + cumul[:, -1]
-        last_seg = group_seg[-1]
-        reach = (group_seg == last_seg).astype(full)
-        to_end = jnp.exp(cumul[:, -1:] - cumul) * reach[None, :]
-        retain = jnp.exp(cumul[:, -1]) * (last_seg == last).astype(full)
-        fresh = jnp.einsum("sn,hsp->hnp", group_b, to_end[:, :, None] * scaled)
-        state = state * retain[:, None, None] + fresh
-        last = last_seg
-        outputs.append(
-            (local_out + from_state).transpose(1, 0, 2).reshape(block, heads * width)
+
+
+def scan_kernel(
+    ends_ref,
+    x_ref,
+    dt_ref,
+    dt_row_ref,
+    rate_ref,
+    rate_col_ref,
+    b_ref,
+    c_ref,
+    seg_col,
+    seg_row,
+    first_ref,
+    out_ref,
+    states_ref,
+    state,
+):
+    index = pl.program_id(0)
+    cumul, cumul_row, rows, cols = block_decay(dt_ref, dt_row_ref, rate_ref, rate_col_ref)
+    carried, reach, keep = edge_flags(ends_ref, index, seg_col)
+    vec_low = b_ref[...].astype(low)
+    read_low = c_ref[...].astype(low)
+    allowed = (seg_col[...] == seg_row[...]) & (cols <= rows)
+    inner = jnp.where(allowed, dot_nt(read_low, vec_low), 0.0)
+
+    @pl.when(index == 0)
+    def begin():
+        state[...] = first_ref[...]
+
+    states_ref[0] = state[...]
+    for pair in range(dt_ref.shape[1] // 2):
+        lanes = slice(pair * 2 * MDIM, (pair + 1) * 2 * MDIM)
+        scaled = x_ref[:, lanes] * pair_columns(dt_ref[...], pair)
+        scaled_low = scaled.astype(low)
+        parts = []
+        for head in (2 * pair, 2 * pair + 1):
+            gaps = cumul[:, head : head + 1] - cumul_row[head : head + 1, :]
+            mixed = inner * jnp.exp(jnp.minimum(gaps, 0.0))
+            parts.append(dot_nn(mixed.astype(low), scaled_low))
+        entry = jnp.exp(pair_columns(cumul, pair)) * carried
+        held = state[:, lanes]
+        out_ref[:, lanes] = pair_lanes(*parts) + dot_nn(read_low, held.astype(low)) * entry
+        state[:, lanes], unused = step_state(
+            held, pair, scaled, cumul, reach, keep, vec_low
         )
-    carry = jnp.exp(since) * (last == before).astype(full)
-    return jnp.concatenate(outputs, 0), state, jnp.concatenate(entries, 0), carry
+
+
+def scan_start_grad_kernel(
+    ends_ref, dt_ref, dt_row_ref, rate_ref, rate_col_ref, c_ref, seg_col, dy_ref, out_ref
+):
+    index = pl.num_programs(0) - 1 - pl.program_id(0)
+    cumul, unused_row, unused_a, unused_b = block_decay(dt_ref, dt_row_ref, rate_ref, rate_col_ref)
+    carried, unused_c, keep = edge_flags(ends_ref, index, seg_col)
+    read_low = c_ref[...].astype(low)
+
+    @pl.when(pl.program_id(0) == 0)
+    def clear():
+        out_ref[...] = jnp.zeros_like(out_ref)
+
+    for pair in range(dt_ref.shape[1] // 2):
+        lanes = slice(pair * 2 * MDIM, (pair + 1) * 2 * MDIM)
+        column = pair_columns(cumul, pair)
+        retain = jnp.exp(column[GROUP - 1 : GROUP, :]) * keep
+        entry = jnp.exp(column) * carried
+        out_ref[:, lanes] = out_ref[:, lanes] * retain + dot_tn(
+            read_low, (dy_ref[:, lanes] * entry).astype(low)
+        )
+
+
+def scan_back_kernel(
+    ends_ref,
+    x_ref,
+    dt_ref,
+    dt_row_ref,
+    rate_ref,
+    rate_col_ref,
+    b_ref,
+    c_ref,
+    seg_col,
+    seg_row,
+    dy_ref,
+    states_ref,
+    last_ref,
+    dx_ref,
+    ddt_ref,
+    dlog_ref,
+    dlog_row_ref,
+    db_ref,
+    dc_ref,
+    state_grad,
+    inner_grad,
+):
+    index = pl.num_programs(0) - 1 - pl.program_id(0)
+    heads = dt_ref.shape[1]
+    cumul, cumul_row, rows, cols = block_decay(dt_ref, dt_row_ref, rate_ref, rate_col_ref)
+    carried, reach, keep = edge_flags(ends_ref, index, seg_col)
+    vec_low = b_ref[...].astype(low)
+    read_low = c_ref[...].astype(low)
+    allowed = (seg_col[...] == seg_row[...]) & (cols <= rows)
+    inner = jnp.where(allowed, dot_nt(read_low, vec_low), 0.0)
+    head_lane = lax.broadcasted_iota(jnp.int32, (GROUP, heads), 1)
+    head_row = lax.broadcasted_iota(jnp.int32, (heads, GROUP), 0)
+    last_row = lax.broadcasted_iota(jnp.int32, (GROUP, 1), 0) == GROUP - 1
+    lane = lax.broadcasted_iota(jnp.int32, (1, 2 * MDIM), 1)
+
+    @pl.when(pl.program_id(0) == 0)
+    def begin():
+        state_grad[...] = last_ref[...]
+
+    inner_grad[...] = jnp.zeros_like(inner_grad)
+    decay_grad = jnp.zeros((GROUP, heads), full)
+    decay_row = jnp.zeros((heads, GROUP), full)
+    step_grad = jnp.zeros((GROUP, heads), full)
+    vec_grad = jnp.zeros(b_ref.shape, full)
+    read_grad = jnp.zeros(c_ref.shape, full)
+    for pair in range(heads // 2):
+        lanes = slice(pair * 2 * MDIM, (pair + 1) * 2 * MDIM)
+        values = x_ref[:, lanes]
+        steps = pair_columns(dt_ref[...], pair)
+        scaled = values * steps
+        scaled_low = scaled.astype(low)
+        grad = dy_ref[:, lanes]
+        grad_low = grad.astype(low)
+        held = states_ref[0, :, lanes]
+        held_low = held.astype(low)
+        later = state_grad[:, lanes]
+        later_low = later.astype(low)
+        column = pair_columns(cumul, pair)
+        end = column[GROUP - 1 : GROUP, :]
+        weight = jnp.exp(end - column) * reach
+        retain = jnp.exp(end) * keep
+        entry = jnp.exp(column) * carried
+        parts = []
+        for side in range(2):
+            head = 2 * pair + side
+            gaps = cumul[:, head : head + 1] - cumul_row[head : head + 1, :]
+            fading = jnp.where(allowed, jnp.exp(jnp.minimum(gaps, 0.0)), 0.0)
+            mixed = inner * fading
+            own_lanes = (lane < MDIM) == (side == 0)
+            outer = dot_nt(jnp.where(own_lanes, grad, 0.0).astype(low), scaled_low)
+            inner_grad[...] += outer * fading
+            slope = outer * mixed
+            decay_grad = jnp.where(
+                head_lane == head, decay_grad + jnp.sum(slope, 1, keepdims=True), decay_grad
+            )
+            decay_row = jnp.where(
+                head_row == head, jnp.sum(slope, 0, keepdims=True), decay_row
+            )
+            parts.append(dot_tn(mixed.astype(low), grad_low))
+        weighted = scaled * weight
+        entered = grad * entry
+        entered_low = entered.astype(low)
+        from_later = dot_nn(vec_low, later_low)
+        scaled_grad = pair_lanes(*parts) + weight * from_later
+        dx_ref[:, lanes] = scaled_grad * steps
+        read_grad += dot_nt(entered_low, held_low)
+        vec_grad += dot_nt(weighted.astype(low), later_low)
+        fresh = weighted * from_later
+        flow = entered * dot_nn(read_low, held_low) - fresh
+        finish = jnp.sum(fresh, 0, keepdims=True) + retain * jnp.sum(later * held, 0, keepdims=True)
+        steps_part = scaled_grad * values
+        for side in range(2):
+            head = 2 * pair + side
+            own_lanes = (lane < MDIM) == (side == 0)
+            total = jnp.sum(jnp.where(own_lanes, flow, 0.0), 1, keepdims=True)
+            ending = jnp.sum(jnp.where(own_lanes, finish, 0.0), 1, keepdims=True)
+            total = total + jnp.where(last_row, ending, 0.0)
+            decay_grad = jnp.where(head_lane == head, decay_grad + total, decay_grad)
+            step_grad = jnp.where(
+                head_lane == head,
+                jnp.sum(jnp.where(own_lanes, steps_part, 0.0), 1, keepdims=True),
+                step_grad,
+            )
+        state_grad[:, lanes] = later * retain + dot_tn(read_low, entered_low)
+    inner_low = inner_grad[...].astype(low)
+    ddt_ref[...] = step_grad
+    dlog_ref[...] = dot_exact((cols >= rows).astype(full), decay_grad)
+    dlog_row_ref[...] = dot_exact(decay_row, (rows >= cols).astype(full))
+    dc_ref[...] = read_grad + dot_nn(inner_low, vec_low)
+    db_ref[...] = vec_grad + dot_tn(inner_low, read_low)
+
+
+def scan_specs(heads, channels, states, reverse, count):
+    def at(i):
+        return count - 1 - i if reverse else i
+
+    tall = lambda columns: pl.BlockSpec((GROUP, columns), lambda i, *_: (at(i), 0))
+    flat = lambda rows: pl.BlockSpec((rows, GROUP), lambda i, *_: (0, at(i)))
+    same = lambda rows, columns: pl.BlockSpec((rows, columns), lambda i, *_: (0, 0))
+    return tall, flat, same, pl.BlockSpec((1, states, channels), lambda i, *_: (at(i), 0, 0))
+
+
+def scan_call(kernel, reverse, ends, inputs, kinds, outs, out_kinds, scratch, dims, flops):
+    heads, channels, states, count = dims
+    tall, flat, same, cube = scan_specs(heads, channels, states, reverse, count)
+
+    def spec(kind, shape):
+        if kind == 0:
+            return tall(shape[1])
+        if kind == 1:
+            return flat(shape[0])
+        return same(*shape) if kind == 2 else cube
+
+    return pl.pallas_call(
+        kernel,
+        grid_spec=pltpu.PrefetchScalarGridSpec(
+            num_scalar_prefetch=1,
+            grid=(count,),
+            in_specs=[spec(kind, value.shape) for kind, value in zip(kinds, inputs)],
+            out_specs=[spec(kind, shape) for kind, shape in zip(out_kinds, outs)],
+            scratch_shapes=scratch,
+        ),
+        out_shape=[jax.ShapeDtypeStruct(shape, full) for shape in outs],
+        compiler_params=vmem_limit(40),
+        cost_estimate=pl.CostEstimate(
+            flops=flops, bytes_accessed=8 * count * GROUP * channels, transcendentals=flops // 256
+        ),
+    )(ends, *inputs)
+
+
+class Scan:
+    def __init__(self, x, dt, rate, b, c, segment, before):
+        self.rows, self.heads = dt.shape
+        self.channels, self.states = x.shape[1], b.shape[1]
+        self.count = self.rows // GROUP
+        self.dims = (self.heads, self.channels, self.states, self.count)
+        self.ends = jnp.concatenate([before[None], segment[GROUP - 1 :: GROUP]])
+        self.x, self.b, self.c = x, b, c
+        self.decay = [dt, dt.T, rate[None, :], rate[:, None]]
+        self.seg_col, self.seg_row = segment[:, None], segment[None, :]
+        self.state_shape = (self.states, self.channels)
+
+    def end(self):
+        return scan_call(
+            scan_end_kernel,
+            False,
+            self.ends,
+            [self.x, *self.decay, self.b, self.seg_col],
+            [0, 0, 1, 2, 2, 0, 0],
+            [self.state_shape],
+            [2],
+            [],
+            self.dims,
+            2 * self.rows * self.channels * self.states,
+        )[0]
+
+    def forward(self, first):
+        return scan_call(
+            scan_kernel,
+            False,
+            self.ends,
+            [self.x, *self.decay, self.b, self.c, self.seg_col, self.seg_row, first],
+            [0, 0, 1, 2, 2, 0, 0, 0, 1, 2],
+            [self.x.shape, (self.count,) + self.state_shape],
+            [0, 3],
+            [pltpu.VMEM(self.state_shape, full)],
+            self.dims,
+            8 * self.rows * self.channels * GROUP,
+        )
+
+    def start_grad(self, grad):
+        return scan_call(
+            scan_start_grad_kernel,
+            True,
+            self.ends,
+            [*self.decay, self.c, self.seg_col, grad],
+            [0, 1, 2, 2, 0, 0, 0],
+            [self.state_shape],
+            [2],
+            [],
+            self.dims,
+            2 * self.rows * self.channels * self.states,
+        )[0]
+
+    def backward(self, grad, states, last):
+        wide = (self.rows, self.heads)
+        return scan_call(
+            scan_back_kernel,
+            True,
+            self.ends,
+            [
+                self.x,
+                *self.decay,
+                self.b,
+                self.c,
+                self.seg_col,
+                self.seg_row,
+                grad,
+                states,
+                last,
+            ],
+            [0, 0, 1, 2, 2, 0, 0, 0, 1, 0, 3, 2],
+            [self.x.shape, wide, wide, wide[::-1], self.b.shape, self.c.shape],
+            [0, 0, 0, 1, 0, 0],
+            [pltpu.VMEM(self.state_shape, full), pltpu.VMEM((GROUP, GROUP), full)],
+            self.dims,
+            24 * self.rows * self.channels * GROUP,
+        )
+
+
+def natural_quarters(relative):
+    state = lax.axis_index(STATE)
+    dp = lax.axis_index(DP)
+    near = [jnp.where(state == 0, *relative[:2]), jnp.where(state == 0, *relative[1::-1])]
+    far = [jnp.where(state == 0, *relative[2:]), jnp.where(state == 0, *relative[:1:-1])]
+    return [jnp.where(dp == 0, a, b) for a, b in zip(near, far)] + [
+        jnp.where(dp == 0, b, a) for a, b in zip(near, far)
+    ]
+
+
+def z_pieces(value):
+    beside = state_swap(value)
+    return [value, beside, dp_swap(value), dp_swap(beside)]
+
+
+def swap_quarters(value):
+    quarter = value.shape[-1] // 4
+    part = [value[..., i * quarter : (i + 1) * quarter] for i in range(4)]
+    return jnp.concatenate([part[1], part[0], part[3], part[2]], -1)
+
+
+def add_everywhere(value):
+    for mask in head_masks()[0]:
+        value = value + head_swap(value, mask)
+    return add_zed(value)
+
+
+def add_zed(value):
+    value = value + state_swap(value)
+    return value + dp_swap(value)
+
+
+def by_state(own, other):
+    state = lax.axis_index(STATE)
+    return jnp.concatenate([jnp.where(state == 0, own, other), jnp.where(state == 0, other, own)], 0)
+
+
+def turn(value, cosine, sine):
+    rows = value.shape[0]
+    cubes = value.reshape(rows, -1, HDIM)
+    half = HDIM // 2
+    swapped = jnp.concatenate([cubes[..., half:], cubes[..., :half]], -1)
+    return (cubes * cosine[:, None, :] + swapped * sine[:, None, :]).reshape(value.shape)
 
 
 def fast_device(
@@ -830,8 +1347,6 @@
     gain_gated,
     proj_output,
 ):
-    zed = ZED
-    everywhere = EVERY
     rows = hidden.shape[0]
     length = cotangent.shape[0]
     width = hidden.shape[1]
@@ -841,44 +1356,50 @@
     state = lax.axis_index(STATE)
     dp = lax.axis_index(DP)
     head = lax.axis_index(HEAD)
+    place = dp * 2 + state
     own_start = state * rows
     orders = head_masks()
     offsets = [chunk_of(orders[0]) * piece, middle + chunk_of(orders[1]) * piece]
-    halves = [(offset, order) for offset, order in zip(offsets, orders)]
-    segment, position, valid = row_layout(lengths[0], length)
-    own_segment = lax.dynamic_slice_in_dim(segment, own_start, rows)
-    own_valid = lax.dynamic_slice_in_dim(valid, own_start, rows)[:, None]
-
-    def cut(value):
-        return [lax.dynamic_slice_in_dim(value, offset, piece, 0) for offset in offsets]
-
-    valid_cut = cut(own_valid)
-
-    gains = lax.all_gather(
-        jnp.concatenate([gain_attn, gain_mlp, gain_mixer]), zed, axis=0, tiled=False
-    ).astype(full)
+
+    heads_wide = w_query.shape[1]
+    half_cols = heads_wide // 2
+
+    def state_columns(values, index):
+        return jnp.concatenate(
+            [lax.dynamic_slice_in_dim(v, index * half_cols, half_cols, 1) for v in values], 1
+        )
+
+    main_pieces = z_pieces_columns(
+        state_columns((w_query, w_key, w_value), state),
+        state_columns((w_query, w_key, w_value), 1 - state),
+    )
+    main_near = jnp.concatenate(main_pieces[:2], 0)
+    main_far = jnp.concatenate(main_pieces[2:], 0)
+    up_pieces = z_pieces_columns(
+        state_columns((up_query, up_key, up_value), state),
+        state_columns((up_query, up_key, up_value), 1 - state),
+    )
+    ups = jnp.concatenate(natural_quarters(up_pieces), 0)
+    rank = down_query.shape[1]
+    column = lax.broadcasted_iota(jnp.int32, (1, 3 * half_cols), 1) // half_cols
+    up_wide = jnp.concatenate(
+        [jnp.where(column == index, ups, jnp.zeros_like(ups)) for index in range(3)], 0
+    )
+
     split_a, split_m = gain_attn.shape[0], gain_mlp.shape[0]
-    attn_gain = gains[:, :split_a].reshape(-1)
-    mlp_gain = gains[:, split_a : split_a + split_m].reshape(-1)
-    mixer_gain = gains[:, split_a + split_m :].reshape(-1)
-
-    query_main = weight_pieces(w_query, 1)
-    key_main = weight_pieces(w_key, 1)
-    value_main = weight_pieces(w_value, 1)
-    ups = jnp.stack([up_query, up_key, up_value], 0)
-    half_cols = up_query.shape[1] // 2
-    ups_mine = lax.dynamic_slice_in_dim(ups, state * half_cols, half_cols, 2)
-    ups_got = state_swap(lax.dynamic_slice_in_dim(ups, (1 - state) * half_cols, half_cols, 2))
-    ups_near = jnp.concatenate(
-        [jnp.where(state == 0, ups_mine, ups_got), jnp.where(state == 0, ups_got, ups_mine)], 1
-    )
-    ups_far = dp_swap(ups_near)
-    ups_all = jnp.concatenate(
-        [jnp.where(dp == 0, ups_near, ups_far), jnp.where(dp == 0, ups_far, ups_near)], 1
-    )
-    query_upper, key_upper, value_upper = ups_all[0], ups_all[1], ups_all[2]
-
-    rank = down_query.shape[1]
+    gains = z_pieces(jnp.concatenate([gain_attn, gain_mlp, gain_mixer]).reshape(-1, 128))
+    gains = [value.reshape(-1).astype(full) for value in gains]
+    attn_gain = jnp.concatenate([value[:split_a] for value in gains])
+    gains = natural_quarters(gains)
+    mlp_gain = jnp.concatenate([value[split_a : split_a + split_m] for value in gains])
+    mixer_gain = jnp.concatenate([value[split_a + split_m :] for value in gains])
+    up_rows = up_mlp.shape[0]
+    step_width = proj_step.shape[1]
+    small = jnp.concatenate([up_mlp, proj_step.reshape(-1, up_mlp.shape[1])], 0)
+    small = natural_quarters(z_pieces(small))
+    mlp_upper = jnp.concatenate([value[:up_rows] for value in small], 0)
+    step_main = jnp.concatenate([value[up_rows:].reshape(-1, step_width) for value in small], 0)
+
     part_a = down_query.shape[0] // head_parts
     part_m = down_mlp.shape[0] // head_parts
     downs = jnp.concatenate(
@@ -890,109 +1411,105 @@
         ],
         0,
     )
-    downs_got = state_swap(downs)
-    downs_near = jnp.stack(
-        [jnp.where(state == 0, downs, downs_got), jnp.where(state == 0, downs_got, downs)], 0
-    )
-    downs_far = dp_swap(downs_near)
-    downs_all = jnp.concatenate(
-        [jnp.where(dp == 0, downs_near, downs_far), jnp.where(dp == 0, downs_far, downs_near)], 0
-    )
     masks = orders[0][::-1]
-    downs_all = gather_rows(downs_all[None], masks, 0)
+    downs_all = gather_rows(jnp.stack(z_pieces(downs), 0)[None], masks, 0)
 
     def down_of(lower, part):
-        return downs_all[:, :, lower : lower + part].transpose(1, 0, 2, 3).reshape(-1, rank)
-
-    query_down = down_of(0, part_a)
-    key_down = down_of(part_a, part_a)
-    value_down = down_of(2 * part_a, part_a)
-    mlp_down = down_of(3 * part_a, part_m)
-
-    joined = jnp.concatenate([hidden, embedding], 1).astype(full)
-    normed_own = rms_norm(joined, attn_gain).astype(low)
-    joined_cut = [
-        jnp.concatenate([a, b], 1).astype(full) for a, b in zip(cut(hidden), cut(embedding))
-    ]
-    normed_far = jnp.concatenate(
-        [
-            gather_rows(state_swap(rms_norm(value, attn_gain).astype(low)), order, 0)
-            for value, (offset, order) in zip(joined_cut, halves)
-        ],
-        0,
-    )
-    normed = jnp.concatenate(
-        [
-            jnp.where(state == 0, normed_own, normed_far),
-            jnp.where(state == 0, normed_far, normed_own),
-        ],
-        0,
-    )
-    head_count = query_main.shape[1] // HDIM
-
-    def project(main, down, upper):
-        reduced = plain_dot(normed, down).astype(low)
-        return (plain_dot(normed, main) + plain_dot(reduced, upper), reduced)
-
-    def as_heads(value):
-        return value.reshape(length, head_count, HDIM)
-
-    query_pre, query_red = project(query_main, query_down, query_upper)
-    key_pre, key_red = project(key_main, key_down, key_upper)
-    value_pre, value_red = project(value_main, value_down, value_upper)
-    queries = rotate(as_heads(query_pre), position).astype(low)
-    keys = rotate(as_heads(key_pre), position).astype(low)
-    values = as_heads(value_pre).astype(low)
+        return downs_all[:, :, lower : lower + part].transpose(1, 0, 2, 3)
+
+    down_wide = jnp.concatenate(
+        [down_of(index * part_a, part_a).reshape(-1, rank) for index in range(3)], 1
+    )
+    down_m = down_of(3 * part_a, part_m)
+    mlp_down = jnp.concatenate(natural_quarters([down_m[i] for i in range(4)]), 0)
+    mlp_down = mlp_down.reshape(-1, rank)
+
+    segment, position, valid = row_layout(lengths[0], length)
+    own_segment = lax.dynamic_slice_in_dim(segment, own_start, rows)
+    own_valid = lax.dynamic_slice_in_dim(valid, own_start, rows)[:, None]
+    lows = first_blocks(segment)
+    half = HDIM // 2
+    angle = position[:, None] * 10000.0 ** (-jnp.arange(half, dtype=full) / half)[None, :]
+    cosine = jnp.concatenate([jnp.cos(angle), jnp.cos(angle)], 1)
+    sine = jnp.concatenate([-jnp.sin(angle), jnp.sin(angle)], 1)
+
+    def cut(value):
+        return [lax.dynamic_slice_in_dim(value, offset, piece, 0) for offset in offsets]
+
+    valid_cut = cut(own_valid)
+
+    quarter = gain_attn.shape[0]
+
+    def quarters(first, second):
+        both = jnp.concatenate([first, second], 1)
+        return jnp.concatenate(
+            [
+                lax.dynamic_slice_in_dim(both, (place ^ index) * quarter, quarter, 1)
+                for index in range(4)
+            ],
+            1,
+        ).astype(full)
+
+    normed_own = rms_norm(quarters(hidden, embedding), attn_gain).astype(low)
+    near_own, far_own = normed_own[:, :width], normed_own[:, width:]
+    joined_cut = [quarters(a, b) for a, b in zip(cut(hidden), cut(embedding))]
+
+    def other_rows(value, order):
+        share = rows // head_parts
+        sent = lax.dynamic_slice_in_dim(value, chunk_of(order) * share, share, 0)
+        sent = jnp.concatenate([sent[:, quarter:], sent[:, :quarter]], 1)
+        return gather_rows(state_swap(sent), order, 0)
+
+    near_other = other_rows(near_own, orders[0])
+    far_other = other_rows(far_own, orders[1])
+
+    def project(near, far):
+        reduced = (plain_dot(near, down_wide[:width]) + plain_dot(far, down_wide[width:])).astype(low)
+        total = plain_dot(near, main_near) + plain_dot(reduced, up_wide)
+        return total + plain_dot(far, main_far), reduced
+
+    pre_own, red_own = project(near_own, far_own)
+    pre_other, red_other = project(near_other, far_other)
+    pre = by_state(pre_own, pre_other)
+    queries = turn(pre[:, :half_cols], cosine, sine).astype(low)
+    keys = turn(pre[:, half_cols : 2 * half_cols], cosine, sine).astype(low)
+    values = pre[:, 2 * half_cols :].astype(low)
 
     (
         mlp_input,
-        up_mlp,
         mlp_output,
         proj_inner,
         proj_gate,
-        proj_step,
         proj_output,
-        value_main,
+        main_far,
     ) = lax.optimization_barrier(
-        (
-            mlp_input,
-            up_mlp,
-            mlp_output,
-            proj_inner,
-            proj_gate,
-            proj_step,
-            proj_output,
-            value_main,
-        )
-    )
-    attn_proj = weight_pieces(attn_output, 0)
-    mlp_main = lax.all_gather(mlp_input, zed, axis=0, tiled=True)
-    mlp_upper = lax.all_gather(up_mlp, zed, axis=0, tiled=True)
-    mlp_proj = lax.all_gather(mlp_output, zed, axis=1, tiled=True)
-    inner_main = lax.all_gather(proj_inner, zed, axis=0, tiled=True)
-    gate_main = lax.all_gather(proj_gate, zed, axis=0, tiled=True)
-    step_main = lax.all_gather(proj_step, zed, axis=0, tiled=True)
-    output_main = lax.all_gather(proj_output, zed, axis=1, tiled=True)
-
-    places = jnp.arange(length, dtype=jnp.int32)
-    allowed = (segment[:, None] == segment[None, :]) & (places[None, :] <= places[:, None])
-    probs = head_probs(queries, keys, allowed)
-    attended = (
-        jnp.einsum("hts,shd->thd", probs.astype(low), values, preferred_element_type=full)
-        .reshape(length, head_count * HDIM)
-        .astype(low)
-    )
+        (mlp_input, mlp_output, proj_inner, proj_gate, proj_output, main_far)
+    )
+    attn_pieces = z_pieces_columns(
+        lax.dynamic_slice_in_dim(attn_output, state * half_cols, half_cols, 0),
+        lax.dynamic_slice_in_dim(attn_output, (1 - state) * half_cols, half_cols, 0),
+    )
+    attn_proj = jnp.concatenate(natural_quarters(attn_pieces), 1)
+    mlp_main = lax.all_gather(mlp_input, ZED, axis=0, tiled=True)
+    mlp_proj = lax.all_gather(mlp_output, ZED, axis=1, tiled=True)
+    mixer_main = lax.all_gather(
+        jnp.concatenate([proj_inner, proj_gate], 1), ZED, axis=0, tiled=True
+    )
+    output_main = lax.all_gather(proj_output, ZED, axis=1, tiled=True)
+
+    attended, lse = attend(queries, keys, values, segment, lows)
 
     def state_halves(value):
         cubes = value.reshape(2, 2, middle, value.shape[1])
-        return [cubes[:, 0], cubes[:, 1]]
+        return [cubes[:, 0].reshape(rows, -1), cubes[:, 1].reshape(rows, -1)]
 
     def from_halves(pair):
-        return jnp.stack(pair, 1).reshape(length, pair[0].shape[-1])
-
+        return jnp.stack([p.reshape(2, middle, -1) for p in pair], 1).reshape(length, -1)
+
+    attended_halves = state_halves(attended)
     branch_cut = [
-        sum_row16(plain_dot(part.reshape(rows, -1), attn_proj).reshape(2, middle, width), order)
-        for part, (offset, order) in zip(state_halves(attended), halves)
+        sum_row16(plain_dot(part, attn_proj).astype(low).reshape(2, middle, width), order)
+        for part, order in zip(attended_halves, orders)
     ]
     first_cut = [
         value.astype(full) + good * branch
@@ -1000,7 +1517,7 @@
     ]
     mlp_normed = [
         gather_rows(rms_norm(value, mlp_gain).astype(low), order, 0)
-        for value, (offset, order) in zip(first_cut, halves)
+        for value, order in zip(first_cut, orders)
     ]
     mlp_red = [plain_dot(value, mlp_down).astype(low) for value in mlp_normed]
     hidden_pre = [
@@ -1009,58 +1526,47 @@
     ]
     activated = [jax.nn.gelu(value, approximate=False).astype(low) for value in hidden_pre]
     second_cut = [
-        value + good * sum_rows(plain_dot(part, mlp_proj), order, 0)
-        for value, good, part, (offset, order) in zip(first_cut, valid_cut, activated, halves)
+        value + good * sum_rows(plain_dot(part, mlp_proj).astype(low), order, 0)
+        for value, good, part, order in zip(first_cut, valid_cut, activated, orders)
     ]
-    mixer_halves = [
-        gather_rows(rms_norm(value, mixer_gain).astype(low), order, 0)
-        for value, (offset, order) in zip(second_cut, halves)
-    ]
-    mixer_normed = jnp.concatenate(mixer_halves, 0)
-
-    inner_pre = plain_dot(mixer_normed, inner_main)
-    gate_pre = plain_dot(mixer_normed, gate_main)
+    mixer_normed = jnp.concatenate(
+        [
+            gather_rows(rms_norm(value, mixer_gain).astype(low), order, 0)
+            for value, order in zip(second_cut, orders)
+        ],
+        0,
+    )
+
+    inner_width = proj_inner.shape[1]
+    mixer_heads = step_width
+    states = proj_input.shape[1]
     small_main = jnp.concatenate([step_main, proj_input, proj_read], 1)
     small_pre = plain_dot(mixer_normed, small_main)
-    mixer_heads = step_main.shape[1]
-    states = proj_input.shape[1]
+    mixer_pre = plain_dot(mixer_normed, mixer_main)
+    inner_pre, gate_pre = mixer_pre[:, :inner_width], mixer_pre[:, inner_width:]
     reach = taps_inner.shape[0] - 1
     edge = state_forward(
         jnp.concatenate([inner_pre[rows - reach :], small_pre[rows - reach :, mixer_heads:]], 1)
     )
-    inner_width = inner_pre.shape[1]
     edge_start = jnp.maximum(own_start - reach, 0)
-    edge_segment = jnp.where(
-        state == 0, -1, lax.dynamic_slice_in_dim(segment, edge_start, reach)
-    )
-    before = edge_segment[-1]
-
-    def mixer_piece(inner_in, small_in, edge_in, taps_x, taps_b, taps_c, shift_in, rate_in):
-        step_in = small_in[:, :mixer_heads]
+    edge_segment = jnp.where(state == 0, -1, lax.dynamic_slice_in_dim(segment, edge_start, reach))
+
+    def conv_piece(inner_in, small_in, edge_in, taps_x, taps_b, taps_c, shift_in):
         input_in = small_in[:, mixer_heads : mixer_heads + states]
         read_in = small_in[:, mixer_heads + states :]
         edge_b = edge_in[:, inner_width : inner_width + states]
         edge_c = edge_in[:, inner_width + states :]
-        inner_conv = jax.nn.silu(
-            conv_edge(inner_in, edge_in[:, :inner_width], taps_x, own_segment, edge_segment)
+        return (
+            jax.nn.silu(
+                conv_edge(inner_in, edge_in[:, :inner_width], taps_x, own_segment, edge_segment)
+            ),
+            jax.nn.silu(conv_edge(input_in, edge_b, taps_b, own_segment, edge_segment)),
+            jax.nn.silu(conv_edge(read_in, edge_c, taps_c, own_segment, edge_segment)),
+            jax.nn.softplus(small_in[:, :mixer_heads] + shift_in[None, :]),
         )
-        input_conv = jax.nn.silu(conv_edge(input_in, edge_b, taps_b, own_segment, edge_segment))
-        read_conv = jax.nn.silu(conv_edge(read_in, edge_c, taps_c, own_segment, edge_segment))
-        step_sizes = jax.nn.softplus(step_in + shift_in[None, :])
-        outputs, last_state, entry, carry = scan_blocks(
-            inner_conv,
-            step_sizes,
-            -jnp.exp(rate_in),
-            input_conv,
-            read_conv,
-            own_segment,
-            before,
-            GROUP,
-        )
-        return outputs, inner_conv, last_state, read_conv, entry
-
-    (scanned_own, inner_conv, last_state, read_conv, entry), mixer_back = jax.vjp(
-        mixer_piece,
+
+    (inner_conv, input_conv, read_conv, steps), conv_back = jax.vjp(
+        conv_piece,
         inner_pre,
         small_pre,
         edge,
@@ -1068,18 +1574,15 @@
         taps_input.astype(full),
         taps_read.astype(full),
         step_bias.astype(full),
-        log_rate.astype(full),
-    )
-    first_state = state_forward(last_state)
+    )
+    rate = -jnp.exp(log_rate.astype(full))
+    scan = Scan(inner_conv, steps, rate, input_conv, read_conv, own_segment, edge_segment[-1])
+    first_state = state_forward(scan.end())
+    scanned, block_states = scan.forward(first_state)
 
     def by_head(value):
         return value.reshape(rows, mixer_heads, MDIM)
 
-    def flat(value):
-        return value.reshape(rows, mixer_heads * MDIM)
-
-    from_first = jnp.einsum("tn,hnp->thp", read_conv, first_state)
-    scanned = scanned_own + flat(from_first * entry[:, :, None])
     skip_full = jnp.repeat(skip_gain.astype(full), MDIM)[None, :]
     combined = scanned + skip_full * inner_conv
     gate_act = jax.nn.silu(gate_pre)
@@ -1097,38 +1600,22 @@
     row_scale = lax.rsqrt(pair[0] / channels + epsilon)[:, None]
     row_total = pair[1][:, None]
     gated = (united * row_scale * gated_gain).astype(low)
-    out_cut = [
-        (
-            value
-            + good
-            * sum_rows(
-                plain_dot(gated[index * middle : (index + 1) * middle], output_main), order, 0
-            )
-        ).astype(low)
-        for index, (value, good, (offset, order)) in enumerate(
-            zip(second_cut, valid_cut, halves)
-        )
-    ]
-    layer_out = from_halves(
-        [gather_row16(value, order) for value, (offset, order) in zip(out_cut, halves)]
-    )
-
-    grad_output_main = left_dot(gated, mix_grad).astype(low)
-    grad_gated_gain = jnp.sum(gated_grad * united * row_scale, 0)
     united_grad = (
         row_scale * gated_gain * gated_grad
         - united * row_scale * row_scale * row_scale * row_total / channels
     )
     combined_grad = united_grad * gate_act
+    last_state_grad = state_backward(scan.start_grad(combined_grad))
+
     sigmoid_gate = jax.nn.sigmoid(gate_pre)
     gate_grad = united_grad * combined * sigmoid_gate * (1.0 + gate_pre * (1.0 - sigmoid_gate))
+    grad_gated_gain = jnp.sum(gated_grad * united * row_scale, 0)
     grad_skip = jnp.sum(by_head(combined_grad * inner_conv), (0, 2))
-    conv_extra = skip_full * combined_grad
-    entry_grad = by_head(combined_grad) * entry[:, :, None]
-    first_state_grad = jnp.einsum("tn,thp->hnp", read_conv, entry_grad)
-    last_state_grad = state_backward(first_state_grad)
-    read_extra = jnp.einsum("thp,hnp->tn", entry_grad, first_state)
-    entry_extra = jnp.sum(by_head(combined_grad) * from_first, 2)
+    scan_grad, step_grad, log_grad, log_rows, input_grad, read_grad = scan.backward(
+        combined_grad, block_states, last_state_grad
+    )
+    log_grad = log_grad - log_rows.T
+    grad_rate = jnp.sum(log_grad * steps, 0) * rate
     (
         inner_grad,
         small_grad,
@@ -1137,27 +1624,29 @@
         grad_taps_b,
         grad_taps_c,
         grad_shift,
-        grad_rate,
-    ) = mixer_back((combined_grad, conv_extra, last_state_grad, read_extra, entry_extra))
+    ) = conv_back(
+        (
+            scan_grad + skip_full * combined_grad,
+            input_grad,
+            read_grad,
+            step_grad + log_grad * rate[None, :],
+        )
+    )
     edge_back = state_backward(edge_grad)
     inner_grad = inner_grad.at[rows - reach :].add(edge_back[:, :inner_width])
     small_grad = small_grad.at[rows - reach :, mixer_heads:].add(edge_back[:, inner_width:])
-    inner_low = inner_grad.astype(low)
-    gate_low = gate_grad.astype(low)
+    inner_low = jnp.concatenate([inner_grad, gate_grad], 1).astype(low)
     small_low = small_grad.astype(low)
     mixer_sum = [
         sum_rows(
-            right_dot(inner_low[part], inner_main)
-            + right_dot(gate_low[part], gate_main)
-            + right_dot(small_low[part], small_main),
+            (right_dot(inner_low[part], mixer_main) + right_dot(small_low[part], small_main)).astype(
+                low
+            ),
             order,
             0,
         )
-        for part, (offset, order) in zip((slice(0, middle), slice(middle, rows)), halves)
+        for part, order in zip((slice(0, middle), slice(middle, rows)), orders)
     ]
-    grad_inner_main = left_dot(mixer_normed, inner_low).astype(low)
-    grad_gate_main = left_dot(mixer_normed, gate_low).astype(low)
-    grad_small_main = left_dot(mixer_normed, small_low)
     upstream_cut = [value.astype(full) for value in cut(cot_own)]
     mixer_backs = [
         norm_back(value, mixer_gain, grad) for value, grad in zip(second_cut, mixer_sum)
@@ -1166,7 +1655,7 @@
     grad_mixer_gain = mixer_backs[0][1] + mixer_backs[1][1]
     mlp_grad = [
         gather_rows((good * grad).astype(low), order, 0)
-        for good, grad, (offset, order) in zip(valid_cut, second_grad, halves)
+        for good, grad, order in zip(valid_cut, second_grad, orders)
     ]
 
     def gelu_part(value):
@@ -1176,11 +1665,10 @@
         jax.vjp(gelu_part, pre)[1](right_dot(grad, mlp_proj))[0].astype(low)
         for pre, grad in zip(hidden_pre, mlp_grad)
     ]
+    mlp_wide = jnp.concatenate([mlp_main, mlp_upper], 0)
     mlp_sums = [
-        sum_rows(
-            jnp.concatenate([right_dot(grad, mlp_main), right_dot(grad, mlp_upper)], 1), order, 0
-        )
-        for grad, (offset, order) in zip(hidden_grad, halves)
+        sum_rows(right_dot(grad, mlp_wide).astype(low), order, 0)
+        for grad, order in zip(hidden_grad, orders)
     ]
     middle_low = [value[:, width:].astype(low) for value in mlp_sums]
     mlp_backs = [
@@ -1189,181 +1677,223 @@
     ]
     first_grad = [grad + back[0] for grad, back in zip(second_grad, mlp_backs)]
     grad_mlp_gain = mlp_backs[0][1] + mlp_backs[1][1]
-    branch_wide = [
-        gather_row16(jnp.concatenate([(good * grad).astype(low), mid], 1), order)
-        for good, grad, mid, (offset, order) in zip(valid_cut, first_grad, middle_low, halves)
+    branch_halves = [
+        gather_row16((good * grad).astype(low), order).reshape(rows, width)
+        for good, grad, order in zip(valid_cut, first_grad, orders)
     ]
-    branch_all = from_halves(branch_wide)
-    branch_grad = branch_all[:, :width]
-    middle_own = lax.dynamic_slice(branch_all, (own_start, width), (rows, rank))
-    activated_own = jnp.concatenate(activated, 0)
-    mlp_normed_own = jnp.concatenate(mlp_normed, 0)
-    hidden_grad_own = jnp.concatenate(hidden_grad, 0)
-    grad_mlp_proj = left_dot(activated_own, jnp.concatenate(mlp_grad, 0)).astype(low)
-    grad_mlp_main = left_dot(mlp_normed_own, hidden_grad_own).astype(low)
-    grad_mlp_upper = left_dot(jnp.concatenate(mlp_red, 0), hidden_grad_own).astype(low)
-    grad_mlp_down = left_dot(mlp_normed_own, middle_own).astype(low)
-
-    def scatter(value, axis):
-        return lax.psum_scatter(value, zed, scatter_dimension=axis, tiled=True).astype(full)
-
-    out_output = scatter(grad_output_main, 1)
-    out_inner = scatter(grad_inner_main, 0)
-    out_gate = scatter(grad_gate_main, 0)
-    out_mlp_output = scatter(grad_mlp_proj, 1)
-    out_mlp_input = scatter(grad_mlp_main, 0)
-    out_up_mlp = scatter(grad_mlp_upper, 0)
-    out_down_mlp = scatter(grad_mlp_down, 0)
-
-    out_attn = grad_pieces(left_dot(attended, branch_grad), 0)
-    attended_grad = as_heads(right_dot(branch_grad, attn_proj))
-    probs_back = head_probs(queries, keys, allowed)
-    score_scale = HDIM ** (-0.5)
-    out_low = attended_grad.astype(low)
-    prob_grad = jnp.einsum("thd,shd->hts", out_low, values, preferred_element_type=full)
-    score_grad = probs_back * (prob_grad - jnp.sum(probs_back * prob_grad, -1, keepdims=True))
-    score_low = score_grad.astype(low)
-    query_back = (
-        jnp.einsum("hts,shd->thd", score_low, keys, preferred_element_type=full) * score_scale
-    )
-    keys_back = (
-        jnp.einsum("hts,thd->shd", score_low, queries, preferred_element_type=full) * score_scale
-    )
-    values_back = jnp.einsum(
-        "hts,thd->shd", probs_back.astype(low), out_low, preferred_element_type=full
-    )
-
-    def as_flat(value):
-        return value.reshape(length, head_count * HDIM).astype(low)
-
-    query_grad = as_flat(rotate(query_back, -position))
-    key_grad = as_flat(rotate(keys_back, -position))
-    value_grad = as_flat(values_back)
-    out_query = grad_pieces(left_dot(normed, query_grad), 1)
-    out_key = grad_pieces(left_dot(normed, key_grad), 1)
-    out_value = grad_pieces(left_dot(normed, value_grad), 1)
-    out_ups = jnp.concatenate(
+
+    attended_grad = from_halves([right_dot(value, attn_proj).astype(low) for value in branch_halves])
+    delta = jnp.sum(
+        (attended_grad.astype(full) * attended.astype(full)).reshape(length, -1, HDIM), -1
+    ).T[:, None, :]
+    query_back, key_back, value_back = attend_back(
+        queries, keys, values, attended_grad, lse, delta, segment, lows
+    )
+    pre_grad = jnp.concatenate(
         [
-            left_dot(query_red, query_grad),
-            left_dot(key_red, key_grad),
-            left_dot(value_red, value_grad),
+            turn(query_back, cosine, -sine).astype(low),
+            turn(key_back, cosine, -sine).astype(low),
+            value_back.astype(low),
         ],
         1,
     )
+    main_wide = jnp.concatenate([main_near, main_far, up_wide], 0)
+    joint = 2 * width
+    normed_sums = []
+    for part, order in zip(state_halves(pre_grad), orders):
+        total = right_dot(part, main_wide).astype(low).reshape(2, middle, -1)
+        total = sum_rows(total, order, 1)
+        away = lax.dynamic_index_in_dim(total, 1 - state, 0, False).astype(low)
+        away = jnp.concatenate([swap_quarters(away[:, :joint]), away[:, joint:]], 1)
+        kept = lax.dynamic_index_in_dim(total, state, 0, False)
+        normed_sums.append(kept + state_swap(away).astype(full))
+    grad_own = lax.dynamic_slice_in_dim(pre_grad, own_start, rows, 0)
+    grad_other = lax.dynamic_slice_in_dim(pre_grad, rows - own_start, rows, 0)
+
+    def main_grad(own, other, lower):
+        part = slice(lower * quarter, (lower + 1) * quarter)
+        return left_dot(own[:, part], grad_own) + left_dot(other[:, part], grad_other)
+
+    beside = main_grad(near_own, near_other, 1) + dp_swap(
+        main_grad(far_own, far_other, 1).astype(low)
+    ).astype(full)
+    beside = state_swap(beside.astype(low)).astype(full)
+    main_total = main_grad(near_own, near_other, 0) + dp_swap(
+        main_grad(far_own, far_other, 0).astype(low)
+    ).astype(full)
+
+    def spread(own, got, index):
+        part = slice(index * half_cols, (index + 1) * half_cols)
+        own, got = own[:, part], got[:, part]
+        return jnp.concatenate(
+            [jnp.where(state == 0, own, got), jnp.where(state == 0, got, own)], 1
+        )
+
+    out_main = [spread(main_total, beside, index) for index in range(3)]
+    red_all = by_state(red_own, red_other)
+    up_grad = jnp.concatenate(
+        [
+            left_dot(
+                red_all[:, index * rank : (index + 1) * rank],
+                pre_grad[:, index * half_cols : (index + 1) * half_cols],
+            )
+            for index in range(3)
+        ],
+        1,
+    )
     rank_half = rank // 2
-    ups_away = lax.dynamic_slice_in_dim(out_ups, (1 - dp) * rank_half, rank_half, 0)
-    ups_sum = lax.dynamic_slice_in_dim(out_ups, dp * rank_half, rank_half, 0) + dp_swap(ups_away)
+    up_sum = lax.dynamic_slice_in_dim(up_grad, dp * rank_half, rank_half, 0) + dp_swap(
+        lax.dynamic_slice_in_dim(up_grad, (1 - dp) * rank_half, rank_half, 0)
+    )
     rank_quarter = rank_half // 2
-    ups_kept = lax.dynamic_slice_in_dim(ups_sum, state * rank_quarter, rank_quarter, 0)
-    ups_back = state_swap(
-        lax.dynamic_slice_in_dim(ups_sum, (1 - state) * rank_quarter, rank_quarter, 0)
-    )
-
-    def up_of(index):
-        part = slice(index * half_cols, (index + 1) * half_cols)
+    up_kept = lax.dynamic_slice_in_dim(up_sum, state * rank_quarter, rank_quarter, 0)
+    up_got = state_swap(
+        lax.dynamic_slice_in_dim(up_sum, (1 - state) * rank_quarter, rank_quarter, 0)
+    )
+    out_up = [spread(up_kept, up_got, index) for index in range(3)]
+    attn_grad = left_dot(attended_halves[0], branch_halves[0]) + left_dot(
+        attended_halves[1], branch_halves[1]
+    )
+    out_attn = grad_pieces(attn_grad.astype(low), 0)
+
+    lows_cut = [value[:, joint:].astype(low) for value in normed_sums]
+    joined_backs = [
+        norm_back(value, attn_gain, total[:, :joint] + right_dot(mid, down_wide))
+        for value, total, mid in zip(joined_cut, normed_sums, lows_cut)
+    ]
+    grad_attn_gain = joined_backs[0][1] + joined_backs[1][1]
+
+    def natural_columns(value):
         return jnp.concatenate(
             [
-                jnp.where(state == 0, ups_kept[:, part], ups_back[:, part]),
-                jnp.where(state == 0, ups_back[:, part], ups_kept[:, part]),
+                lax.dynamic_slice_in_dim(value, (place ^ index) * quarter, quarter, -1)
+                for index in range(4)
             ],
-            1,
+            -1,
         )
 
-    normed_parts = state_halves(
+    input_cut = []
+    for grad, back in zip(first_grad, joined_backs):
+        joined_grad = natural_columns(back[0])
+        input_cut.append(
+            (
+                (grad + joined_grad[:, :width]).astype(low),
+                joined_grad[:, width:].astype(low),
+            )
+        )
+    grad_hidden, grad_embedding = (
         jnp.concatenate(
-            [
-                right_dot(query_grad, query_main)
-                + right_dot(key_grad, key_main)
-                + right_dot(value_grad, value_main),
-                right_dot(query_grad, query_upper),
-                right_dot(key_grad, key_upper),
-                right_dot(value_grad, value_upper),
-            ],
-            1,
+            [gather_rows(pieces[index], order, 0) for pieces, order in zip(input_cut, orders)], 0
         )
-    )
-    normed_sums = [sum_row16(part, order) for part, (offset, order) in zip(normed_parts, halves)]
-    joint = 2 * width
-    lows = [value[:, joint:].astype(low) for value in normed_sums]
-    joined_backs = [
-        norm_back(
-            value,
-            attn_gain,
-            total[:, :joint]
-            + right_dot(mid[:, :rank], query_down)
-            + right_dot(mid[:, rank : 2 * rank], key_down)
-            + right_dot(mid[:, 2 * rank :], value_down),
-        )
-        for value, total, mid in zip(joined_cut, normed_sums, lows)
-    ]
-    grad_attn_gain = joined_backs[0][1] + joined_backs[1][1]
-    input_grads = jnp.concatenate(
-        [
-            gather_rows(
-                jnp.concatenate(
-                    [(grad + back[0][:, :width]).astype(low), back[0][:, width:].astype(low)], 1
-                ),
+        for index in range(2)
+    )
+
+    out_cut = [
+        (
+            value
+            + good
+            * sum_rows(
+                plain_dot(gated[index * middle : (index + 1) * middle], output_main).astype(low),
                 order,
                 0,
             )
-            for grad, back, (offset, order) in zip(first_grad, joined_backs, halves)
-        ],
-        0,
-    )
-    grad_hidden = input_grads[:, :width]
-    grad_embedding = input_grads[:, width:]
-
-    lows_all = from_halves(
-        [gather_row16(value, order) for value, (offset, order) in zip(lows, halves)]
-    )
-    quarter = gain_attn.shape[0]
-
-    def down_rows(index):
-        start = (index * 2 + state) * quarter + head * part_a
-        columns = lax.dynamic_slice_in_dim(normed, start, part_a, 1)
-        return left_dot(columns, lows_all)
-
-    down_sum = down_rows(dp) + dp_swap(down_rows(1 - dp).astype(low)).astype(full)
-    down_all = gather_rows(down_sum.astype(low)[None], masks, 0)
-    down_all = down_all.reshape(quarter, 3 * rank).astype(full)
+        ).astype(low)
+        for index, (value, good, order) in enumerate(zip(second_cut, valid_cut, orders))
+    ]
+    layer_out = from_halves([gather_row16(value, order) for value, order in zip(out_cut, orders)])
+
+    def scatter(value, axis):
+        return lax.psum_scatter(
+            value.astype(low), ZED, scatter_dimension=axis, tiled=True
+        ).astype(full)
+
+    out_output = scatter(left_dot(gated, mix_grad), 1)
+    out_mixer = scatter(left_dot(mixer_normed, inner_low), 0)
+    mlp_normed_own = jnp.concatenate(mlp_normed, 0)
+    hidden_grad_own = jnp.concatenate(hidden_grad, 0)
+    out_mlp_output = scatter(
+        left_dot(jnp.concatenate(activated, 0), jnp.concatenate(mlp_grad, 0)), 1
+    )
+    out_mlp_input = scatter(left_dot(mlp_normed_own, hidden_grad_own), 0)
+    out_up_mlp = scatter(left_dot(jnp.concatenate(mlp_red, 0), hidden_grad_own), 0)
+
+    middle_own = jnp.concatenate(
+        [gather_rows(value, order, 0) for value, order in zip(middle_low, orders)], 0
+    )
+    lows_halves = [gather_row16(value, order) for value, order in zip(lows_cut, orders)]
+    lows_own, lows_other = (
+        jnp.concatenate(
+            [lax.dynamic_index_in_dim(value, index, 0, False) for value in lows_halves], 0
+        )
+        for index in (state, 1 - state)
+    )
+
+    def down_rows(own, other):
+        start = head * part_a
+        own = lax.dynamic_slice_in_dim(own, start, part_a, 1)
+        other = lax.dynamic_slice_in_dim(other, start, part_a, 1)
+        return left_dot(own, lows_own) + left_dot(other, lows_other)
+
+    down_sum = down_rows(near_own, near_other) + dp_swap(
+        down_rows(far_own, far_other).astype(low)
+    ).astype(full)
+    columns = mlp_normed_own.reshape(rows, 4, head_parts, part_m)
+    columns = lax.dynamic_index_in_dim(columns, head, 2, False).reshape(rows, 4 * part_m)
+    mlp_down_grad = left_dot(columns, middle_own).reshape(4, part_m, rank)
+    kept = lax.dynamic_slice_in_dim(mlp_down_grad, 2 * dp, 2, 0) + dp_swap(
+        lax.dynamic_slice_in_dim(mlp_down_grad, 2 * (1 - dp), 2, 0)
+    )
+    kept = lax.dynamic_index_in_dim(kept, state, 0, False) + state_swap(
+        lax.dynamic_index_in_dim(kept, 1 - state, 0, False)
+    )
+    down_all = gather_rows(down_sum.astype(low)[None], masks, 0).reshape(quarter, 3 * rank)
+    down_all = down_all.astype(full)
     out_downs = [down_all[:, index * rank : (index + 1) * rank] for index in range(3)]
-
-    small_total, taps_b_total, taps_c_total = lax.psum(
-        (grad_small_main[:, mixer_heads:], grad_taps_b, grad_taps_c), everywhere
-    )
-    out_step = lax.psum_scatter(
-        grad_small_main[:, :mixer_heads], zed, scatter_dimension=0, tiled=True
-    )
-    gated_total, taps_x_total, head_total = lax.psum(
-        (grad_gated_gain, grad_taps_x, jnp.stack([grad_shift, grad_rate, grad_skip], 0)), zed
-    )
+    out_down_mlp = gather_rows(kept.astype(low)[None], masks, 0).reshape(-1, rank).astype(full)
+
+    small_main_grad = left_dot(mixer_normed, small_low)
+    vector_grad = sum_rows(small_main_grad[:, mixer_heads:], masks, 0)
+    vector_grad = gather_rows(add_zed(vector_grad), masks, 0)
+    step_rows = small_main_grad[:, :mixer_heads].reshape(4, -1, mixer_heads)
+    kept = lax.dynamic_slice_in_dim(step_rows, 2 * dp, 2, 0) + dp_swap(
+        lax.dynamic_slice_in_dim(step_rows, 2 * (1 - dp), 2, 0)
+    )
+    out_step = lax.dynamic_index_in_dim(kept, state, 0, False) + state_swap(
+        lax.dynamic_index_in_dim(kept, 1 - state, 0, False)
+    )
+    taps_total = add_everywhere(jnp.concatenate([grad_taps_b, grad_taps_c], 1))
+    own_total = add_zed(
+        jnp.concatenate(
+            [grad_gated_gain, grad_taps_x.reshape(-1), grad_shift, grad_rate, grad_skip]
+        )
+    )
+    gated_total = own_total[:inner_width]
+    taps_end = inner_width * (reach + 2)
+    taps_x_total = own_total[inner_width:taps_end].reshape(reach + 1, inner_width)
+    head_total = own_total[taps_end:].reshape(3, mixer_heads)
+    attn_gain_grad = natural_columns(grad_attn_gain)
+    gain_total = add_everywhere(
+        jnp.concatenate([attn_gain_grad, grad_mlp_gain, grad_mixer_gain]).reshape(-1, 128)
+    ).reshape(-1)
+
+    def gain_of(start, size):
+        return lax.dynamic_slice_in_dim(gain_total, start + place * size, size)
+
     once = (head == 0).astype(full)
     square_sum = jnp.zeros((), full)
-    out_up = [up_of(index) for index in range(3)]
-    for value in [out_query, out_key, out_value, out_attn, out_mlp_input, out_up_mlp]:
-        square_sum = square_sum + jnp.sum(value * value)
-    for value in [out_mlp_output] + out_up:
+    for value in out_main + out_up + [out_attn, out_mlp_input, out_up_mlp, out_mlp_output]:
         square_sum = square_sum + jnp.sum(value * value)
     for value in out_downs + [out_down_mlp]:
         square_sum = square_sum + once * jnp.sum(value * value)
-    square_total, gain_total = lax.psum(
-        (square_sum, jnp.concatenate([grad_attn_gain, grad_mlp_gain, grad_mixer_gain])),
-        everywhere,
-    )
-    place = dp * 2 + state
-    wide = 2 * width
-
-    def gain_of(start, size, total):
-        return lax.dynamic_slice_in_dim(gain_total[start : start + total], place * size, size)
-
+    square_total = lax.psum(square_sum, EVERY)
     return (
         layer_out,
         grad_hidden,
         grad_embedding,
-        gain_of(0, split_a, wide),
-        out_query,
-        out_key,
-        out_value,
+        gain_of(0, split_a),
+        out_main[0],
+        out_main[1],
+        out_main[2],
         out_downs[0],
         out_downs[1],
         out_downs[2],
@@ -1371,20 +1901,20 @@
         out_up[1],
         out_up[2],
         out_attn,
-        gain_of(wide, split_m, width),
+        gain_of(joint, split_m),
         out_mlp_input,
         out_down_mlp,
         out_up_mlp,
         out_mlp_output,
-        gain_of(wide + width, split_m, width),
-        out_inner,
-        out_gate,
+        gain_of(joint + width, split_m),
+        out_mixer[:, :inner_width],
+        out_mixer[:, inner_width:],
         out_step,
-        small_total[:, :states],
-        small_total[:, states:],
+        vector_grad[:, :states],
+        vector_grad[:, states:],
         taps_x_total,
-        taps_b_total,
-        taps_c_total,
+        taps_total[:, :states],
+        taps_total[:, states:],
         head_total[0],
         head_total[1],
         head_total[2],
@@ -1392,6 +1922,11 @@
         out_output,
         jnp.sqrt(square_total),
     )
+
+
+def z_pieces_columns(mine, theirs):
+    got = state_swap(theirs)
+    return [mine, got, dp_swap(mine), dp_swap(got)]
 
 
 def pick_device(mesh):

time: 2060 us -> 1770 us (0.86)
  matrix products: 425 us -> 205 us
  other arithmetic: 373 us -> 249 us
  Pallas kernels: 0 us -> 71.1 us
  blocking collectives: 101 us -> 39.5 us
  starting transfers between devices: 133 us -> 188 us
    dot_general x42 -> x0, matrix products: 103 us -> none  [the longest x1 22.1 us: fast_device(): jnp.einsum('thd,shd->hts', out_low, values, preferred_element_type=full)]
    pallas_call x0 -> x6, Pallas kernels: none -> 71.1 us  [the longest x4 34.4 us: scan_call(): pl.pallas_call(kernel, grid_spec=pltpu.PrefetchScalarGridSpec(num_scalar_...]
    dot_general x40 -> x17, matrix products: 115 us -> 61.5 us  [right_dot(): lax.dot_general(left, right, (((1,), (1,)), ((), ())), preferred_element_...]
    ppermute x23 -> x27, waiting for transfers between devices: 206 us -> 160 us  [state_swap(): return lax.ppermute(value, STATE, [(0, 1), (1, 0)])]
    all_gather x3 -> x0, blocking collectives: 45.5 us -> none  [the longest x1 17.6 us: fast_device(): mlp_upper = lax.all_gather(up_mlp, zed, axis=0, tiled=True)]
    another operation x39 -> x8, other arithmetic: 48.5 us -> 12.2 us  [the longest x4 9.37 us: from_halves(): jnp.stack([p.reshape(2, middle, -1) for p in pair], 1).reshape(length, -1)]
    dot_general x24, matrix products: 116 us -> 80 us  [plain_dot(): return jnp.dot(left, right, preferred_element_type=jnp.float32)]
    ppermute x16 -> x23, starting transfers between devices: 16.9 us -> 52.1 us  [dp_swap(): return lax.ppermute(value, DP, [(0, 1), (1, 0)])]
  transfers between devices with their start and end apart: 150 -> 183, of which waited for: 78 -> 90; matrix products, arithmetic and copies ran while one was open for 37% -> 29% of each run, Pallas kernels for 0% -> 3%
where the time goes in v2:
time: 1770 us; the launch traced here: 1760 us
  waiting for transfers between devices  767 us (43%)
  other arithmetic  249 us (14%)
  local copies, waits for them, and re-layouts  206 us (12%)
  matrix products  205 us (12%)
  starting transfers between devices  188 us (11%)
  Pallas kernels  71.1 us (4%)
  blocking collectives  39.5 us (2%)
  between operations  31.4 us (2%)
    ppermute x120, waiting for transfers between devices, head_swap(): return lax.ppermute(value, HEAD, [(i, i ^ mask) for i in range(count)])  326 us
    ppermute x23, waiting for transfers between devices, dp_swap(): return lax.ppermute(value, DP, [(0, 1), (1, 0)])  218 us
    ppermute x27, waiting for transfers between devices, state_swap(): return lax.ppermute(value, STATE, [(0, 1), (1, 0)])  160 us
    ppermute x120, starting transfers between devices, head_swap(): return lax.ppermute(value, HEAD, [(i, i ^ mask) for i in range(count)])  98 us
    unnamed x734, local copies, waits for them, and re-layouts  86.7 us
    dot_general x24, matrix products, plain_dot(): return jnp.dot(left, right, preferred_element_type=jnp.float32)  80 us
    dot_general x24, matrix products, left_dot(): lax.dot_general(left, right, (((0,), (0,)), ((), ())), preferred_element_...  63.4 us
    dot_general x17, matrix products, right_dot(): lax.dot_general(left, right, (((1,), (1,)), ((), ())), preferred_element_...  61.5 us
  transfers between devices with their start and end apart: 183, of which 90 were waited for; matrix products, arithmetic and copies ran while one was open for 29% of the time, Pallas kernels for 3%

profile of v2, /device:TPU:0, one launch (start us, length us, event | category | flops | bytes accessed | tf_op | source)
XLA Modules:
  0.0 1756.3 jit_solution(6536881561340409358)
XLA Ops:
  84.8 11.1 collective-permute-done.6
  99.3 12.9 collective-permute-done.12
  121.6 9.1 collective-permute-done.16
  134.8 51.6 %collective-permute-done.3 = bf16[1024,768]{1,0:T(8,128)(2,1)S(1)} collective-permute-done((bf16[1024,768]{1,0:T(8,128)(2,1)S(1)}, bf16[1024,768]{1,0:T(8,128)(2,1)S(1)}, u32[]{:S(2)}, u32[]{:S(2)}) %collective-permute-start.3) | collective-permute-done | bytes 1572896 | tf_op jit(solution)/shard_map/ppermute | solution.py:632
  197.1 59.8 %collective-permute-done.14 = bf16[1024,768]{1,0:T(8,128)(2,1)} collective-permute-done((bf16[1024,768]{1,0:T(8,128)(2,1)S(1)}, bf16[1024,768]{1,0:T(8,128)(2,1)}, u32[]{:S(2)}, u32[]{:S(2)}) %collective-permute-start.14) | collective-permute-done | bytes 1572896 | tf_op jit(solution)/shard_map/ppermute | solution.py:636
  294.8 7.5 broadcast_select_fusion.14
  330.0 16.8 shard_map.585
  374.1 17.9 %collective-permute-done.43 = bf16[2,128,2048]{2,1,0:T(8,128)(2,1)S(1)} collective-permute-done((bf16[2,128,2048]{2,1,0:T(8,128)(2,1)S(1)}, bf16[2,128,2048]{2,1,0:T(8,128)(2,1)S(1)}, u32[]{:S(2)}, u32[]{:S(2)}) %collective-permute-start.43) | collective-permute-done | bytes 1048608 | tf_op jit(solution)/shard_map/ppermute | solution.py:628
  398.5 8.7 collective-permute-done.44
  415.1 24.5 %collective-permute-done.45 = bf16[64,2048]{1,0:T(8,128)(2,1)} collective-permute-done((bf16[64,2048]{1,0:T(8,128)(2,1)S(1)}, bf16[64,2048]{1,0:T(8,128)(2,1)}, u32[]{:S(2)}, u32[]{:S(2)}) %collective-permute-start.45) | collective-permute-done | bytes 262176 | tf_op jit(solution)/shard_map/ppermute | solution.py:632
  439.7 10.6 collective-permute-done.29
  464.3 9.2 collective-permute-done.47
  486.8 8.9 multiply_convert_fusion.2
  495.7 38.1 %all-gather.7.cloned.1.call-done = bf16[1024,2048]{1,0:T(8,128)(2,1)} async-done(((bf16[1024,512]{1,0:T(8,128)(2,1)}), bf16[1024,2048]{1,0:T(8,128)(2,1)}) %all-gather.7.cloned.1.call-update) | async-done | bytes 4194320 | tf_op jit(solution)/shard_map/all_gather | solution.py:1494
  544.6 8.9 multiply_convert_fusion.3
  566.7 9.6 collective-permute-done.50
  597.3 9.1 collective-permute-done.40
  620.5 18.9 %all-gather.9.cloned.1.call-done = bf16[2048,1024]{1,0:T(8,128)(2,1)} async-done(((bf16[512,1024]{1,0:T(8,128)(2,1)}), bf16[2048,1024]{1,0:T(8,128)(2,1)}) %all-gather.9.cloned.1.call-update) | async-done | bytes 4194320 | tf_op jit(solution)/shard_map/all_gather | solution.py:1495
  639.4 8.5 fusion.304
  674.7 7.1 shard_map.587
  685.4 8.2 multiply_reduce_fusion.12
  718.1 17.1 shard_map.589
  775.3 7.9 collective-permute-done.68
  787.3 7.2 collective-permute-done.90
  828.0 7.5 collective-permute-done.80
  852.2 8.8 convolution_convert_fusion.6
  903.6 7.9 collective-permute-start.173
  913.2 8.7 collective-permute-start.168
  926.4 14.6 collective-permute-done.163
  943.8 7.0 collective-permute-done.165
  971.8 8.2 collective-permute-done.63
  1010.6 9.9 collective-permute-done.65
  1044.4 10.1 collective-permute-done.96
  1110.4 13.6 collective-permute-done.86
  1127.1 22.3 %collective-permute-done.87 = bf16[2,128,2048]{2,1,0:T(8,128)(2,1)S(1)} collective-permute-done((bf16[2,128,2048]{2,1,0:T(8,128)(2,1)S(1)}, bf16[2,128,2048]{2,1,0:T(8,128)(2,1)S(1)}, u32[]{:S(2)}, u32[]{:S(2)}) %collective-permute-start.87) | collective-permute-done | bytes 1048608 | tf_op jit(solution)/shard_map/ppermute | solution.py:628
  1161.2 8.5 copy.198
  1200.5 19.8 %shard_map.590 = (f32[2048,256]{1,0:T(8,128)S(1)}, f32[2048,256]{1,0:T(8,128)S(1)}, f32[2048,256]{1,0:T(8,128)S(1)}) custom-call(s32[8]{0:T(128)S(1)} %copy-done.31, bf16[2048,256]{1,0:T(8,128)(2,1)S(1)} %copy-done.19, bf16[2048,256]{1,0:T(8,128)(2,1)S(1)} %copy-done.17, bf16[2048,256]{1,0:T(8,128)(2,1)S(1)} %copy-done.15, bf16[2048,256]{1,0:T(8,128)(2,1)S(1)} %bitcast.325, ...), custom_call_target="tpu_custom_call" | custom-call | flops 5368709120 | bytes 10485760 | tf_op jit(solution)/shard_map/pallas_call | solution.py:884
  1275.7 13.2 convolution_convert_fusion.1
  1297.3 13.2 convolution_convert_fusion
  1314.0 107.8 %collective-permute-done.142 = f32[64,768]{1,0:T(8,128)S(1)} collective-permute-done((f32[64,768]{1,0:T(8,128)S(1)}, f32[64,768]{1,0:T(8,128)S(1)}, u32[]{:S(2)}, u32[]{:S(2)}) %collective-permute-start.142) | collective-permute-done | bytes 196640 | tf_op jit(solution)/shard_map/ppermute | solution.py:636
  1424.9 10.0 collective-permute-done.143
  1463.6 19.1 %collective-permute-done.129 = bf16[1024,768]{0,1:T(8,128)(2,1)} collective-permute-done((bf16[1024,768]{0,1:T(8,128)(2,1)}, bf16[1024,768]{0,1:T(8,128)(2,1)}, u32[]{:S(2)}, u32[]{:S(2)}) %collective-permute-start.129) | collective-permute-done | bytes 1572896 | tf_op jit(solution)/shard_map/ppermute | solution.py:632
  1525.2 21.5 %collective-permute-done.103 = bf16[2,128,4480]{2,1,0:T(8,128)(2,1)} collective-permute-done((bf16[2,128,4480]{2,1,0:T(8,128)(2,1)}, bf16[2,128,4480]{2,1,0:T(8,128)(2,1)}, u32[]{:S(2)}, u32[]{:S(2)}) %collective-permute-start.103) | collective-permute-done | bytes 2293792 | tf_op jit(solution)/shard_map/ppermute | solution.py:628
  1551.9 7.0 collective-permute-done.110
  1562.7 19.3 %collective-permute-done.104 = bf16[2,64,4480]{2,1,0:T(8,128)(2,1)S(1)} collective-permute-done((bf16[2,64,4480]{2,1,0:T(8,128)(2,1)S(1)}, bf16[2,64,4480]{2,1,0:T(8,128)(2,1)S(1)}, u32[]{:S(2)}, u32[]{:S(2)}) %collective-permute-start.104) | collective-permute-done | bytes 1146912 | tf_op jit(solution)/shard_map/ppermute | solution.py:628
  1589.7 13.8 collective-permute-done.112
  1639.4 6.7 collective-permute-done.135
  1696.5 39.5 %psum.7 = f32[]{:T(128)} all-reduce(f32[]{:T(128)S(6)} %add.1273), channel_id=1, replica_groups=mesh['dp'=2,'head'=8,'state'=2] {'dp','head','state'}, use_global_device_ids=true, to_apply=%region_62.63 | all-reduce | flops 1 | bytes 8 | tf_op jit(solution)/shard_map/psum | solution.py:1888
  (1637 shorter events, 917.5 us)
Async XLA Ops:
  7.2 469.4 %all-gather.5.cloned.1.call-start = ((), (), s32[]{:S(2)}) async-start(), calls=%async_computation.5 | async-start | bytes 5242880 | tf_op jit(solution)/shard_map/all_gather | solution.py:1493
  11.3 53.2 %collective-permute-start = (bf16[16,128]{1,0:T(8,128)(2,1)}, bf16[16,128]{1,0:T(8,128)(2,1)}, u32[]{:S(2)}, u32[]{:S(2)}) collective-permute-start(bf16[16,128]{1,0:T(8,128)(2,1)} %bitcast.2), channel_id=1, source_target_pairs={{0,1},{1,0},{2,3},{3,2},{4,5},{5,4},{6,7},{7,6},{8,9},{9,8},{10,11... | collective-permute-start | bytes 12296 | tf_op jit(solution)/shard_map/ppermute | solution.py:632
  14.3 52.5 %collective-permute-start.1 = (bf16[16,128]{1,0:T(8,128)(2,1)}, bf16[16,128]{1,0:T(8,128)(2,1)}, u32[]{:S(2)}, u32[]{:S(2)}) collective-permute-start(bf16[16,128]{1,0:T(8,128)(2,1)} %bitcast.2), channel_id=1, source_target_pairs={{0,16},{16,0},{1,17},{17,1},{2,18},{18,2},{3,19},{19,3},{4,20},{20... | collective-permute-start | bytes 12296 | tf_op jit(solution)/shard_map/ppermute | solution.py:636
  19.1 61.9 %collective-permute-start.4 = (bf16[448,128]{1,0:T(8,128)(2,1)}, bf16[448,128]{1,0:T(8,128)(2,1)S(1)}, u32[]{:S(2)}, u32[]{:S(2)}) collective-permute-start(bf16[448,128]{1,0:T(8,128)(2,1)} %get-tuple-element.606), channel_id=1, source_target_pairs={{0,1},{1,0},{2,3},{3,2},{4,5},{5,4},{6,7},{7,6},{8,9},{9,8},{10,11... | collective-permute-start | bytes 344072 | tf_op jit(solution)/shard_map/ppermute | solution.py:632
  19.5 64.6 %collective-permute-start.5 = (bf16[448,128]{1,0:T(8,128)(2,1)}, bf16[448,128]{1,0:T(8,128)(2,1)S(1)}, u32[]{:S(2)}, u32[]{:S(2)}) collective-permute-start(bf16[448,128]{1,0:T(8,128)(2,1)} %get-tuple-element.606), channel_id=1, source_target_pairs={{0,16},{16,0},{1,17},{17,1},{2,18},{18,2},{3,19},{19,3},{4,20},{20... | collective-permute-start | bytes 344072 | tf_op jit(solution)/shard_map/ppermute | solution.py:636
  22.9 56.6 %collective-permute-start.11 = (bf16[32,768]{1,0:T(8,128)(2,1)}, bf16[32,768]{1,0:T(8,128)(2,1)}, u32[]{:S(2)}, u32[]{:S(2)}) collective-permute-start(bf16[32,768]{1,0:T(8,128)(2,1)} %pad_maximum_fusion.135), channel_id=1, source_target_pairs={{0,16},{16,0},{1,17},{17,1},{2,18},{18,2},{3,19},{19,3},{4,20},{20... | collective-permute-start | bytes 147464 | tf_op jit(solution)/shard_map/ppermute | solution.py:636
  79.5 37.1 %collective-permute-start.15 = (bf16[128,2048]{1,0:T(8,128)(2,1)S(1)}, bf16[128,2048]{1,0:T(8,128)(2,1)S(1)}, u32[]{:S(2)}, u32[]{:S(2)}) collective-permute-start(bf16[128,2048]{1,0:T(8,128)(2,1)S(1)} %pad_maximum_fusion.88), channel_id=1, source_target_pairs={{0,1},{1,0},{2,3},{3,2},{4,5},{5,4},{6,7},{7,6},{8,9},{9,8},{10,11... | collective-permute-start | bytes 1572872 | tf_op jit(solution)/shard_map/ppermute | solution.py:632
  113.1 78.5 %collective-permute-start.13 = (bf16[1024,768]{1,0:T(8,128)(2,1)S(1)}, bf16[1024,768]{1,0:T(8,128)(2,1)S(1)}, u32[]{:S(2)}, u32[]{:S(2)}) collective-permute-start(bf16[1024,768]{1,0:T(8,128)(2,1)S(1)} %copy-done.167), channel_id=1, source_target_pairs={{0,16},{16,0},{1,17},{17,1},{2,18},{18,2},{3,19},{19,3},{4,20},{20... | collective-permute-start | bytes 4718600 | tf_op jit(solution)/shard_map/ppermute | solution.py:636
  116.6 69.9 %collective-permute-start.3 = (bf16[1024,768]{1,0:T(8,128)(2,1)S(1)}, bf16[1024,768]{1,0:T(8,128)(2,1)S(1)}, u32[]{:S(2)}, u32[]{:S(2)}) collective-permute-start(bf16[1024,768]{1,0:T(8,128)(2,1)S(1)} %copy-done.162), channel_id=1, source_target_pairs={{0,1},{1,0},{2,3},{3,2},{4,5},{5,4},{6,7},{7,6},{8,9},{9,8},{10,11... | collective-permute-start | bytes 4718600 | tf_op jit(solution)/shard_map/ppermute | solution.py:632
  121.0 72.0 %collective-permute-start.8 = (bf16[2,4,448,128]{3,2,0,1:T(8,128)(2,1)S(1)}, bf16[2,4,448,128]{3,2,0,1:T(8,128)(2,1)S(1)}, u32[]{:S(2)}, u32[]{:S(2)}) collective-permute-start(bf16[2,4,448,128]{3,2,0,1:T(8,128)(2,1)S(1)} %pad_maximum_fusion.75), channel_id=1, source_target_pairs={{0,4},{2,6},{4,0},{6,2},{8,12},{10,14},{12,8},{14,10},{1,5},{3,7},... | collective-permute-start | bytes 2752520 | tf_op jit(solution)/shard_map/ppermute | solution.py:628
  130.9 63.9 %collective-permute-start.17 = (bf16[256,2048]{1,0:T(8,128)(2,1)S(1)}, bf16[256,2048]{1,0:T(8,128)(2,1)S(1)}, u32[]{:S(2)}, u32[]{:S(2)}) collective-permute-start(bf16[256,2048]{1,0:T(8,128)(2,1)S(1)} %pad_maximum_fusion.53), channel_id=1, source_target_pairs={{0,4},{2,6},{4,0},{6,2},{8,12},{10,14},{12,8},{14,10},{1,5},{3,7},... | collective-permute-start | bytes 3145736 | tf_op jit(solution)/shard_map/ppermute | solution.py:628
  134.3 61.5 %collective-permute-start.21 = (bf16[256,2048]{1,0:T(8,128)(2,1)S(1)}, bf16[256,2048]{1,0:T(8,128)(2,1)S(1)}, u32[]{:S(2)}, u32[]{:S(2)}) collective-permute-start(bf16[256,2048]{1,0:T(8,128)(2,1)S(1)} %pad_maximum_fusion.54), channel_id=1, source_target_pairs={{0,8},{2,10},{4,12},{6,14},{8,0},{10,2},{12,4},{14,6},{1,9},{3,11}... | collective-permute-start | bytes 3145736 | tf_op jit(solution)/shard_map/ppermute | solution.py:628
  186.5 70.4 %collective-permute-start.14 = (bf16[1024,768]{1,0:T(8,128)(2,1)S(1)}, bf16[1024,768]{1,0:T(8,128)(2,1)}, u32[]{:S(2)}, u32[]{:S(2)}) collective-permute-start(bf16[1024,768]{1,0:T(8,128)(2,1)S(1)} %collective-permute-done.3), channel_id=1, source_target_pairs={{0,16},{16,0},{1,17},{17,1},{2,18},{18,2},{3,19},{19,3},{4,20},{20... | collective-permute-start | bytes 4718600 | tf_op jit(solution)/shard_map/ppermute | solution.py:636
  193.2 69.2 %collective-permute-start.9 = (bf16[4,4,448,128]{3,2,0,1:T(8,128)(2,1)S(1)}, bf16[4,4,448,128]{3,2,0,1:T(8,128)(2,1)S(1)}, u32[]{:S(2)}, u32[]{:S(2)}) collective-permute-start(bf16[4,4,448,128]{3,2,0,1:T(8,128)(2,1)S(1)} %pad_maximum_fusion.33), channel_id=1, source_target_pairs={{0,8},{2,10},{4,12},{6,14},{8,0},{10,2},{12,4},{14,6},{1,9},{3,11}... | collective-permute-start | bytes 5505032 | tf_op jit(solution)/shard_map/ppermute | solution.py:628
  195.7 78.0 %collective-permute-start.18 = (bf16[512,2048]{1,0:T(8,128)(2,1)S(1)}, bf16[512,2048]{1,0:T(8,128)(2,1)S(1)}, u32[]{:S(2)}, u32[]{:S(2)}) collective-permute-start(bf16[512,2048]{1,0:T(8,128)(2,1)S(1)} %pad_maximum_fusion.21), channel_id=1, source_target_pairs={{0,2},{2,0},{4,6},{6,4},{8,10},{10,8},{12,14},{14,12},{1,3},{3,1},... | collective-permute-start | bytes 6291464 | tf_op jit(solution)/shard_map/ppermute | solution.py:628
  196.6 71.9 %collective-permute-start.22 = (bf16[512,2048]{1,0:T(8,128)(2,1)S(1)}, bf16[512,2048]{1,0:T(8,128)(2,1)}, u32[]{:S(2)}, u32[]{:S(2)}) collective-permute-start(bf16[512,2048]{1,0:T(8,128)(2,1)S(1)} %pad_maximum_fusion.22), channel_id=1, source_target_pairs={{0,2},{2,0},{4,6},{6,4},{8,10},{10,8},{12,14},{14,12},{1,3},{3,1},... | collective-permute-start | bytes 6291464 | tf_op jit(solution)/shard_map/ppermute | solution.py:628
  356.5 177.2 %all-gather.7.cloned.1.call-start = ((), (), s32[]{:S(2)}) async-start(), calls=%async_computation.6 | async-start | bytes 5242880 | tf_op jit(solution)/shard_map/all_gather | solution.py:1494
  357.1 54.2 %collective-permute-start.34 = (bf16[36,1024]{1,0:T(8,128)(2,1)S(1)}, bf16[36,1024]{1,0:T(8,128)(2,1)S(1)}, u32[]{:S(2)}, u32[]{:S(2)}) collective-permute-start(bf16[36,1024]{1,0:T(8,128)(2,1)S(1)} %constant_dynamic-update-slice_fusion.5), channel_id=1, source_target_pairs={{0,16},{16,0},{1,17},{17,1},{2,18},{18,2},{3,19},{19,3},{4,20},{20... | collective-permute-start | bytes 221192 | tf_op jit(solution)/shard_map/ppermute | solution.py:636
  374.0 37.9 %collective-permute-start.35 = (bf16[36,1024]{1,0:T(8,128)(2,1)S(1)}, bf16[36,1024]{1,0:T(8,128)(2,1)S(1)}, u32[]{:S(2)}, u32[]{:S(2)}) collective-permute-start(bf16[36,1024]{1,0:T(8,128)(2,1)S(1)} %collective-permute-done.33), channel_id=1, source_target_pairs={{0,16},{16,0},{1,17},{17,1},{2,18},{18,2},{3,19},{19,3},{4,20},{20... | collective-permute-start | bytes 221192 | tf_op jit(solution)/shard_map/ppermute | solution.py:636
  410.3 40.0 %collective-permute-start.29 = (bf16[64,2048]{1,0:T(8,128)(2,1)}, bf16[64,2048]{1,0:T(8,128)(2,1)}, u32[]{:S(2)}, u32[]{:S(2)}) collective-permute-start(bf16[64,2048]{1,0:T(8,128)(2,1)} %fusion.187), channel_id=1, source_target_pairs={{0,1},{1,0},{2,3},{3,2},{4,5},{5,4},{6,7},{7,6},{8,9},{9,8},{10,11... | collective-permute-start | bytes 786440 | tf_op jit(solution)/shard_map/ppermute | solution.py:632
  413.5 225.9 %all-gather.9.cloned.1.call-start = ((), (), s32[]{:S(2)}) async-start(), calls=%async_computation.7 | async-start | bytes 5242880 | tf_op jit(solution)/shard_map/all_gather | solution.py:1495
  476.1 63.6 %collective-permute-start.32 = (bf16[256,2048]{1,0:T(8,128)(2,1)}, bf16[256,2048]{1,0:T(8,128)(2,1)}, u32[]{:S(2)}, u32[]{:S(2)}) collective-permute-start(bf16[256,2048]{1,0:T(8,128)(2,1)} %pad_maximum_fusion.58), channel_id=1, source_target_pairs={{0,2},{2,0},{4,6},{6,4},{8,10},{10,8},{12,14},{14,12},{1,3},{3,1},... | collective-permute-start | bytes 3145736 | tf_op jit(solution)/shard_map/ppermute | solution.py:628
  559.9 125.5 %all-gather.11.cloned.1.call-start = ((), (), s32[]{:S(2)}) async-start(), calls=%async_computation.8 | async-start | bytes 2621440 | tf_op jit(solution)/shard_map/all_gather | solution.py:1498
  614.7 418.3 %reduce-scatter.14.cloned.1.call-start = ((), (), s32[]{:S(2)}) async-start(), calls=%async_computation.13 | async-start | bytes 2621440 | tf_op jit(solution)/shard_map/reduce_scatter | solution.py:1806
  714.8 51.1 %collective-permute-start.67 = (bf16[256,2048]{1,0:T(8,128)(2,1)}, bf16[256,2048]{1,0:T(8,128)(2,1)}, u32[]{:S(2)}, u32[]{:S(2)}) collective-permute-start(bf16[256,2048]{1,0:T(8,128)(2,1)} %constant_dynamic-slice_fusion.25), channel_id=1, source_target_pairs={{0,2},{2,0},{4,6},{6,4},{8,10},{10,8},{12,14},{14,12},{1,3},{3,1},... | collective-permute-start | bytes 3145736 | tf_op jit(solution)/shard_map/ppermute | solution.py:628
  717.2 53.0 %collective-permute-start.60 = (bf16[256,2048]{1,0:T(8,128)(2,1)}, bf16[256,2048]{1,0:T(8,128)(2,1)}, u32[]{:S(2)}, u32[]{:S(2)}) collective-permute-start(bf16[256,2048]{1,0:T(8,128)(2,1)} %constant_dynamic-slice_fusion.26), channel_id=1, source_target_pairs={{0,2},{2,0},{4,6},{6,4},{8,10},{10,8},{12,14},{14,12},{1,3},{3,1},... | collective-permute-start | bytes 3145736 | tf_op jit(solution)/shard_map/ppermute | solution.py:628
  816.8 218.3 %reduce-scatter.8.cloned.1.call-start = ((), (), s32[]{:S(2)}) async-start(), calls=%async_computation.10 | async-start | bytes 327680 | tf_op jit(solution)/shard_map/reduce_scatter | solution.py:1806
  851.8 320.0 %reduce-scatter.12.cloned.1.call-start = ((), (), s32[]{:S(2)}) async-start(), calls=%async_computation.12 | async-start | bytes 5242880 | tf_op jit(solution)/shard_map/reduce_scatter | solution.py:1806
  861.1 595.1 %reduce-scatter.6.cloned.1.call-start = ((), (), s32[]{:S(2)}) async-start(), calls=%async_computation.9 | async-start | bytes 5242880 | tf_op jit(solution)/shard_map/reduce_scatter | solution.py:1806
  959.0 500.9 %reduce-scatter.10.cloned.1.call-start = ((), (), s32[]{:S(2)}) async-start(), calls=%async_computation.11 | async-start | bytes 5242880 | tf_op jit(solution)/shard_map/reduce_scatter | solution.py:1806
  1022.4 65.0 %collective-permute-start.66 = (bf16[2,256,2048]{2,1,0:T(8,128)(2,1)}, bf16[2,256,2048]{2,1,0:T(8,128)(2,1)}, u32[]{:S(2)}, u32[]{:S(2)}) collective-permute-start(bf16[2,256,2048]{2,1,0:T(8,128)(2,1)} %pad_maximum_fusion.25), channel_id=1, source_target_pairs={{0,2},{2,0},{4,6},{6,4},{8,10},{10,8},{12,14},{14,12},{1,3},{3,1},... | collective-permute-start | bytes 6291464 | tf_op jit(solution)/shard_map/ppermute | solution.py:628
  1024.5 65.7 %collective-permute-start.73 = (bf16[2,256,2048]{2,1,0:T(8,128)(2,1)}, bf16[2,256,2048]{2,1,0:T(8,128)(2,1)}, u32[]{:S(2)}, u32[]{:S(2)}) collective-permute-start(bf16[2,256,2048]{2,1,0:T(8,128)(2,1)} %pad_maximum_fusion.26), channel_id=1, source_target_pairs={{0,2},{2,0},{4,6},{6,4},{8,10},{10,8},{12,14},{14,12},{1,3},{3,1},... | collective-permute-start | bytes 6291464 | tf_op jit(solution)/shard_map/ppermute | solution.py:628
  1071.1 38.4 %collective-permute-start.85 = (bf16[64,2048]{1,0:T(8,128)(2,1)S(1)}, bf16[64,2048]{1,0:T(8,128)(2,1)S(1)}, u32[]{:S(2)}, u32[]{:S(2)}) collective-permute-start(bf16[64,2048]{1,0:T(8,128)(2,1)S(1)} %get-tuple-element.299), channel_id=1, source_target_pairs={{0,1},{1,0},{2,3},{3,2},{4,5},{5,4},{6,7},{7,6},{8,9},{9,8},{10,11... | collective-permute-start | bytes 786440 | tf_op jit(solution)/shard_map/ppermute | solution.py:632
  1071.5 38.7 %collective-permute-start.98 = (bf16[64,2048]{1,0:T(8,128)(2,1)S(1)}, bf16[64,2048]{1,0:T(8,128)(2,1)S(1)}, u32[]{:S(2)}, u32[]{:S(2)}) collective-permute-start(bf16[64,2048]{1,0:T(8,128)(2,1)S(1)} %get-tuple-element.658), channel_id=1, source_target_pairs={{0,1},{1,0},{2,3},{3,2},{4,5},{5,4},{6,7},{7,6},{8,9},{9,8},{10,11... | collective-permute-start | bytes 786440 | tf_op jit(solution)/shard_map/ppermute | solution.py:632
  1260.2 191.0 %collective-permute-start.127 = (bf16[1024,768]{0,1:T(8,128)(2,1)}, bf16[1024,768]{0,1:T(8,128)(2,1)}, u32[]{:S(2)}, u32[]{:S(2)}) collective-permute-start(bf16[1024,768]{0,1:T(8,128)(2,1)} %add_convert_fusion.4), channel_id=1, source_target_pairs={{0,16},{16,0},{1,17},{17,1},{2,18},{18,2},{3,19},{19,3},{4,20},{20... | collective-permute-start | bytes 4718600 | tf_op jit(solution)/shard_map/ppermute | solution.py:636
  1268.8 171.3 %collective-permute-start.128 = (bf16[1024,768]{0,1:T(8,128)(2,1)}, bf16[1024,768]{0,1:T(8,128)(2,1)}, u32[]{:S(2)}, u32[]{:S(2)}) collective-permute-start(bf16[1024,768]{0,1:T(8,128)(2,1)} %add_convert_fusion.3), channel_id=1, source_target_pairs={{0,16},{16,0},{1,17},{17,1},{2,18},{18,2},{3,19},{19,3},{4,20},{20... | collective-permute-start | bytes 4718600 | tf_op jit(solution)/shard_map/ppermute | solution.py:636
  1268.9 152.9 %collective-permute-start.142 = (f32[64,768]{1,0:T(8,128)S(1)}, f32[64,768]{1,0:T(8,128)S(1)}, u32[]{:S(2)}, u32[]{:S(2)}) collective-permute-start(f32[64,768]{1,0:T(8,128)S(1)} %constant_dynamic-slice_fusion.11), channel_id=1, source_target_pairs={{0,16},{16,0},{1,17},{17,1},{2,18},{18,2},{3,19},{19,3},{4,20},{20... | collective-permute-start | bytes 589832 | tf_op jit(solution)/shard_map/ppermute | solution.py:636
  1274.1 164.7 %collective-permute-start.144 = (bf16[256,1024]{1,0:T(8,128)(2,1)}, bf16[256,1024]{1,0:T(8,128)(2,1)}, u32[]{:S(2)}, u32[]{:S(2)}) collective-permute-start(bf16[256,1024]{1,0:T(8,128)(2,1)} %constant_dynamic-slice_fusion.9), channel_id=1, source_target_pairs={{0,16},{16,0},{1,17},{17,1},{2,18},{18,2},{3,19},{19,3},{4,20},{20... | collective-permute-start | bytes 1572872 | tf_op jit(solution)/shard_map/ppermute | solution.py:636
  1293.7 194.0 %collective-permute-start.102 = (bf16[2,256,4480]{2,1,0:T(8,128)(2,1)}, bf16[2,256,4480]{2,1,0:T(8,128)(2,1)}, u32[]{:S(2)}, u32[]{:S(2)}) collective-permute-start(bf16[2,256,4480]{2,1,0:T(8,128)(2,1)} %constant_dynamic-slice_fusion.18), channel_id=1, source_target_pairs={{0,2},{2,0},{4,6},{6,4},{8,10},{10,8},{12,14},{14,12},{1,3},{3,1},... | collective-permute-start | bytes 13762568 | tf_op jit(solution)/shard_map/ppermute | solution.py:628
  1434.9 62.5 %collective-permute-start.109 = (bf16[2,256,4480]{2,1,0:T(8,128)(2,1)}, bf16[2,256,4480]{2,1,0:T(8,128)(2,1)}, u32[]{:S(2)}, u32[]{:S(2)}) collective-permute-start(bf16[2,256,4480]{2,1,0:T(8,128)(2,1)} %constant_dynamic-slice_fusion.14), channel_id=1, source_target_pairs={{0,2},{2,0},{4,6},{6,4},{8,10},{10,8},{12,14},{14,12},{1,3},{3,1},... | collective-permute-start | bytes 13762568 | tf_op jit(solution)/shard_map/ppermute | solution.py:628
  1444.7 38.0 %collective-permute-start.129 = (bf16[1024,768]{0,1:T(8,128)(2,1)}, bf16[1024,768]{0,1:T(8,128)(2,1)}, u32[]{:S(2)}, u32[]{:S(2)}) collective-permute-start(bf16[1024,768]{0,1:T(8,128)(2,1)} %add_convert_fusion.2), channel_id=1, source_target_pairs={{0,1},{1,0},{2,3},{3,2},{4,5},{5,4},{6,7},{7,6},{8,9},{9,8},{10,11... | collective-permute-start | bytes 4718600 | tf_op jit(solution)/shard_map/ppermute | solution.py:632
  1494.9 51.8 %collective-permute-start.103 = (bf16[2,128,4480]{2,1,0:T(8,128)(2,1)}, bf16[2,128,4480]{2,1,0:T(8,128)(2,1)}, u32[]{:S(2)}, u32[]{:S(2)}) collective-permute-start(bf16[2,128,4480]{2,1,0:T(8,128)(2,1)} %dynamic-slice_convert_fusion.1), channel_id=1, source_target_pairs={{0,4},{2,6},{4,0},{6,2},{8,12},{10,14},{12,8},{14,10},{1,5},{3,7},... | collective-permute-start | bytes 6881288 | tf_op jit(solution)/shard_map/ppermute | solution.py:628
  1505.8 53.1 %collective-permute-start.110 = (bf16[2,128,4480]{2,1,0:T(8,128)(2,1)}, bf16[2,128,4480]{2,1,0:T(8,128)(2,1)}, u32[]{:S(2)}, u32[]{:S(2)}) collective-permute-start(bf16[2,128,4480]{2,1,0:T(8,128)(2,1)} %dynamic-slice_convert_fusion), channel_id=1, source_target_pairs={{0,8},{2,10},{4,12},{6,14},{8,0},{10,2},{12,4},{14,6},{1,9},{3,11}... | collective-permute-start | bytes 6881288 | tf_op jit(solution)/shard_map/ppermute | solution.py:628
  1618.3 37.9 %collective-permute-start.106 = (bf16[64,2048]{1,0:T(8,128)(2,1)S(1)}, bf16[64,2048]{1,0:T(8,128)(2,1)S(1)}, u32[]{:S(2)}, u32[]{:S(2)}) collective-permute-start(bf16[64,2048]{1,0:T(8,128)(2,1)S(1)} %fusion.161), channel_id=1, source_target_pairs={{0,8},{2,10},{4,12},{6,14},{8,0},{10,2},{12,4},{14,6},{1,9},{3,11}... | collective-permute-start | bytes 786440 | tf_op jit(solution)/shard_map/ppermute | solution.py:628
  1671.3 65.4 %collective-permute-start.118 = (bf16[256,2048]{1,0:T(8,128)(2,1)}, bf16[256,2048]{1,0:T(8,128)(2,1)}, u32[]{:S(2)}, u32[]{:S(2)}) collective-permute-start(bf16[256,2048]{1,0:T(8,128)(2,1)} %pad_maximum_fusion.72), channel_id=1, source_target_pairs={{0,2},{2,0},{4,6},{6,4},{8,10},{10,8},{12,14},{14,12},{1,3},{3,1},... | collective-permute-start | bytes 3145736 | tf_op jit(solution)/shard_map/ppermute | solution.py:628
  1672.8 65.6 %collective-permute-start.121 = (bf16[256,2048]{1,0:T(8,128)(2,1)}, bf16[256,2048]{1,0:T(8,128)(2,1)}, u32[]{:S(2)}, u32[]{:S(2)}) collective-permute-start(bf16[256,2048]{1,0:T(8,128)(2,1)} %pad_maximum_fusion.73), channel_id=1, source_target_pairs={{0,2},{2,0},{4,6},{6,4},{8,10},{10,8},{12,14},{14,12},{1,3},{3,1},... | collective-permute-start | bytes 3145736 | tf_op jit(solution)/shard_map/ppermute | solution.py:628
  1680.5 61.9 %collective-permute-start.108 = (bf16[256,2048]{1,0:T(8,128)(2,1)}, bf16[256,2048]{1,0:T(8,128)(2,1)}, u32[]{:S(2)}, u32[]{:S(2)}) collective-permute-start(bf16[256,2048]{1,0:T(8,128)(2,1)} %pad_maximum_fusion.70), channel_id=1, source_target_pairs={{0,2},{2,0},{4,6},{6,4},{8,10},{10,8},{12,14},{14,12},{1,3},{3,1},... | collective-permute-start | bytes 3145736 | tf_op jit(solution)/shard_map/ppermute | solution.py:628
  1696.4 47.9 %collective-permute-start.115 = (bf16[256,2048]{1,0:T(8,128)(2,1)}, bf16[256,2048]{1,0:T(8,128)(2,1)}, u32[]{:S(2)}, u32[]{:S(2)}) collective-permute-start(bf16[256,2048]{1,0:T(8,128)(2,1)} %pad_maximum_fusion.71), channel_id=1, source_target_pairs={{0,2},{2,0},{4,6},{6,4},{8,10},{10,8},{12,14},{14,12},{1,3},{3,1},... | collective-permute-start | bytes 3145736 | tf_op jit(solution)/shard_map/ppermute | solution.py:628
  (486 other events, 6718.8 us)
Sparse Core Ops, SparseCore 0:
  356.7 94.4 all-gather.4
  452.7 80.9 all-gather.6
  560.0 79.3 all-gather.8
  640.8 44.4 all-gather.10
  816.9 51.9 reduce-scatter.13
  871.2 18.9 reduce-scatter.7
  892.5 86.1 reduce-scatter.11
  981.0 81.3 reduce-scatter.5
  1064.7 89.4 reduce-scatter.9

commit v3 on v2

--- a/solution.py
+++ b/solution.py
@@ -808,11 +808,20 @@
     lse_ref[...] = lse.T[0:1, :][None]
 
 
+def half_block(index, blocks):
+    per_state = blocks // 2
+    per_half = per_state // 2
+    inside = index % per_state
+    return inside // per_half * per_state + index // per_state * per_half + inside % per_half
+
+
 def attend(queries, keys, values, segment, lows):
     length, columns = queries.shape
     heads = columns // HDIM
+    blocks = length // ROWS_Q
     whole = pl.BlockSpec((length, HDIM), lambda h, i, *_: (0, h))
     block = pl.BlockSpec((ROWS_Q, HDIM), lambda h, i, *_: (i, h))
+    placed = pl.BlockSpec((ROWS_Q, HDIM), lambda h, i, *_: (half_block(i, blocks), h))
     return pl.pallas_call(
         attend_kernel,
         grid_spec=pltpu.PrefetchScalarGridSpec(
@@ -825,7 +834,7 @@
                 pl.BlockSpec((ROWS_Q, 1), lambda h, i, *_: (i, 0)),
                 pl.BlockSpec((1, length), lambda h, i, *_: (0, 0)),
             ],
-            out_specs=[block, pl.BlockSpec((1, 1, ROWS_Q), lambda h, i, *_: (h, 0, i))],
+            out_specs=[placed, pl.BlockSpec((1, 1, ROWS_Q), lambda h, i, *_: (h, 0, i))],
         ),
         out_shape=[
             jax.ShapeDtypeStruct((length, columns), low),
@@ -840,7 +849,7 @@
 
 
 def attend_back_kernel(
-    low_ref, q_ref, k_ref, v_ref, do_ref, lse_ref, delta_ref, seg_col, seg_row, dq_ref, dk_ref, dv_ref
+    low_ref, q_ref, k_ref, v_ref, do_ref, o_ref, lse_ref, seg_col, seg_row, dq_ref, dk_ref, dv_ref
 ):
     index = pl.program_id(1)
     scale = q_ref.shape[1] ** (-0.5)
@@ -848,7 +857,14 @@
     grad = do_ref[...]
     own = seg_row[...]
     lse = lse_ref[0]
-    delta = delta_ref[0]
+    ones = jnp.ones((8, HDIM), full)
+    delta = lax.dot_general(
+        ones,
+        grad.astype(full) * o_ref[...].astype(full),
+        (((1,), (1,)), ((), ())),
+        precision=highest,
+        preferred_element_type=full,
+    )[0:1, :]
     place = index * ROWS_Q + lax.broadcasted_iota(jnp.int32, (ROWS_K, ROWS_Q), 1)
 
     @pl.when(index == 0)
@@ -874,11 +890,13 @@
     dq_ref[...] = total * scale
 
 
-def attend_back(queries, keys, values, grads, lse, delta, segment, lows):
+def attend_back(queries, keys, values, grads, outs, lse, segment, lows):
     length, columns = queries.shape
     heads = columns // HDIM
+    blocks = length // ROWS_Q
     whole = pl.BlockSpec((length, HDIM), lambda h, i, *_: (0, h))
     block = pl.BlockSpec((ROWS_Q, HDIM), lambda h, i, *_: (i, h))
+    placed = pl.BlockSpec((ROWS_Q, HDIM), lambda h, i, *_: (half_block(i, blocks), h))
     line = pl.BlockSpec((1, 1, ROWS_Q), lambda h, i, *_: (h, 0, i))
     shape = jax.ShapeDtypeStruct((length, columns), full)
     return pl.pallas_call(
@@ -890,8 +908,8 @@
                 block,
                 whole,
                 whole,
-                block,
-                line,
+                placed,
+                placed,
                 line,
                 pl.BlockSpec((length, 1), lambda h, i, *_: (0, 0)),
                 pl.BlockSpec((1, ROWS_Q), lambda h, i, *_: (0, i)),
@@ -904,7 +922,88 @@
             flops=5 * length * length * columns, bytes_accessed=20 * length * columns,
             transcendentals=length * length * heads // 2,
         ),
-    )(lows, queries, keys, values, grads, lse, delta, segment[:, None], segment[None, :])
+    )(lows, queries, keys, values, grads, outs, lse, segment[:, None], segment[None, :])
+
+
+def rope_kernel(state_ref, own_ref, other_ref, cos_ref, sin_ref, q_ref, k_ref, v_ref):
+    per_state = pl.num_programs(0) // 2
+    own = pl.program_id(0) // per_state == state_ref[0]
+    columns = q_ref.shape[1]
+    for index, out in enumerate((q_ref, k_ref, v_ref)):
+        for start in range(0, columns, HDIM):
+            lanes = slice(index * columns + start, index * columns + start + HDIM)
+            value = jnp.where(own, own_ref[:, lanes], other_ref[:, lanes])
+            if index < 2:
+                value = value * cos_ref[...] + pltpu.roll(value, HDIM // 2, 1) * sin_ref[...]
+            out[:, start : start + HDIM] = value.astype(low)
+
+
+def rope(state, own, other, cosine, sine):
+    length = cosine.shape[0]
+    columns = own.shape[1] // 3
+    per_state = length // ROWS_Q // 2
+    part = pl.BlockSpec((ROWS_Q, own.shape[1]), lambda i, *_: (i % per_state, 0))
+    angle = pl.BlockSpec((ROWS_Q, HDIM), lambda i, *_: (i, 0))
+    out = pl.BlockSpec((ROWS_Q, columns), lambda i, *_: (i, 0))
+    return pl.pallas_call(
+        rope_kernel,
+        grid_spec=pltpu.PrefetchScalarGridSpec(
+            num_scalar_prefetch=1,
+            grid=(length // ROWS_Q,),
+            in_specs=[part, part, angle, angle],
+            out_specs=[out] * 3,
+        ),
+        out_shape=[jax.ShapeDtypeStruct((length, columns), low)] * 3,
+        compiler_params=vmem_limit(32),
+        cost_estimate=pl.CostEstimate(
+            flops=12 * length * columns, bytes_accessed=36 * length * columns, transcendentals=0
+        ),
+    )(state[None], own, other, cosine, sine)
+
+
+def rope_back_kernel(q_ref, k_ref, v_ref, cos_ref, sin_ref, out_ref):
+    columns = q_ref.shape[1]
+    for index, part in enumerate((q_ref, k_ref, v_ref)):
+        for start in range(0, columns, HDIM):
+            value = part[:, start : start + HDIM]
+            if index < 2:
+                value = value * cos_ref[...] - pltpu.roll(value, HDIM // 2, 1) * sin_ref[...]
+            lanes = slice(index * columns + start, index * columns + start + HDIM)
+            out_ref[:, lanes] = value.astype(low)
+
+
+def rope_back(query, key, value, cosine, sine):
+    length, columns = query.shape
+    blocks = length // ROWS_Q
+    part = pl.BlockSpec((ROWS_Q, columns), lambda i: (i, 0))
+    angle = pl.BlockSpec((ROWS_Q, HDIM), lambda i: (i, 0))
+    return pl.pallas_call(
+        rope_back_kernel,
+        grid=(blocks,),
+        in_specs=[part, part, part, angle, angle],
+        out_specs=pl.BlockSpec((ROWS_Q, 3 * columns), lambda i: (half_block(i, blocks), 0)),
+        out_shape=jax.ShapeDtypeStruct((length, 3 * columns), low),
+        compiler_params=vmem_limit(32),
+        cost_estimate=pl.CostEstimate(
+            flops=12 * length * columns, bytes_accessed=24 * length * columns, transcendentals=0
+        ),
+    )(query, key, value, cosine, sine)
+
+
+def hold_kernel(*refs):
+    pass
+
+
+def hold(value, *after):
+    anywhere = pl.BlockSpec(memory_space=pl.ANY)
+    return pl.pallas_call(
+        hold_kernel,
+        in_specs=[anywhere] * (1 + len(after)),
+        out_specs=anywhere,
+        out_shape=jax.ShapeDtypeStruct(value.shape, value.dtype),
+        input_output_aliases={0: 0},
+        cost_estimate=pl.CostEstimate(flops=0, bytes_accessed=0, transcendentals=0),
+    )(value, *after)
 
 
 def first_blocks(segment):
@@ -1276,39 +1375,10 @@
     ]
 
 
-def z_pieces(value):
-    beside = state_swap(value)
-    return [value, beside, dp_swap(value), dp_swap(beside)]
-
-
 def swap_quarters(value):
     quarter = value.shape[-1] // 4
     part = [value[..., i * quarter : (i + 1) * quarter] for i in range(4)]
     return jnp.concatenate([part[1], part[0], part[3], part[2]], -1)
-
-
-def add_everywhere(value):
-    for mask in head_masks()[0]:
-        value = value + head_swap(value, mask)
-    return add_zed(value)
-
-
-def add_zed(value):
-    value = value + state_swap(value)
-    return value + dp_swap(value)
-
-
-def by_state(own, other):
-    state = lax.axis_index(STATE)
-    return jnp.concatenate([jnp.where(state == 0, own, other), jnp.where(state == 0, other, own)], 0)
-
-
-def turn(value, cosine, sine):
-    rows = value.shape[0]
-    cubes = value.reshape(rows, -1, HDIM)
-    half = HDIM // 2
-    swapped = jnp.concatenate([cubes[..., half:], cubes[..., :half]], -1)
-    return (cubes * cosine[:, None, :] + swapped * sine[:, None, :]).reshape(value.shape)
 
 
 def fast_device(
@@ -1369,50 +1439,50 @@
             [lax.dynamic_slice_in_dim(v, index * half_cols, half_cols, 1) for v in values], 1
         )
 
-    main_pieces = z_pieces_columns(
-        state_columns((w_query, w_key, w_value), state),
-        state_columns((w_query, w_key, w_value), 1 - state),
-    )
-    main_near = jnp.concatenate(main_pieces[:2], 0)
-    main_far = jnp.concatenate(main_pieces[2:], 0)
-    up_pieces = z_pieces_columns(
-        state_columns((up_query, up_key, up_value), state),
-        state_columns((up_query, up_key, up_value), 1 - state),
-    )
-    ups = jnp.concatenate(natural_quarters(up_pieces), 0)
+    mine = state_columns((w_query, w_key, w_value), state)
+    got = state_swap(state_columns((w_query, w_key, w_value), 1 - state))
+    cutting = mine.shape[0] // 2
+    far_mine = [dp_swap(mine[:cutting]), dp_swap(mine[cutting:])]
+    far_got = [dp_swap(got[:cutting]), dp_swap(got[cutting:])]
+
     rank = down_query.shape[1]
+    part_a = down_query.shape[0] // head_parts
+    part_m = down_mlp.shape[0] // head_parts
+    split_a, split_m = gain_attn.shape[0], gain_mlp.shape[0]
+    up_rows = up_query.shape[0]
+
+    def small_pack(index):
+        return jnp.concatenate(
+            [
+                jnp.concatenate([gain_attn, gain_mlp, gain_mixer]).reshape(-1, rank),
+                lax.dynamic_slice_in_dim(down_query, head * part_a, part_a, 0),
+                lax.dynamic_slice_in_dim(down_key, head * part_a, part_a, 0),
+                lax.dynamic_slice_in_dim(down_value, head * part_a, part_a, 0),
+                lax.dynamic_slice_in_dim(down_mlp, head * part_m, part_m, 0),
+                state_columns((up_query, up_key, up_value), index).reshape(-1, rank),
+            ],
+            0,
+        )
+
+    pack = jnp.stack([small_pack(state), state_swap(small_pack(1 - state))], 0)
+    pack = jnp.concatenate([pack, dp_swap(pack)], 0)
+    gain_rows = (split_a + 2 * split_m) // rank
+    gains = pack[:, :gain_rows].reshape(4, -1).astype(full)
+    attn_gain = gains[:, :split_a].reshape(-1)
+    gains = natural_quarters([gains[index] for index in range(4)])
+    mlp_gain = jnp.concatenate([value[split_a : split_a + split_m] for value in gains])
+    mixer_gain = jnp.concatenate([value[split_a + split_m :] for value in gains])
+    down_end = gain_rows + 3 * part_a + part_m
+    ups = natural_quarters(
+        [pack[index, down_end:].reshape(up_rows, 3 * half_cols) for index in range(4)]
+    )
+    ups = jnp.concatenate(ups, 0)
     column = lax.broadcasted_iota(jnp.int32, (1, 3 * half_cols), 1) // half_cols
     up_wide = jnp.concatenate(
         [jnp.where(column == index, ups, jnp.zeros_like(ups)) for index in range(3)], 0
     )
-
-    split_a, split_m = gain_attn.shape[0], gain_mlp.shape[0]
-    gains = z_pieces(jnp.concatenate([gain_attn, gain_mlp, gain_mixer]).reshape(-1, 128))
-    gains = [value.reshape(-1).astype(full) for value in gains]
-    attn_gain = jnp.concatenate([value[:split_a] for value in gains])
-    gains = natural_quarters(gains)
-    mlp_gain = jnp.concatenate([value[split_a : split_a + split_m] for value in gains])
-    mixer_gain = jnp.concatenate([value[split_a + split_m :] for value in gains])
-    up_rows = up_mlp.shape[0]
-    step_width = proj_step.shape[1]
-    small = jnp.concatenate([up_mlp, proj_step.reshape(-1, up_mlp.shape[1])], 0)
-    small = natural_quarters(z_pieces(small))
-    mlp_upper = jnp.concatenate([value[:up_rows] for value in small], 0)
-    step_main = jnp.concatenate([value[up_rows:].reshape(-1, step_width) for value in small], 0)
-
-    part_a = down_query.shape[0] // head_parts
-    part_m = down_mlp.shape[0] // head_parts
-    downs = jnp.concatenate(
-        [
-            lax.dynamic_slice_in_dim(down_query, head * part_a, part_a, 0),
-            lax.dynamic_slice_in_dim(down_key, head * part_a, part_a, 0),
-            lax.dynamic_slice_in_dim(down_value, head * part_a, part_a, 0),
-            lax.dynamic_slice_in_dim(down_mlp, head * part_m, part_m, 0),
-        ],
-        0,
-    )
     masks = orders[0][::-1]
-    downs_all = gather_rows(jnp.stack(z_pieces(downs), 0)[None], masks, 0)
+    downs_all = gather_rows(pack[None, :, gain_rows:down_end], masks, 0)
 
     def down_of(lower, part):
         return downs_all[:, :, lower : lower + part].transpose(1, 0, 2, 3)
@@ -1454,14 +1524,22 @@
     near_own, far_own = normed_own[:, :width], normed_own[:, width:]
     joined_cut = [quarters(a, b) for a, b in zip(cut(hidden), cut(embedding))]
 
-    def other_rows(value, order):
-        share = rows // head_parts
+    share = rows // head_parts
+
+    def sent_rows(value, order):
         sent = lax.dynamic_slice_in_dim(value, chunk_of(order) * share, share, 0)
-        sent = jnp.concatenate([sent[:, quarter:], sent[:, :quarter]], 1)
-        return gather_rows(state_swap(sent), order, 0)
-
-    near_other = other_rows(near_own, orders[0])
-    far_other = other_rows(far_own, orders[1])
+        return jnp.concatenate([sent[:, quarter:], sent[:, :quarter]], 1)
+
+    sent = jnp.stack([sent_rows(near_own, orders[0]), sent_rows(far_own, orders[1])], 0)
+    sent = state_swap(hold(sent, far_mine[0]))
+    sent = hold(sent, far_mine[1])
+    near_other = gather_rows(sent[0], orders[0][1:], 0)
+    far_other = gather_rows(sent[1], orders[1][1:], 0)
+    near_other = hold(near_other, far_got[0])
+    near_other = gather_rows(near_other, orders[0][:1], 0)
+    far_other = gather_rows(far_other, orders[1][:1], 0)
+    main_near = jnp.concatenate([mine, got], 0)
+    main_far = jnp.concatenate(far_mine + far_got, 0)
 
     def project(near, far):
         reduced = (plain_dot(near, down_wide[:width]) + plain_dot(far, down_wide[width:])).astype(low)
@@ -1470,43 +1548,42 @@
 
     pre_own, red_own = project(near_own, far_own)
     pre_other, red_other = project(near_other, far_other)
-    pre = by_state(pre_own, pre_other)
-    queries = turn(pre[:, :half_cols], cosine, sine).astype(low)
-    keys = turn(pre[:, half_cols : 2 * half_cols], cosine, sine).astype(low)
-    values = pre[:, 2 * half_cols :].astype(low)
-
-    (
-        mlp_input,
-        mlp_output,
-        proj_inner,
-        proj_gate,
-        proj_output,
-        main_far,
-    ) = lax.optimization_barrier(
-        (mlp_input, mlp_output, proj_inner, proj_gate, proj_output, main_far)
-    )
-    attn_pieces = z_pieces_columns(
-        lax.dynamic_slice_in_dim(attn_output, state * half_cols, half_cols, 0),
-        lax.dynamic_slice_in_dim(attn_output, (1 - state) * half_cols, half_cols, 0),
-    )
-    attn_proj = jnp.concatenate(natural_quarters(attn_pieces), 1)
-    mlp_main = lax.all_gather(mlp_input, ZED, axis=0, tiled=True)
+    queries, keys, values = rope(state, pre_own, pre_other, cosine, sine)
+
+    attn_mine = lax.dynamic_slice_in_dim(attn_output, state * half_cols, half_cols, 0)
+    attn_got = state_swap(
+        lax.dynamic_slice_in_dim(attn_output, (1 - state) * half_cols, half_cols, 0)
+    )
+    attn_pair = jnp.stack([attn_mine, attn_got], 0)
+    attn_far = dp_swap(attn_pair)
+    attn_proj = jnp.concatenate(
+        natural_quarters([attn_pair[0], attn_pair[1], attn_far[0], attn_far[1]]), 1
+    )
+    mlp_cut = mlp_input.shape[1] // 2
+    mlp_input = hold(mlp_input, far_got[1])
+    mlp_first = lax.all_gather(mlp_input[:, :mlp_cut], ZED, axis=0, tiled=True)
+    mlp_second = lax.all_gather(mlp_input[:, mlp_cut:], ZED, axis=0, tiled=True)
+    mlp_main = jnp.concatenate([mlp_first, mlp_second], 1)
     mlp_proj = lax.all_gather(mlp_output, ZED, axis=1, tiled=True)
     mixer_main = lax.all_gather(
         jnp.concatenate([proj_inner, proj_gate], 1), ZED, axis=0, tiled=True
     )
     output_main = lax.all_gather(proj_output, ZED, axis=1, tiled=True)
+    step_width = proj_step.shape[1]
+    small = jnp.concatenate([up_mlp, proj_step.reshape(-1, up_mlp.shape[1])], 0)
+    small = hold(small, far_got[1])
+    small = jnp.stack([small, state_swap(small)], 0)
+    small_far = dp_swap(small)
+    small = natural_quarters([small[0], small[1], small_far[0], small_far[1]])
+    mlp_upper = jnp.concatenate([value[: up_mlp.shape[0]] for value in small], 0)
+    step_main = jnp.concatenate(
+        [value[up_mlp.shape[0] :].reshape(-1, step_width) for value in small], 0
+    )
 
     attended, lse = attend(queries, keys, values, segment, lows)
 
-    def state_halves(value):
-        cubes = value.reshape(2, 2, middle, value.shape[1])
-        return [cubes[:, 0].reshape(rows, -1), cubes[:, 1].reshape(rows, -1)]
-
-    def from_halves(pair):
-        return jnp.stack([p.reshape(2, middle, -1) for p in pair], 1).reshape(length, -1)
-
-    attended_halves = state_halves(attended)
+    attended = hold(attended, mlp_first)
+    attended_halves = [attended[:rows], attended[rows:]]
     branch_cut = [
         sum_row16(plain_dot(part, attn_proj).astype(low).reshape(2, middle, width), order)
         for part, order in zip(attended_halves, orders)
@@ -1635,7 +1712,20 @@
     edge_back = state_backward(edge_grad)
     inner_grad = inner_grad.at[rows - reach :].add(edge_back[:, :inner_width])
     small_grad = small_grad.at[rows - reach :, mixer_heads:].add(edge_back[:, inner_width:])
+    out_cut = [
+        (
+            value
+            + good
+            * sum_rows(
+                plain_dot(gated[index * middle : (index + 1) * middle], output_main).astype(low),
+                order,
+                0,
+            )
+        ).astype(low)
+        for index, (value, good, order) in enumerate(zip(second_cut, valid_cut, orders))
+    ]
     inner_low = jnp.concatenate([inner_grad, gate_grad], 1).astype(low)
+    inner_low = hold(inner_low, *out_cut)
     small_low = small_grad.astype(low)
     mixer_sum = [
         sum_rows(
@@ -1682,79 +1772,64 @@
         for good, grad, order in zip(valid_cut, first_grad, orders)
     ]
 
-    attended_grad = from_halves([right_dot(value, attn_proj).astype(low) for value in branch_halves])
-    delta = jnp.sum(
-        (attended_grad.astype(full) * attended.astype(full)).reshape(length, -1, HDIM), -1
-    ).T[:, None, :]
+    layer_halves = [gather_row16(value, order) for value, order in zip(out_cut, orders)]
+    layer_out = jnp.stack(layer_halves, 1).reshape(length, width)
+    attended_grad = jnp.concatenate(
+        [right_dot(value, attn_proj).astype(low) for value in branch_halves], 0
+    )
     query_back, key_back, value_back = attend_back(
-        queries, keys, values, attended_grad, lse, delta, segment, lows
-    )
-    pre_grad = jnp.concatenate(
-        [
-            turn(query_back, cosine, -sine).astype(low),
-            turn(key_back, cosine, -sine).astype(low),
-            value_back.astype(low),
-        ],
-        1,
-    )
+        queries, keys, values, attended_grad, attended, lse, segment, lows
+    )
+    attn_grad = left_dot(attended_halves[0], branch_halves[0]) + left_dot(
+        attended_halves[1], branch_halves[1]
+    )
+    out_attn = grad_pieces(attn_grad.astype(low), 0)
+    pre_grad = rope_back(query_back, key_back, value_back, cosine, sine)
+    pre_grad = hold(pre_grad, *layer_halves, out_attn)
     main_wide = jnp.concatenate([main_near, main_far, up_wide], 0)
     joint = 2 * width
     normed_sums = []
-    for part, order in zip(state_halves(pre_grad), orders):
+    for part, order in zip((pre_grad[:rows], pre_grad[rows:]), orders):
         total = right_dot(part, main_wide).astype(low).reshape(2, middle, -1)
         total = sum_rows(total, order, 1)
         away = lax.dynamic_index_in_dim(total, 1 - state, 0, False).astype(low)
         away = jnp.concatenate([swap_quarters(away[:, :joint]), away[:, joint:]], 1)
         kept = lax.dynamic_index_in_dim(total, state, 0, False)
         normed_sums.append(kept + state_swap(away).astype(full))
-    grad_own = lax.dynamic_slice_in_dim(pre_grad, own_start, rows, 0)
-    grad_other = lax.dynamic_slice_in_dim(pre_grad, rows - own_start, rows, 0)
-
-    def main_grad(own, other, lower):
-        part = slice(lower * quarter, (lower + 1) * quarter)
-        return left_dot(own[:, part], grad_own) + left_dot(other[:, part], grad_other)
-
-    beside = main_grad(near_own, near_other, 1) + dp_swap(
-        main_grad(far_own, far_other, 1).astype(low)
-    ).astype(full)
-    beside = state_swap(beside.astype(low)).astype(full)
-    main_total = main_grad(near_own, near_other, 0) + dp_swap(
-        main_grad(far_own, far_other, 0).astype(low)
-    ).astype(full)
-
-    def spread(own, got, index):
-        part = slice(index * half_cols, (index + 1) * half_cols)
-        own, got = own[:, part], got[:, part]
-        return jnp.concatenate(
-            [jnp.where(state == 0, own, got), jnp.where(state == 0, got, own)], 1
-        )
-
-    out_main = [spread(main_total, beside, index) for index in range(3)]
-    red_all = by_state(red_own, red_other)
+    cubes = pre_grad.reshape(2, 2, middle, -1)
+    grad_own, grad_other = (
+        lax.dynamic_index_in_dim(cubes, index, 1, False).reshape(rows, -1)
+        for index in (state, 1 - state)
+    )
+    wide_grad = left_dot(red_own, grad_own) + left_dot(red_other, grad_other)
     up_grad = jnp.concatenate(
         [
-            left_dot(
-                red_all[:, index * rank : (index + 1) * rank],
-                pre_grad[:, index * half_cols : (index + 1) * half_cols],
-            )
+            wide_grad[index * rank : (index + 1) * rank, index * half_cols : (index + 1) * half_cols]
             for index in range(3)
         ],
         1,
     )
-    rank_half = rank // 2
-    up_sum = lax.dynamic_slice_in_dim(up_grad, dp * rank_half, rank_half, 0) + dp_swap(
-        lax.dynamic_slice_in_dim(up_grad, (1 - dp) * rank_half, rank_half, 0)
-    )
-    rank_quarter = rank_half // 2
-    up_kept = lax.dynamic_slice_in_dim(up_sum, state * rank_quarter, rank_quarter, 0)
-    up_got = state_swap(
-        lax.dynamic_slice_in_dim(up_sum, (1 - state) * rank_quarter, rank_quarter, 0)
-    )
-    out_up = [spread(up_kept, up_got, index) for index in range(3)]
-    attn_grad = left_dot(attended_halves[0], branch_halves[0]) + left_dot(
-        attended_halves[1], branch_halves[1]
-    )
-    out_attn = grad_pieces(attn_grad.astype(low), 0)
+
+    def main_grad(own, other, lower, index):
+        part = slice(lower * quarter, (lower + 1) * quarter)
+        main = left_dot(own[:, part], grad_own) + left_dot(other[:, part], grad_other)
+        ups = lax.dynamic_slice_in_dim(up_grad, (place ^ index) * up_rows, up_rows, 0)
+        return jnp.concatenate([main, ups], 0).astype(low)
+
+    def by_dp(near, far):
+        both = jnp.concatenate([jnp.where(dp == 0, near, far), jnp.where(dp == 0, far, near)], 0)
+        return lax.psum_scatter(both, DP, scatter_dimension=0, tiled=True)
+
+    beside = by_dp(main_grad(near_own, near_other, 1, 1), main_grad(far_own, far_other, 1, 3))
+    main_total = by_dp(main_grad(near_own, near_other, 0, 0), main_grad(far_own, far_other, 0, 2))
+    beside_got = state_swap(beside)
+
+    def spread(own, got, index):
+        part = slice(index * half_cols, (index + 1) * half_cols)
+        own, got = own[:, part].astype(full), got[:, part].astype(full)
+        return jnp.concatenate(
+            [jnp.where(state == 0, own, got), jnp.where(state == 0, got, own)], 1
+        )
 
     lows_cut = [value[:, joint:].astype(low) for value in normed_sums]
     joined_backs = [
@@ -1788,20 +1863,6 @@
         for index in range(2)
     )
 
-    out_cut = [
-        (
-            value
-            + good
-            * sum_rows(
-                plain_dot(gated[index * middle : (index + 1) * middle], output_main).astype(low),
-                order,
-                0,
-            )
-        ).astype(low)
-        for index, (value, good, order) in enumerate(zip(second_cut, valid_cut, orders))
-    ]
-    layer_out = from_halves([gather_row16(value, order) for value, order in zip(out_cut, orders)])
-
     def scatter(value, axis):
         return lax.psum_scatter(
             value.astype(low), ZED, scatter_dimension=axis, tiled=True
@@ -1817,9 +1878,6 @@
     out_mlp_input = scatter(left_dot(mlp_normed_own, hidden_grad_own), 0)
     out_up_mlp = scatter(left_dot(jnp.concatenate(mlp_red, 0), hidden_grad_own), 0)
 
-    middle_own = jnp.concatenate(
-        [gather_rows(value, order, 0) for value, order in zip(middle_low, orders)], 0
-    )
     lows_halves = [gather_row16(value, order) for value, order in zip(lows_cut, orders)]
     lows_own, lows_other = (
         jnp.concatenate(
@@ -1837,47 +1895,49 @@
     down_sum = down_rows(near_own, near_other) + dp_swap(
         down_rows(far_own, far_other).astype(low)
     ).astype(full)
-    columns = mlp_normed_own.reshape(rows, 4, head_parts, part_m)
-    columns = lax.dynamic_index_in_dim(columns, head, 2, False).reshape(rows, 4 * part_m)
-    mlp_down_grad = left_dot(columns, middle_own).reshape(4, part_m, rank)
-    kept = lax.dynamic_slice_in_dim(mlp_down_grad, 2 * dp, 2, 0) + dp_swap(
-        lax.dynamic_slice_in_dim(mlp_down_grad, 2 * (1 - dp), 2, 0)
-    )
-    kept = lax.dynamic_index_in_dim(kept, state, 0, False) + state_swap(
-        lax.dynamic_index_in_dim(kept, 1 - state, 0, False)
-    )
     down_all = gather_rows(down_sum.astype(low)[None], masks, 0).reshape(quarter, 3 * rank)
     down_all = down_all.astype(full)
     out_downs = [down_all[:, index * rank : (index + 1) * rank] for index in range(3)]
-    out_down_mlp = gather_rows(kept.astype(low)[None], masks, 0).reshape(-1, rank).astype(full)
+
+    def placed(value, axis):
+        shape = list(value.shape)
+        shape[axis] *= head_parts
+        return lax.dynamic_update_slice_in_dim(
+            jnp.zeros(shape, full), value, head * value.shape[axis], axis
+        )
 
     small_main_grad = left_dot(mixer_normed, small_low)
-    vector_grad = sum_rows(small_main_grad[:, mixer_heads:], masks, 0)
-    vector_grad = gather_rows(add_zed(vector_grad), masks, 0)
-    step_rows = small_main_grad[:, :mixer_heads].reshape(4, -1, mixer_heads)
-    kept = lax.dynamic_slice_in_dim(step_rows, 2 * dp, 2, 0) + dp_swap(
-        lax.dynamic_slice_in_dim(step_rows, 2 * (1 - dp), 2, 0)
-    )
-    out_step = lax.dynamic_index_in_dim(kept, state, 0, False) + state_swap(
-        lax.dynamic_index_in_dim(kept, 1 - state, 0, False)
-    )
-    taps_total = add_everywhere(jnp.concatenate([grad_taps_b, grad_taps_c], 1))
-    own_total = add_zed(
-        jnp.concatenate(
-            [grad_gated_gain, grad_taps_x.reshape(-1), grad_shift, grad_rate, grad_skip]
-        )
-    )
-    gated_total = own_total[:inner_width]
-    taps_end = inner_width * (reach + 2)
-    taps_x_total = own_total[inner_width:taps_end].reshape(reach + 1, inner_width)
-    head_total = own_total[taps_end:].reshape(3, mixer_heads)
-    attn_gain_grad = natural_columns(grad_attn_gain)
-    gain_total = add_everywhere(
-        jnp.concatenate([attn_gain_grad, grad_mlp_gain, grad_mixer_gain]).reshape(-1, 128)
-    ).reshape(-1)
-
-    def gain_of(start, size):
-        return lax.dynamic_slice_in_dim(gain_total, start + place * size, size)
+    small_sum = jnp.concatenate(
+        [small_main_grad[:, mixer_heads:], placed(small_main_grad[:, :mixer_heads], 1)], 1
+    )
+    small_sum = lax.psum(small_sum, EVERY)
+    vector_grad = small_sum[:, : 2 * states]
+    out_step = lax.dynamic_slice(
+        small_sum,
+        (place * split_m, 2 * states + head * mixer_heads),
+        (split_m, mixer_heads),
+    )
+    normed_cut = [
+        lax.dynamic_slice_in_dim(value, chunk_of(order) * piece, piece, 0)
+        for value, order in zip(mlp_normed, orders)
+    ]
+    mlp_down_grad = left_dot(jnp.concatenate(normed_cut, 0), jnp.concatenate(middle_low, 0))
+    mlp_down_grad = lax.psum(hold(mlp_down_grad, main_total), EVERY)
+    out_down_mlp = lax.dynamic_slice_in_dim(mlp_down_grad, place * split_m, split_m, 0)
+
+    beside_got = hold(beside_got, grad_hidden)
+    out_all = [spread(main_total, beside_got, index) for index in range(3)]
+    out_main = [value[:quarter] for value in out_all]
+    out_up = [value[quarter:] for value in out_all]
+    flat_sums = [
+        placed(grad_taps_x, 1),
+        placed(jnp.stack([grad_shift, grad_rate, grad_skip]), 1),
+        placed(grad_gated_gain, 0),
+        jnp.concatenate([grad_taps_b, grad_taps_c], 1),
+        natural_columns(grad_attn_gain),
+        grad_mlp_gain,
+        grad_mixer_gain,
+    ]
 
     once = (head == 0).astype(full)
     square_sum = jnp.zeros((), full)
@@ -1885,12 +1945,27 @@
         square_sum = square_sum + jnp.sum(value * value)
     for value in out_downs + [out_down_mlp]:
         square_sum = square_sum + once * jnp.sum(value * value)
-    square_total = lax.psum(square_sum, EVERY)
+    totals = lax.psum(
+        jnp.concatenate([value.reshape(-1) for value in flat_sums] + [square_sum[None]]), EVERY
+    )
+    pieces = []
+    for value in flat_sums:
+        pieces.append(totals[: value.size].reshape(value.shape))
+        totals = totals[value.size :]
+    taps_x_total, head_total, gated_total, taps_total, attn_total, mlp_total, mixer_total = pieces
+
+    def of_head(value, size):
+        return lax.dynamic_slice_in_dim(value, head * size, size, value.ndim - 1)
+
+    def of_place(value, size):
+        return lax.dynamic_slice_in_dim(value, place * size, size)
+
+    head_total = of_head(head_total, mixer_heads)
     return (
         layer_out,
         grad_hidden,
         grad_embedding,
-        gain_of(0, split_a),
+        of_place(attn_total, split_a),
         out_main[0],
         out_main[1],
         out_main[2],
@@ -1901,32 +1976,27 @@
         out_up[1],
         out_up[2],
         out_attn,
-        gain_of(joint, split_m),
+        of_place(mlp_total, split_m),
         out_mlp_input,
         out_down_mlp,
         out_up_mlp,
         out_mlp_output,
-        gain_of(joint + width, split_m),
+        of_place(mixer_total, split_m),
         out_mixer[:, :inner_width],
         out_mixer[:, inner_width:],
         out_step,
         vector_grad[:, :states],
         vector_grad[:, states:],
-        taps_x_total,
+        of_head(taps_x_total, inner_width),
         taps_total[:, :states],
         taps_total[:, states:],
         head_total[0],
         head_total[1],
         head_total[2],
-        gated_total,
+        of_head(gated_total, inner_width),
         out_output,
-        jnp.sqrt(square_total),
-    )
-
-
-def z_pieces_columns(mine, theirs):
-    got = state_swap(theirs)
-    return [mine, got, dp_swap(mine), dp_swap(got)]
+        jnp.sqrt(totals[0]),
+    )
 
 
 def pick_device(mesh):

time: 1770 us -> 1870 us (1.056)
  waiting for transfers between devices: 767 us -> 958 us
  starting transfers between devices: 188 us -> 118 us
  blocking collectives: 39.5 us -> 0 us
  other arithmetic: 249 us -> 271 us
  Pallas kernels: 71.1 us -> 90.5 us
    psum x0 -> x2, waiting for transfers between devices: none -> 250 us  [the longest x1 126 us: fast_device(): lax.psum(jnp.concatenate([value.reshape(-1) for value in flat_sums] + [sq...]
    reduce_scatter x0 -> x2, waiting for transfers between devices: none -> 50.8 us  [by_dp(): return lax.psum_scatter(both, DP, scatter_dimension=0, tiled=True)]
    ppermute x120 -> x99, waiting for transfers between devices: 326 us -> 278 us  [head_swap(): return lax.ppermute(value, HEAD, [(i, i ^ mask) for i in range(count)])]
    ppermute x23 -> x9, waiting for transfers between devices: 218 us -> 178 us  [dp_swap(): return lax.ppermute(value, DP, [(0, 1), (1, 0)])]
    psum x1 -> x0, blocking collectives: 39.5 us -> none  [fast_device(): square_total = lax.psum(square_sum, EVERY)]
    all_gather x1, waiting for transfers between devices: 38.1 us -> 0.01 us  [fast_device(): mlp_proj = lax.all_gather(mlp_output, ZED, axis=1, tiled=True)]
    ppermute x27 -> x17, waiting for transfers between devices: 160 us -> 198 us  [state_swap(): return lax.ppermute(value, STATE, [(0, 1), (1, 0)])]
    ppermute x23 -> x9, starting transfers between devices: 52.1 us -> 15.1 us  [dp_swap(): return lax.ppermute(value, DP, [(0, 1), (1, 0)])]
  transfers between devices with their start and end apart: 183 -> 143, of which waited for: 90 -> 69; matrix products, arithmetic and copies ran while one was open for 29% -> 30% of each run, Pallas kernels for 3% -> 5%
where the time goes in v3:
time: 1870 us; the launch traced here: 1860 us
  waiting for transfers between devices  958 us (51%)
  other arithmetic  271 us (14%)
  local copies, waits for them, and re-layouts  201 us (11%)
  matrix products  192 us (10%)
  starting transfers between devices  118 us (6%)
  Pallas kernels  90.5 us (5%)
  between operations  32.2 us (2%)
    ppermute x99, waiting for transfers between devices, head_swap(): return lax.ppermute(value, HEAD, [(i, i ^ mask) for i in range(count)])  278 us
    ppermute x17, waiting for transfers between devices, state_swap(): return lax.ppermute(value, STATE, [(0, 1), (1, 0)])  198 us
    ppermute x9, waiting for transfers between devices, dp_swap(): return lax.ppermute(value, DP, [(0, 1), (1, 0)])  178 us
    psum x1, waiting for transfers between devices, fast_device(): lax.psum(jnp.concatenate([value.reshape(-1) for value in flat_sums] + [sq...  126 us
    psum x1, waiting for transfers between devices, fast_device(): mlp_down_grad = lax.psum(hold(mlp_down_grad, main_total), EVERY)  124 us
    unnamed x850, local copies, waits for them, and re-layouts  100 us
    ppermute x99, starting transfers between devices, head_swap(): return lax.ppermute(value, HEAD, [(i, i ^ mask) for i in range(count)])  78.5 us
    dot_general x24, matrix products, plain_dot(): return jnp.dot(left, right, preferred_element_type=jnp.float32)  73.8 us
  transfers between devices with their start and end apart: 143, of which 69 were waited for; matrix products, arithmetic and copies ran while one was open for 30% of the time, Pallas kernels for 5%

profile of v3, /device:TPU:0, one launch (start us, length us, event | category | flops | bytes accessed | tf_op | source)
XLA Modules:
  0.0 1864.6 jit_solution(5561080077725760824)
XLA Ops:
  14.6 34.4 %collective-permute-done.2 = bf16[1024,768]{1,0:T(8,128)(2,1)S(1)} collective-permute-done((bf16[1024,768]{1,0:T(8,128)(2,1)S(1)}, bf16[1024,768]{1,0:T(8,128)(2,1)S(1)}, u32[]{:S(2)}, u32[]{:S(2)}) %collective-permute-start.2) | collective-permute-done | bytes 1572896 | tf_op jit(solution)/shard_map/ppermute | solution.py:632
  53.1 33.8 %collective-permute-done.9.refs_1_ = bf16[512,768]{1,0:T(8,128)(2,1)S(1)} collective-permute-done((bf16[512,768]{1,0:T(8,128)(2,1)S(1)}, bf16[512,768]{1,0:T(8,128)(2,1)S(1)}, u32[]{:S(2)}, u32[]{:S(2)}) %collective-permute-start.9) | collective-permute-done | bytes 786464 | tf_op jit(solution)/shard_map/ppermute | solution.py:636
  142.5 34.1 %collective-permute-done.17 = bf16[256,512]{1,0:T(8,128)(2,1)} collective-permute-done((bf16[256,512]{1,0:T(8,128)(2,1)}, bf16[256,512]{1,0:T(8,128)(2,1)}, u32[]{:S(2)}, u32[]{:S(2)}) %collective-permute-start.17) | collective-permute-done | bytes 262176 | tf_op jit(solution)/shard_map/ppermute | solution.py:632
  182.8 78.8 %collective-permute-done.1 = bf16[2,656,128]{2,1,0:T(8,128)(2,1)S(1)} collective-permute-done((bf16[2,656,128]{2,1,0:T(8,128)(2,1)S(1)}, bf16[2,656,128]{2,1,0:T(8,128)(2,1)S(1)}, u32[]{:S(2)}, u32[]{:S(2)}) %collective-permute-start.1) | collective-permute-done | bytes 335904 | tf_op jit(solution)/shard_map/ppermute | solution.py:636
  293.3 7.2 fusion.137
  304.3 76.6 %collective-permute-done.10.refs_0_ = bf16[2,128,2048]{2,1,0:T(8,128)(2,1)} collective-permute-done((bf16[2,128,2048]{2,1,0:T(8,128)(2,1)}, bf16[2,128,2048]{2,1,0:T(8,128)(2,1)}, u32[]{:S(2)}, u32[]{:S(2)}) %collective-permute-start.10) | collective-permute-done | bytes 1048608 | tf_op jit(solution)/shard_map/ppermute | solution.py:632
  410.7 47.3 %collective-permute-done.15 = bf16[256,2048]{1,0:T(8,128)(2,1)S(1)} collective-permute-done((bf16[256,2048]{1,0:T(8,128)(2,1)S(1)}, bf16[256,2048]{1,0:T(8,128)(2,1)S(1)}, u32[]{:S(2)}, u32[]{:S(2)}) %collective-permute-start.15) | collective-permute-done | bytes 1048608 | tf_op jit(solution)/shard_map/ppermute | solution.py:628
  500.7 22.4 %shard_map.589 = (bf16[2048,256]{1,0:T(8,128)(2,1)S(1)}, f32[2,1,2048]{2,1,0:T(1,128)S(1)}) custom-call(s32[8]{0:T(128)S(1)} %and_select_fusion.low_ref, bf16[2048,256]{1,0:T(8,128)(2,1)S(1)} %get-tuple-element.74.q_ref, bf16[2048,256]{1,0:T(8,128)(2,1)S(1)} %get-tuple-element.75.k_ref, bf16[2048,256]{1,0:T(8,128)(2,1)S(1)} %get-tuple-element.76.v_ref, ...), custom_call_target="tpu_custom_call" | custom-call | flops 2147483648 | bytes 4194304 | tf_op jit(solution)/shard_map/pallas_call | solution.py:825
  538.5 10.2 collective-permute-done.27
  560.7 18.5 collective-permute-done.35
  583.0 9.7 collective-permute-done.36
  622.2 6.7 collective-permute-done.24
  636.7 9.3 multiply_convert_fusion.3
  656.8 8.9 multiply_convert_fusion.2
  672.1 10.9 collective-permute-done.29
  704.4 8.7 collective-permute-done.32
  729.0 8.6 fusion.282
  749.3 6.6 fusion.76
  765.9 7.1 shard_map.594
  776.0 9.8 multiply_reduce_fusion.12
  814.7 17.2 shard_map.596
  867.1 10.0 collective-permute-done.53
  905.2 11.5 collective-permute-done.82
  944.3 6.5 collective-permute-done.85
  974.4 9.1 convolution_convert_fusion.6
  988.8 6.7 collective-permute-done.62
  1003.0 7.6 collective-permute-done.63
  1014.4 16.7 collective-permute-done.57
  1046.4 6.3 fusion.22
  1058.4 11.4 collective-permute-done.88
  1092.2 12.5 collective-permute-done.77
  1108.1 11.6 collective-permute-done.78
  1121.9 6.2 fusion.19
  1128.2 9.1 collective-permute-done.92
  1166.7 52.3 %collective-permute-done.94 = bf16[256,1024]{1,0:T(8,128)(2,1)S(1)} collective-permute-done((bf16[256,1024]{1,0:T(8,128)(2,1)S(1)}, bf16[256,1024]{1,0:T(8,128)(2,1)S(1)}, u32[]{:S(2)}, u32[]{:S(2)}) %collective-permute-start.94) | collective-permute-done | bytes 524320 | tf_op jit(solution)/shard_map/ppermute | solution.py:636
  1219.4 29.2 %shard_map.598 = (f32[2048,256]{1,0:T(8,128)S(1)}, f32[2048,256]{1,0:T(8,128)S(1)}, f32[2048,256]{1,0:T(8,128)S(1)}) custom-call(s32[8]{0:T(128)S(1)} %copy-done.30, bf16[2048,256]{1,0:T(8,128)(2,1)S(1)} %copy-done.24, bf16[2048,256]{1,0:T(8,128)(2,1)S(1)} %copy-done.26, bf16[2048,256]{1,0:T(8,128)(2,1)S(1)} %copy-done.28, ...), custom_call_target="tpu_custom_call" | custom-call | flops 5368709120 | bytes 10485760 | tf_op jit(solution)/shard_map/pallas_call | solution.py:902
  1273.7 14.1 convolution_convert_fusion.1
  1292.8 12.9 convolution_convert_fusion
  1327.6 7.5 pad_maximum_fusion.1
  1335.1 8.5 copy.168
  1351.6 8.7 convert_add_fusion.1
  1380.5 50.8 %reduce-scatter.10.cloned.1.call-done = bf16[1056,768]{1,0:T(8,128)(2,1)} async-done(((bf16[2112,768]{1,0:T(8,128)(2,1)}), bf16[1056,768]{1,0:T(8,128)(2,1)}) %reduce-scatter.10.cloned.1.call-update) | async-done | bytes 1622032 | tf_op jit(solution)/shard_map/reduce_scatter | solution.py:1821
  1444.7 123.8 %all-reduce.31.cloned.1.call-done = f32[2048,128]{1,0:T(8,128)} async-done(((f32[2048,128]{1,0:T(8,128)}), f32[2048,128]{1,0:T(8,128)}) %all-reduce.31.cloned.1.call-update) | async-done | bytes 1048592 | tf_op jit(solution)/shard_map/psum | solution.py:1925
  1578.7 13.8 collective-permute-done.106
  1593.8 8.9 collective-permute-done.99
  1611.9 8.9 collective-permute-done.118
  1668.4 8.6 collective-permute-done.128
  1716.9 125.8 %all-reduce.33.cloned.1.call-done = (f32[29377]{0:T(1024)}, f32[2048,192]{0,1:T(8,128)}) async-done(((f32[29377]{0:T(1024)}, f32[2048,192]{0,1:T(8,128)}), (f32[29377]{0:T(1024)}, f32[2048,192]{0,1:T(8,128)})) %all-reduce.33.cloned.1.call-update) | async-done | bytes 1690388 | tf_op jit(solution)/shard_map/psum | solution.py:1948
  (1651 shorter events, 766.6 us)
Async XLA Ops:
  7.2 519.9 %all-gather.6.cloned.1.call-start = ((), (), s32[]{:S(2)}) async-start(), calls=%async_computation.7 | async-start | bytes 2621440 | tf_op jit(solution)/shard_map/all_gather | solution.py:1564
  11.5 37.5 %collective-permute-start.2 = (bf16[1024,768]{1,0:T(8,128)(2,1)S(1)}, bf16[1024,768]{1,0:T(8,128)(2,1)S(1)}, u32[]{:S(2)}, u32[]{:S(2)}) collective-permute-start(bf16[1024,768]{1,0:T(8,128)(2,1)S(1)} %pad_maximum_fusion.36), channel_id=1, source_target_pairs={{0,1},{1,0},{2,3},{3,2},{4,5},{5,4},{6,7},{7,6},{8,9},{9,8},{10,11... | collective-permute-start | bytes 4718600 | tf_op jit(solution)/shard_map/ppermute | solution.py:632
  50.4 36.5 %collective-permute-start.9 = (bf16[512,768]{1,0:T(8,128)(2,1)S(1)}, bf16[512,768]{1,0:T(8,128)(2,1)S(1)}, u32[]{:S(2)}, u32[]{:S(2)}) collective-permute-start(bf16[512,768]{1,0:T(8,128)(2,1)S(1)} %get-tuple-element.299), channel_id=1, source_target_pairs={{0,16},{16,0},{1,17},{17,1},{2,18},{18,2},{3,19},{19,3},{4,20},{20... | collective-permute-start | bytes 2359304 | tf_op jit(solution)/shard_map/ppermute | solution.py:636
  90.1 507.5 %all-gather.8.cloned.1.call-start = ((), (), s32[]{:S(2)}) async-start(), calls=%async_computation.8 | async-start | bytes 2621440 | tf_op jit(solution)/shard_map/all_gather | solution.py:1565
  90.8 555.2 %all-gather.10.cloned.1.call-start = ((), (), s32[]{:S(2)}) async-start(), calls=%async_computation.9 | async-start | bytes 5242880 | tf_op jit(solution)/shard_map/all_gather | solution.py:1567
  91.6 637.4 %all-gather.12.cloned.1.call-start = ((), (), s32[]{:S(2)}) async-start(), calls=%async_computation.10 | async-start | bytes 5242880 | tf_op jit(solution)/shard_map/all_gather | solution.py:1568
  99.4 40.2 %collective-permute-start = (bf16[656,128]{1,0:T(8,128)(2,1)}, bf16[656,128]{1,0:T(8,128)(2,1)}, u32[]{:S(2)}, u32[]{:S(2)}) collective-permute-start(bf16[656,128]{1,0:T(8,128)(2,1)} %constant_dynamic-update-slice_fusion.8), channel_id=1, source_target_pairs={{0,1},{1,0},{2,3},{3,2},{4,5},{5,4},{6,7},{7,6},{8,9},{9,8},{10,11... | collective-permute-start | bytes 503816 | tf_op jit(solution)/shard_map/ppermute | solution.py:632
  102.5 184.8 %collective-permute-start.6 = (bf16[512,768]{1,0:T(8,128)(2,1)}, bf16[512,768]{1,0:T(8,128)(2,1)}, u32[]{:S(2)}, u32[]{:S(2)}) collective-permute-start(bf16[512,768]{1,0:T(8,128)(2,1)} %get-tuple-element.302), channel_id=1, source_target_pairs={{0,16},{16,0},{1,17},{17,1},{2,18},{18,2},{3,19},{19,3},{4,20},{20... | collective-permute-start | bytes 2359304 | tf_op jit(solution)/shard_map/ppermute | solution.py:636
  105.9 198.4 %collective-permute-start.7 = (bf16[512,768]{1,0:T(8,128)(2,1)}, bf16[512,768]{1,0:T(8,128)(2,1)}, u32[]{:S(2)}, u32[]{:S(2)}) collective-permute-start(bf16[512,768]{1,0:T(8,128)(2,1)} %get-tuple-element.301), channel_id=1, source_target_pairs={{0,16},{16,0},{1,17},{17,1},{2,18},{18,2},{3,19},{19,3},{4,20},{20... | collective-permute-start | bytes 2359304 | tf_op jit(solution)/shard_map/ppermute | solution.py:636
  106.7 69.8 %collective-permute-start.17 = (bf16[256,512]{1,0:T(8,128)(2,1)}, bf16[256,512]{1,0:T(8,128)(2,1)}, u32[]{:S(2)}, u32[]{:S(2)}) collective-permute-start(bf16[256,512]{1,0:T(8,128)(2,1)} %get-tuple-element.437), channel_id=1, source_target_pairs={{0,1},{1,0},{2,3},{3,2},{4,5},{5,4},{6,7},{7,6},{8,9},{9,8},{10,11... | collective-permute-start | bytes 786440 | tf_op jit(solution)/shard_map/ppermute | solution.py:632
  108.9 667.0 %all-gather.14.cloned.1.call-start = ((), (), s32[]{:S(2)}) async-start(), calls=%async_computation.11 | async-start | bytes 2621440 | tf_op jit(solution)/shard_map/all_gather | solution.py:1571
  140.5 121.1 %collective-permute-start.1 = (bf16[2,656,128]{2,1,0:T(8,128)(2,1)S(1)}, bf16[2,656,128]{2,1,0:T(8,128)(2,1)S(1)}, u32[]{:S(2)}, u32[]{:S(2)}) collective-permute-start(bf16[2,656,128]{2,1,0:T(8,128)(2,1)S(1)} %pad_maximum_fusion.116), channel_id=1, source_target_pairs={{0,16},{16,0},{1,17},{17,1},{2,18},{18,2},{3,19},{19,3},{4,20},{20... | collective-permute-start | bytes 1007624 | tf_op jit(solution)/shard_map/ppermute | solution.py:636
  178.5 106.3 %collective-permute-start.18 = (bf16[2,256,512]{2,1,0:T(8,128)(2,1)}, bf16[2,256,512]{2,1,0:T(8,128)(2,1)}, u32[]{:S(2)}, u32[]{:S(2)}) collective-permute-start(bf16[2,256,512]{2,1,0:T(8,128)(2,1)} %pad_maximum_fusion.88), channel_id=1, source_target_pairs={{0,16},{16,0},{1,17},{17,1},{2,18},{18,2},{3,19},{19,3},{4,20},{20... | collective-permute-start | bytes 1572872 | tf_op jit(solution)/shard_map/ppermute | solution.py:636
  287.3 93.5 %collective-permute-start.10 = (bf16[2,128,2048]{2,1,0:T(8,128)(2,1)}, bf16[2,128,2048]{2,1,0:T(8,128)(2,1)}, u32[]{:S(2)}, u32[]{:S(2)}) collective-permute-start(bf16[2,128,2048]{2,1,0:T(8,128)(2,1)} %shard_map.585), channel_id=1, source_target_pairs={{0,1},{1,0},{2,3},{3,2},{4,5},{5,4},{6,7},{7,6},{8,9},{9,8},{10,11... | collective-permute-start | bytes 3145736 | tf_op jit(solution)/shard_map/ppermute | solution.py:632
  290.7 96.9 %collective-permute-start.4 = (bf16[2,4,448,128]{3,2,0,1:T(8,128)(2,1)}, bf16[2,4,448,128]{3,2,0,1:T(8,128)(2,1)}, u32[]{:S(2)}, u32[]{:S(2)}) collective-permute-start(bf16[2,4,448,128]{3,2,0,1:T(8,128)(2,1)} %pad_maximum_fusion.77), channel_id=1, source_target_pairs={{0,4},{2,6},{4,0},{6,2},{8,12},{10,14},{12,8},{14,10},{1,5},{3,7},... | collective-permute-start | bytes 2752520 | tf_op jit(solution)/shard_map/ppermute | solution.py:628
  292.2 109.7 %collective-permute-start.8 = (bf16[512,768]{1,0:T(8,128)(2,1)}, bf16[512,768]{1,0:T(8,128)(2,1)}, u32[]{:S(2)}, u32[]{:S(2)}) collective-permute-start(bf16[512,768]{1,0:T(8,128)(2,1)} %get-tuple-element.300), channel_id=1, source_target_pairs={{0,16},{16,0},{1,17},{17,1},{2,18},{18,2},{3,19},{19,3},{4,20},{20... | collective-permute-start | bytes 2359304 | tf_op jit(solution)/shard_map/ppermute | solution.py:636
  390.6 72.6 %collective-permute-start.5 = (bf16[4,4,448,128]{3,2,0,1:T(8,128)(2,1)}, bf16[4,4,448,128]{3,2,0,1:T(8,128)(2,1)}, u32[]{:S(2)}, u32[]{:S(2)}) collective-permute-start(bf16[4,4,448,128]{3,2,0,1:T(8,128)(2,1)} %pad_maximum_fusion.30), channel_id=1, source_target_pairs={{0,8},{2,10},{4,12},{6,14},{8,0},{10,2},{12,4},{14,6},{1,9},{3,11}... | collective-permute-start | bytes 5505032 | tf_op jit(solution)/shard_map/ppermute | solution.py:628
  399.0 59.0 %collective-permute-start.15 = (bf16[256,2048]{1,0:T(8,128)(2,1)S(1)}, bf16[256,2048]{1,0:T(8,128)(2,1)S(1)}, u32[]{:S(2)}, u32[]{:S(2)}) collective-permute-start(bf16[256,2048]{1,0:T(8,128)(2,1)S(1)} %pad_maximum_fusion.56), channel_id=1, source_target_pairs={{0,8},{2,10},{4,12},{6,14},{8,0},{10,2},{12,4},{14,6},{1,9},{3,11}... | collective-permute-start | bytes 3145736 | tf_op jit(solution)/shard_map/ppermute | solution.py:628
  400.4 60.2 %collective-permute-start.12 = (bf16[256,2048]{1,0:T(8,128)(2,1)S(1)}, bf16[256,2048]{1,0:T(8,128)(2,1)S(1)}, u32[]{:S(2)}, u32[]{:S(2)}) collective-permute-start(bf16[256,2048]{1,0:T(8,128)(2,1)S(1)} %pad_maximum_fusion.55), channel_id=1, source_target_pairs={{0,4},{2,6},{4,0},{6,2},{8,12},{10,14},{12,8},{14,10},{1,5},{3,7},... | collective-permute-start | bytes 3145736 | tf_op jit(solution)/shard_map/ppermute | solution.py:628
  695.1 630.3 %reduce-scatter.20.cloned.1.call-start = ((), (), s32[]{:S(2)}) async-start(), calls=%async_computation.19 | async-start | bytes 2621440 | tf_op jit(solution)/shard_map/reduce_scatter | solution.py:1867
  810.7 50.2 %collective-permute-start.52 = (bf16[256,2048]{1,0:T(8,128)(2,1)}, bf16[256,2048]{1,0:T(8,128)(2,1)}, u32[]{:S(2)}, u32[]{:S(2)}) collective-permute-start(bf16[256,2048]{1,0:T(8,128)(2,1)} %constant_dynamic-slice_fusion.19), channel_id=1, source_target_pairs={{0,2},{2,0},{4,6},{6,4},{8,10},{10,8},{12,14},{14,12},{1,3},{3,1},... | collective-permute-start | bytes 3145736 | tf_op jit(solution)/shard_map/ppermute | solution.py:628
  813.0 51.3 %collective-permute-start.59 = (bf16[256,2048]{1,0:T(8,128)(2,1)}, bf16[256,2048]{1,0:T(8,128)(2,1)}, u32[]{:S(2)}, u32[]{:S(2)}) collective-permute-start(bf16[256,2048]{1,0:T(8,128)(2,1)} %constant_dynamic-slice_fusion.18), channel_id=1, source_target_pairs={{0,2},{2,0},{4,6},{6,4},{8,10},{10,8},{12,14},{14,12},{1,3},{3,1},... | collective-permute-start | bytes 3145736 | tf_op jit(solution)/shard_map/ppermute | solution.py:628
  933.8 409.8 %reduce-scatter.14.cloned.1.call-start = ((), (), s32[]{:S(2)}) async-start(), calls=%async_computation.15 | async-start | bytes 327680 | tf_op jit(solution)/shard_map/reduce_scatter | solution.py:1867
  956.1 30.4 %collective-permute-start.55 = (bf16[64,2048]{1,0:T(8,128)(2,1)S(1)}, bf16[64,2048]{1,0:T(8,128)(2,1)}, u32[]{:S(2)}, u32[]{:S(2)}) collective-permute-start(bf16[64,2048]{1,0:T(8,128)(2,1)S(1)} %copy-done.170), channel_id=1, source_target_pairs={{0,1},{1,0},{2,3},{3,2},{4,5},{5,4},{6,7},{7,6},{8,9},{9,8},{10,11... | collective-permute-start | bytes 786440 | tf_op jit(solution)/shard_map/ppermute | solution.py:632
  974.0 374.6 %reduce-scatter.18.cloned.1.call-start = ((), (), s32[]{:S(2)}) async-start(), calls=%async_computation.18 | async-start | bytes 5242880 | tf_op jit(solution)/shard_map/reduce_scatter | solution.py:1867
  983.7 389.1 %reduce-scatter.16.cloned.1.call-start = ((), (), s32[]{:S(2)}) async-start(), calls=%async_computation.16 | async-start | bytes 5242880 | tf_op jit(solution)/shard_map/reduce_scatter | solution.py:1867
  1002.0 29.1 %collective-permute-start.57 = (bf16[2,128,2048]{2,1,0:T(8,128)(2,1)S(1)}, bf16[2,128,2048]{2,1,0:T(8,128)(2,1)S(1)}, u32[]{:S(2)}, u32[]{:S(2)}) collective-permute-start(bf16[2,128,2048]{2,1,0:T(8,128)(2,1)S(1)} %pad_maximum_fusion.65), channel_id=1, source_target_pairs={{0,4},{2,6},{4,0},{6,2},{8,12},{10,14},{12,8},{14,10},{1,5},{3,7},... | collective-permute-start | bytes 3145736 | tf_op jit(solution)/shard_map/ppermute | solution.py:628
  1033.5 108.7 %collective-permute-start.58 = (bf16[2,256,2048]{2,1,0:T(8,128)(2,1)}, bf16[2,256,2048]{2,1,0:T(8,128)(2,1)}, u32[]{:S(2)}, u32[]{:S(2)}) collective-permute-start(bf16[2,256,2048]{2,1,0:T(8,128)(2,1)} %pad_maximum_fusion.24), channel_id=1, source_target_pairs={{0,2},{2,0},{4,6},{6,4},{8,10},{10,8},{12,14},{14,12},{1,3},{3,1},... | collective-permute-start | bytes 6291464 | tf_op jit(solution)/shard_map/ppermute | solution.py:628
  1052.8 323.6 %reduce-scatter.12.cloned.1.call-start = ((), (), s32[]{:S(2)}) async-start(), calls=%async_computation.14 | async-start | bytes 5242880 | tf_op jit(solution)/shard_map/reduce_scatter | solution.py:1867
  1086.9 63.5 %collective-permute-start.65 = (bf16[2,256,2048]{2,1,0:T(8,128)(2,1)}, bf16[2,256,2048]{2,1,0:T(8,128)(2,1)}, u32[]{:S(2)}, u32[]{:S(2)}) collective-permute-start(bf16[2,256,2048]{2,1,0:T(8,128)(2,1)} %pad_maximum_fusion.25), channel_id=1, source_target_pairs={{0,2},{2,0},{4,6},{6,4},{8,10},{10,8},{12,14},{14,12},{1,3},{3,1},... | collective-permute-start | bytes 6291464 | tf_op jit(solution)/shard_map/ppermute | solution.py:628
  1106.1 31.2 %collective-permute-start.92 = (bf16[2,128,2048]{2,1,0:T(8,128)(2,1)}, bf16[2,128,2048]{2,1,0:T(8,128)(2,1)}, u32[]{:S(2)}, u32[]{:S(2)}) collective-permute-start(bf16[2,128,2048]{2,1,0:T(8,128)(2,1)} %pad_maximum_fusion.70), channel_id=1, source_target_pairs={{0,8},{2,10},{4,12},{6,14},{8,0},{10,2},{12,4},{14,6},{1,9},{3,11}... | collective-permute-start | bytes 3145736 | tf_op jit(solution)/shard_map/ppermute | solution.py:628
  1128.1 251.9 %reduce-scatter.8.cloned.1.call-start = ((), (), s32[]{:S(2)}) async-start(), calls=%async_computation.12 | async-start | bytes 4866048 | tf_op jit(solution)/shard_map/reduce_scatter | solution.py:1821
  1163.8 55.3 %collective-permute-start.94 = (bf16[256,1024]{1,0:T(8,128)(2,1)S(1)}, bf16[256,1024]{1,0:T(8,128)(2,1)S(1)}, u32[]{:S(2)}, u32[]{:S(2)}) collective-permute-start(bf16[256,1024]{1,0:T(8,128)(2,1)S(1)} %constant_dynamic-slice_fusion.12), channel_id=1, source_target_pairs={{0,16},{16,0},{1,17},{17,1},{2,18},{18,2},{3,19},{19,3},{4,20},{20... | collective-permute-start | bytes 1572872 | tf_op jit(solution)/shard_map/ppermute | solution.py:636
  1219.2 33.4 %collective-permute-start.95 = (bf16[256,512]{1,0:T(8,128)(2,1)S(1)}, bf16[256,512]{1,0:T(8,128)(2,1)S(1)}, u32[]{:S(2)}, u32[]{:S(2)}) collective-permute-start(bf16[256,512]{1,0:T(8,128)(2,1)S(1)} %dynamic-slice_convert_fusion.20), channel_id=1, source_target_pairs={{0,1},{1,0},{2,3},{3,2},{4,5},{5,4},{6,7},{7,6},{8,9},{9,8},{10,11... | collective-permute-start | bytes 786440 | tf_op jit(solution)/shard_map/ppermute | solution.py:632
  1271.9 159.4 %reduce-scatter.10.cloned.1.call-start = ((), (), s32[]{:S(2)}) async-start(), calls=%async_computation.13 | async-start | bytes 4866048 | tf_op jit(solution)/shard_map/reduce_scatter | solution.py:1821
  1292.8 58.8 %collective-permute-start.96 = (bf16[2,256,4480]{2,1,0:T(8,128)(2,1)}, bf16[2,256,4480]{2,1,0:T(8,128)(2,1)}, u32[]{:S(2)}, u32[]{:S(2)}) collective-permute-start(bf16[2,256,4480]{2,1,0:T(8,128)(2,1)} %constant_dynamic-slice_fusion.11), channel_id=1, source_target_pairs={{0,2},{2,0},{4,6},{6,4},{8,10},{10,8},{12,14},{14,12},{1,3},{3,1},... | collective-permute-start | bytes 13762568 | tf_op jit(solution)/shard_map/ppermute | solution.py:628
  1310.5 53.7 %collective-permute-start.103 = (bf16[2,256,4480]{2,1,0:T(8,128)(2,1)}, bf16[2,256,4480]{2,1,0:T(8,128)(2,1)}, u32[]{:S(2)}, u32[]{:S(2)}) collective-permute-start(bf16[2,256,4480]{2,1,0:T(8,128)(2,1)} %constant_dynamic-slice_fusion.7), channel_id=1, source_target_pairs={{0,2},{2,0},{4,6},{6,4},{8,10},{10,8},{12,14},{14,12},{1,3},{3,1},... | collective-permute-start | bytes 13762568 | tf_op jit(solution)/shard_map/ppermute | solution.py:628
  1322.6 245.9 %all-reduce.31.cloned.1.call-start = ((), (), s32[]{:S(2)}) async-start(), calls=%async_computation.17 | async-start | bytes 2097152 | tf_op jit(solution)/shard_map/psum | solution.py:1925
  1364.2 67.1 %collective-permute-start.97 = (bf16[2,128,4480]{2,1,0:T(8,128)(2,1)}, bf16[2,128,4480]{2,1,0:T(8,128)(2,1)}, u32[]{:S(2)}, u32[]{:S(2)}) collective-permute-start(bf16[2,128,4480]{2,1,0:T(8,128)(2,1)} %dynamic-slice_convert_fusion.1), channel_id=1, source_target_pairs={{0,4},{2,6},{4,0},{6,2},{8,12},{10,14},{12,8},{14,10},{1,5},{3,7},... | collective-permute-start | bytes 6881288 | tf_op jit(solution)/shard_map/ppermute | solution.py:628
  1372.7 63.8 %collective-permute-start.104 = (bf16[2,128,4480]{2,1,0:T(8,128)(2,1)}, bf16[2,128,4480]{2,1,0:T(8,128)(2,1)}, u32[]{:S(2)}, u32[]{:S(2)}) collective-permute-start(bf16[2,128,4480]{2,1,0:T(8,128)(2,1)} %dynamic-slice_convert_fusion), channel_id=1, source_target_pairs={{0,8},{2,10},{4,12},{6,14},{8,0},{10,2},{12,4},{14,6},{1,9},{3,11}... | collective-permute-start | bytes 6881288 | tf_op jit(solution)/shard_map/ppermute | solution.py:628
  1380.0 462.7 %all-reduce.33.cloned.1.call-start = ((), (), s32[]{:S(2)}) async-start(), calls=%async_computation.20 | async-start | bytes 3383296 | tf_op jit(solution)/shard_map/psum | solution.py:1948
  1431.3 256.0 %collective-permute-start.116 = (bf16[1056,768]{1,0:T(8,128)(2,1)}, bf16[1056,768]{1,0:T(8,128)(2,1)S(1)}, u32[]{:S(2)}, u32[]{:S(2)}) collective-permute-start(bf16[1056,768]{1,0:T(8,128)(2,1)} %reduce-scatter.10.cloned.1.call-done), channel_id=1, source_target_pairs={{0,1},{1,0},{2,3},{3,2},{4,5},{5,4},{6,7},{7,6},{8,9},{9,8},{10,11... | collective-permute-start | bytes 4866056 | tf_op jit(solution)/shard_map/ppermute | solution.py:632
  1435.0 136.5 %collective-permute-start.98 = (bf16[2,64,4480]{2,1,0:T(8,128)(2,1)S(1)}, bf16[2,64,4480]{2,1,0:T(8,128)(2,1)}, u32[]{:S(2)}, u32[]{:S(2)}) collective-permute-start(bf16[2,64,4480]{2,1,0:T(8,128)(2,1)S(1)} %dynamic-slice_convert_fusion.3), channel_id=1, source_target_pairs={{0,8},{2,10},{4,12},{6,14},{8,0},{10,2},{12,4},{14,6},{1,9},{3,11}... | collective-permute-start | bytes 3440648 | tf_op jit(solution)/shard_map/ppermute | solution.py:628
  1443.3 130.6 %collective-permute-start.105 = (bf16[2,64,4480]{2,1,0:T(8,128)(2,1)}, bf16[2,64,4480]{2,1,0:T(8,128)(2,1)}, u32[]{:S(2)}, u32[]{:S(2)}) collective-permute-start(bf16[2,64,4480]{2,1,0:T(8,128)(2,1)} %dynamic-slice_convert_fusion.2), channel_id=1, source_target_pairs={{0,4},{2,6},{4,0},{6,2},{8,12},{10,14},{12,8},{14,10},{1,5},{3,7},... | collective-permute-start | bytes 3440648 | tf_op jit(solution)/shard_map/ppermute | solution.py:628
  1650.0 31.1 %collective-permute-start.102 = (bf16[256,2048]{1,0:T(8,128)(2,1)}, bf16[256,2048]{1,0:T(8,128)(2,1)}, u32[]{:S(2)}, u32[]{:S(2)}) collective-permute-start(bf16[256,2048]{1,0:T(8,128)(2,1)} %pad_maximum_fusion.73), channel_id=1, source_target_pairs={{0,2},{2,0},{4,6},{6,4},{8,10},{10,8},{12,14},{14,12},{1,3},{3,1},... | collective-permute-start | bytes 3145736 | tf_op jit(solution)/shard_map/ppermute | solution.py:628
  1654.6 28.6 %collective-permute-start.109 = (bf16[256,2048]{1,0:T(8,128)(2,1)}, bf16[256,2048]{1,0:T(8,128)(2,1)}, u32[]{:S(2)}, u32[]{:S(2)}) collective-permute-start(bf16[256,2048]{1,0:T(8,128)(2,1)} %pad_maximum_fusion.74), channel_id=1, source_target_pairs={{0,2},{2,0},{4,6},{6,4},{8,10},{10,8},{12,14},{14,12},{1,3},{3,1},... | collective-permute-start | bytes 3145736 | tf_op jit(solution)/shard_map/ppermute | solution.py:628
  1665.2 45.8 %collective-permute-start.112 = (bf16[256,2048]{1,0:T(8,128)(2,1)}, bf16[256,2048]{1,0:T(8,128)(2,1)}, u32[]{:S(2)}, u32[]{:S(2)}) collective-permute-start(bf16[256,2048]{1,0:T(8,128)(2,1)} %pad_maximum_fusion.75), channel_id=1, source_target_pairs={{0,2},{2,0},{4,6},{6,4},{8,10},{10,8},{12,14},{14,12},{1,3},{3,1},... | collective-permute-start | bytes 3145736 | tf_op jit(solution)/shard_map/ppermute | solution.py:628
  1677.0 35.9 %collective-permute-start.115 = (bf16[256,2048]{1,0:T(8,128)(2,1)}, bf16[256,2048]{1,0:T(8,128)(2,1)}, u32[]{:S(2)}, u32[]{:S(2)}) collective-permute-start(bf16[256,2048]{1,0:T(8,128)(2,1)} %pad_maximum_fusion.76), channel_id=1, source_target_pairs={{0,2},{2,0},{4,6},{6,4},{8,10},{10,8},{12,14},{14,12},{1,3},{3,1},... | collective-permute-start | bytes 3145736 | tf_op jit(solution)/shard_map/ppermute | solution.py:628
  (505 other events, 6069.6 us)
Sparse Core Ops, SparseCore 0:
  90.2 113.0 all-gather.5
  205.5 61.1 all-gather.7
  268.2 116.8 all-gather.9
  387.1 80.8 all-gather.11
  695.2 44.0 all-gather.13
  933.9 49.3 reduce-scatter.19
  986.2 18.9 reduce-scatter.13
  1007.5 74.9 reduce-scatter.17
  1084.9 79.9 reduce-scatter.15
  1167.1 95.0 reduce-scatter.11
  1272.0 77.8 reduce-scatter.7
  1352.1 79.0 reduce-scatter.9
  1437.9 130.6 all-reduce.30
  1711.1 131.5 all-reduce.32

commit v4 on v3

--- a/solution.py
+++ b/solution.py
@@ -842,8 +842,8 @@
         ],
         compiler_params=vmem_limit(40),
         cost_estimate=pl.CostEstimate(
-            flops=2 * length * length * columns, bytes_accessed=8 * length * columns,
-            transcendentals=length * length * heads // 2,
+            flops=22 * length * length * columns, bytes_accessed=8 * length * columns,
+            transcendentals=0,
         ),
     )(lows, queries, keys, values, segment[:, None], segment[None, :])
 
@@ -919,8 +919,8 @@
         out_shape=[shape, shape, shape],
         compiler_params=vmem_limit(40),
         cost_estimate=pl.CostEstimate(
-            flops=5 * length * length * columns, bytes_accessed=20 * length * columns,
-            transcendentals=length * length * heads // 2,
+            flops=30 * length * length * columns, bytes_accessed=20 * length * columns,
+            transcendentals=0,
         ),
     )(lows, queries, keys, values, grads, outs, lse, segment[:, None], segment[None, :])
 
@@ -1280,7 +1280,7 @@
         out_shape=[jax.ShapeDtypeStruct(shape, full) for shape in outs],
         compiler_params=vmem_limit(40),
         cost_estimate=pl.CostEstimate(
-            flops=flops, bytes_accessed=8 * count * GROUP * channels, transcendentals=flops // 256
+            flops=flops, bytes_accessed=8 * count * GROUP * channels, transcendentals=0
         ),
     )(ends, *inputs)
 
@@ -1308,7 +1308,7 @@
             [2],
             [],
             self.dims,
-            2 * self.rows * self.channels * self.states,
+            160 * self.rows * self.channels * self.states,
         )[0]
 
     def forward(self, first):
@@ -1322,7 +1322,7 @@
             [0, 3],
             [pltpu.VMEM(self.state_shape, full)],
             self.dims,
-            8 * self.rows * self.channels * GROUP,
+            56 * self.rows * self.channels * GROUP,
         )
 
     def start_grad(self, grad):
@@ -1336,7 +1336,7 @@
             [2],
             [],
             self.dims,
-            2 * self.rows * self.channels * self.states,
+            160 * self.rows * self.channels * self.states,
         )[0]
 
     def backward(self, grad, states, last):
@@ -1361,7 +1361,7 @@
             [0, 0, 0, 1, 0, 0],
             [pltpu.VMEM(self.state_shape, full), pltpu.VMEM((GROUP, GROUP), full)],
             self.dims,
-            24 * self.rows * self.channels * GROUP,
+            144 * self.rows * self.channels * GROUP,
         )
 
 
@@ -1439,12 +1439,6 @@
             [lax.dynamic_slice_in_dim(v, index * half_cols, half_cols, 1) for v in values], 1
         )
 
-    mine = state_columns((w_query, w_key, w_value), state)
-    got = state_swap(state_columns((w_query, w_key, w_value), 1 - state))
-    cutting = mine.shape[0] // 2
-    far_mine = [dp_swap(mine[:cutting]), dp_swap(mine[cutting:])]
-    far_got = [dp_swap(got[:cutting]), dp_swap(got[cutting:])]
-
     rank = down_query.shape[1]
     part_a = down_query.shape[0] // head_parts
     part_m = down_mlp.shape[0] // head_parts
@@ -1459,13 +1453,32 @@
                 lax.dynamic_slice_in_dim(down_key, head * part_a, part_a, 0),
                 lax.dynamic_slice_in_dim(down_value, head * part_a, part_a, 0),
                 lax.dynamic_slice_in_dim(down_mlp, head * part_m, part_m, 0),
+                up_mlp.reshape(-1, rank),
+                proj_step.reshape(-1, rank),
                 state_columns((up_query, up_key, up_value), index).reshape(-1, rank),
             ],
             0,
         )
 
     pack = jnp.stack([small_pack(state), state_swap(small_pack(1 - state))], 0)
-    pack = jnp.concatenate([pack, dp_swap(pack)], 0)
+    pack_far = dp_swap(pack)
+    mine = hold(state_columns((w_query, w_key, w_value), state), pack_far)
+    got = state_swap(hold(state_columns((w_query, w_key, w_value), 1 - state), pack))
+    cutting = mine.shape[0] // 2
+    far_mine = [dp_swap(mine[:cutting]), dp_swap(mine[cutting:])]
+    far_got = [dp_swap(got[:cutting]), dp_swap(got[cutting:])]
+
+    share = rows // head_parts
+    sent = jnp.stack(
+        [
+            lax.dynamic_slice_in_dim(value, chunk_of(order) * share, share, 0)
+            for value, order in zip((hidden, embedding), orders)
+        ],
+        0,
+    )
+    sent = state_swap(sent)
+
+    pack = jnp.concatenate([pack, pack_far], 0)
     gain_rows = (split_a + 2 * split_m) // rank
     gains = pack[:, :gain_rows].reshape(4, -1).astype(full)
     attn_gain = gains[:, :split_a].reshape(-1)
@@ -1473,8 +1486,23 @@
     mlp_gain = jnp.concatenate([value[split_a : split_a + split_m] for value in gains])
     mixer_gain = jnp.concatenate([value[split_a + split_m :] for value in gains])
     down_end = gain_rows + 3 * part_a + part_m
+    step_width = proj_step.shape[1]
+    step_start = down_end + up_mlp.size // rank
+    step_end = step_start + proj_step.size // rank
+    mlp_upper = jnp.concatenate(
+        natural_quarters(
+            [pack[index, down_end:step_start].reshape(up_mlp.shape) for index in range(4)]
+        ),
+        0,
+    )
+    step_main = jnp.concatenate(
+        natural_quarters(
+            [pack[index, step_start:step_end].reshape(proj_step.shape) for index in range(4)]
+        ),
+        0,
+    )
     ups = natural_quarters(
-        [pack[index, down_end:].reshape(up_rows, 3 * half_cols) for index in range(4)]
+        [pack[index, step_end:].reshape(up_rows, 3 * half_cols) for index in range(4)]
     )
     ups = jnp.concatenate(ups, 0)
     column = lax.broadcasted_iota(jnp.int32, (1, 3 * half_cols), 1) // half_cols
@@ -1511,45 +1539,48 @@
     quarter = gain_attn.shape[0]
 
     def quarters(first, second):
-        both = jnp.concatenate([first, second], 1)
-        return jnp.concatenate(
-            [
-                lax.dynamic_slice_in_dim(both, (place ^ index) * quarter, quarter, 1)
-                for index in range(4)
-            ],
-            1,
-        ).astype(full)
-
-    normed_own = rms_norm(quarters(hidden, embedding), attn_gain).astype(low)
-    near_own, far_own = normed_own[:, :width], normed_own[:, width:]
-    joined_cut = [quarters(a, b) for a, b in zip(cut(hidden), cut(embedding))]
-
-    share = rows // head_parts
-
-    def sent_rows(value, order):
-        sent = lax.dynamic_slice_in_dim(value, chunk_of(order) * share, share, 0)
-        return jnp.concatenate([sent[:, quarter:], sent[:, :quarter]], 1)
-
-    sent = jnp.stack([sent_rows(near_own, orders[0]), sent_rows(far_own, orders[1])], 0)
-    sent = state_swap(hold(sent, far_mine[0]))
-    sent = hold(sent, far_mine[1])
-    near_other = gather_rows(sent[0], orders[0][1:], 0)
-    far_other = gather_rows(sent[1], orders[1][1:], 0)
-    near_other = hold(near_other, far_got[0])
-    near_other = gather_rows(near_other, orders[0][:1], 0)
-    far_other = gather_rows(far_other, orders[1][:1], 0)
+        parts = []
+        for index in range(4):
+            start = (state ^ (index % 2)) * quarter
+            part = [lax.dynamic_slice_in_dim(v, start, quarter, 1) for v in (first, second)]
+            parts.append(jnp.where(dp == index // 2, *part).astype(full))
+        return parts
+
+    def joint_scale(first, second):
+        squares = [jnp.sum(jnp.square(v.astype(full)), 1, keepdims=True) for v in (first, second)]
+        return lax.rsqrt((squares[0] + squares[1]) / (2 * width) + epsilon)
+
+    def normed_rows(first, second):
+        scale = joint_scale(first, second)
+        parts = [
+            (part * scale * attn_gain[index * quarter : (index + 1) * quarter]).astype(low)
+            for index, part in enumerate(quarters(first, second))
+        ]
+        return jnp.concatenate(parts[:2], 1), jnp.concatenate(parts[2:], 1)
+
+    near_own, far_own = normed_rows(hidden, embedding)
+    joined_cut = [
+        jnp.concatenate(quarters(a, b), 1) for a, b in zip(cut(hidden), cut(embedding))
+    ]
+
+    others = [gather_rows(sent[i], orders[i], 0) for i in range(2)]
+    others[0] = hold(others[0], others[1], cosine, sine, down_wide)
+    near_other, far_other = normed_rows(*others)
     main_near = jnp.concatenate([mine, got], 0)
+
+    def project_near(near, far):
+        reduced = (plain_dot(near, down_wide[:width]) + plain_dot(far, down_wide[width:])).astype(low)
+        return plain_dot(near, main_near) + plain_dot(reduced, up_wide), reduced
+
+    pre_own, red_own = project_near(near_own, far_own)
+    pre_other, red_other = project_near(near_other, far_other)
+    far_got[0] = hold(far_got[0], pre_own, pre_other)
     main_far = jnp.concatenate(far_mine + far_got, 0)
-
-    def project(near, far):
-        reduced = (plain_dot(near, down_wide[:width]) + plain_dot(far, down_wide[width:])).astype(low)
-        total = plain_dot(near, main_near) + plain_dot(reduced, up_wide)
-        return total + plain_dot(far, main_far), reduced
-
-    pre_own, red_own = project(near_own, far_own)
-    pre_other, red_other = project(near_other, far_other)
+    pre_own = pre_own + plain_dot(far_own, main_far)
+    pre_other = pre_other + plain_dot(far_other, main_far)
     queries, keys, values = rope(state, pre_own, pre_other, cosine, sine)
 
+    attn_output = hold(attn_output, *far_mine)
     attn_mine = lax.dynamic_slice_in_dim(attn_output, state * half_cols, half_cols, 0)
     attn_got = state_swap(
         lax.dynamic_slice_in_dim(attn_output, (1 - state) * half_cols, half_cols, 0)
@@ -1560,26 +1591,10 @@
         natural_quarters([attn_pair[0], attn_pair[1], attn_far[0], attn_far[1]]), 1
     )
     mlp_cut = mlp_input.shape[1] // 2
-    mlp_input = hold(mlp_input, far_got[1])
+    mlp_input = hold(mlp_input, far_got[0], far_got[1], *far_mine, attn_far)
     mlp_first = lax.all_gather(mlp_input[:, :mlp_cut], ZED, axis=0, tiled=True)
     mlp_second = lax.all_gather(mlp_input[:, mlp_cut:], ZED, axis=0, tiled=True)
     mlp_main = jnp.concatenate([mlp_first, mlp_second], 1)
-    mlp_proj = lax.all_gather(mlp_output, ZED, axis=1, tiled=True)
-    mixer_main = lax.all_gather(
-        jnp.concatenate([proj_inner, proj_gate], 1), ZED, axis=0, tiled=True
-    )
-    output_main = lax.all_gather(proj_output, ZED, axis=1, tiled=True)
-    step_width = proj_step.shape[1]
-    small = jnp.concatenate([up_mlp, proj_step.reshape(-1, up_mlp.shape[1])], 0)
-    small = hold(small, far_got[1])
-    small = jnp.stack([small, state_swap(small)], 0)
-    small_far = dp_swap(small)
-    small = natural_quarters([small[0], small[1], small_far[0], small_far[1]])
-    mlp_upper = jnp.concatenate([value[: up_mlp.shape[0]] for value in small], 0)
-    step_main = jnp.concatenate(
-        [value[up_mlp.shape[0] :].reshape(-1, step_width) for value in small], 0
-    )
-
     attended, lse = attend(queries, keys, values, segment, lows)
 
     attended = hold(attended, mlp_first)
@@ -1588,6 +1603,11 @@
         sum_row16(plain_dot(part, attn_proj).astype(low).reshape(2, middle, width), order)
         for part, order in zip(attended_halves, orders)
     ]
+    mlp_proj = lax.all_gather(mlp_output, ZED, axis=1, tiled=True)
+    mixer_main = lax.all_gather(
+        jnp.concatenate([proj_inner, proj_gate], 1), ZED, axis=0, tiled=True
+    )
+    output_main = lax.all_gather(proj_output, ZED, axis=1, tiled=True)
     first_cut = [
         value.astype(full) + good * branch
         for value, good, branch in zip(cut(hidden), valid_cut, branch_cut)
@@ -1727,16 +1747,13 @@
     inner_low = jnp.concatenate([inner_grad, gate_grad], 1).astype(low)
     inner_low = hold(inner_low, *out_cut)
     small_low = small_grad.astype(low)
-    mixer_sum = [
-        sum_rows(
-            (right_dot(inner_low[part], mixer_main) + right_dot(small_low[part], small_main)).astype(
-                low
-            ),
-            order,
-            0,
-        )
-        for part, order in zip((slice(0, middle), slice(middle, rows)), orders)
+    mixer_parts = [
+        (right_dot(inner_low[part], mixer_main) + right_dot(small_low[part], small_main)).astype(low)
+        for part in (slice(0, middle), slice(middle, rows))
     ]
+    mixer_sum = [sum_rows(part, order, 0) for part, order in zip(mixer_parts, orders)]
+    inner_later = hold(inner_low, *mixer_parts)
+    small_later = hold(small_low, *mixer_parts)
     upstream_cut = [value.astype(full) for value in cut(cot_own)]
     mixer_backs = [
         norm_back(value, mixer_gain, grad) for value, grad in zip(second_cut, mixer_sum)
@@ -1756,10 +1773,8 @@
         for pre, grad in zip(hidden_pre, mlp_grad)
     ]
     mlp_wide = jnp.concatenate([mlp_main, mlp_upper], 0)
-    mlp_sums = [
-        sum_rows(right_dot(grad, mlp_wide).astype(low), order, 0)
-        for grad, order in zip(hidden_grad, orders)
-    ]
+    mlp_parts = [right_dot(grad, mlp_wide).astype(low) for grad in hidden_grad]
+    mlp_sums = [sum_rows(part, order, 0) for part, order in zip(mlp_parts, orders)]
     middle_low = [value[:, width:].astype(low) for value in mlp_sums]
     mlp_backs = [
         norm_back(value, mlp_gain, total[:, :width] + right_dot(mid, mlp_down))
@@ -1772,26 +1787,21 @@
         for good, grad, order in zip(valid_cut, first_grad, orders)
     ]
 
-    layer_halves = [gather_row16(value, order) for value, order in zip(out_cut, orders)]
-    layer_out = jnp.stack(layer_halves, 1).reshape(length, width)
     attended_grad = jnp.concatenate(
         [right_dot(value, attn_proj).astype(low) for value in branch_halves], 0
     )
     query_back, key_back, value_back = attend_back(
         queries, keys, values, attended_grad, attended, lse, segment, lows
     )
-    attn_grad = left_dot(attended_halves[0], branch_halves[0]) + left_dot(
-        attended_halves[1], branch_halves[1]
-    )
-    out_attn = grad_pieces(attn_grad.astype(low), 0)
     pre_grad = rope_back(query_back, key_back, value_back, cosine, sine)
-    pre_grad = hold(pre_grad, *layer_halves, out_attn)
     main_wide = jnp.concatenate([main_near, main_far, up_wide], 0)
     joint = 2 * width
+    normed_parts = [
+        right_dot(part, main_wide).astype(low) for part in (pre_grad[:rows], pre_grad[rows:])
+    ]
     normed_sums = []
-    for part, order in zip((pre_grad[:rows], pre_grad[rows:]), orders):
-        total = right_dot(part, main_wide).astype(low).reshape(2, middle, -1)
-        total = sum_rows(total, order, 1)
+    for part, order in zip(normed_parts, orders):
+        total = sum_rows(part.reshape(2, middle, -1), order, 1)
         away = lax.dynamic_index_in_dim(total, 1 - state, 0, False).astype(low)
         away = jnp.concatenate([swap_quarters(away[:, :joint]), away[:, joint:]], 1)
         kept = lax.dynamic_index_in_dim(total, state, 0, False)
@@ -1821,8 +1831,11 @@
         return lax.psum_scatter(both, DP, scatter_dimension=0, tiled=True)
 
     beside = by_dp(main_grad(near_own, near_other, 1, 1), main_grad(far_own, far_other, 1, 3))
-    main_total = by_dp(main_grad(near_own, near_other, 0, 0), main_grad(far_own, far_other, 0, 2))
-    beside_got = state_swap(beside)
+    main_total = by_dp(
+        hold(main_grad(near_own, near_other, 0, 0), *normed_sums),
+        main_grad(far_own, far_other, 0, 2),
+    )
+    beside_got = state_swap(hold(beside, *normed_sums))
 
     def spread(own, got, index):
         part = slice(index * half_cols, (index + 1) * half_cols)
@@ -1848,53 +1861,58 @@
         )
 
     input_cut = []
-    for grad, back in zip(first_grad, joined_backs):
+    for grad, back, order in zip(first_grad, joined_backs, orders):
         joined_grad = natural_columns(back[0])
-        input_cut.append(
-            (
-                (grad + joined_grad[:, :width]).astype(low),
-                joined_grad[:, width:].astype(low),
-            )
-        )
-    grad_hidden, grad_embedding = (
-        jnp.concatenate(
-            [gather_rows(pieces[index], order, 0) for pieces, order in zip(input_cut, orders)], 0
-        )
-        for index in range(2)
-    )
+        joined_grad = jnp.concatenate([joined_grad[:, :width] + grad, joined_grad[:, width:]], 1)
+        input_cut.append(joined_grad.astype(low))
+    input_halves = [gather_rows(value, order, 0) for value, order in zip(input_cut, orders)]
+    layer_halves = [
+        gather_row16(hold(value, *input_halves), order) for value, order in zip(out_cut, orders)
+    ]
+    layer_out = jnp.concatenate(
+        [layer_halves[0][0], layer_halves[1][0], layer_halves[0][1], layer_halves[1][1]], 0
+    )
+    grad_hidden = jnp.concatenate([value[:, :width] for value in input_halves], 0)
+    grad_embedding = jnp.concatenate([value[:, width:] for value in input_halves], 0)
 
     def scatter(value, axis):
-        return lax.psum_scatter(
-            value.astype(low), ZED, scatter_dimension=axis, tiled=True
-        ).astype(full)
-
+        value = lax.psum_scatter(value.astype(low), ZED, scatter_dimension=axis, tiled=True)
+        return hold(value, *input_cut).astype(full)
+
+    attn_grad = left_dot(attended_halves[0], branch_halves[0]) + left_dot(
+        attended_halves[1], branch_halves[1]
+    )
+    out_attn = grad_pieces(hold(attn_grad.astype(low), *input_halves), 0)
     out_output = scatter(left_dot(gated, mix_grad), 1)
-    out_mixer = scatter(left_dot(mixer_normed, inner_low), 0)
+    out_mixer = scatter(left_dot(mixer_normed, inner_later), 0)
     mlp_normed_own = jnp.concatenate(mlp_normed, 0)
-    hidden_grad_own = jnp.concatenate(hidden_grad, 0)
+    hidden_grad_own = hold(jnp.concatenate(hidden_grad, 0), *mlp_parts)
+    mlp_grad_own = hold(jnp.concatenate(mlp_grad, 0), *mlp_parts)
     out_mlp_output = scatter(
-        left_dot(jnp.concatenate(activated, 0), jnp.concatenate(mlp_grad, 0)), 1
+        left_dot(jnp.concatenate(activated, 0), mlp_grad_own), 1
     )
     out_mlp_input = scatter(left_dot(mlp_normed_own, hidden_grad_own), 0)
     out_up_mlp = scatter(left_dot(jnp.concatenate(mlp_red, 0), hidden_grad_own), 0)
 
-    lows_halves = [gather_row16(value, order) for value, order in zip(lows_cut, orders)]
-    lows_own, lows_other = (
-        jnp.concatenate(
-            [lax.dynamic_index_in_dim(value, index, 0, False) for value in lows_halves], 0
+    def by_order(value):
+        bits = value.reshape((2,) * (len(orders[0])) + (piece, value.shape[1]))
+        count = len(orders[0])
+        turned = [0] + list(range(count - 1, 0, -1)) + [count, count + 1]
+        return bits.transpose(turned).reshape(value.shape)
+
+    lows_own = gather_rows(jnp.stack(lows_cut, 0), orders[0], 1)
+    lows_own = [lows_own[0], by_order(lows_own[1])]
+    lows_own = jnp.concatenate(lows_own, 0)
+    down_parts = [
+        left_dot(
+            lax.dynamic_slice_in_dim(value, index * quarter + head * part_a, part_a, 1), lows_own
         )
-        for index in (state, 1 - state)
-    )
-
-    def down_rows(own, other):
-        start = head * part_a
-        own = lax.dynamic_slice_in_dim(own, start, part_a, 1)
-        other = lax.dynamic_slice_in_dim(other, start, part_a, 1)
-        return left_dot(own, lows_own) + left_dot(other, lows_other)
-
-    down_sum = down_rows(near_own, near_other) + dp_swap(
-        down_rows(far_own, far_other).astype(low)
-    ).astype(full)
+        for value in (near_own, far_own)
+        for index in range(2)
+    ]
+    away = hold(jnp.stack([down_parts[1], down_parts[3]], 0).astype(low), *input_halves)
+    away = state_swap(away).astype(full)
+    down_sum = down_parts[0] + away[0] + dp_swap((down_parts[2] + away[1]).astype(low))
     down_all = gather_rows(down_sum.astype(low)[None], masks, 0).reshape(quarter, 3 * rank)
     down_all = down_all.astype(full)
     out_downs = [down_all[:, index * rank : (index + 1) * rank] for index in range(3)]
@@ -1906,53 +1924,53 @@
             jnp.zeros(shape, full), value, head * value.shape[axis], axis
         )
 
-    small_main_grad = left_dot(mixer_normed, small_low)
-    small_sum = jnp.concatenate(
-        [small_main_grad[:, mixer_heads:], placed(small_main_grad[:, :mixer_heads], 1)], 1
-    )
-    small_sum = lax.psum(small_sum, EVERY)
-    vector_grad = small_sum[:, : 2 * states]
-    out_step = lax.dynamic_slice(
-        small_sum,
-        (place * split_m, 2 * states + head * mixer_heads),
-        (split_m, mixer_heads),
-    )
+    small_main_grad = hold(left_dot(mixer_normed, small_later), *input_halves)
     normed_cut = [
         lax.dynamic_slice_in_dim(value, chunk_of(order) * piece, piece, 0)
         for value, order in zip(mlp_normed, orders)
     ]
     mlp_down_grad = left_dot(jnp.concatenate(normed_cut, 0), jnp.concatenate(middle_low, 0))
-    mlp_down_grad = lax.psum(hold(mlp_down_grad, main_total), EVERY)
-    out_down_mlp = lax.dynamic_slice_in_dim(mlp_down_grad, place * split_m, split_m, 0)
-
-    beside_got = hold(beside_got, grad_hidden)
+    pair_grad = jnp.concatenate([small_main_grad[:, mixer_heads:], mlp_down_grad], 1)
+    wide = pair_grad.shape[1]
+    heads_grad = placed(jnp.stack([grad_shift, grad_rate, grad_skip]), 1)
+    flat_sums = [
+        placed(small_main_grad[:, :mixer_heads].T, 0),
+        placed(grad_taps_x, 1),
+        placed(grad_gated_gain, 0),
+        grad_mlp_gain,
+        grad_mixer_gain,
+        jnp.concatenate([grad_taps_b, grad_taps_c], 1),
+        jnp.pad(heads_grad.reshape(-1), (0, -heads_grad.size % wide)),
+    ]
+    packed = jnp.concatenate([value.reshape(-1, wide) for value in flat_sums], 0)
+    lines = pair_grad.shape[0] // 8
+    packed = jnp.pad(packed, ((0, -packed.shape[0] % lines), (0, 0)))
+    pair_grad = jnp.concatenate([pair_grad, packed], 0)
+    pair_grad = sum_rows(pair_grad, masks, 0)
+    pair_grad = pair_grad + state_swap(pair_grad)
+    pair_grad = pair_grad + dp_swap(pair_grad)
+    pair_grad = gather_rows(pair_grad.astype(low), masks, 0).astype(full)
+    vector_grad = pair_grad[:width, : 2 * states]
+    out_down_mlp = lax.dynamic_slice(pair_grad, (place * split_m, 2 * states), (split_m, rank))
+    packed = pair_grad[width:]
+    pieces = []
+    for value in flat_sums:
+        count = value.size // wide
+        pieces.append(packed[:count].reshape(value.shape))
+        packed = packed[count:]
+    step_total, taps_x_total, gated_total, mlp_total, mixer_total, taps_total, head_total = pieces
+    head_total = head_total[: heads_grad.size].reshape(heads_grad.shape)
+
     out_all = [spread(main_total, beside_got, index) for index in range(3)]
     out_main = [value[:quarter] for value in out_all]
     out_up = [value[quarter:] for value in out_all]
-    flat_sums = [
-        placed(grad_taps_x, 1),
-        placed(jnp.stack([grad_shift, grad_rate, grad_skip]), 1),
-        placed(grad_gated_gain, 0),
-        jnp.concatenate([grad_taps_b, grad_taps_c], 1),
-        natural_columns(grad_attn_gain),
-        grad_mlp_gain,
-        grad_mixer_gain,
-    ]
-
     once = (head == 0).astype(full)
     square_sum = jnp.zeros((), full)
     for value in out_main + out_up + [out_attn, out_mlp_input, out_up_mlp, out_mlp_output]:
         square_sum = square_sum + jnp.sum(value * value)
     for value in out_downs + [out_down_mlp]:
         square_sum = square_sum + once * jnp.sum(value * value)
-    totals = lax.psum(
-        jnp.concatenate([value.reshape(-1) for value in flat_sums] + [square_sum[None]]), EVERY
-    )
-    pieces = []
-    for value in flat_sums:
-        pieces.append(totals[: value.size].reshape(value.shape))
-        totals = totals[value.size :]
-    taps_x_total, head_total, gated_total, taps_total, attn_total, mlp_total, mixer_total = pieces
+    square_total, attn_total = lax.psum((square_sum, natural_columns(grad_attn_gain)), EVERY)
 
     def of_head(value, size):
         return lax.dynamic_slice_in_dim(value, head * size, size, value.ndim - 1)
@@ -1961,6 +1979,9 @@
         return lax.dynamic_slice_in_dim(value, place * size, size)
 
     head_total = of_head(head_total, mixer_heads)
+    out_step = lax.dynamic_slice(
+        step_total, (head * mixer_heads, place * split_m), (mixer_heads, split_m)
+    ).T
     return (
         layer_out,
         grad_hidden,
@@ -1995,7 +2016,7 @@
         head_total[2],
         of_head(gated_total, inner_width),
         out_output,
-        jnp.sqrt(totals[0]),
+        jnp.sqrt(square_total),
     )
 
 

time: 1870 us -> 1500 us (0.80)
  waiting for transfers between devices: 958 us -> 555 us
  blocking collectives: 0 us -> 38.6 us
  local copies, waits for them, and re-layouts: 201 us -> 171 us
    psum x2 -> x0, waiting for transfers between devices: 250 us -> none  [the longest x1 126 us: fast_device(): lax.psum(jnp.concatenate([value.reshape(-1) for value in flat_sums] + [sq...]
    ppermute x9, waiting for transfers between devices: 178 us -> 86.9 us  [dp_swap(): return lax.ppermute(value, DP, [(0, 1), (1, 0)])]
    ppermute x17 -> x16, waiting for transfers between devices: 198 us -> 119 us  [state_swap(): return lax.ppermute(value, STATE, [(0, 1), (1, 0)])]
    ppermute x99 -> x96, waiting for transfers between devices: 278 us -> 344 us  [head_swap(): return lax.ppermute(value, HEAD, [(i, i ^ mask) for i in range(count)])]
    reduce_scatter x2, waiting for transfers between devices: 50.8 us -> 0.01 us  [by_dp(): return lax.psum_scatter(both, DP, scatter_dimension=0, tiled=True)]
    psum x0 -> x1, blocking collectives: none -> 38.6 us  [fast_device(): lax.psum((square_sum, natural_columns(grad_attn_gain)), EVERY)]
    convert_element_type x4 -> x6, other arithmetic: 7.14 us -> 28.6 us  [the longest x2 25.3 us: normed_rows(): (part * scale * attn_gain[index * quarter:(index + 1) * quarter]).astype(...]
    unnamed x850 -> x890, local copies, waits for them, and re-layouts: 100 us -> 87.1 us
  transfers between devices with their start and end apart: 143 -> 137, of which waited for: 69 -> 68; matrix products, arithmetic and copies ran while one was open for 30% -> 38% of each run, Pallas kernels for 5% -> 5%
where the time goes in v4:
time: 1500 us; the launch traced here: 1490 us
  waiting for transfers between devices  555 us (37%)
  other arithmetic  279 us (19%)
  matrix products  206 us (14%)
  local copies, waits for them, and re-layouts  171 us (11%)
  starting transfers between devices  126 us (8%)
  Pallas kernels  83 us (6%)
  blocking collectives  38.6 us (3%)
  between operations  33 us (2%)
    ppermute x96, waiting for transfers between devices, head_swap(): return lax.ppermute(value, HEAD, [(i, i ^ mask) for i in range(count)])  344 us
    ppermute x16, waiting for transfers between devices, state_swap(): return lax.ppermute(value, STATE, [(0, 1), (1, 0)])  119 us
    unnamed x890, local copies, waits for them, and re-layouts  87.1 us
    ppermute x9, waiting for transfers between devices, dp_swap(): return lax.ppermute(value, DP, [(0, 1), (1, 0)])  86.9 us
    dot_general x24, matrix products, plain_dot(): return jnp.dot(left, right, preferred_element_type=jnp.float32)  80.1 us
    ppermute x96, starting transfers between devices, head_swap(): return lax.ppermute(value, HEAD, [(i, i ^ mask) for i in range(count)])  76 us
    dot_general x23, matrix products, left_dot(): lax.dot_general(left, right, (((0,), (0,)), ((), ())), preferred_element_...  66.9 us
    dot_general x17, matrix products, right_dot(): lax.dot_general(left, right, (((1,), (1,)), ((), ())), preferred_element_...  58.8 us
  transfers between devices with their start and end apart: 137, of which 68 were waited for; matrix products, arithmetic and copies ran while one was open for 38% of the time, Pallas kernels for 5%

profile of v4, /device:TPU:0, one launch (start us, length us, event | category | flops | bytes accessed | tf_op | source)
XLA Modules:
  0.0 1492.0 jit_solution(1463109565329917067)
XLA Ops:
  37.9 8.4 collective-permute-done
  51.3 19.6 %collective-permute-done.1.refs_1_ = bf16[2,944,128]{2,1,0:T(8,128)(2,1)S(1)} collective-permute-done((bf16[2,944,128]{2,1,0:T(8,128)(2,1)}, bf16[2,944,128]{2,1,0:T(8,128)(2,1)S(1)}, u32[]{:S(2)}, u32[]{:S(2)}) %collective-permute-start.1) | collective-permute-done | bytes 483360 | tf_op jit(solution)/shard_map/ppermute | solution.py:636
  77.7 7.9 multiply_convert_fusion.7
  96.5 33.5 %collective-permute-done.6.refs_1_.refs_3_ = bf16[512,768]{1,0:T(8,128)(2,1)} collective-permute-done((bf16[512,768]{1,0:T(8,128)(2,1)}, bf16[512,768]{1,0:T(8,128)(2,1)}, u32[]{:S(2)}, u32[]{:S(2)}) %collective-permute-start.6) | collective-permute-done | bytes 786464 | tf_op jit(solution)/shard_map/ppermute | solution.py:636
  131.3 15.1 %collective-permute-done.7.refs_2_.refs_4_ = bf16[512,768]{1,0:T(8,128)(2,1)} collective-permute-done((bf16[512,768]{1,0:T(8,128)(2,1)}, bf16[512,768]{1,0:T(8,128)(2,1)}, u32[]{:S(2)}, u32[]{:S(2)}) %collective-permute-start.7) | collective-permute-done | bytes 786464 | tf_op jit(solution)/shard_map/ppermute | solution.py:636
  152.5 14.3 collective-permute-done.17
  179.1 35.7 %collective-permute-done.5 = bf16[4,4,448,128]{3,2,1,0:T(8,128)(2,1)S(1)} collective-permute-done((bf16[4,4,448,128]{3,2,1,0:T(8,128)(2,1)S(1)}, bf16[4,4,448,128]{3,2,1,0:T(8,128)(2,1)S(1)}, u32[]{:S(2)}, u32[]{:S(2)}) %collective-permute-start.5) | collective-permute-done | bytes 1835040 | tf_op jit(solution)/shard_map/ppermute | solution.py:628
  227.9 6.5 fusion.83.refs_1_
  247.2 17.4 %multiply_convert_fusion.3 = (bf16[1024,1024]{1,0:T(8,128)(2,1)S(1)}, bf16[1024,1024]{1,0:T(8,128)(2,1)S(1)}, bf16[1024,1024]{1,0:T(8,128)(2,1)S(1)}, bf16[1024,1024]{1,0:T(8,128)(2,1)S(1)}) fusion(f32[1024]{0:T(1024)S(1)} %add_rsqrt_fusion, f32[1024]{0:T(1024)S(1)} %bitcast.451, pred[]{:T(512)S(6)} %eq.173, bf16[1024,2048]{1,0:T(8,128)(2,1)S(1)} %copy-done.35, ...), kind=kLoop, calls=%fused_computation.75 | loop fusion | flops 37748736 | bytes 16797706 | tf_op jit(solution)/shard_map/convert_element_type | solution.py:1556
  271.2 6.5 fusion.84.refs_2_
  288.0 6.7 fusion.70.other_ref
  302.7 18.9 %shard_map.590 = (bf16[2048,256]{1,0:T(8,128)(2,1)S(1)}, f32[2,1,2048]{2,1,0:T(1,128)S(1)}) custom-call(s32[8]{0:T(128)S(1)} %and_select_fusion.low_ref, bf16[2048,256]{1,0:T(8,128)(2,1)S(1)} %get-tuple-element.74.q_ref, bf16[2048,256]{1,0:T(8,128)(2,1)S(1)} %get-tuple-element.75.k_ref, bf16[2048,256]{1,0:T(8,128)(2,1)S(1)} %get-tuple-element.76.v_ref, ...), custom_call_target="tpu_custom_call" | custom-call | flops 23622320128 | bytes 4194304 | tf_op jit(solution)/shard_map/pallas_call | solution.py:825
  350.7 18.7 %collective-permute-done.33 = bf16[2,128,2048]{2,1,0:T(8,128)(2,1)S(1)} collective-permute-done((bf16[2,128,2048]{2,1,0:T(8,128)(2,1)S(1)}, bf16[2,128,2048]{2,1,0:T(8,128)(2,1)S(1)}, u32[]{:S(2)}, u32[]{:S(2)}) %collective-permute-start.33) | collective-permute-done | bytes 1048608 | tf_op jit(solution)/shard_map/ppermute | solution.py:628
  374.9 9.6 collective-permute-done.34
  390.5 25.0 %collective-permute-done.35 = bf16[64,2048]{1,0:T(8,128)(2,1)S(1)} collective-permute-done((bf16[64,2048]{1,0:T(8,128)(2,1)S(1)}, bf16[64,2048]{1,0:T(8,128)(2,1)S(1)}, u32[]{:S(2)}, u32[]{:S(2)}) %collective-permute-start.35) | collective-permute-done | bytes 262176 | tf_op jit(solution)/shard_map/ppermute | solution.py:632
  415.6 21.9 %collective-permute-done.22 = bf16[64,2048]{1,0:T(8,128)(2,1)S(1)} collective-permute-done((bf16[64,2048]{1,0:T(8,128)(2,1)S(1)}, bf16[64,2048]{1,0:T(8,128)(2,1)S(1)}, u32[]{:S(2)}, u32[]{:S(2)}) %collective-permute-start.22) | collective-permute-done | bytes 262176 | tf_op jit(solution)/shard_map/ppermute | solution.py:632
  455.5 6.7 collective-permute-done.24
  469.8 9.1 multiply_convert_fusion.11
  489.9 8.9 multiply_convert_fusion.10
  510.1 9.1 collective-permute-done.27
  542.7 8.0 collective-permute-done.30
  564.9 8.9 fusion.255
  599.0 7.1 shard_map.595
  608.4 8.2 multiply_reduce_fusion.16
  641.6 17.1 %shard_map.597 = (f32[1024,512]{1,0:T(8,128)S(1)}, f32[1024,8]{1,0:T(8,128)S(1)}, f32[1024,8]{1,0:T(8,128)S(1)}, f32[8,1024]{1,0:T(8,128)S(1)}, f32[1024,64]{1,0:T(8,128)S(1)}, /*index=5*/f32[1024,64]{1,0:T(8,128)S(1)}) custom-call(s32[5]{0:T(128)S(1)} %get-tuple-element.658.ends_ref, f32[1024,512]{1,0:T(8,128)S(1)} %get-tuple-element.308.x_ref, ...), custom_call_target="tpu_custom_call" | custom-call | flops 19327352832 | bytes 4194304 | tf_op jit(solution)/shard_map/pallas_call | solution.py:1271
  686.1 11.4 collective-permute-done.51
  733.3 10.3 collective-permute-done.72
  777.2 6.8 collective-permute-done.75
  807.4 9.4 convolution_convert_fusion.7
  824.0 11.1 collective-permute-done.78
  851.7 7.2 collective-permute-done.67
  880.3 19.5 %collective-permute-done.69 = bf16[2,128,2048]{2,1,0:T(8,128)(2,1)S(1)} collective-permute-done((bf16[2,128,2048]{2,1,0:T(8,128)(2,1)S(1)}, bf16[2,128,2048]{2,1,0:T(8,128)(2,1)S(1)}, u32[]{:S(2)}, u32[]{:S(2)}) %collective-permute-start.69) | collective-permute-done | bytes 1048608 | tf_op jit(solution)/shard_map/ppermute | solution.py:628
  908.3 9.5 fusion.8
  931.9 25.3 %shard_map.599 = (f32[2048,256]{1,0:T(8,128)S(1)}, f32[2048,256]{1,0:T(8,128)S(1)}, f32[2048,256]{1,0:T(8,128)S(1)}) custom-call(s32[8]{0:T(128)S(1)} %copy-done.32, bf16[2048,256]{1,0:T(8,128)(2,1)S(1)} %copy-done.26, bf16[2048,256]{1,0:T(8,128)(2,1)S(1)} %copy-done.28, bf16[2048,256]{1,0:T(8,128)(2,1)S(1)} %copy-done.30, ...), custom_call_target="tpu_custom_call" | custom-call | flops 32212254720 | bytes 10485760 | tf_op jit(solution)/shard_map/pallas_call | solution.py:902
  1006.6 11.1 convolution_convert_fusion.1
  1023.1 11.7 convolution_convert_fusion
  1073.0 38.5 %collective-permute-done.85 = bf16[2,128,4480]{2,1,0:T(8,128)(2,1)} collective-permute-done((bf16[2,128,4480]{2,1,0:T(8,128)(2,1)}, bf16[2,128,4480]{2,1,0:T(8,128)(2,1)}, u32[]{:S(2)}, u32[]{:S(2)}) %collective-permute-start.85) | collective-permute-done | bytes 2293792 | tf_op jit(solution)/shard_map/ppermute | solution.py:628
  1119.2 23.1 %collective-permute-done.86 = bf16[2,64,4480]{2,1,0:T(8,128)(2,1)S(1)} collective-permute-done((bf16[2,64,4480]{2,1,0:T(8,128)(2,1)S(1)}, bf16[2,64,4480]{2,1,0:T(8,128)(2,1)S(1)}, u32[]{:S(2)}, u32[]{:S(2)}) %collective-permute-start.86) | collective-permute-done | bytes 1146912 | tf_op jit(solution)/shard_map/ppermute | solution.py:628
  1147.5 13.8 collective-permute-done.94
  1162.8 7.2 collective-permute-done.87
  1207.3 17.3 %collective-permute-done.96 = bf16[128,4096]{1,0:T(8,128)(2,1)S(1)} collective-permute-done((bf16[128,4096]{1,0:T(8,128)(2,1)S(1)}, bf16[128,4096]{1,0:T(8,128)(2,1)S(1)}, u32[]{:S(2)}, u32[]{:S(2)}) %collective-permute-start.96) | collective-permute-done | bytes 1048608 | tf_op jit(solution)/shard_map/ppermute | solution.py:628
  1276.0 8.2 collective-permute-start.115
  1289.4 12.3 collective-permute-done.102
  1302.8 8.4 collective-permute-done.111
  1315.4 15.8 %collective-permute-done.113 = bf16[2,128,384]{2,1,0:T(8,128)(2,1)S(1)} collective-permute-done((bf16[2,128,384]{2,1,0:T(8,128)(2,1)S(1)}, bf16[2,128,384]{2,1,0:T(8,128)(2,1)S(1)}, u32[]{:S(2)}, u32[]{:S(2)}) %collective-permute-start.113) | collective-permute-done | bytes 196640 | tf_op jit(solution)/shard_map/ppermute | solution.py:628
  1367.5 10.3 collective-permute-done.121
  1383.4 7.0 collective-permute-done.123
  1426.4 38.6 %all-reduce.29 = (f32[4096]{0:T(1024)S(1)}, f32[]{:T(128)}) all-reduce(f32[4096]{0:T(1024)S(1)} %pad_maximum_fusion.143, f32[]{:T(128)S(6)} %add.1250), channel_id=1, replica_groups=mesh['dp'=2,'head'=8,'state'=2] {'dp','head','state'}, use_global_device_ids=true, to_apply=%region_24.25 | all-reduce | flops 4097 | bytes 32776 | tf_op jit(solution)/shard_map/psum | solution.py:1973
  (1706 shorter events, 776.5 us)
Async XLA Ops:
  7.2 317.6 %all-gather.6.cloned.1.call-start = ((), (), s32[]{:S(2)}) async-start(), calls=%async_computation.7 | async-start | bytes 2621440 | tf_op jit(solution)/shard_map/all_gather | solution.py:1595
  14.7 70.9 %collective-permute-start.9 = (bf16[2,128,2048]{2,1,0:T(8,128)(2,1)}, bf16[2,128,2048]{2,1,0:T(8,128)(2,1)}, u32[]{:S(2)}, u32[]{:S(2)}) collective-permute-start(bf16[2,128,2048]{2,1,0:T(8,128)(2,1)} %pad_maximum_fusion.76), channel_id=1, source_target_pairs={{0,1},{1,0},{2,3},{3,2},{4,5},{5,4},{6,7},{7,6},{8,9},{9,8},{10,11... | collective-permute-start | bytes 3145736 | tf_op jit(solution)/shard_map/ppermute | solution.py:632
  74.6 55.4 %collective-permute-start.6 = (bf16[512,768]{1,0:T(8,128)(2,1)}, bf16[512,768]{1,0:T(8,128)(2,1)}, u32[]{:S(2)}, u32[]{:S(2)}) collective-permute-start(bf16[512,768]{1,0:T(8,128)(2,1)} %get-tuple-element.432), channel_id=1, source_target_pairs={{0,16},{16,0},{1,17},{17,1},{2,18},{18,2},{3,19},{19,3},{4,20},{20... | collective-permute-start | bytes 2359304 | tf_op jit(solution)/shard_map/ppermute | solution.py:636
  74.6 71.8 %collective-permute-start.7 = (bf16[512,768]{1,0:T(8,128)(2,1)}, bf16[512,768]{1,0:T(8,128)(2,1)}, u32[]{:S(2)}, u32[]{:S(2)}) collective-permute-start(bf16[512,768]{1,0:T(8,128)(2,1)} %get-tuple-element.433), channel_id=1, source_target_pairs={{0,16},{16,0},{1,17},{17,1},{2,18},{18,2},{3,19},{19,3},{4,20},{20... | collective-permute-start | bytes 2359304 | tf_op jit(solution)/shard_map/ppermute | solution.py:636
  88.7 58.9 %collective-permute-start.10 = (bf16[128,2048]{1,0:T(8,128)(2,1)}, bf16[128,2048]{1,0:T(8,128)(2,1)}, u32[]{:S(2)}, u32[]{:S(2)}) collective-permute-start(bf16[128,2048]{1,0:T(8,128)(2,1)} %get-tuple-element.489), channel_id=1, source_target_pairs={{0,8},{2,10},{4,12},{6,14},{8,0},{10,2},{12,4},{14,6},{1,9},{3,11}... | collective-permute-start | bytes 1572872 | tf_op jit(solution)/shard_map/ppermute | solution.py:628
  90.1 57.6 %collective-permute-start.13 = (bf16[128,2048]{1,0:T(8,128)(2,1)}, bf16[128,2048]{1,0:T(8,128)(2,1)}, u32[]{:S(2)}, u32[]{:S(2)}) collective-permute-start(bf16[128,2048]{1,0:T(8,128)(2,1)} %get-tuple-element.488), channel_id=1, source_target_pairs={{0,4},{2,6},{4,0},{6,2},{8,12},{10,14},{12,8},{14,10},{1,5},{3,7},... | collective-permute-start | bytes 1572872 | tf_op jit(solution)/shard_map/ppermute | solution.py:628
  92.4 79.7 %collective-permute-start.2 = (bf16[1024,768]{1,0:T(8,128)(2,1)}, bf16[1024,768]{1,0:T(8,128)(2,1)}, u32[]{:S(2)}, u32[]{:S(2)}) collective-permute-start(bf16[1024,768]{1,0:T(8,128)(2,1)} %shard_map.586), channel_id=1, source_target_pairs={{0,1},{1,0},{2,3},{3,2},{4,5},{5,4},{6,7},{7,6},{8,9},{9,8},{10,11... | collective-permute-start | bytes 4718600 | tf_op jit(solution)/shard_map/ppermute | solution.py:632
  130.0 40.0 %collective-permute-start.4 = (bf16[2,4,448,128]{3,2,1,0:T(8,128)(2,1)}, bf16[2,4,448,128]{3,2,1,0:T(8,128)(2,1)}, u32[]{:S(2)}, u32[]{:S(2)}) collective-permute-start(bf16[2,4,448,128]{3,2,1,0:T(8,128)(2,1)} %pad_maximum_fusion.97), channel_id=1, source_target_pairs={{0,4},{2,6},{4,0},{6,2},{8,12},{10,14},{12,8},{14,10},{1,5},{3,7},... | collective-permute-start | bytes 2752520 | tf_op jit(solution)/shard_map/ppermute | solution.py:628
  149.4 25.8 %collective-permute-start.11 = (bf16[256,2048]{1,0:T(8,128)(2,1)S(1)}, bf16[256,2048]{1,0:T(8,128)(2,1)S(1)}, u32[]{:S(2)}, u32[]{:S(2)}) collective-permute-start(bf16[256,2048]{1,0:T(8,128)(2,1)S(1)} %pad_maximum_fusion.77), channel_id=1, source_target_pairs={{0,4},{2,6},{4,0},{6,2},{8,12},{10,14},{12,8},{14,10},{1,5},{3,7},... | collective-permute-start | bytes 3145736 | tf_op jit(solution)/shard_map/ppermute | solution.py:628
  150.9 27.3 %collective-permute-start.14 = (bf16[256,2048]{1,0:T(8,128)(2,1)S(1)}, bf16[256,2048]{1,0:T(8,128)(2,1)S(1)}, u32[]{:S(2)}, u32[]{:S(2)}) collective-permute-start(bf16[256,2048]{1,0:T(8,128)(2,1)S(1)} %pad_maximum_fusion.78), channel_id=1, source_target_pairs={{0,8},{2,10},{4,12},{6,14},{8,0},{10,2},{12,4},{14,6},{1,9},{3,11}... | collective-permute-start | bytes 3145736 | tf_op jit(solution)/shard_map/ppermute | solution.py:628
  167.7 110.0 %collective-permute-start.18 = (bf16[2,256,512]{2,1,0:T(8,128)(2,1)}, bf16[2,256,512]{2,1,0:T(8,128)(2,1)}, u32[]{:S(2)}, u32[]{:S(2)}) collective-permute-start(bf16[2,256,512]{2,1,0:T(8,128)(2,1)} %pad_maximum_fusion.108), channel_id=1, source_target_pairs={{0,16},{16,0},{1,17},{17,1},{2,18},{18,2},{3,19},{19,3},{4,20},{20... | collective-permute-start | bytes 1572872 | tf_op jit(solution)/shard_map/ppermute | solution.py:636
  171.5 43.3 %collective-permute-start.5 = (bf16[4,4,448,128]{3,2,1,0:T(8,128)(2,1)S(1)}, bf16[4,4,448,128]{3,2,1,0:T(8,128)(2,1)S(1)}, u32[]{:S(2)}, u32[]{:S(2)}) collective-permute-start(bf16[4,4,448,128]{3,2,1,0:T(8,128)(2,1)S(1)} %pad_maximum_fusion.45), channel_id=1, source_target_pairs={{0,8},{2,10},{4,12},{6,14},{8,0},{10,2},{12,4},{14,6},{1,9},{3,11}... | collective-permute-start | bytes 5505032 | tf_op jit(solution)/shard_map/ppermute | solution.py:628
  174.7 103.0 %collective-permute-start.8 = (bf16[512,768]{1,0:T(8,128)(2,1)}, bf16[512,768]{1,0:T(8,128)(2,1)}, u32[]{:S(2)}, u32[]{:S(2)}) collective-permute-start(bf16[512,768]{1,0:T(8,128)(2,1)} %get-tuple-element.438), channel_id=1, source_target_pairs={{0,16},{16,0},{1,17},{17,1},{2,18},{18,2},{3,19},{19,3},{4,20},{20... | collective-permute-start | bytes 2359304 | tf_op jit(solution)/shard_map/ppermute | solution.py:636
  175.2 102.5 %collective-permute-start.16 = (bf16[512,768]{1,0:T(8,128)(2,1)}, bf16[512,768]{1,0:T(8,128)(2,1)}, u32[]{:S(2)}, u32[]{:S(2)}) collective-permute-start(bf16[512,768]{1,0:T(8,128)(2,1)} %get-tuple-element.439), channel_id=1, source_target_pairs={{0,16},{16,0},{1,17},{17,1},{2,18},{18,2},{3,19},{19,3},{4,20},{20... | collective-permute-start | bytes 2359304 | tf_op jit(solution)/shard_map/ppermute | solution.py:636
  178.2 56.2 %collective-permute-start.12 = (bf16[512,2048]{1,0:T(8,128)(2,1)S(1)}, bf16[512,2048]{1,0:T(8,128)(2,1)S(1)}, u32[]{:S(2)}, u32[]{:S(2)}) collective-permute-start(bf16[512,2048]{1,0:T(8,128)(2,1)S(1)} %pad_maximum_fusion.33), channel_id=1, source_target_pairs={{0,2},{2,0},{4,6},{6,4},{8,10},{10,8},{12,14},{14,12},{1,3},{3,1},... | collective-permute-start | bytes 6291464 | tf_op jit(solution)/shard_map/ppermute | solution.py:628
  280.1 160.2 %all-gather.8.cloned.1.call-start = ((), (), s32[]{:S(2)}) async-start(), calls=%async_computation.8 | async-start | bytes 2621440 | tf_op jit(solution)/shard_map/all_gather | solution.py:1596
  280.8 198.1 %all-gather.10.cloned.1.call-start = ((), (), s32[]{:S(2)}) async-start(), calls=%async_computation.9 | async-start | bytes 5242880 | tf_op jit(solution)/shard_map/all_gather | solution.py:1606
  281.6 283.3 %all-gather.12.cloned.1.call-start = ((), (), s32[]{:S(2)}) async-start(), calls=%async_computation.10 | async-start | bytes 5242880 | tf_op jit(solution)/shard_map/all_gather | solution.py:1607
  282.7 325.6 %all-gather.14.cloned.1.call-start = ((), (), s32[]{:S(2)}) async-start(), calls=%async_computation.11 | async-start | bytes 2621440 | tf_op jit(solution)/shard_map/all_gather | solution.py:1610
  348.3 26.1 %collective-permute-start.20 = (bf16[2,128,2048]{2,1,0:T(8,128)(2,1)S(1)}, bf16[2,128,2048]{2,1,0:T(8,128)(2,1)S(1)}, u32[]{:S(2)}, u32[]{:S(2)}) collective-permute-start(bf16[2,128,2048]{2,1,0:T(8,128)(2,1)S(1)} %dynamic-slice_convert_fusion.5), channel_id=1, source_target_pairs={{0,4},{2,6},{4,0},{6,2},{8,12},{10,14},{12,8},{14,10},{1,5},{3,7},... | collective-permute-start | bytes 3145736 | tf_op jit(solution)/shard_map/ppermute | solution.py:628
  384.7 30.9 %collective-permute-start.35 = (bf16[64,2048]{1,0:T(8,128)(2,1)S(1)}, bf16[64,2048]{1,0:T(8,128)(2,1)S(1)}, u32[]{:S(2)}, u32[]{:S(2)}) collective-permute-start(bf16[64,2048]{1,0:T(8,128)(2,1)S(1)} %fusion.159), channel_id=1, source_target_pairs={{0,1},{1,0},{2,3},{3,2},{4,5},{5,4},{6,7},{7,6},{8,9},{9,8},{10,11... | collective-permute-start | bytes 786440 | tf_op jit(solution)/shard_map/ppermute | solution.py:632
  386.6 50.8 %collective-permute-start.22 = (bf16[64,2048]{1,0:T(8,128)(2,1)S(1)}, bf16[64,2048]{1,0:T(8,128)(2,1)S(1)}, u32[]{:S(2)}, u32[]{:S(2)}) collective-permute-start(bf16[64,2048]{1,0:T(8,128)(2,1)S(1)} %fusion.158), channel_id=1, source_target_pairs={{0,1},{1,0},{2,3},{3,2},{4,5},{5,4},{6,7},{7,6},{8,9},{9,8},{10,11... | collective-permute-start | bytes 786440 | tf_op jit(solution)/shard_map/ppermute | solution.py:632
  502.7 673.7 %reduce-scatter.20.cloned.1.call-start = ((), (), s32[]{:S(2)}) async-start(), calls=%async_computation.18 | async-start | bytes 2621440 | tf_op jit(solution)/shard_map/reduce_scatter | solution.py:1879
  638.6 42.0 %collective-permute-start.50 = (bf16[256,2048]{1,0:T(8,128)(2,1)}, bf16[256,2048]{1,0:T(8,128)(2,1)}, u32[]{:S(2)}, u32[]{:S(2)}) collective-permute-start(bf16[256,2048]{1,0:T(8,128)(2,1)} %constant_dynamic-slice_fusion.16), channel_id=1, source_target_pairs={{0,2},{2,0},{4,6},{6,4},{8,10},{10,8},{12,14},{14,12},{1,3},{3,1},... | collective-permute-start | bytes 3145736 | tf_op jit(solution)/shard_map/ppermute | solution.py:628
  641.0 43.0 %collective-permute-start.55 = (bf16[256,2048]{1,0:T(8,128)(2,1)}, bf16[256,2048]{1,0:T(8,128)(2,1)}, u32[]{:S(2)}, u32[]{:S(2)}) collective-permute-start(bf16[256,2048]{1,0:T(8,128)(2,1)} %constant_dynamic-slice_fusion.15), channel_id=1, source_target_pairs={{0,2},{2,0},{4,6},{6,4},{8,10},{10,8},{12,14},{14,12},{1,3},{3,1},... | collective-permute-start | bytes 3145736 | tf_op jit(solution)/shard_map/ppermute | solution.py:628
  727.4 451.1 %reduce-scatter.18.cloned.1.call-start = ((), (), s32[]{:S(2)}) async-start(), calls=%async_computation.17 | async-start | bytes 5242880 | tf_op jit(solution)/shard_map/reduce_scatter | solution.py:1879
  766.7 416.0 %reduce-scatter.16.cloned.1.call-start = ((), (), s32[]{:S(2)}) async-start(), calls=%async_computation.16 | async-start | bytes 5242880 | tf_op jit(solution)/shard_map/reduce_scatter | solution.py:1879
  816.8 369.5 %reduce-scatter.12.cloned.1.call-start = ((), (), s32[]{:S(2)}) async-start(), calls=%async_computation.14 | async-start | bytes 5242880 | tf_op jit(solution)/shard_map/reduce_scatter | solution.py:1879
  871.9 27.9 %collective-permute-start.69 = (bf16[2,128,2048]{2,1,0:T(8,128)(2,1)S(1)}, bf16[2,128,2048]{2,1,0:T(8,128)(2,1)S(1)}, u32[]{:S(2)}, u32[]{:S(2)}) collective-permute-start(bf16[2,128,2048]{2,1,0:T(8,128)(2,1)S(1)} %pad_maximum_fusion.88), channel_id=1, source_target_pairs={{0,4},{2,6},{4,0},{6,2},{8,12},{10,14},{12,8},{14,10},{1,5},{3,7},... | collective-permute-start | bytes 3145736 | tf_op jit(solution)/shard_map/ppermute | solution.py:628
  917.8 272.2 %reduce-scatter.10.cloned.1.call-start = ((), (), s32[]{:S(2)}) async-start(), calls=%async_computation.13 | async-start | bytes 4866048 | tf_op jit(solution)/shard_map/reduce_scatter | solution.py:1831
  973.3 222.1 %reduce-scatter.14.cloned.1.call-start = ((), (), s32[]{:S(2)}) async-start(), calls=%async_computation.15 | async-start | bytes 327680 | tf_op jit(solution)/shard_map/reduce_scatter | solution.py:1879
  1001.5 391.9 %reduce-scatter.8.cloned.1.call-start = ((), (), s32[]{:S(2)}) async-start(), calls=%async_computation.12 | async-start | bytes 4866048 | tf_op jit(solution)/shard_map/reduce_scatter | solution.py:1831
  1022.7 31.6 %collective-permute-start.84 = (bf16[2,256,4480]{2,1,0:T(8,128)(2,1)}, bf16[2,256,4480]{2,1,0:T(8,128)(2,1)}, u32[]{:S(2)}, u32[]{:S(2)}) collective-permute-start(bf16[2,256,4480]{2,1,0:T(8,128)(2,1)} %constant_dynamic-slice_fusion.10), channel_id=1, source_target_pairs={{0,2},{2,0},{4,6},{6,4},{8,10},{10,8},{12,14},{14,12},{1,3},{3,1},... | collective-permute-start | bytes 13762568 | tf_op jit(solution)/shard_map/ppermute | solution.py:628
  1059.1 52.4 %collective-permute-start.85 = (bf16[2,128,4480]{2,1,0:T(8,128)(2,1)}, bf16[2,128,4480]{2,1,0:T(8,128)(2,1)}, u32[]{:S(2)}, u32[]{:S(2)}) collective-permute-start(bf16[2,128,4480]{2,1,0:T(8,128)(2,1)} %dynamic-slice_convert_fusion.1), channel_id=1, source_target_pairs={{0,4},{2,6},{4,0},{6,2},{8,12},{10,14},{12,8},{14,10},{1,5},{3,7},... | collective-permute-start | bytes 6881288 | tf_op jit(solution)/shard_map/ppermute | solution.py:628
  1065.8 52.8 %collective-permute-start.92 = (bf16[2,128,4480]{2,1,0:T(8,128)(2,1)S(1)}, bf16[2,128,4480]{2,1,0:T(8,128)(2,1)S(1)}, u32[]{:S(2)}, u32[]{:S(2)}) collective-permute-start(bf16[2,128,4480]{2,1,0:T(8,128)(2,1)S(1)} %dynamic-slice_convert_fusion), channel_id=1, source_target_pairs={{0,8},{2,10},{4,12},{6,14},{8,0},{10,2},{12,4},{14,6},{1,9},{3,11}... | collective-permute-start | bytes 6881288 | tf_op jit(solution)/shard_map/ppermute | solution.py:628
  1113.9 28.4 %collective-permute-start.86 = (bf16[2,64,4480]{2,1,0:T(8,128)(2,1)S(1)}, bf16[2,64,4480]{2,1,0:T(8,128)(2,1)S(1)}, u32[]{:S(2)}, u32[]{:S(2)}) collective-permute-start(bf16[2,64,4480]{2,1,0:T(8,128)(2,1)S(1)} %dynamic-slice_convert_fusion.3), channel_id=1, source_target_pairs={{0,8},{2,10},{4,12},{6,14},{8,0},{10,2},{12,4},{14,6},{1,9},{3,11}... | collective-permute-start | bytes 3440648 | tf_op jit(solution)/shard_map/ppermute | solution.py:628
  1173.5 28.8 %collective-permute-start.95 = (bf16[64,4096]{1,0:T(8,128)(2,1)S(1)}, bf16[64,4096]{1,0:T(8,128)(2,1)}, u32[]{:S(2)}, u32[]{:S(2)}) collective-permute-start(bf16[64,4096]{1,0:T(8,128)(2,1)S(1)} %pad_maximum_fusion.121.refs_2_), channel_id=1, source_target_pairs={{0,4},{2,6},{4,0},{6,2},{8,12},{10,14},{12,8},{14,10},{1,5},{3,7},... | collective-permute-start | bytes 1572872 | tf_op jit(solution)/shard_map/ppermute | solution.py:628
  1174.7 30.4 %collective-permute-start.88 = (bf16[64,4096]{1,0:T(8,128)(2,1)S(1)}, bf16[64,4096]{1,0:T(8,128)(2,1)}, u32[]{:S(2)}, u32[]{:S(2)}) collective-permute-start(bf16[64,4096]{1,0:T(8,128)(2,1)S(1)} %pad_maximum_fusion.119.refs_1_), channel_id=1, source_target_pairs={{0,8},{2,10},{4,12},{6,14},{8,0},{10,2},{12,4},{14,6},{1,9},{3,11}... | collective-permute-start | bytes 1572872 | tf_op jit(solution)/shard_map/ppermute | solution.py:628
  1190.1 203.3 %collective-permute-start.106 = (bf16[1056,768]{1,0:T(8,128)(2,1)}, bf16[1056,768]{1,0:T(8,128)(2,1)}, u32[]{:S(2)}, u32[]{:S(2)}) collective-permute-start(bf16[1056,768]{1,0:T(8,128)(2,1)} %shard_map.604), channel_id=1, source_target_pairs={{0,1},{1,0},{2,3},{3,2},{4,5},{5,4},{6,7},{7,6},{8,9},{9,8},{10,11... | collective-permute-start | bytes 4866056 | tf_op jit(solution)/shard_map/ppermute | solution.py:632
  1256.1 28.1 %collective-permute-start.110 = (bf16[2,128,384]{2,1,0:T(8,128)(2,1)}, bf16[2,128,384]{2,1,0:T(8,128)(2,1)}, u32[]{:S(2)}, u32[]{:S(2)}) collective-permute-start(bf16[2,128,384]{2,1,0:T(8,128)(2,1)} %shard_map.605), channel_id=1, source_target_pairs={{0,1},{1,0},{2,3},{3,2},{4,5},{5,4},{6,7},{7,6},{8,9},{9,8},{10,11... | collective-permute-start | bytes 589832 | tf_op jit(solution)/shard_map/ppermute | solution.py:632
  1257.0 29.5 %collective-permute-start.98 = (bf16[64,2048]{1,0:T(8,128)(2,1)S(1)}, bf16[64,2048]{1,0:T(8,128)(2,1)}, u32[]{:S(2)}, u32[]{:S(2)}) collective-permute-start(bf16[64,2048]{1,0:T(8,128)(2,1)S(1)} %copy-done.158), channel_id=1, source_target_pairs={{0,1},{1,0},{2,3},{3,2},{4,5},{5,4},{6,7},{7,6},{8,9},{9,8},{10,11... | collective-permute-start | bytes 786440 | tf_op jit(solution)/shard_map/ppermute | solution.py:632
  1273.7 57.9 %collective-permute-start.117 = (bf16[1408,256]{1,0:T(8,128)(2,1)}, bf16[1408,256]{1,0:T(8,128)(2,1)}, u32[]{:S(2)}, u32[]{:S(2)}) collective-permute-start(bf16[1408,256]{1,0:T(8,128)(2,1)} %dynamic-slice_convert_fusion.6), channel_id=1, source_target_pairs={{0,8},{2,10},{4,12},{6,14},{8,0},{10,2},{12,4},{14,6},{1,9},{3,11}... | collective-permute-start | bytes 2162696 | tf_op jit(solution)/shard_map/ppermute | solution.py:628
  1276.0 37.9 %collective-permute-start.115 = (bf16[256,1024]{1,0:T(8,128)(2,1)S(1)}, bf16[256,1024]{1,0:T(8,128)(2,1)S(1)}, u32[]{:S(2)}, u32[]{:S(2)}) collective-permute-start(bf16[256,1024]{1,0:T(8,128)(2,1)S(1)} %constant_dynamic-slice_fusion.2), channel_id=1, source_target_pairs={{0,16},{16,0},{1,17},{17,1},{2,18},{18,2},{3,19},{19,3},{4,20},{20... | collective-permute-start | bytes 1572872 | tf_op jit(solution)/shard_map/ppermute | solution.py:636
  1301.7 32.2 %collective-permute-start.99 = (bf16[2,64,2048]{2,1,0:T(8,128)(2,1)S(1)}, bf16[2,64,2048]{2,1,0:T(8,128)(2,1)S(1)}, u32[]{:S(2)}, u32[]{:S(2)}) collective-permute-start(bf16[2,64,2048]{2,1,0:T(8,128)(2,1)S(1)} %pad_maximum_fusion.122), channel_id=1, source_target_pairs={{0,8},{2,10},{4,12},{6,14},{8,0},{10,2},{12,4},{14,6},{1,9},{3,11}... | collective-permute-start | bytes 1572872 | tf_op jit(solution)/shard_map/ppermute | solution.py:628
  1336.0 29.7 %collective-permute-start.100 = (bf16[2,128,2048]{2,1,0:T(8,128)(2,1)}, bf16[2,128,2048]{2,1,0:T(8,128)(2,1)}, u32[]{:S(2)}, u32[]{:S(2)}) collective-permute-start(bf16[2,128,2048]{2,1,0:T(8,128)(2,1)} %pad_maximum_fusion.94), channel_id=1, source_target_pairs={{0,4},{2,6},{4,0},{6,2},{8,12},{10,14},{12,8},{14,10},{1,5},{3,7},... | collective-permute-start | bytes 3145736 | tf_op jit(solution)/shard_map/ppermute | solution.py:628
  1338.7 42.2 %collective-permute-start.104 = (bf16[2,128,2048]{2,1,0:T(8,128)(2,1)}, bf16[2,128,2048]{2,1,0:T(8,128)(2,1)S(1)}, u32[]{:S(2)}, u32[]{:S(2)}) collective-permute-start(bf16[2,128,2048]{2,1,0:T(8,128)(2,1)} %pad_maximum_fusion.95), channel_id=1, source_target_pairs={{0,8},{2,10},{4,12},{6,14},{8,0},{10,2},{12,4},{14,6},{1,9},{3,11}... | collective-permute-start | bytes 3145736 | tf_op jit(solution)/shard_map/ppermute | solution.py:628
  1379.5 92.2 %collective-permute-start.101 = (bf16[2,256,2048]{2,1,0:T(8,128)(2,1)}, bf16[2,256,2048]{2,1,0:T(8,128)(2,1)}, u32[]{:S(2)}, u32[]{:S(2)}) collective-permute-start(bf16[2,256,2048]{2,1,0:T(8,128)(2,1)} %pad_maximum_fusion.40), channel_id=1, source_target_pairs={{0,2},{2,0},{4,6},{6,4},{8,10},{10,8},{12,14},{14,12},{1,3},{3,1},... | collective-permute-start | bytes 6291464 | tf_op jit(solution)/shard_map/ppermute | solution.py:628
  1383.4 92.2 %collective-permute-start.105 = (bf16[2,256,2048]{2,1,0:T(8,128)(2,1)}, bf16[2,256,2048]{2,1,0:T(8,128)(2,1)}, u32[]{:S(2)}, u32[]{:S(2)}) collective-permute-start(bf16[2,256,2048]{2,1,0:T(8,128)(2,1)} %pad_maximum_fusion.41), channel_id=1, source_target_pairs={{0,2},{2,0},{4,6},{6,4},{8,10},{10,8},{12,14},{14,12},{1,3},{3,1},... | collective-permute-start | bytes 6291464 | tf_op jit(solution)/shard_map/ppermute | solution.py:628
  (515 other events, 4924.1 us)
Sparse Core Ops, SparseCore 0:
  280.2 44.5 all-gather.5
  327.0 44.6 all-gather.7
  373.2 88.6 all-gather.9
  463.4 81.0 all-gather.11
  545.9 44.4 all-gather.13
  727.6 47.5 reduce-scatter.19
  777.6 76.2 reduce-scatter.17
  856.2 78.0 reduce-scatter.15
  936.7 77.2 reduce-scatter.11
  1016.1 80.6 reduce-scatter.9
  1099.6 18.5 reduce-scatter.13
  1195.5 84.7 reduce-scatter.7

commit v5 on v4

--- a/solution.py
+++ b/solution.py
@@ -994,7 +994,7 @@
     pass
 
 
-def hold(value, *after):
+def hold(value, *after, cost=0):
     anywhere = pl.BlockSpec(memory_space=pl.ANY)
     return pl.pallas_call(
         hold_kernel,
@@ -1002,7 +1002,9 @@
         out_specs=anywhere,
         out_shape=jax.ShapeDtypeStruct(value.shape, value.dtype),
         input_output_aliases={0: 0},
-        cost_estimate=pl.CostEstimate(flops=0, bytes_accessed=0, transcendentals=0),
+        cost_estimate=pl.CostEstimate(
+            flops=cost * 1_100_000_000, bytes_accessed=0, transcendentals=0
+        ),
     )(value, *after)
 
 
@@ -1375,6 +1377,35 @@
     ]
 
 
+def natural_heads(value):
+    count = lax.axis_size(HEAD).bit_length() - 1
+    cubes = value.reshape((2,) * count + value.shape[1:])
+    turned = list(range(count - 1, -1, -1)) + list(range(count, cubes.ndim))
+    return cubes.transpose(turned).reshape(value.shape)
+
+
+def cut_rows(value, order, axis):
+    bit = bit_of(order[0])
+    half = value.shape[axis] // 2
+    return (
+        lax.dynamic_slice_in_dim(value, (1 - bit) * half, half, axis),
+        lax.dynamic_slice_in_dim(value, bit * half, half, axis),
+    )
+
+
+def sum_products(pieces, product, order, axis):
+    away = product(pieces[0]).astype(low)
+    value = product(pieces[1]) + head_swap(away, order[0]).astype(full)
+    return away, sum_rows(value, order[1:], axis)
+
+
+def finish_state(total, swap=lambda value: value):
+    state = lax.axis_index(STATE)
+    away = swap(lax.dynamic_index_in_dim(total, 1 - state, 0, False).astype(low))
+    kept = lax.dynamic_index_in_dim(total, state, 0, False)
+    return kept + state_swap(away).astype(full)
+
+
 def swap_quarters(value):
     quarter = value.shape[-1] // 4
     part = [value[..., i * quarter : (i + 1) * quarter] for i in range(4)]
@@ -1510,7 +1541,7 @@
         [jnp.where(column == index, ups, jnp.zeros_like(ups)) for index in range(3)], 0
     )
     masks = orders[0][::-1]
-    downs_all = gather_rows(pack[None, :, gain_rows:down_end], masks, 0)
+    downs_all = natural_heads(gather_rows(pack[None, :, gain_rows:down_end], orders[0], 0))
 
     def down_of(lower, part):
         return downs_all[:, :, lower : lower + part].transpose(1, 0, 2, 3)
@@ -1599,10 +1630,13 @@
 
     attended = hold(attended, mlp_first)
     attended_halves = [attended[:rows], attended[rows:]]
-    branch_cut = [
-        sum_row16(plain_dot(part, attn_proj).astype(low).reshape(2, middle, width), order)
-        for part, order in zip(attended_halves, orders)
-    ]
+    def branch_product(part):
+        return plain_dot(part.reshape(-1, part.shape[2]), attn_proj).reshape(2, -1, width)
+
+    branch_cut = []
+    for part, order in zip(attended_halves, orders):
+        pieces = cut_rows(part.reshape(2, middle, -1), order, 1)
+        branch_cut.append(finish_state(sum_products(pieces, branch_product, order, 1)[1]))
     mlp_proj = lax.all_gather(mlp_output, ZED, axis=1, tiled=True)
     mixer_main = lax.all_gather(
         jnp.concatenate([proj_inner, proj_gate], 1), ZED, axis=0, tiled=True
@@ -1623,7 +1657,11 @@
     ]
     activated = [jax.nn.gelu(value, approximate=False).astype(low) for value in hidden_pre]
     second_cut = [
-        value + good * sum_rows(plain_dot(part, mlp_proj).astype(low), order, 0)
+        value
+        + good
+        * sum_products(
+            cut_rows(part, order, 0), lambda rows: plain_dot(rows, mlp_proj), order, 0
+        )[1]
         for value, good, part, order in zip(first_cut, valid_cut, activated, orders)
     ]
     mixer_normed = jnp.concatenate(
@@ -1736,24 +1774,36 @@
         (
             value
             + good
-            * sum_rows(
-                plain_dot(gated[index * middle : (index + 1) * middle], output_main).astype(low),
+            * sum_products(
+                cut_rows(gated[index * middle : (index + 1) * middle], order, 0),
+                lambda rows: plain_dot(rows, output_main),
                 order,
                 0,
-            )
+            )[1]
         ).astype(low)
         for index, (value, good, order) in enumerate(zip(second_cut, valid_cut, orders))
     ]
     inner_low = jnp.concatenate([inner_grad, gate_grad], 1).astype(low)
     inner_low = hold(inner_low, *out_cut)
     small_low = small_grad.astype(low)
-    mixer_parts = [
-        (right_dot(inner_low[part], mixer_main) + right_dot(small_low[part], small_main)).astype(low)
-        for part in (slice(0, middle), slice(middle, rows))
-    ]
-    mixer_sum = [sum_rows(part, order, 0) for part, order in zip(mixer_parts, orders)]
+    def mixer_product(rows):
+        return right_dot(rows[0], mixer_main) + right_dot(rows[1], small_main)
+
+    mixer_parts, mixer_sum = [], []
+    for index, order in enumerate(orders):
+        part = slice(index * middle, (index + 1) * middle)
+        pieces = zip(cut_rows(inner_low[part], order, 0), cut_rows(small_low[part], order, 0))
+        away, total = sum_products(list(pieces), mixer_product, order, 0)
+        mixer_parts.append(away)
+        mixer_sum.append(total)
     inner_later = hold(inner_low, *mixer_parts)
     small_later = hold(small_low, *mixer_parts)
+
+    def scatter(value, axis):
+        return lax.psum_scatter(value.astype(low), ZED, scatter_dimension=axis, tiled=True)
+
+    sum_output = scatter(left_dot(gated, hold(mix_grad, *mixer_parts)), 1)
+    sum_mixer = scatter(left_dot(mixer_normed, inner_later), 0)
     upstream_cut = [value.astype(full) for value in cut(cot_own)]
     mixer_backs = [
         norm_back(value, mixer_gain, grad) for value, grad in zip(second_cut, mixer_sum)
@@ -1773,14 +1823,22 @@
         for pre, grad in zip(hidden_pre, mlp_grad)
     ]
     mlp_wide = jnp.concatenate([mlp_main, mlp_upper], 0)
-    mlp_parts = [right_dot(grad, mlp_wide).astype(low) for grad in hidden_grad]
-    mlp_sums = [sum_rows(part, order, 0) for part, order in zip(mlp_parts, orders)]
+    mlp_parts, mlp_sums = [], []
+    for grad, order in zip(hidden_grad, orders):
+        away, total = sum_products(
+            cut_rows(grad, order, 0), lambda rows: right_dot(rows, mlp_wide), order, 0
+        )
+        mlp_parts.append(away)
+        mlp_sums.append(total)
     middle_low = [value[:, width:].astype(low) for value in mlp_sums]
     mlp_backs = [
         norm_back(value, mlp_gain, total[:, :width] + right_dot(mid, mlp_down))
         for value, total, mid in zip(first_cut, mlp_sums, middle_low)
     ]
     first_grad = [grad + back[0] for grad, back in zip(second_grad, mlp_backs)]
+    first_grad[0] = hold(first_grad[0], sum_output)
+    mlp_grad_own = hold(jnp.concatenate(mlp_grad, 0), *mlp_parts)
+    sum_mlp_output = scatter(left_dot(jnp.concatenate(activated, 0), mlp_grad_own), 1)
     grad_mlp_gain = mlp_backs[0][1] + mlp_backs[1][1]
     branch_halves = [
         gather_row16((good * grad).astype(low), order).reshape(rows, width)
@@ -1790,22 +1848,30 @@
     attended_grad = jnp.concatenate(
         [right_dot(value, attn_proj).astype(low) for value in branch_halves], 0
     )
+    attended_grad = hold(attended_grad, sum_mixer)
     query_back, key_back, value_back = attend_back(
         queries, keys, values, attended_grad, attended, lse, segment, lows
     )
-    pre_grad = rope_back(query_back, key_back, value_back, cosine, sine)
+    out_got = state_swap(jnp.stack(out_cut, 0))
+    pre_grad = hold(rope_back(query_back, key_back, value_back, cosine, sine), out_got)
     main_wide = jnp.concatenate([main_near, main_far, up_wide], 0)
     joint = 2 * width
-    normed_parts = [
-        right_dot(part, main_wide).astype(low) for part in (pre_grad[:rows], pre_grad[rows:])
-    ]
-    normed_sums = []
-    for part, order in zip(normed_parts, orders):
-        total = sum_rows(part.reshape(2, middle, -1), order, 1)
-        away = lax.dynamic_index_in_dim(total, 1 - state, 0, False).astype(low)
-        away = jnp.concatenate([swap_quarters(away[:, :joint]), away[:, joint:]], 1)
-        kept = lax.dynamic_index_in_dim(total, state, 0, False)
-        normed_sums.append(kept + state_swap(away).astype(full))
+    def normed_product(part):
+        return right_dot(part.reshape(-1, part.shape[2]), main_wide).reshape(2, -1, main_wide.shape[0])
+
+    normed_parts, normed_totals = [], []
+    for part, order in zip((pre_grad[:rows], pre_grad[rows:]), orders):
+        pieces = cut_rows(part.reshape(2, middle, -1), order, 1)
+        away, total = sum_products(pieces, normed_product, order, 1)
+        normed_parts.append(away)
+        normed_totals.append(total)
+    normed_totals[0] = hold(normed_totals[0], sum_mlp_output)
+    def swap_joint(value):
+        return jnp.concatenate([swap_quarters(value[:, :joint]), value[:, joint:]], 1)
+
+    normed_sums = [finish_state(total, swap_joint) for total in normed_totals]
+    normed_sums[0] = hold(normed_sums[0], normed_sums[1], cost=100)
+    pre_grad = hold(pre_grad, *normed_parts)
     cubes = pre_grad.reshape(2, 2, middle, -1)
     grad_own, grad_other = (
         lax.dynamic_index_in_dim(cubes, index, 1, False).reshape(rows, -1)
@@ -1845,55 +1911,6 @@
         )
 
     lows_cut = [value[:, joint:].astype(low) for value in normed_sums]
-    joined_backs = [
-        norm_back(value, attn_gain, total[:, :joint] + right_dot(mid, down_wide))
-        for value, total, mid in zip(joined_cut, normed_sums, lows_cut)
-    ]
-    grad_attn_gain = joined_backs[0][1] + joined_backs[1][1]
-
-    def natural_columns(value):
-        return jnp.concatenate(
-            [
-                lax.dynamic_slice_in_dim(value, (place ^ index) * quarter, quarter, -1)
-                for index in range(4)
-            ],
-            -1,
-        )
-
-    input_cut = []
-    for grad, back, order in zip(first_grad, joined_backs, orders):
-        joined_grad = natural_columns(back[0])
-        joined_grad = jnp.concatenate([joined_grad[:, :width] + grad, joined_grad[:, width:]], 1)
-        input_cut.append(joined_grad.astype(low))
-    input_halves = [gather_rows(value, order, 0) for value, order in zip(input_cut, orders)]
-    layer_halves = [
-        gather_row16(hold(value, *input_halves), order) for value, order in zip(out_cut, orders)
-    ]
-    layer_out = jnp.concatenate(
-        [layer_halves[0][0], layer_halves[1][0], layer_halves[0][1], layer_halves[1][1]], 0
-    )
-    grad_hidden = jnp.concatenate([value[:, :width] for value in input_halves], 0)
-    grad_embedding = jnp.concatenate([value[:, width:] for value in input_halves], 0)
-
-    def scatter(value, axis):
-        value = lax.psum_scatter(value.astype(low), ZED, scatter_dimension=axis, tiled=True)
-        return hold(value, *input_cut).astype(full)
-
-    attn_grad = left_dot(attended_halves[0], branch_halves[0]) + left_dot(
-        attended_halves[1], branch_halves[1]
-    )
-    out_attn = grad_pieces(hold(attn_grad.astype(low), *input_halves), 0)
-    out_output = scatter(left_dot(gated, mix_grad), 1)
-    out_mixer = scatter(left_dot(mixer_normed, inner_later), 0)
-    mlp_normed_own = jnp.concatenate(mlp_normed, 0)
-    hidden_grad_own = hold(jnp.concatenate(hidden_grad, 0), *mlp_parts)
-    mlp_grad_own = hold(jnp.concatenate(mlp_grad, 0), *mlp_parts)
-    out_mlp_output = scatter(
-        left_dot(jnp.concatenate(activated, 0), mlp_grad_own), 1
-    )
-    out_mlp_input = scatter(left_dot(mlp_normed_own, hidden_grad_own), 0)
-    out_up_mlp = scatter(left_dot(jnp.concatenate(mlp_red, 0), hidden_grad_own), 0)
-
     def by_order(value):
         bits = value.reshape((2,) * (len(orders[0])) + (piece, value.shape[1]))
         count = len(orders[0])
@@ -1903,20 +1920,6 @@
     lows_own = gather_rows(jnp.stack(lows_cut, 0), orders[0], 1)
     lows_own = [lows_own[0], by_order(lows_own[1])]
     lows_own = jnp.concatenate(lows_own, 0)
-    down_parts = [
-        left_dot(
-            lax.dynamic_slice_in_dim(value, index * quarter + head * part_a, part_a, 1), lows_own
-        )
-        for value in (near_own, far_own)
-        for index in range(2)
-    ]
-    away = hold(jnp.stack([down_parts[1], down_parts[3]], 0).astype(low), *input_halves)
-    away = state_swap(away).astype(full)
-    down_sum = down_parts[0] + away[0] + dp_swap((down_parts[2] + away[1]).astype(low))
-    down_all = gather_rows(down_sum.astype(low)[None], masks, 0).reshape(quarter, 3 * rank)
-    down_all = down_all.astype(full)
-    out_downs = [down_all[:, index * rank : (index + 1) * rank] for index in range(3)]
-
     def placed(value, axis):
         shape = list(value.shape)
         shape[axis] *= head_parts
@@ -1924,7 +1927,7 @@
             jnp.zeros(shape, full), value, head * value.shape[axis], axis
         )
 
-    small_main_grad = hold(left_dot(mixer_normed, small_later), *input_halves)
+    small_main_grad = hold(left_dot(mixer_normed, small_later), *normed_totals)
     normed_cut = [
         lax.dynamic_slice_in_dim(value, chunk_of(order) * piece, piece, 0)
         for value, order in zip(mlp_normed, orders)
@@ -1947,8 +1950,90 @@
     packed = jnp.pad(packed, ((0, -packed.shape[0] % lines), (0, 0)))
     pair_grad = jnp.concatenate([pair_grad, packed], 0)
     pair_grad = sum_rows(pair_grad, masks, 0)
+    joined_backs = [
+        norm_back(value, attn_gain, total[:, :joint] + right_dot(mid, down_wide))
+        for value, total, mid in zip(joined_cut, normed_sums, lows_cut)
+    ]
+    grad_attn_gain = joined_backs[0][1] + joined_backs[1][1]
+
+    def natural_columns(value):
+        return jnp.concatenate(
+            [
+                lax.dynamic_slice_in_dim(value, (place ^ index) * quarter, quarter, -1)
+                for index in range(4)
+            ],
+            -1,
+        )
+
+    input_cut = []
+    for grad, back, own, got in zip(first_grad, joined_backs, out_cut, out_got):
+        joined_grad = natural_columns(back[0])
+        input_cut.append(
+            jnp.concatenate(
+                [
+                    (joined_grad[:, :width] + grad).astype(low),
+                    joined_grad[:, width:].astype(low),
+                    jnp.where(state == 0, own, got),
+                    jnp.where(state == 0, got, own),
+                ],
+                1,
+            )
+        )
+    input_cut[0] = hold(input_cut[0], input_cut[1], lows_own, pair_grad, cost=100)
+    input_cut[1] = hold(input_cut[1], lows_own, pair_grad)
+    quads = []
+    input_halves = []
+    core = bit_of(orders[0][0])
+    for value, order in zip(input_cut, orders):
+        value = gather_rows(value, order[1:], 0)
+        value = hold(value, beside_got)
+        got = head_swap(value, order[0])
+        input_halves += [value, got]
+        quads += [(value, got), (got, value)]
+
+    def whole_rows(start):
+        columns = slice(start, start + width)
+        return [jnp.where(core == 0, a[:, columns], b[:, columns]) for a, b in quads]
+
+    grad_hidden = jnp.concatenate(whole_rows(0), 0)
+    grad_embedding = jnp.concatenate(whole_rows(width), 0)
+    layer_out = jnp.concatenate(whole_rows(2 * width) + whole_rows(3 * width), 0)
+
+    attn_grad = left_dot(attended_halves[0], branch_halves[0]) + left_dot(
+        attended_halves[1], branch_halves[1]
+    )
+    out_attn = grad_pieces(hold(attn_grad.astype(low), *input_halves), 0)
+    def settled(value):
+        return hold(value, *input_halves).astype(full)
+
+    mlp_normed_own = jnp.concatenate(mlp_normed, 0)
+    hidden_grad_own = hold(jnp.concatenate(hidden_grad, 0), *normed_parts)
+    out_output = settled(sum_output)
+    out_mixer = settled(sum_mixer)
+    out_mlp_output = settled(sum_mlp_output)
+    out_mlp_input = settled(scatter(left_dot(mlp_normed_own, hidden_grad_own), 0))
+    out_up_mlp = settled(scatter(left_dot(jnp.concatenate(mlp_red, 0), hidden_grad_own), 0))
+
+    down_parts = [
+        left_dot(
+            lax.dynamic_slice_in_dim(value, index * quarter + head * part_a, part_a, 1), lows_own
+        )
+        for value in (near_own, far_own)
+        for index in range(2)
+    ]
+    away = jnp.stack([down_parts[1], down_parts[3]], 0).astype(low)
+    away = state_swap(hold(away, *input_halves)).astype(full)
+    down_sum = down_parts[0] + away[0] + dp_swap((down_parts[2] + away[1]).astype(low))
+    down_all = gather_rows(down_sum.astype(low)[None], masks, 0).reshape(quarter, 3 * rank)
+    down_all = down_all.astype(full)
+    out_downs = [down_all[:, index * rank : (index + 1) * rank] for index in range(3)]
+
+    pair_grad = hold(pair_grad, *input_halves)
     pair_grad = pair_grad + state_swap(pair_grad)
     pair_grad = pair_grad + dp_swap(pair_grad)
+    row = lax.broadcasted_iota(jnp.int32, (pair_grad.shape[0], 1), 0)
+    in_main = head * pair_grad.shape[0] + row < width
+    down_m_squares = jnp.sum(jnp.where(in_main, jnp.square(pair_grad[:, 2 * states :]), 0.0))
     pair_grad = gather_rows(pair_grad.astype(low), masks, 0).astype(full)
     vector_grad = pair_grad[:width, : 2 * states]
     out_down_mlp = lax.dynamic_slice(pair_grad, (place * split_m, 2 * states), (split_m, rank))
@@ -1961,16 +2046,20 @@
     step_total, taps_x_total, gated_total, mlp_total, mixer_total, taps_total, head_total = pieces
     head_total = head_total[: heads_grad.size].reshape(heads_grad.shape)
 
+    main_total = hold(main_total, *input_halves)
     out_all = [spread(main_total, beside_got, index) for index in range(3)]
     out_main = [value[:quarter] for value in out_all]
     out_up = [value[quarter:] for value in out_all]
-    once = (head == 0).astype(full)
-    square_sum = jnp.zeros((), full)
+    square_sum = jnp.sum(jnp.square(down_sum)) + 0.25 * down_m_squares
     for value in out_main + out_up + [out_attn, out_mlp_input, out_up_mlp, out_mlp_output]:
         square_sum = square_sum + jnp.sum(value * value)
-    for value in out_downs + [out_down_mlp]:
-        square_sum = square_sum + once * jnp.sum(value * value)
-    square_total, attn_total = lax.psum((square_sum, natural_columns(grad_attn_gain)), EVERY)
+    last = natural_columns(grad_attn_gain)
+    last = jnp.concatenate([last, jnp.broadcast_to(square_sum, (rank,))]).reshape(-1, rank)
+    for mask in orders[0]:
+        last = last + head_swap(last, mask)
+    last = last + state_swap(last)
+    last = (last + dp_swap(last)).reshape(-1)
+    attn_total, square_total = last[:joint], last[joint]
 
     def of_head(value, size):
         return lax.dynamic_slice_in_dim(value, head * size, size, value.ndim - 1)

time: 1500 us -> 1470 us (0.980)
  matrix products: 206 us -> 247 us
  blocking collectives: 38.6 us -> 0 us
  waiting for transfers between devices: 555 us -> 533 us
  other arithmetic: 279 us -> 264 us
    psum x1 -> x0, blocking collectives: 38.6 us -> none  [fast_device(): lax.psum((square_sum, natural_columns(grad_attn_gain)), EVERY)]
    ppermute x16, waiting for transfers between devices: 119 us -> 82.6 us  [state_swap(): return lax.ppermute(value, STATE, [(0, 1), (1, 0)])]
    ppermute x96 -> x93, waiting for transfers between devices: 344 us -> 323 us  [head_swap(): return lax.ppermute(value, HEAD, [(i, i ^ mask) for i in range(count)])]
    dot_general x17 -> x25, matrix products: 58.8 us -> 80 us  [right_dot(): lax.dot_general(left, right, (((1,), (1,)), ((), ())), preferred_element_...]
    ppermute x9 -> x10, waiting for transfers between devices: 86.9 us -> 107 us  [dp_swap(): return lax.ppermute(value, DP, [(0, 1), (1, 0)])]
    add x33 -> x21, other arithmetic: 31.8 us -> 12.1 us  [sum_rows(): value = kept.astype(full) + head_swap(away, mask).astype(full)]
    dot_general x24 -> x30, matrix products: 80.1 us -> 97.1 us  [plain_dot(): return jnp.dot(left, right, preferred_element_type=jnp.float32)]
    unnamed x5 -> x12, other arithmetic: 0.02 us -> 15.7 us
  transfers between devices with their start and end apart: 137 -> 135, of which waited for: 68 -> 69; matrix products, arithmetic and copies ran while one was open for 38% -> 40% of each run, Pallas kernels for 5% -> 5%
where the time goes in v5:
time: 1470 us; the launch traced here: 1460 us
  waiting for transfers between devices  533 us (36%)
  other arithmetic  264 us (18%)
  matrix products  247 us (17%)
  local copies, waits for them, and re-layouts  176 us (12%)
  starting transfers between devices  132 us (9%)
  Pallas kernels  82.4 us (6%)
  between operations  30.6 us (2%)
    ppermute x93, waiting for transfers between devices, head_swap(): return lax.ppermute(value, HEAD, [(i, i ^ mask) for i in range(count)])  323 us
    ppermute x10, waiting for transfers between devices, dp_swap(): return lax.ppermute(value, DP, [(0, 1), (1, 0)])  107 us
    dot_general x30, matrix products, plain_dot(): return jnp.dot(left, right, preferred_element_type=jnp.float32)  97.1 us
    unnamed x868, local copies, waits for them, and re-layouts  90.4 us
    ppermute x16, waiting for transfers between devices, state_swap(): return lax.ppermute(value, STATE, [(0, 1), (1, 0)])  82.6 us
    ppermute x93, starting transfers between devices, head_swap(): return lax.ppermute(value, HEAD, [(i, i ^ mask) for i in range(count)])  80.5 us
    dot_general x25, matrix products, right_dot(): lax.dot_general(left, right, (((1,), (1,)), ((), ())), preferred_element_...  80 us
    dot_general x23, matrix products, left_dot(): lax.dot_general(left, right, (((0,), (0,)), ((), ())), preferred_element_...  69.6 us
  transfers between devices with their start and end apart: 135, of which 69 were waited for; matrix products, arithmetic and copies ran while one was open for 40% of the time, Pallas kernels for 5%

profile of v5, /device:TPU:0, one launch (start us, length us, event | category | flops | bytes accessed | tf_op | source)
XLA Modules:
  0.0 1464.6 jit_solution(5145182542598599023)
XLA Ops:
  44.2 19.8 %collective-permute-done.1.refs_1_ = bf16[2,944,128]{2,1,0:T(8,128)(2,1)S(1)} collective-permute-done((bf16[2,944,128]{2,1,0:T(8,128)(2,1)}, bf16[2,944,128]{2,1,0:T(8,128)(2,1)S(1)}, u32[]{:S(2)}, u32[]{:S(2)}) %collective-permute-start.1) | collective-permute-done | bytes 483360 | tf_op jit(solution)/shard_map/ppermute | solution.py:636
  72.4 7.9 multiply_convert_fusion.7
  90.6 32.8 %collective-permute-done.7.refs_2_.refs_4_ = bf16[512,768]{1,0:T(8,128)(2,1)} collective-permute-done((bf16[512,768]{1,0:T(8,128)(2,1)}, bf16[512,768]{1,0:T(8,128)(2,1)}, u32[]{:S(2)}, u32[]{:S(2)}) %collective-permute-start.7) | collective-permute-done | bytes 786464 | tf_op jit(solution)/shard_map/ppermute | solution.py:636
  124.9 14.0 collective-permute-done.6.refs_1_.refs_3_
  144.0 13.9 collective-permute-done.17
  185.3 16.3 %fusion.72.refs_1_ = f32[1024,768]{1,0:T(8,128)} fusion(f32[1024,768]{1,0:T(8,128)S(1)} %fusion.209, bf16[1024,768]{1,0:T(8,128)(2,1)} %collective-permute-done.2, bf16[1024,768]{1,0:T(8,128)(2,1)S(1)} %copy-done.43, bf16[1024,1024]{1,0:T(8,128)(2,1)S(1)} %copy-done.52, bf16[1024,1024]{1,0:T(8,128)(2,1)S(1)} %get-tuple-element.319), kind=kOutput, calls=%fused_computation.285 | convolution fusion | flops 3236691968 | bytes 13631488 | tf_op jit(solution)/shard_map/dot_general | solution.py:22
  226.9 6.5 fusion.73.refs_2_
  233.4 15.8 %collective-permute-done.8.refs_0_ = bf16[512,768]{1,0:T(8,128)(2,1)} collective-permute-done((bf16[512,768]{1,0:T(8,128)(2,1)}, bf16[512,768]{1,0:T(8,128)(2,1)}, u32[]{:S(2)}, u32[]{:S(2)}) %collective-permute-start.8) | collective-permute-done | bytes 786464 | tf_op jit(solution)/shard_map/ppermute | solution.py:636
  258.4 6.8 fusion.60.own_ref
  272.9 18.9 %shard_map.590 = (bf16[2048,256]{1,0:T(8,128)(2,1)S(1)}, f32[2,1,2048]{2,1,0:T(1,128)S(1)}) custom-call(s32[8]{0:T(128)S(1)} %and_select_fusion.low_ref, bf16[2048,256]{1,0:T(8,128)(2,1)S(1)} %get-tuple-element.74.q_ref, bf16[2048,256]{1,0:T(8,128)(2,1)S(1)} %get-tuple-element.75.k_ref, bf16[2048,256]{1,0:T(8,128)(2,1)S(1)} %get-tuple-element.76.v_ref, ...), custom_call_target="tpu_custom_call" | custom-call | flops 23622320128 | bytes 4194304 | tf_op jit(solution)/shard_map/pallas_call | solution.py:825
  314.6 19.3 %collective-permute-done.33 = bf16[2,128,2048]{2,1,0:T(8,128)(2,1)S(1)} collective-permute-done((bf16[2,128,2048]{2,1,0:T(8,128)(2,1)S(1)}, bf16[2,128,2048]{2,1,0:T(8,128)(2,1)S(1)}, u32[]{:S(2)}, u32[]{:S(2)}) %collective-permute-start.33) | collective-permute-done | bytes 1048608 | tf_op jit(solution)/shard_map/ppermute | solution.py:628
  338.4 10.0 collective-permute-done.34
  353.2 8.5 collective-permute-done.35
  361.7 20.8 %collective-permute-done.22 = bf16[64,2048]{1,0:T(8,128)(2,1)S(1)} collective-permute-done((bf16[64,2048]{1,0:T(8,128)(2,1)S(1)}, bf16[64,2048]{1,0:T(8,128)(2,1)S(1)}, u32[]{:S(2)}, u32[]{:S(2)}) %collective-permute-start.22) | collective-permute-done | bytes 262176 | tf_op jit(solution)/shard_map/ppermute | solution.py:632
  411.7 9.4 multiply_convert_fusion.10
  421.1 8.5 all-gather.10.cloned.1.call-done
  436.9 9.0 multiply_convert_fusion.11
  455.0 11.0 collective-permute-done.40
  487.5 8.6 collective-permute-done.43
  510.2 7.9 fusion.313
  525.7 6.5 fusion.49
  546.8 7.1 shard_map.595
  556.1 8.1 multiply_reduce_fusion.16
  589.8 17.1 %shard_map.597 = (f32[1024,512]{1,0:T(8,128)S(1)}, f32[1024,8]{1,0:T(8,128)S(1)}, f32[1024,8]{1,0:T(8,128)S(1)}, f32[8,1024]{1,0:T(8,128)S(1)}, f32[1024,64]{1,0:T(8,128)S(1)}, /*index=5*/f32[1024,64]{1,0:T(8,128)S(1)}) custom-call(s32[5]{0:T(128)S(1)} %get-tuple-element.635.ends_ref, f32[1024,512]{1,0:T(8,128)S(1)} %get-tuple-element.298.x_ref, ...), custom_call_target="tpu_custom_call" | custom-call | flops 19327352832 | bytes 4194304 | tf_op jit(solution)/shard_map/pallas_call | solution.py:1273
  639.8 8.9 collective-permute-done.53
  673.6 10.9 collective-permute-done.72
  742.0 6.5 convolution_convert_fusion.5
  760.2 9.2 collective-permute-done.78
  790.2 17.0 %collective-permute-done.80 = bf16[64,2048]{1,0:T(8,128)(2,1)S(1)} collective-permute-done((bf16[64,2048]{1,0:T(8,128)(2,1)S(1)}, bf16[64,2048]{1,0:T(8,128)(2,1)S(1)}, u32[]{:S(2)}, u32[]{:S(2)}) %collective-permute-start.80) | collective-permute-done | bytes 262176 | tf_op jit(solution)/shard_map/ppermute | solution.py:632
  808.4 15.4 %collective-permute-done.67 = bf16[64,2048]{1,0:T(8,128)(2,1)S(1)} collective-permute-done((bf16[64,2048]{1,0:T(8,128)(2,1)S(1)}, bf16[64,2048]{1,0:T(8,128)(2,1)S(1)}, u32[]{:S(2)}, u32[]{:S(2)}) %collective-permute-start.67) | collective-permute-done | bytes 262176 | tf_op jit(solution)/shard_map/ppermute | solution.py:632
  827.9 11.1 collective-permute-done.68
  841.4 15.7 %collective-permute-done.82 = bf16[2,128,2048]{2,1,0:T(8,128)(2,1)S(1)} collective-permute-done((bf16[2,128,2048]{2,1,0:T(8,128)(2,1)S(1)}, bf16[2,128,2048]{2,1,0:T(8,128)(2,1)S(1)}, u32[]{:S(2)}, u32[]{:S(2)}) %collective-permute-start.82) | collective-permute-done | bytes 1048608 | tf_op jit(solution)/shard_map/ppermute | solution.py:628
  892.9 25.0 %shard_map.603 = (f32[2048,256]{1,0:T(8,128)S(1)}, f32[2048,256]{1,0:T(8,128)S(1)}, f32[2048,256]{1,0:T(8,128)S(1)}) custom-call(s32[8]{0:T(128)S(1)} %copy-done.32, bf16[2048,256]{1,0:T(8,128)(2,1)S(1)} %copy-done.26, bf16[2048,256]{1,0:T(8,128)(2,1)S(1)} %copy-done.28, bf16[2048,256]{1,0:T(8,128)(2,1)S(1)} %copy-done.30, bf16[2048,256]{1,0:T(8,128)(2,1)S(1)} %copy-done.5, ...), custom_call_target="tpu_custom_call" | custom-call | flops 32212254720 | bytes 10485760 | tf_op jit(solution)/shard_map/pallas_call | solution.py:902
  923.6 9.7 convolution_convert_fusion.refs_2_
  933.3 8.9 convolution_convert_fusion.1.refs_1_
  965.5 8.8 fusion.12
  1007.0 8.2 convert_add_fusion
  1018.6 6.7 add_convert_fusion
  1025.4 8.1 convert_add_fusion.1
  1044.6 24.6 %collective-permute-done.90 = bf16[2,128,4480]{2,1,0:T(8,128)(2,1)S(1)} collective-permute-done((bf16[2,128,4480]{2,1,0:T(8,128)(2,1)}, bf16[2,128,4480]{2,1,0:T(8,128)(2,1)S(1)}, u32[]{:S(2)}, u32[]{:S(2)}) %collective-permute-start.90) | collective-permute-done | bytes 2293792 | tf_op jit(solution)/shard_map/ppermute | solution.py:628
  1074.2 17.4 %collective-permute-done.86 = bf16[2,128,4480]{2,1,0:T(8,128)(2,1)} collective-permute-done((bf16[2,128,4480]{2,1,0:T(8,128)(2,1)}, bf16[2,128,4480]{2,1,0:T(8,128)(2,1)}, u32[]{:S(2)}, u32[]{:S(2)}) %collective-permute-start.86) | collective-permute-done | bytes 2293792 | tf_op jit(solution)/shard_map/ppermute | solution.py:628
  1095.8 19.9 %collective-permute-done.91 = bf16[2,64,4480]{2,1,0:T(8,128)(2,1)S(1)} collective-permute-done((bf16[2,64,4480]{2,1,0:T(8,128)(2,1)S(1)}, bf16[2,64,4480]{2,1,0:T(8,128)(2,1)S(1)}, u32[]{:S(2)}, u32[]{:S(2)}) %collective-permute-start.91) | collective-permute-done | bytes 1146912 | tf_op jit(solution)/shard_map/ppermute | solution.py:628
  1201.8 19.4 %collective-permute-done.103 = bf16[64,8192]{1,0:T(8,128)(2,1)} collective-permute-done((bf16[64,8192]{1,0:T(8,128)(2,1)}, bf16[64,8192]{1,0:T(8,128)(2,1)}, u32[]{:S(2)}, u32[]{:S(2)}) %collective-permute-start.103) | collective-permute-done | bytes 1048608 | tf_op jit(solution)/shard_map/ppermute | solution.py:628
  1231.4 40.0 %collective-permute-done.104 = bf16[128,8192]{1,0:T(8,128)(2,1)S(1)} collective-permute-done((bf16[128,8192]{1,0:T(8,128)(2,1)S(1)}, bf16[128,8192]{1,0:T(8,128)(2,1)S(1)}, u32[]{:S(2)}, u32[]{:S(2)}) %collective-permute-start.104) | collective-permute-done | bytes 2097184 | tf_op jit(solution)/shard_map/ppermute | solution.py:628
  1295.6 16.2 %collective-permute-start.110 = (bf16[256,1024]{1,0:T(8,128)(2,1)}, bf16[256,1024]{1,0:T(8,128)(2,1)}, u32[]{:S(2)}, u32[]{:S(2)}) collective-permute-start(bf16[256,1024]{1,0:T(8,128)(2,1)} %constant_dynamic-slice_fusion.2), channel_id=1, source_target_pairs={{0,16},{16,0},{1,17},{17,1},{2,18},{18,2},{3,19},{19,3},{4,20},{20... | collective-permute-start | bytes 1572872 | tf_op jit(solution)/shard_map/ppermute | solution.py:636
  1365.9 7.2 collective-permute-done.107
  1379.9 13.8 collective-permute-done.109
  1433.1 11.7 collective-permute-done.122
  (1677 shorter events, 788.9 us)
Async XLA Ops:
  7.3 290.7 %all-gather.6.cloned.1.call-start = ((), (), s32[]{:S(2)}) async-start(), calls=%async_computation.7 | async-start | bytes 2621440 | tf_op jit(solution)/shard_map/all_gather | solution.py:1626
  20.5 59.8 %collective-permute-start.9 = (bf16[2,128,2048]{2,1,0:T(8,128)(2,1)}, bf16[2,128,2048]{2,1,0:T(8,128)(2,1)}, u32[]{:S(2)}, u32[]{:S(2)}) collective-permute-start(bf16[2,128,2048]{2,1,0:T(8,128)(2,1)} %pad_maximum_fusion.72), channel_id=1, source_target_pairs={{0,1},{1,0},{2,3},{3,2},{4,5},{5,4},{6,7},{7,6},{8,9},{9,8},{10,11... | collective-permute-start | bytes 3145736 | tf_op jit(solution)/shard_map/ppermute | solution.py:632
  69.4 54.0 %collective-permute-start.7 = (bf16[512,768]{1,0:T(8,128)(2,1)}, bf16[512,768]{1,0:T(8,128)(2,1)}, u32[]{:S(2)}, u32[]{:S(2)}) collective-permute-start(bf16[512,768]{1,0:T(8,128)(2,1)} %get-tuple-element.420), channel_id=1, source_target_pairs={{0,16},{16,0},{1,17},{17,1},{2,18},{18,2},{3,19},{19,3},{4,20},{20... | collective-permute-start | bytes 2359304 | tf_op jit(solution)/shard_map/ppermute | solution.py:636
  69.4 69.4 %collective-permute-start.6 = (bf16[512,768]{1,0:T(8,128)(2,1)}, bf16[512,768]{1,0:T(8,128)(2,1)}, u32[]{:S(2)}, u32[]{:S(2)}) collective-permute-start(bf16[512,768]{1,0:T(8,128)(2,1)} %get-tuple-element.419), channel_id=1, source_target_pairs={{0,16},{16,0},{1,17},{17,1},{2,18},{18,2},{3,19},{19,3},{4,20},{20... | collective-permute-start | bytes 2359304 | tf_op jit(solution)/shard_map/ppermute | solution.py:636
  83.4 56.6 %collective-permute-start.13 = (bf16[128,2048]{1,0:T(8,128)(2,1)}, bf16[128,2048]{1,0:T(8,128)(2,1)}, u32[]{:S(2)}, u32[]{:S(2)}) collective-permute-start(bf16[128,2048]{1,0:T(8,128)(2,1)} %get-tuple-element.467), channel_id=1, source_target_pairs={{0,4},{2,6},{4,0},{6,2},{8,12},{10,14},{12,8},{14,10},{1,5},{3,7},... | collective-permute-start | bytes 1572872 | tf_op jit(solution)/shard_map/ppermute | solution.py:628
  84.9 55.1 %collective-permute-start.10 = (bf16[128,2048]{1,0:T(8,128)(2,1)}, bf16[128,2048]{1,0:T(8,128)(2,1)}, u32[]{:S(2)}, u32[]{:S(2)}) collective-permute-start(bf16[128,2048]{1,0:T(8,128)(2,1)} %get-tuple-element.468), channel_id=1, source_target_pairs={{0,8},{2,10},{4,12},{6,14},{8,0},{10,2},{12,4},{14,6},{1,9},{3,11}... | collective-permute-start | bytes 1572872 | tf_op jit(solution)/shard_map/ppermute | solution.py:628
  86.3 77.2 %collective-permute-start.2 = (bf16[1024,768]{1,0:T(8,128)(2,1)}, bf16[1024,768]{1,0:T(8,128)(2,1)}, u32[]{:S(2)}, u32[]{:S(2)}) collective-permute-start(bf16[1024,768]{1,0:T(8,128)(2,1)} %shard_map.586), channel_id=1, source_target_pairs={{0,1},{1,0},{2,3},{3,2},{4,5},{5,4},{6,7},{7,6},{8,9},{9,8},{10,11... | collective-permute-start | bytes 4718600 | tf_op jit(solution)/shard_map/ppermute | solution.py:632
  123.4 38.5 %collective-permute-start.4 = (bf16[2,4,448,128]{3,2,1,0:T(8,128)(2,1)}, bf16[2,4,448,128]{3,2,1,0:T(8,128)(2,1)}, u32[]{:S(2)}, u32[]{:S(2)}) collective-permute-start(bf16[2,4,448,128]{3,2,1,0:T(8,128)(2,1)} %pad_maximum_fusion.89), channel_id=1, source_target_pairs={{0,4},{2,6},{4,0},{6,2},{8,12},{10,14},{12,8},{14,10},{1,5},{3,7},... | collective-permute-start | bytes 2752520 | tf_op jit(solution)/shard_map/ppermute | solution.py:628
  142.7 27.0 %collective-permute-start.11 = (bf16[256,2048]{1,0:T(8,128)(2,1)S(1)}, bf16[256,2048]{1,0:T(8,128)(2,1)S(1)}, u32[]{:S(2)}, u32[]{:S(2)}) collective-permute-start(bf16[256,2048]{1,0:T(8,128)(2,1)S(1)} %pad_maximum_fusion.73), channel_id=1, source_target_pairs={{0,4},{2,6},{4,0},{6,2},{8,12},{10,14},{12,8},{14,10},{1,5},{3,7},... | collective-permute-start | bytes 3145736 | tf_op jit(solution)/shard_map/ppermute | solution.py:628
  158.7 90.5 %collective-permute-start.18 = (bf16[2,256,512]{2,1,0:T(8,128)(2,1)}, bf16[2,256,512]{2,1,0:T(8,128)(2,1)}, u32[]{:S(2)}, u32[]{:S(2)}) collective-permute-start(bf16[2,256,512]{2,1,0:T(8,128)(2,1)} %pad_maximum_fusion.100), channel_id=1, source_target_pairs={{0,16},{16,0},{1,17},{17,1},{2,18},{18,2},{3,19},{19,3},{4,20},{20... | collective-permute-start | bytes 1572872 | tf_op jit(solution)/shard_map/ppermute | solution.py:636
  166.1 83.2 %collective-permute-start.16 = (bf16[512,768]{1,0:T(8,128)(2,1)}, bf16[512,768]{1,0:T(8,128)(2,1)}, u32[]{:S(2)}, u32[]{:S(2)}) collective-permute-start(bf16[512,768]{1,0:T(8,128)(2,1)} %get-tuple-element.426), channel_id=1, source_target_pairs={{0,16},{16,0},{1,17},{17,1},{2,18},{18,2},{3,19},{19,3},{4,20},{20... | collective-permute-start | bytes 2359304 | tf_op jit(solution)/shard_map/ppermute | solution.py:636
  166.1 83.2 %collective-permute-start.8 = (bf16[512,768]{1,0:T(8,128)(2,1)}, bf16[512,768]{1,0:T(8,128)(2,1)}, u32[]{:S(2)}, u32[]{:S(2)}) collective-permute-start(bf16[512,768]{1,0:T(8,128)(2,1)} %get-tuple-element.425), channel_id=1, source_target_pairs={{0,16},{16,0},{1,17},{17,1},{2,18},{18,2},{3,19},{19,3},{4,20},{20... | collective-permute-start | bytes 2359304 | tf_op jit(solution)/shard_map/ppermute | solution.py:636
  169.7 32.0 %collective-permute-start.15 = (bf16[512,2048]{1,0:T(8,128)(2,1)S(1)}, bf16[512,2048]{1,0:T(8,128)(2,1)S(1)}, u32[]{:S(2)}, u32[]{:S(2)}) collective-permute-start(bf16[512,2048]{1,0:T(8,128)(2,1)S(1)} %pad_maximum_fusion.32), channel_id=1, source_target_pairs={{0,2},{2,0},{4,6},{6,4},{8,10},{10,8},{12,14},{14,12},{1,3},{3,1},... | collective-permute-start | bytes 6291464 | tf_op jit(solution)/shard_map/ppermute | solution.py:628
  170.5 31.1 %collective-permute-start.12 = (bf16[512,2048]{1,0:T(8,128)(2,1)S(1)}, bf16[512,2048]{1,0:T(8,128)(2,1)S(1)}, u32[]{:S(2)}, u32[]{:S(2)}) collective-permute-start(bf16[512,2048]{1,0:T(8,128)(2,1)S(1)} %pad_maximum_fusion.31), channel_id=1, source_target_pairs={{0,2},{2,0},{4,6},{6,4},{8,10},{10,8},{12,14},{14,12},{1,3},{3,1},... | collective-permute-start | bytes 6291464 | tf_op jit(solution)/shard_map/ppermute | solution.py:628
  251.7 134.1 %all-gather.8.cloned.1.call-start = ((), (), s32[]{:S(2)}) async-start(), calls=%async_computation.8 | async-start | bytes 2621440 | tf_op jit(solution)/shard_map/all_gather | solution.py:1627
  252.4 177.2 %all-gather.10.cloned.1.call-start = ((), (), s32[]{:S(2)}) async-start(), calls=%async_computation.9 | async-start | bytes 5242880 | tf_op jit(solution)/shard_map/all_gather | solution.py:1640
  253.2 257.0 %all-gather.12.cloned.1.call-start = ((), (), s32[]{:S(2)}) async-start(), calls=%async_computation.10 | async-start | bytes 5242880 | tf_op jit(solution)/shard_map/all_gather | solution.py:1641
  254.3 301.8 %all-gather.14.cloned.1.call-start = ((), (), s32[]{:S(2)}) async-start(), calls=%async_computation.11 | async-start | bytes 2621440 | tf_op jit(solution)/shard_map/all_gather | solution.py:1644
  301.6 487.3 %reduce-scatter.8.cloned.1.call-start = ((), (), s32[]{:S(2)}) async-start(), calls=%async_computation.12 | async-start | bytes 2621440 | tf_op jit(solution)/shard_map/reduce_scatter | solution.py:1803
  308.6 25.3 %collective-permute-start.33 = (bf16[2,128,2048]{2,1,0:T(8,128)(2,1)S(1)}, bf16[2,128,2048]{2,1,0:T(8,128)(2,1)S(1)}, u32[]{:S(2)}, u32[]{:S(2)}) collective-permute-start(bf16[2,128,2048]{2,1,0:T(8,128)(2,1)S(1)} %dynamic-slice_convert_fusion.4), channel_id=1, source_target_pairs={{0,8},{2,10},{4,12},{6,14},{8,0},{10,2},{12,4},{14,6},{1,9},{3,11}... | collective-permute-start | bytes 3145736 | tf_op jit(solution)/shard_map/ppermute | solution.py:628
  312.2 25.8 %collective-permute-start.20 = (bf16[2,128,2048]{2,1,0:T(8,128)(2,1)S(1)}, bf16[2,128,2048]{2,1,0:T(8,128)(2,1)S(1)}, u32[]{:S(2)}, u32[]{:S(2)}) collective-permute-start(bf16[2,128,2048]{2,1,0:T(8,128)(2,1)S(1)} %dynamic-slice_convert_fusion.5), channel_id=1, source_target_pairs={{0,4},{2,6},{4,0},{6,2},{8,12},{10,14},{12,8},{14,10},{1,5},{3,7},... | collective-permute-start | bytes 3145736 | tf_op jit(solution)/shard_map/ppermute | solution.py:628
  350.7 31.7 %collective-permute-start.22 = (bf16[64,2048]{1,0:T(8,128)(2,1)S(1)}, bf16[64,2048]{1,0:T(8,128)(2,1)S(1)}, u32[]{:S(2)}, u32[]{:S(2)}) collective-permute-start(bf16[64,2048]{1,0:T(8,128)(2,1)S(1)} %fusion.171), channel_id=1, source_target_pairs={{0,1},{1,0},{2,3},{3,2},{4,5},{5,4},{6,7},{7,6},{8,9},{9,8},{10,11... | collective-permute-start | bytes 786440 | tf_op jit(solution)/shard_map/ppermute | solution.py:632
  586.9 46.3 %collective-permute-start.52 = (bf16[256,2048]{1,0:T(8,128)(2,1)}, bf16[256,2048]{1,0:T(8,128)(2,1)}, u32[]{:S(2)}, u32[]{:S(2)}) collective-permute-start(bf16[256,2048]{1,0:T(8,128)(2,1)} %convolution_convert_fusion.10), channel_id=1, source_target_pairs={{0,2},{2,0},{4,6},{6,4},{8,10},{10,8},{12,14},{14,12},{1,3},{3,1},... | collective-permute-start | bytes 3145736 | tf_op jit(solution)/shard_map/ppermute | solution.py:628
  588.6 47.7 %collective-permute-start.55 = (bf16[256,2048]{1,0:T(8,128)(2,1)}, bf16[256,2048]{1,0:T(8,128)(2,1)}, u32[]{:S(2)}, u32[]{:S(2)}) collective-permute-start(bf16[256,2048]{1,0:T(8,128)(2,1)} %convolution_convert_fusion.9), channel_id=1, source_target_pairs={{0,2},{2,0},{4,6},{6,4},{8,10},{10,8},{12,14},{14,12},{1,3},{3,1},... | collective-permute-start | bytes 3145736 | tf_op jit(solution)/shard_map/ppermute | solution.py:628
  723.3 164.0 %reduce-scatter.10.cloned.1.call-start = ((), (), s32[]{:S(2)}) async-start(), calls=%async_computation.13 | async-start | bytes 5242880 | tf_op jit(solution)/shard_map/reduce_scatter | solution.py:1803
  748.6 373.5 %reduce-scatter.12.cloned.1.call-start = ((), (), s32[]{:S(2)}) async-start(), calls=%async_computation.14 | async-start | bytes 5242880 | tf_op jit(solution)/shard_map/reduce_scatter | solution.py:1803
  790.1 33.7 %collective-permute-start.67 = (bf16[64,2048]{1,0:T(8,128)(2,1)S(1)}, bf16[64,2048]{1,0:T(8,128)(2,1)S(1)}, u32[]{:S(2)}, u32[]{:S(2)}) collective-permute-start(bf16[64,2048]{1,0:T(8,128)(2,1)S(1)} %multiply_convert_fusion.14), channel_id=1, source_target_pairs={{0,1},{1,0},{2,3},{3,2},{4,5},{5,4},{6,7},{7,6},{8,9},{9,8},{10,11... | collective-permute-start | bytes 786440 | tf_op jit(solution)/shard_map/ppermute | solution.py:632
  825.6 31.5 %collective-permute-start.82 = (bf16[2,128,2048]{2,1,0:T(8,128)(2,1)S(1)}, bf16[2,128,2048]{2,1,0:T(8,128)(2,1)S(1)}, u32[]{:S(2)}, u32[]{:S(2)}) collective-permute-start(bf16[2,128,2048]{2,1,0:T(8,128)(2,1)S(1)} %pad_maximum_fusion.86), channel_id=1, source_target_pairs={{0,8},{2,10},{4,12},{6,14},{8,0},{10,2},{12,4},{14,6},{1,9},{3,11}... | collective-permute-start | bytes 3145736 | tf_op jit(solution)/shard_map/ppermute | solution.py:628
  827.9 93.6 %collective-permute-start.84 = (bf16[2,64,2048]{2,1,0:T(8,128)(2,1)}, bf16[2,64,2048]{2,1,0:T(8,128)(2,1)}, u32[]{:S(2)}, u32[]{:S(2)}) collective-permute-start(bf16[2,64,2048]{2,1,0:T(8,128)(2,1)} %pad_maximum_fusion.110), channel_id=1, source_target_pairs={{0,1},{1,0},{2,3},{3,2},{4,5},{5,4},{6,7},{7,6},{8,9},{9,8},{10,11... | collective-permute-start | bytes 1572872 | tf_op jit(solution)/shard_map/ppermute | solution.py:632
  874.2 298.6 %reduce-scatter.14.cloned.1.call-start = ((), (), s32[]{:S(2)}) async-start(), calls=%async_computation.15 | async-start | bytes 4866048 | tf_op jit(solution)/shard_map/reduce_scatter | solution.py:1897
  958.4 353.4 %reduce-scatter.18.cloned.1.call-start = ((), (), s32[]{:S(2)}) async-start(), calls=%async_computation.17 | async-start | bytes 5242880 | tf_op jit(solution)/shard_map/reduce_scatter | solution.py:1803
  963.9 43.1 %collective-permute-start.89 = (bf16[2,256,4480]{2,1,0:T(8,128)(2,1)}, bf16[2,256,4480]{2,1,0:T(8,128)(2,1)}, u32[]{:S(2)}, u32[]{:S(2)}) collective-permute-start(bf16[2,256,4480]{2,1,0:T(8,128)(2,1)} %convolution_convert_fusion.refs_2_), channel_id=1, source_target_pairs={{0,2},{2,0},{4,6},{6,4},{8,10},{10,8},{12,14},{14,12},{1,3},{3,1},... | collective-permute-start | bytes 13762568 | tf_op jit(solution)/shard_map/ppermute | solution.py:628
  974.3 337.5 %reduce-scatter.20.cloned.1.call-start = ((), (), s32[]{:S(2)}) async-start(), calls=%async_computation.18 | async-start | bytes 327680 | tf_op jit(solution)/shard_map/reduce_scatter | solution.py:1803
  982.2 43.1 %collective-permute-start.85 = (bf16[2,256,4480]{2,1,0:T(8,128)(2,1)}, bf16[2,256,4480]{2,1,0:T(8,128)(2,1)}, u32[]{:S(2)}, u32[]{:S(2)}) collective-permute-start(bf16[2,256,4480]{2,1,0:T(8,128)(2,1)} %convolution_convert_fusion.1.refs_1_), channel_id=1, source_target_pairs={{0,2},{2,0},{4,6},{6,4},{8,10},{10,8},{12,14},{14,12},{1,3},{3,1},... | collective-permute-start | bytes 13762568 | tf_op jit(solution)/shard_map/ppermute | solution.py:628
  1016.9 52.3 %collective-permute-start.90 = (bf16[2,128,4480]{2,1,0:T(8,128)(2,1)}, bf16[2,128,4480]{2,1,0:T(8,128)(2,1)S(1)}, u32[]{:S(2)}, u32[]{:S(2)}) collective-permute-start(bf16[2,128,4480]{2,1,0:T(8,128)(2,1)} %dynamic-slice_convert_fusion), channel_id=1, source_target_pairs={{0,8},{2,10},{4,12},{6,14},{8,0},{10,2},{12,4},{14,6},{1,9},{3,11}... | collective-permute-start | bytes 6881288 | tf_op jit(solution)/shard_map/ppermute | solution.py:628
  1038.7 53.0 %collective-permute-start.86 = (bf16[2,128,4480]{2,1,0:T(8,128)(2,1)}, bf16[2,128,4480]{2,1,0:T(8,128)(2,1)}, u32[]{:S(2)}, u32[]{:S(2)}) collective-permute-start(bf16[2,128,4480]{2,1,0:T(8,128)(2,1)} %dynamic-slice_convert_fusion.1), channel_id=1, source_target_pairs={{0,4},{2,6},{4,0},{6,2},{8,12},{10,14},{12,8},{14,10},{1,5},{3,7},... | collective-permute-start | bytes 6881288 | tf_op jit(solution)/shard_map/ppermute | solution.py:628
  1041.8 278.2 %reduce-scatter.16.cloned.1.call-start = ((), (), s32[]{:S(2)}) async-start(), calls=%async_computation.16 | async-start | bytes 4866048 | tf_op jit(solution)/shard_map/reduce_scatter | solution.py:1897
  1072.3 43.4 %collective-permute-start.91 = (bf16[2,64,4480]{2,1,0:T(8,128)(2,1)S(1)}, bf16[2,64,4480]{2,1,0:T(8,128)(2,1)S(1)}, u32[]{:S(2)}, u32[]{:S(2)}) collective-permute-start(bf16[2,64,4480]{2,1,0:T(8,128)(2,1)S(1)} %dynamic-slice_convert_fusion.2), channel_id=1, source_target_pairs={{0,4},{2,6},{4,0},{6,2},{8,12},{10,14},{12,8},{14,10},{1,5},{3,7},... | collective-permute-start | bytes 3440648 | tf_op jit(solution)/shard_map/ppermute | solution.py:628
  1094.0 26.5 %collective-permute-start.87 = (bf16[2,64,4480]{2,1,0:T(8,128)(2,1)S(1)}, bf16[2,64,4480]{2,1,0:T(8,128)(2,1)S(1)}, u32[]{:S(2)}, u32[]{:S(2)}) collective-permute-start(bf16[2,64,4480]{2,1,0:T(8,128)(2,1)S(1)} %dynamic-slice_convert_fusion.3), channel_id=1, source_target_pairs={{0,8},{2,10},{4,12},{6,14},{8,0},{10,2},{12,4},{14,6},{1,9},{3,11}... | collective-permute-start | bytes 3440648 | tf_op jit(solution)/shard_map/ppermute | solution.py:628
  1134.3 25.9 %collective-permute-start.88 = (bf16[64,4480]{1,0:T(8,128)(2,1)}, bf16[64,4480]{1,0:T(8,128)(2,1)}, u32[]{:S(2)}, u32[]{:S(2)}) collective-permute-start(bf16[64,4480]{1,0:T(8,128)(2,1)} %constant_dynamic-update-slice_fusion.41), channel_id=1, source_target_pairs={{0,1},{1,0},{2,3},{3,2},{4,5},{5,4},{6,7},{7,6},{8,9},{9,8},{10,11... | collective-permute-start | bytes 1720328 | tf_op jit(solution)/shard_map/ppermute | solution.py:632
  1147.4 31.4 %collective-permute-start.96 = (bf16[1408,256]{1,0:T(8,128)(2,1)}, bf16[1408,256]{1,0:T(8,128)(2,1)}, u32[]{:S(2)}, u32[]{:S(2)}) collective-permute-start(bf16[1408,256]{1,0:T(8,128)(2,1)} %dynamic-slice_convert_fusion.6), channel_id=1, source_target_pairs={{0,8},{2,10},{4,12},{6,14},{8,0},{10,2},{12,4},{14,6},{1,9},{3,11}... | collective-permute-start | bytes 2162696 | tf_op jit(solution)/shard_map/ppermute | solution.py:628
  1172.9 101.9 %collective-permute-start.101 = (bf16[1056,768]{1,0:T(8,128)(2,1)}, bf16[1056,768]{1,0:T(8,128)(2,1)S(1)}, u32[]{:S(2)}, u32[]{:S(2)}) collective-permute-start(bf16[1056,768]{1,0:T(8,128)(2,1)} %shard_map.613), channel_id=1, source_target_pairs={{0,1},{1,0},{2,3},{3,2},{4,5},{5,4},{6,7},{7,6},{8,9},{9,8},{10,11... | collective-permute-start | bytes 4866056 | tf_op jit(solution)/shard_map/ppermute | solution.py:632
  1195.4 25.9 %collective-permute-start.103 = (bf16[64,8192]{1,0:T(8,128)(2,1)}, bf16[64,8192]{1,0:T(8,128)(2,1)}, u32[]{:S(2)}, u32[]{:S(2)}) collective-permute-start(bf16[64,8192]{1,0:T(8,128)(2,1)} %shard_map.615), channel_id=1, source_target_pairs={{0,4},{2,6},{4,0},{6,2},{8,12},{10,14},{12,8},{14,10},{1,5},{3,7},... | collective-permute-start | bytes 3145736 | tf_op jit(solution)/shard_map/ppermute | solution.py:628
  1201.0 26.3 %collective-permute-start.99 = (bf16[64,8192]{1,0:T(8,128)(2,1)}, bf16[64,8192]{1,0:T(8,128)(2,1)S(1)}, u32[]{:S(2)}, u32[]{:S(2)}) collective-permute-start(bf16[64,8192]{1,0:T(8,128)(2,1)} %shard_map.611), channel_id=1, source_target_pairs={{0,8},{2,10},{4,12},{6,14},{8,0},{10,2},{12,4},{14,6},{1,9},{3,11}... | collective-permute-start | bytes 3145736 | tf_op jit(solution)/shard_map/ppermute | solution.py:628
  1223.2 48.3 %collective-permute-start.104 = (bf16[128,8192]{1,0:T(8,128)(2,1)S(1)}, bf16[128,8192]{1,0:T(8,128)(2,1)S(1)}, u32[]{:S(2)}, u32[]{:S(2)}) collective-permute-start(bf16[128,8192]{1,0:T(8,128)(2,1)S(1)} %pad_maximum_fusion.37), channel_id=1, source_target_pairs={{0,8},{2,10},{4,12},{6,14},{8,0},{10,2},{12,4},{14,6},{1,9},{3,11}... | collective-permute-start | bytes 6291464 | tf_op jit(solution)/shard_map/ppermute | solution.py:628
  1230.6 46.6 %collective-permute-start.100 = (bf16[128,8192]{1,0:T(8,128)(2,1)}, bf16[128,8192]{1,0:T(8,128)(2,1)}, u32[]{:S(2)}, u32[]{:S(2)}) collective-permute-start(bf16[128,8192]{1,0:T(8,128)(2,1)} %pad_maximum_fusion.36), channel_id=1, source_target_pairs={{0,4},{2,6},{4,0},{6,2},{8,12},{10,14},{12,8},{14,10},{1,5},{3,7},... | collective-permute-start | bytes 6291464 | tf_op jit(solution)/shard_map/ppermute | solution.py:628
  1292.2 70.8 %collective-permute-start.106 = (bf16[2,128,384]{2,1,0:T(8,128)(2,1)}, bf16[2,128,384]{2,1,0:T(8,128)(2,1)S(1)}, u32[]{:S(2)}, u32[]{:S(2)}) collective-permute-start(bf16[2,128,384]{2,1,0:T(8,128)(2,1)} %shard_map.617), channel_id=1, source_target_pairs={{0,1},{1,0},{2,3},{3,2},{4,5},{5,4},{6,7},{7,6},{8,9},{9,8},{10,11... | collective-permute-start | bytes 589832 | tf_op jit(solution)/shard_map/ppermute | solution.py:632
  1295.6 83.0 %collective-permute-start.110 = (bf16[256,1024]{1,0:T(8,128)(2,1)}, bf16[256,1024]{1,0:T(8,128)(2,1)}, u32[]{:S(2)}, u32[]{:S(2)}) collective-permute-start(bf16[256,1024]{1,0:T(8,128)(2,1)} %constant_dynamic-slice_fusion.2), channel_id=1, source_target_pairs={{0,16},{16,0},{1,17},{17,1},{2,18},{18,2},{3,19},{19,3},{4,20},{20... | collective-permute-start | bytes 1572872 | tf_op jit(solution)/shard_map/ppermute | solution.py:636
  (497 other events, 3879.0 us)
Sparse Core Ops, SparseCore 0:
  251.8 46.1 all-gather.5
  300.1 44.6 all-gather.7
  346.4 83.0 all-gather.9
  431.0 79.1 all-gather.11
  511.6 44.4 all-gather.13
  723.5 51.0 reduce-scatter.7
  777.5 98.5 reduce-scatter.9
  879.0 82.4 reduce-scatter.11
  963.8 89.3 reduce-scatter.13
  1056.0 75.7 reduce-scatter.17
  1134.6 22.0 reduce-scatter.19
  1201.1 93.3 reduce-scatter.15

commit v6 on v5

--- a/solution.py
+++ b/solution.py
@@ -1949,7 +1949,7 @@
     lines = pair_grad.shape[0] // 8
     packed = jnp.pad(packed, ((0, -packed.shape[0] % lines), (0, 0)))
     pair_grad = jnp.concatenate([pair_grad, packed], 0)
-    pair_grad = sum_rows(pair_grad, masks, 0)
+    pair_grad = sum_rows(pair_grad, orders[0], 0)
     joined_backs = [
         norm_back(value, attn_gain, total[:, :joint] + right_dot(mid, down_wide))
         for value, total, mid in zip(joined_cut, normed_sums, lows_cut)
@@ -1991,14 +1991,6 @@
         input_halves += [value, got]
         quads += [(value, got), (got, value)]
 
-    def whole_rows(start):
-        columns = slice(start, start + width)
-        return [jnp.where(core == 0, a[:, columns], b[:, columns]) for a, b in quads]
-
-    grad_hidden = jnp.concatenate(whole_rows(0), 0)
-    grad_embedding = jnp.concatenate(whole_rows(width), 0)
-    layer_out = jnp.concatenate(whole_rows(2 * width) + whole_rows(3 * width), 0)
-
     attn_grad = left_dot(attended_halves[0], branch_halves[0]) + left_dot(
         attended_halves[1], branch_halves[1]
     )
@@ -2024,17 +2016,29 @@
     away = jnp.stack([down_parts[1], down_parts[3]], 0).astype(low)
     away = state_swap(hold(away, *input_halves)).astype(full)
     down_sum = down_parts[0] + away[0] + dp_swap((down_parts[2] + away[1]).astype(low))
-    down_all = gather_rows(down_sum.astype(low)[None], masks, 0).reshape(quarter, 3 * rank)
+    down_all = natural_heads(gather_rows(down_sum.astype(low)[None], orders[0], 0))
+    down_all = down_all.reshape(quarter, 3 * rank)
     down_all = down_all.astype(full)
     out_downs = [down_all[:, index * rank : (index + 1) * rank] for index in range(3)]
 
     pair_grad = hold(pair_grad, *input_halves)
     pair_grad = pair_grad + state_swap(pair_grad)
     pair_grad = pair_grad + dp_swap(pair_grad)
+    quads = [(hold(a, down_sum, pair_grad), b) for a, b in (quads[0], quads[2])]
+    quads = [pair for a, b in quads for pair in ((a, b), (b, a))]
+
+    def whole_rows(start):
+        columns = slice(start, start + width)
+        return [jnp.where(core == 0, a[:, columns], b[:, columns]) for a, b in quads]
+
+    grad_hidden = jnp.concatenate(whole_rows(0), 0)
+    grad_embedding = jnp.concatenate(whole_rows(width), 0)
+    layer_out = jnp.concatenate(whole_rows(2 * width) + whole_rows(3 * width), 0)
+
     row = lax.broadcasted_iota(jnp.int32, (pair_grad.shape[0], 1), 0)
-    in_main = head * pair_grad.shape[0] + row < width
+    in_main = chunk_of(orders[0]) * pair_grad.shape[0] + row < width
     down_m_squares = jnp.sum(jnp.where(in_main, jnp.square(pair_grad[:, 2 * states :]), 0.0))
-    pair_grad = gather_rows(pair_grad.astype(low), masks, 0).astype(full)
+    pair_grad = gather_rows(pair_grad.astype(low), orders[0], 0).astype(full)
     vector_grad = pair_grad[:width, : 2 * states]
     out_down_mlp = lax.dynamic_slice(pair_grad, (place * split_m, 2 * states), (split_m, rank))
     packed = pair_grad[width:]

time: 1470 us -> 1450 us (0.986)
  matrix products: 247 us -> 229 us
  starting transfers between devices: 132 us -> 116 us
    ppermute x10, starting transfers between devices: 31.2 us -> 15.7 us  [dp_swap(): return lax.ppermute(value, DP, [(0, 1), (1, 0)])]
    unnamed x868 -> x894, local copies, waits for them, and re-layouts: 90.4 us -> 91.1 us
  transfers between devices with their start and end apart: 135 -> 135, of which waited for: 69 -> 66; matrix products, arithmetic and copies ran while one was open for 40% -> 41% of each run, Pallas kernels for 5% -> 6%
where the time goes in v6:
time: 1450 us; the launch traced here: 1440 us
  waiting for transfers between devices  524 us (36%)
  other arithmetic  277 us (19%)
  matrix products  229 us (16%)
  local copies, waits for them, and re-layouts  176 us (12%)
  starting transfers between devices  116 us (8%)
  Pallas kernels  88 us (6%)
  between operations  30.9 us (2%)
    ppermute x93, waiting for transfers between devices, head_swap(): return lax.ppermute(value, HEAD, [(i, i ^ mask) for i in range(count)])  308 us
    ppermute x10, waiting for transfers between devices, dp_swap(): return lax.ppermute(value, DP, [(0, 1), (1, 0)])  104 us
    ppermute x16, waiting for transfers between devices, state_swap(): return lax.ppermute(value, STATE, [(0, 1), (1, 0)])  92.8 us
    unnamed x894, local copies, waits for them, and re-layouts  91.1 us
    dot_general x30, matrix products, plain_dot(): return jnp.dot(left, right, preferred_element_type=jnp.float32)  87.6 us
    ppermute x93, starting transfers between devices, head_swap(): return lax.ppermute(value, HEAD, [(i, i ^ mask) for i in range(count)])  79.9 us
    dot_general x25, matrix products, right_dot(): lax.dot_general(left, right, (((1,), (1,)), ((), ())), preferred_element_...  78.8 us
    dot_general x23, matrix products, left_dot(): lax.dot_general(left, right, (((0,), (0,)), ((), ())), preferred_element_...  62.2 us
  transfers between devices with their start and end apart: 135, of which 66 were waited for; matrix products, arithmetic and copies ran while one was open for 41% of the time, Pallas kernels for 6%

profile of v6, /device:TPU:0, one launch (start us, length us, event | category | flops | bytes accessed | tf_op | source)
XLA Modules:
  0.0 1441.2 jit_solution(17177262420604532419)
XLA Ops:
  44.3 19.8 %collective-permute-done.1.refs_1_ = bf16[2,944,128]{2,1,0:T(8,128)(2,1)S(1)} collective-permute-done((bf16[2,944,128]{2,1,0:T(8,128)(2,1)}, bf16[2,944,128]{2,1,0:T(8,128)(2,1)S(1)}, u32[]{:S(2)}, u32[]{:S(2)}) %collective-permute-start.1) | collective-permute-done | bytes 483360 | tf_op jit(solution)/shard_map/ppermute | solution.py:636
  72.5 8.1 multiply_convert_fusion.7
  90.8 32.6 %collective-permute-done.7.refs_2_.refs_4_ = bf16[512,768]{1,0:T(8,128)(2,1)} collective-permute-done((bf16[512,768]{1,0:T(8,128)(2,1)}, bf16[512,768]{1,0:T(8,128)(2,1)}, u32[]{:S(2)}, u32[]{:S(2)}) %collective-permute-start.7) | collective-permute-done | bytes 786464 | tf_op jit(solution)/shard_map/ppermute | solution.py:636
  124.9 13.9 collective-permute-done.6.refs_1_.refs_3_
  144.0 14.1 collective-permute-done.17
  185.6 6.7 fusion.72.refs_1_
  217.3 6.5 fusion.73.refs_2_
  223.8 25.7 %collective-permute-done.8.refs_0_ = bf16[512,768]{1,0:T(8,128)(2,1)} collective-permute-done((bf16[512,768]{1,0:T(8,128)(2,1)}, bf16[512,768]{1,0:T(8,128)(2,1)}, u32[]{:S(2)}, u32[]{:S(2)}) %collective-permute-start.8) | collective-permute-done | bytes 786464 | tf_op jit(solution)/shard_map/ppermute | solution.py:636
  258.9 6.8 fusion.60.own_ref
  273.3 21.2 %shard_map.590 = (bf16[2048,256]{1,0:T(8,128)(2,1)S(1)}, f32[2,1,2048]{2,1,0:T(1,128)S(1)}) custom-call(s32[8]{0:T(128)S(1)} %and_select_fusion.low_ref, bf16[2048,256]{1,0:T(8,128)(2,1)S(1)} %get-tuple-element.74.q_ref, bf16[2048,256]{1,0:T(8,128)(2,1)S(1)} %get-tuple-element.75.k_ref, bf16[2048,256]{1,0:T(8,128)(2,1)S(1)} %get-tuple-element.76.v_ref, ...), custom_call_target="tpu_custom_call" | custom-call | flops 23622320128 | bytes 4194304 | tf_op jit(solution)/shard_map/pallas_call | solution.py:825
  315.0 19.2 %collective-permute-done.33 = bf16[2,128,2048]{2,1,0:T(8,128)(2,1)S(1)} collective-permute-done((bf16[2,128,2048]{2,1,0:T(8,128)(2,1)S(1)}, bf16[2,128,2048]{2,1,0:T(8,128)(2,1)S(1)}, u32[]{:S(2)}, u32[]{:S(2)}) %collective-permute-start.33) | collective-permute-done | bytes 1048608 | tf_op jit(solution)/shard_map/ppermute | solution.py:628
  338.8 9.9 collective-permute-done.34
  353.5 8.6 collective-permute-done.35
  362.1 20.3 %collective-permute-done.22 = bf16[64,2048]{1,0:T(8,128)(2,1)S(1)} collective-permute-done((bf16[64,2048]{1,0:T(8,128)(2,1)S(1)}, bf16[64,2048]{1,0:T(8,128)(2,1)S(1)}, u32[]{:S(2)}, u32[]{:S(2)}) %collective-permute-start.22) | collective-permute-done | bytes 262176 | tf_op jit(solution)/shard_map/ppermute | solution.py:632
  410.6 9.5 multiply_convert_fusion.11
  420.1 9.8 all-gather.10.cloned.1.call-done
  437.1 9.1 multiply_convert_fusion.10
  455.3 11.0 collective-permute-done.27
  489.3 7.0 collective-permute-done.43
  510.3 7.9 fusion.313
  525.8 6.6 fusion.49
  547.0 7.2 shard_map.595
  556.5 8.2 multiply_reduce_fusion.16
  589.9 17.4 %shard_map.597 = (f32[1024,512]{1,0:T(8,128)S(1)}, f32[1024,8]{1,0:T(8,128)S(1)}, f32[1024,8]{1,0:T(8,128)S(1)}, f32[8,1024]{1,0:T(8,128)S(1)}, f32[1024,64]{1,0:T(8,128)S(1)}, /*index=5*/f32[1024,64]{1,0:T(8,128)S(1)}) custom-call(s32[5]{0:T(128)S(1)} %get-tuple-element.635.ends_ref, f32[1024,512]{1,0:T(8,128)S(1)} %get-tuple-element.298.x_ref, ...), custom_call_target="tpu_custom_call" | custom-call | flops 19327352832 | bytes 4194304 | tf_op jit(solution)/shard_map/pallas_call | solution.py:1273
  640.3 9.2 collective-permute-done.53
  674.1 11.0 collective-permute-done.72
  705.3 6.2 collective-permute-done.61
  741.9 6.6 convolution_convert_fusion.5
  759.4 9.2 collective-permute-done.78
  789.3 17.7 %collective-permute-done.80 = bf16[64,2048]{1,0:T(8,128)(2,1)S(1)} collective-permute-done((bf16[64,2048]{1,0:T(8,128)(2,1)S(1)}, bf16[64,2048]{1,0:T(8,128)(2,1)S(1)}, u32[]{:S(2)}, u32[]{:S(2)}) %collective-permute-start.80) | collective-permute-done | bytes 262176 | tf_op jit(solution)/shard_map/ppermute | solution.py:632
  808.5 12.8 collective-permute-done.67
  825.4 11.0 collective-permute-done.68
  839.1 19.1 %collective-permute-done.82 = bf16[2,128,2048]{2,1,0:T(8,128)(2,1)S(1)} collective-permute-done((bf16[2,128,2048]{2,1,0:T(8,128)(2,1)S(1)}, bf16[2,128,2048]{2,1,0:T(8,128)(2,1)S(1)}, u32[]{:S(2)}, u32[]{:S(2)}) %collective-permute-start.82) | collective-permute-done | bytes 1048608 | tf_op jit(solution)/shard_map/ppermute | solution.py:628
  869.0 6.3 convolution_convert_fusion.4
  893.4 27.9 %shard_map.603 = (f32[2048,256]{1,0:T(8,128)S(1)}, f32[2048,256]{1,0:T(8,128)S(1)}, f32[2048,256]{1,0:T(8,128)S(1)}) custom-call(s32[8]{0:T(128)S(1)} %copy-done.32, bf16[2048,256]{1,0:T(8,128)(2,1)S(1)} %copy-done.26, bf16[2048,256]{1,0:T(8,128)(2,1)S(1)} %copy-done.28, bf16[2048,256]{1,0:T(8,128)(2,1)S(1)} %copy-done.30, bf16[2048,256]{1,0:T(8,128)(2,1)S(1)} %copy-done.5, ...), custom_call_target="tpu_custom_call" | custom-call | flops 32212254720 | bytes 10485760 | tf_op jit(solution)/shard_map/pallas_call | solution.py:902
  926.9 9.7 convolution_convert_fusion.refs_2_
  936.7 8.8 convolution_convert_fusion.1.refs_1_
  1002.7 6.4 fusion.12
  1009.1 7.9 convert_add_fusion
  1021.4 8.1 convert_add_fusion.1
  1042.0 28.7 %collective-permute-done.90 = bf16[2,128,4480]{2,1,0:T(8,128)(2,1)S(1)} collective-permute-done((bf16[2,128,4480]{2,1,0:T(8,128)(2,1)}, bf16[2,128,4480]{2,1,0:T(8,128)(2,1)S(1)}, u32[]{:S(2)}, u32[]{:S(2)}) %collective-permute-start.90) | collective-permute-done | bytes 2293792 | tf_op jit(solution)/shard_map/ppermute | solution.py:628
  1075.5 12.2 collective-permute-done.86
  1092.7 18.5 %collective-permute-done.91 = bf16[2,64,4480]{2,1,0:T(8,128)(2,1)S(1)} collective-permute-done((bf16[2,64,4480]{2,1,0:T(8,128)(2,1)S(1)}, bf16[2,64,4480]{2,1,0:T(8,128)(2,1)S(1)}, u32[]{:S(2)}, u32[]{:S(2)}) %collective-permute-start.91) | collective-permute-done | bytes 1146912 | tf_op jit(solution)/shard_map/ppermute | solution.py:628
  1143.6 10.6 collective-permute-done.92
  1159.0 7.2 collective-permute-done.88
  1212.1 15.4 %collective-permute-done.99 = bf16[64,8192]{1,0:T(8,128)(2,1)} collective-permute-done((bf16[64,8192]{1,0:T(8,128)(2,1)}, bf16[64,8192]{1,0:T(8,128)(2,1)}, u32[]{:S(2)}, u32[]{:S(2)}) %collective-permute-start.99) | collective-permute-done | bytes 1048608 | tf_op jit(solution)/shard_map/ppermute | solution.py:628
  1240.4 37.9 %collective-permute-done.100 = bf16[128,8192]{1,0:T(8,128)(2,1)S(1)} collective-permute-done((bf16[128,8192]{1,0:T(8,128)(2,1)S(1)}, bf16[128,8192]{1,0:T(8,128)(2,1)S(1)}, u32[]{:S(2)}, u32[]{:S(2)}) %collective-permute-start.100) | collective-permute-done | bytes 2097184 | tf_op jit(solution)/shard_map/ppermute | solution.py:628
  1351.0 7.2 collective-permute-done.109
  (1707 shorter events, 788.0 us)
Async XLA Ops:
  7.3 291.0 %all-gather.6.cloned.1.call-start = ((), (), s32[]{:S(2)}) async-start(), calls=%async_computation.7 | async-start | bytes 2621440 | tf_op jit(solution)/shard_map/all_gather | solution.py:1626
  20.5 60.1 %collective-permute-start.9 = (bf16[2,128,2048]{2,1,0:T(8,128)(2,1)}, bf16[2,128,2048]{2,1,0:T(8,128)(2,1)}, u32[]{:S(2)}, u32[]{:S(2)}) collective-permute-start(bf16[2,128,2048]{2,1,0:T(8,128)(2,1)} %pad_maximum_fusion.72), channel_id=1, source_target_pairs={{0,1},{1,0},{2,3},{3,2},{4,5},{5,4},{6,7},{7,6},{8,9},{9,8},{10,11... | collective-permute-start | bytes 3145736 | tf_op jit(solution)/shard_map/ppermute | solution.py:632
  69.4 54.0 %collective-permute-start.7 = (bf16[512,768]{1,0:T(8,128)(2,1)}, bf16[512,768]{1,0:T(8,128)(2,1)}, u32[]{:S(2)}, u32[]{:S(2)}) collective-permute-start(bf16[512,768]{1,0:T(8,128)(2,1)} %get-tuple-element.420), channel_id=1, source_target_pairs={{0,16},{16,0},{1,17},{17,1},{2,18},{18,2},{3,19},{19,3},{4,20},{20... | collective-permute-start | bytes 2359304 | tf_op jit(solution)/shard_map/ppermute | solution.py:636
  69.4 69.4 %collective-permute-start.6 = (bf16[512,768]{1,0:T(8,128)(2,1)}, bf16[512,768]{1,0:T(8,128)(2,1)}, u32[]{:S(2)}, u32[]{:S(2)}) collective-permute-start(bf16[512,768]{1,0:T(8,128)(2,1)} %get-tuple-element.419), channel_id=1, source_target_pairs={{0,16},{16,0},{1,17},{17,1},{2,18},{18,2},{3,19},{19,3},{4,20},{20... | collective-permute-start | bytes 2359304 | tf_op jit(solution)/shard_map/ppermute | solution.py:636
  83.7 56.3 %collective-permute-start.13 = (bf16[128,2048]{1,0:T(8,128)(2,1)}, bf16[128,2048]{1,0:T(8,128)(2,1)}, u32[]{:S(2)}, u32[]{:S(2)}) collective-permute-start(bf16[128,2048]{1,0:T(8,128)(2,1)} %get-tuple-element.467), channel_id=1, source_target_pairs={{0,4},{2,6},{4,0},{6,2},{8,12},{10,14},{12,8},{14,10},{1,5},{3,7},... | collective-permute-start | bytes 1572872 | tf_op jit(solution)/shard_map/ppermute | solution.py:628
  85.2 54.8 %collective-permute-start.10 = (bf16[128,2048]{1,0:T(8,128)(2,1)}, bf16[128,2048]{1,0:T(8,128)(2,1)}, u32[]{:S(2)}, u32[]{:S(2)}) collective-permute-start(bf16[128,2048]{1,0:T(8,128)(2,1)} %get-tuple-element.468), channel_id=1, source_target_pairs={{0,8},{2,10},{4,12},{6,14},{8,0},{10,2},{12,4},{14,6},{1,9},{3,11}... | collective-permute-start | bytes 1572872 | tf_op jit(solution)/shard_map/ppermute | solution.py:628
  86.5 77.2 %collective-permute-start.2 = (bf16[1024,768]{1,0:T(8,128)(2,1)}, bf16[1024,768]{1,0:T(8,128)(2,1)}, u32[]{:S(2)}, u32[]{:S(2)}) collective-permute-start(bf16[1024,768]{1,0:T(8,128)(2,1)} %shard_map.586), channel_id=1, source_target_pairs={{0,1},{1,0},{2,3},{3,2},{4,5},{5,4},{6,7},{7,6},{8,9},{9,8},{10,11... | collective-permute-start | bytes 4718600 | tf_op jit(solution)/shard_map/ppermute | solution.py:632
  123.4 38.7 %collective-permute-start.4 = (bf16[2,4,448,128]{3,2,1,0:T(8,128)(2,1)}, bf16[2,4,448,128]{3,2,1,0:T(8,128)(2,1)}, u32[]{:S(2)}, u32[]{:S(2)}) collective-permute-start(bf16[2,4,448,128]{3,2,1,0:T(8,128)(2,1)} %pad_maximum_fusion.89), channel_id=1, source_target_pairs={{0,4},{2,6},{4,0},{6,2},{8,12},{10,14},{12,8},{14,10},{1,5},{3,7},... | collective-permute-start | bytes 2752520 | tf_op jit(solution)/shard_map/ppermute | solution.py:628
  142.7 27.2 %collective-permute-start.11 = (bf16[256,2048]{1,0:T(8,128)(2,1)S(1)}, bf16[256,2048]{1,0:T(8,128)(2,1)S(1)}, u32[]{:S(2)}, u32[]{:S(2)}) collective-permute-start(bf16[256,2048]{1,0:T(8,128)(2,1)S(1)} %pad_maximum_fusion.73), channel_id=1, source_target_pairs={{0,4},{2,6},{4,0},{6,2},{8,12},{10,14},{12,8},{14,10},{1,5},{3,7},... | collective-permute-start | bytes 3145736 | tf_op jit(solution)/shard_map/ppermute | solution.py:628
  159.0 90.6 %collective-permute-start.18 = (bf16[2,256,512]{2,1,0:T(8,128)(2,1)}, bf16[2,256,512]{2,1,0:T(8,128)(2,1)}, u32[]{:S(2)}, u32[]{:S(2)}) collective-permute-start(bf16[2,256,512]{2,1,0:T(8,128)(2,1)} %pad_maximum_fusion.100), channel_id=1, source_target_pairs={{0,16},{16,0},{1,17},{17,1},{2,18},{18,2},{3,19},{19,3},{4,20},{20... | collective-permute-start | bytes 1572872 | tf_op jit(solution)/shard_map/ppermute | solution.py:636
  166.4 83.3 %collective-permute-start.16 = (bf16[512,768]{1,0:T(8,128)(2,1)}, bf16[512,768]{1,0:T(8,128)(2,1)}, u32[]{:S(2)}, u32[]{:S(2)}) collective-permute-start(bf16[512,768]{1,0:T(8,128)(2,1)} %get-tuple-element.426), channel_id=1, source_target_pairs={{0,16},{16,0},{1,17},{17,1},{2,18},{18,2},{3,19},{19,3},{4,20},{20... | collective-permute-start | bytes 2359304 | tf_op jit(solution)/shard_map/ppermute | solution.py:636
  166.4 83.2 %collective-permute-start.8 = (bf16[512,768]{1,0:T(8,128)(2,1)}, bf16[512,768]{1,0:T(8,128)(2,1)}, u32[]{:S(2)}, u32[]{:S(2)}) collective-permute-start(bf16[512,768]{1,0:T(8,128)(2,1)} %get-tuple-element.425), channel_id=1, source_target_pairs={{0,16},{16,0},{1,17},{17,1},{2,18},{18,2},{3,19},{19,3},{4,20},{20... | collective-permute-start | bytes 2359304 | tf_op jit(solution)/shard_map/ppermute | solution.py:636
  252.0 132.7 %all-gather.8.cloned.1.call-start = ((), (), s32[]{:S(2)}) async-start(), calls=%async_computation.8 | async-start | bytes 2621440 | tf_op jit(solution)/shard_map/all_gather | solution.py:1627
  252.7 177.1 %all-gather.10.cloned.1.call-start = ((), (), s32[]{:S(2)}) async-start(), calls=%async_computation.9 | async-start | bytes 5242880 | tf_op jit(solution)/shard_map/all_gather | solution.py:1640
  253.5 256.8 %all-gather.12.cloned.1.call-start = ((), (), s32[]{:S(2)}) async-start(), calls=%async_computation.10 | async-start | bytes 5242880 | tf_op jit(solution)/shard_map/all_gather | solution.py:1641
  254.8 301.6 %all-gather.14.cloned.1.call-start = ((), (), s32[]{:S(2)}) async-start(), calls=%async_computation.11 | async-start | bytes 2621440 | tf_op jit(solution)/shard_map/all_gather | solution.py:1644
  301.8 486.2 %reduce-scatter.8.cloned.1.call-start = ((), (), s32[]{:S(2)}) async-start(), calls=%async_computation.12 | async-start | bytes 2621440 | tf_op jit(solution)/shard_map/reduce_scatter | solution.py:1803
  351.1 31.3 %collective-permute-start.22 = (bf16[64,2048]{1,0:T(8,128)(2,1)S(1)}, bf16[64,2048]{1,0:T(8,128)(2,1)S(1)}, u32[]{:S(2)}, u32[]{:S(2)}) collective-permute-start(bf16[64,2048]{1,0:T(8,128)(2,1)S(1)} %fusion.171), channel_id=1, source_target_pairs={{0,1},{1,0},{2,3},{3,2},{4,5},{5,4},{6,7},{7,6},{8,9},{9,8},{10,11... | collective-permute-start | bytes 786440 | tf_op jit(solution)/shard_map/ppermute | solution.py:632
  407.1 26.6 %collective-permute-start.38 = (bf16[256,2048]{1,0:T(8,128)(2,1)}, bf16[256,2048]{1,0:T(8,128)(2,1)}, u32[]{:S(2)}, u32[]{:S(2)}) collective-permute-start(bf16[256,2048]{1,0:T(8,128)(2,1)} %pad_maximum_fusion.80), channel_id=1, source_target_pairs={{0,2},{2,0},{4,6},{6,4},{8,10},{10,8},{12,14},{14,12},{1,3},{3,1},... | collective-permute-start | bytes 3145736 | tf_op jit(solution)/shard_map/ppermute | solution.py:628
  587.3 46.5 %collective-permute-start.52 = (bf16[256,2048]{1,0:T(8,128)(2,1)}, bf16[256,2048]{1,0:T(8,128)(2,1)}, u32[]{:S(2)}, u32[]{:S(2)}) collective-permute-start(bf16[256,2048]{1,0:T(8,128)(2,1)} %convolution_convert_fusion.10), channel_id=1, source_target_pairs={{0,2},{2,0},{4,6},{6,4},{8,10},{10,8},{12,14},{14,12},{1,3},{3,1},... | collective-permute-start | bytes 3145736 | tf_op jit(solution)/shard_map/ppermute | solution.py:628
  589.0 48.0 %collective-permute-start.55 = (bf16[256,2048]{1,0:T(8,128)(2,1)}, bf16[256,2048]{1,0:T(8,128)(2,1)}, u32[]{:S(2)}, u32[]{:S(2)}) collective-permute-start(bf16[256,2048]{1,0:T(8,128)(2,1)} %convolution_convert_fusion.9), channel_id=1, source_target_pairs={{0,2},{2,0},{4,6},{6,4},{8,10},{10,8},{12,14},{14,12},{1,3},{3,1},... | collective-permute-start | bytes 3145736 | tf_op jit(solution)/shard_map/ppermute | solution.py:628
  723.8 164.1 %reduce-scatter.10.cloned.1.call-start = ((), (), s32[]{:S(2)}) async-start(), calls=%async_computation.13 | async-start | bytes 5242880 | tf_op jit(solution)/shard_map/reduce_scatter | solution.py:1803
  748.6 369.7 %reduce-scatter.12.cloned.1.call-start = ((), (), s32[]{:S(2)}) async-start(), calls=%async_computation.14 | async-start | bytes 5242880 | tf_op jit(solution)/shard_map/reduce_scatter | solution.py:1803
  789.2 32.1 %collective-permute-start.67 = (bf16[64,2048]{1,0:T(8,128)(2,1)S(1)}, bf16[64,2048]{1,0:T(8,128)(2,1)S(1)}, u32[]{:S(2)}, u32[]{:S(2)}) collective-permute-start(bf16[64,2048]{1,0:T(8,128)(2,1)S(1)} %multiply_convert_fusion.14), channel_id=1, source_target_pairs={{0,1},{1,0},{2,3},{3,2},{4,5},{5,4},{6,7},{7,6},{8,9},{9,8},{10,11... | collective-permute-start | bytes 786440 | tf_op jit(solution)/shard_map/ppermute | solution.py:632
  823.2 35.0 %collective-permute-start.82 = (bf16[2,128,2048]{2,1,0:T(8,128)(2,1)S(1)}, bf16[2,128,2048]{2,1,0:T(8,128)(2,1)S(1)}, u32[]{:S(2)}, u32[]{:S(2)}) collective-permute-start(bf16[2,128,2048]{2,1,0:T(8,128)(2,1)S(1)} %pad_maximum_fusion.86), channel_id=1, source_target_pairs={{0,8},{2,10},{4,12},{6,14},{8,0},{10,2},{12,4},{14,6},{1,9},{3,11}... | collective-permute-start | bytes 3145736 | tf_op jit(solution)/shard_map/ppermute | solution.py:628
  825.4 99.4 %collective-permute-start.84 = (bf16[2,64,2048]{2,1,0:T(8,128)(2,1)}, bf16[2,64,2048]{2,1,0:T(8,128)(2,1)}, u32[]{:S(2)}, u32[]{:S(2)}) collective-permute-start(bf16[2,64,2048]{2,1,0:T(8,128)(2,1)} %pad_maximum_fusion.110), channel_id=1, source_target_pairs={{0,1},{1,0},{2,3},{3,2},{4,5},{5,4},{6,7},{7,6},{8,9},{9,8},{10,11... | collective-permute-start | bytes 1572872 | tf_op jit(solution)/shard_map/ppermute | solution.py:632
  875.3 304.0 %reduce-scatter.14.cloned.1.call-start = ((), (), s32[]{:S(2)}) async-start(), calls=%async_computation.15 | async-start | bytes 4866048 | tf_op jit(solution)/shard_map/reduce_scatter | solution.py:1897
  961.7 343.0 %reduce-scatter.20.cloned.1.call-start = ((), (), s32[]{:S(2)}) async-start(), calls=%async_computation.18 | async-start | bytes 327680 | tf_op jit(solution)/shard_map/reduce_scatter | solution.py:1803
  965.9 43.1 %collective-permute-start.89 = (bf16[2,256,4480]{2,1,0:T(8,128)(2,1)}, bf16[2,256,4480]{2,1,0:T(8,128)(2,1)}, u32[]{:S(2)}, u32[]{:S(2)}) collective-permute-start(bf16[2,256,4480]{2,1,0:T(8,128)(2,1)} %convolution_convert_fusion.refs_2_), channel_id=1, source_target_pairs={{0,2},{2,0},{4,6},{6,4},{8,10},{10,8},{12,14},{14,12},{1,3},{3,1},... | collective-permute-start | bytes 13762568 | tf_op jit(solution)/shard_map/ppermute | solution.py:628
  986.4 34.9 %collective-permute-start.85 = (bf16[2,256,4480]{2,1,0:T(8,128)(2,1)}, bf16[2,256,4480]{2,1,0:T(8,128)(2,1)}, u32[]{:S(2)}, u32[]{:S(2)}) collective-permute-start(bf16[2,256,4480]{2,1,0:T(8,128)(2,1)} %convolution_convert_fusion.1.refs_1_), channel_id=1, source_target_pairs={{0,2},{2,0},{4,6},{6,4},{8,10},{10,8},{12,14},{14,12},{1,3},{3,1},... | collective-permute-start | bytes 13762568 | tf_op jit(solution)/shard_map/ppermute | solution.py:628
  992.3 312.4 %reduce-scatter.18.cloned.1.call-start = ((), (), s32[]{:S(2)}) async-start(), calls=%async_computation.17 | async-start | bytes 5242880 | tf_op jit(solution)/shard_map/reduce_scatter | solution.py:1803
  1018.7 52.0 %collective-permute-start.90 = (bf16[2,128,4480]{2,1,0:T(8,128)(2,1)}, bf16[2,128,4480]{2,1,0:T(8,128)(2,1)S(1)}, u32[]{:S(2)}, u32[]{:S(2)}) collective-permute-start(bf16[2,128,4480]{2,1,0:T(8,128)(2,1)} %dynamic-slice_convert_fusion), channel_id=1, source_target_pairs={{0,8},{2,10},{4,12},{6,14},{8,0},{10,2},{12,4},{14,6},{1,9},{3,11}... | collective-permute-start | bytes 6881288 | tf_op jit(solution)/shard_map/ppermute | solution.py:628
  1034.7 53.0 %collective-permute-start.86 = (bf16[2,128,4480]{2,1,0:T(8,128)(2,1)}, bf16[2,128,4480]{2,1,0:T(8,128)(2,1)}, u32[]{:S(2)}, u32[]{:S(2)}) collective-permute-start(bf16[2,128,4480]{2,1,0:T(8,128)(2,1)} %dynamic-slice_convert_fusion.1), channel_id=1, source_target_pairs={{0,4},{2,6},{4,0},{6,2},{8,12},{10,14},{12,8},{14,10},{1,5},{3,7},... | collective-permute-start | bytes 6881288 | tf_op jit(solution)/shard_map/ppermute | solution.py:628
  1039.2 274.1 %reduce-scatter.16.cloned.1.call-start = ((), (), s32[]{:S(2)}) async-start(), calls=%async_computation.16 | async-start | bytes 4866048 | tf_op jit(solution)/shard_map/reduce_scatter | solution.py:1897
  1074.3 36.9 %collective-permute-start.91 = (bf16[2,64,4480]{2,1,0:T(8,128)(2,1)S(1)}, bf16[2,64,4480]{2,1,0:T(8,128)(2,1)S(1)}, u32[]{:S(2)}, u32[]{:S(2)}) collective-permute-start(bf16[2,64,4480]{2,1,0:T(8,128)(2,1)S(1)} %dynamic-slice_convert_fusion.2), channel_id=1, source_target_pairs={{0,4},{2,6},{4,0},{6,2},{8,12},{10,14},{12,8},{14,10},{1,5},{3,7},... | collective-permute-start | bytes 3440648 | tf_op jit(solution)/shard_map/ppermute | solution.py:628
  1126.4 27.7 %collective-permute-start.92 = (bf16[64,4480]{1,0:T(8,128)(2,1)}, bf16[64,4480]{1,0:T(8,128)(2,1)}, u32[]{:S(2)}, u32[]{:S(2)}) collective-permute-start(bf16[64,4480]{1,0:T(8,128)(2,1)} %constant_dynamic-update-slice_fusion.46), channel_id=1, source_target_pairs={{0,1},{1,0},{2,3},{3,2},{4,5},{5,4},{6,7},{7,6},{8,9},{9,8},{10,11... | collective-permute-start | bytes 1720328 | tf_op jit(solution)/shard_map/ppermute | solution.py:632
  1130.6 35.7 %collective-permute-start.88 = (bf16[64,4480]{1,0:T(8,128)(2,1)}, bf16[64,4480]{1,0:T(8,128)(2,1)}, u32[]{:S(2)}, u32[]{:S(2)}) collective-permute-start(bf16[64,4480]{1,0:T(8,128)(2,1)} %constant_dynamic-update-slice_fusion.41), channel_id=1, source_target_pairs={{0,1},{1,0},{2,3},{3,2},{4,5},{5,4},{6,7},{7,6},{8,9},{9,8},{10,11... | collective-permute-start | bytes 1720328 | tf_op jit(solution)/shard_map/ppermute | solution.py:632
  1143.6 42.0 %collective-permute-start.96 = (bf16[1408,256]{1,0:T(8,128)(2,1)}, bf16[1408,256]{1,0:T(8,128)(2,1)}, u32[]{:S(2)}, u32[]{:S(2)}) collective-permute-start(bf16[1408,256]{1,0:T(8,128)(2,1)} %dynamic-slice_convert_fusion.6), channel_id=1, source_target_pairs={{0,2},{2,0},{4,6},{6,4},{8,10},{10,8},{12,14},{14,12},{1,3},{3,1},... | collective-permute-start | bytes 2162696 | tf_op jit(solution)/shard_map/ppermute | solution.py:628
  1179.3 102.4 %collective-permute-start.101 = (bf16[1056,768]{1,0:T(8,128)(2,1)}, bf16[1056,768]{1,0:T(8,128)(2,1)S(1)}, u32[]{:S(2)}, u32[]{:S(2)}) collective-permute-start(bf16[1056,768]{1,0:T(8,128)(2,1)} %shard_map.613), channel_id=1, source_target_pairs={{0,1},{1,0},{2,3},{3,2},{4,5},{5,4},{6,7},{7,6},{8,9},{9,8},{10,11... | collective-permute-start | bytes 4866056 | tf_op jit(solution)/shard_map/ppermute | solution.py:632
  1211.1 26.4 %collective-permute-start.103 = (bf16[64,8192]{1,0:T(8,128)(2,1)}, bf16[64,8192]{1,0:T(8,128)(2,1)S(1)}, u32[]{:S(2)}, u32[]{:S(2)}) collective-permute-start(bf16[64,8192]{1,0:T(8,128)(2,1)} %shard_map.615), channel_id=1, source_target_pairs={{0,4},{2,6},{4,0},{6,2},{8,12},{10,14},{12,8},{14,10},{1,5},{3,7},... | collective-permute-start | bytes 3145736 | tf_op jit(solution)/shard_map/ppermute | solution.py:628
  1229.3 49.0 %collective-permute-start.100 = (bf16[128,8192]{1,0:T(8,128)(2,1)S(1)}, bf16[128,8192]{1,0:T(8,128)(2,1)S(1)}, u32[]{:S(2)}, u32[]{:S(2)}) collective-permute-start(bf16[128,8192]{1,0:T(8,128)(2,1)S(1)} %pad_maximum_fusion.36), channel_id=1, source_target_pairs={{0,4},{2,6},{4,0},{6,2},{8,12},{10,14},{12,8},{14,10},{1,5},{3,7},... | collective-permute-start | bytes 6291464 | tf_op jit(solution)/shard_map/ppermute | solution.py:628
  1239.6 43.3 %collective-permute-start.104 = (bf16[128,8192]{1,0:T(8,128)(2,1)}, bf16[128,8192]{1,0:T(8,128)(2,1)}, u32[]{:S(2)}, u32[]{:S(2)}) collective-permute-start(bf16[128,8192]{1,0:T(8,128)(2,1)} %pad_maximum_fusion.37), channel_id=1, source_target_pairs={{0,8},{2,10},{4,12},{6,14},{8,0},{10,2},{12,4},{14,6},{1,9},{3,11}... | collective-permute-start | bytes 6291464 | tf_op jit(solution)/shard_map/ppermute | solution.py:628
  1298.3 31.3 %collective-permute-start.106 = (bf16[2,128,384]{2,1,0:T(8,128)(2,1)}, bf16[2,128,384]{2,1,0:T(8,128)(2,1)}, u32[]{:S(2)}, u32[]{:S(2)}) collective-permute-start(bf16[2,128,384]{2,1,0:T(8,128)(2,1)} %shard_map.617), channel_id=1, source_target_pairs={{0,1},{1,0},{2,3},{3,2},{4,5},{5,4},{6,7},{7,6},{8,9},{9,8},{10,11... | collective-permute-start | bytes 589832 | tf_op jit(solution)/shard_map/ppermute | solution.py:632
  1299.6 41.8 %collective-permute-start.108 = (f32[352,256]{1,0:T(8,128)}, f32[352,256]{1,0:T(8,128)S(1)}, u32[]{:S(2)}, u32[]{:S(2)}) collective-permute-start(f32[352,256]{1,0:T(8,128)} %shard_map.618), channel_id=1, source_target_pairs={{0,1},{1,0},{2,3},{3,2},{4,5},{5,4},{6,7},{7,6},{8,9},{9,8},{10,11... | collective-permute-start | bytes 1081352 | tf_op jit(solution)/shard_map/ppermute | solution.py:632
  1302.2 43.4 %collective-permute-start.110 = (bf16[256,1024]{1,0:T(8,128)(2,1)}, bf16[256,1024]{1,0:T(8,128)(2,1)}, u32[]{:S(2)}, u32[]{:S(2)}) collective-permute-start(bf16[256,1024]{1,0:T(8,128)(2,1)} %constant_dynamic-slice_fusion.2), channel_id=1, source_target_pairs={{0,16},{16,0},{1,17},{17,1},{2,18},{18,2},{3,19},{19,3},{4,20},{20... | collective-permute-start | bytes 1572872 | tf_op jit(solution)/shard_map/ppermute | solution.py:636
  1348.5 37.0 %collective-permute-start.111 = (bf16[256,512]{1,0:T(8,128)(2,1)}, bf16[256,512]{1,0:T(8,128)(2,1)}, u32[]{:S(2)}, u32[]{:S(2)}) collective-permute-start(bf16[256,512]{1,0:T(8,128)(2,1)} %dynamic-slice_convert_fusion.22), channel_id=1, source_target_pairs={{0,1},{1,0},{2,3},{3,2},{4,5},{5,4},{6,7},{7,6},{8,9},{9,8},{10,11... | collective-permute-start | bytes 786440 | tf_op jit(solution)/shard_map/ppermute | solution.py:632
  1351.0 67.7 %collective-permute-start.119 = (bf16[4,128,384]{2,1,0:T(8,128)(2,1)}, bf16[4,128,384]{2,1,0:T(8,128)(2,1)}, u32[]{:S(2)}, u32[]{:S(2)}) collective-permute-start(bf16[4,128,384]{2,1,0:T(8,128)(2,1)} %pad_maximum_fusion.118), channel_id=1, source_target_pairs={{0,2},{2,0},{4,6},{6,4},{8,10},{10,8},{12,14},{14,12},{1,3},{3,1},... | collective-permute-start | bytes 1179656 | tf_op jit(solution)/shard_map/ppermute | solution.py:628
  1358.9 48.7 %collective-permute-start.120 = (bf16[352,256]{1,0:T(8,128)(2,1)S(1)}, bf16[352,256]{1,0:T(8,128)(2,1)}, u32[]{:S(2)}, u32[]{:S(2)}) collective-permute-start(bf16[352,256]{1,0:T(8,128)(2,1)S(1)} %get-tuple-element.258), channel_id=1, source_target_pairs={{0,8},{2,10},{4,12},{6,14},{8,0},{10,2},{12,4},{14,6},{1,9},{3,11}... | collective-permute-start | bytes 540680 | tf_op jit(solution)/shard_map/ppermute | solution.py:628
  (510 other events, 3994.1 us)
Sparse Core Ops, SparseCore 0:
  252.1 46.1 all-gather.5
  300.4 44.7 all-gather.7
  346.7 83.0 all-gather.9
  431.3 78.9 all-gather.11
  511.7 44.4 all-gather.13
  723.9 51.1 reduce-scatter.7
  778.1 98.5 reduce-scatter.9
  879.6 78.8 reduce-scatter.11
  961.7 82.4 reduce-scatter.13
  1047.0 18.6 reduce-scatter.19
  1068.0 87.3 reduce-scatter.17
  1211.2 80.3 reduce-scatter.15
